TPU v7x, 32 devices: a whole 2x2x4 slice. The times are simulated.
32 devices in a mesh: row: 2 (over core), bulk: 16 (over z, y, x).
Axes of the slice: x: 2, y: 2, z: 4, core: 2. Of those that a mesh axis runs over, the one named last changes fastest.
Arguments:
- residual_in: float32 [512, 16384], P('row', 'bulk'), may hold values from -6 to 6
- amplitudes: float32 [512, 2048], P('row', 'bulk'), may hold values from -6 to 6
- integral_tiles: float32 [256, 128, 128], P('bulk', 'row'), may hold values from -0.375 to 0.375
- tile_reader: int32 [256, 1], P('bulk'), may hold values from 0 to 15; in each aligned block of 16 rows (0 to 15, 16 to 31, ...) at most 2 rows name the same one
- tile_k: int32 [256], P('bulk'), may hold values from 0 to 15
- tile_column: int32 [256], P('bulk'), may hold values from 0 to 7
Outputs:
- residual_out: float32 [512, 16384], P('row', 'bulk')
Inputs may be any that keep to these rules, and one draw needn't show every extreme that they name: `tile_reader`: among the 16 tiles stored on one index of bulk (aligned blocks of 16 entries), at most 2 name the same reader; some block has exactly 2 for some reader.
All inputs are finite; a program needn't handle non-finite values.
Results may differ from a plain program's by a relative error of at most 0.0003.
Values sent between devices are 32-bit elements; how exact they have to be, the bound alone decides.
No kernel may reach another device: no remote copies, remote signals or barrier semaphores. Data moves between devices by JAX's collectives and lax.ppermute only.
A program may use at most 64 MiB of HBM per device.

v0:
```python
import functools

import jax
import jax.numpy as jnp
from jax import lax
from jax.experimental import pallas as pl
from jax.experimental.pallas import tpu as pltpu
from jax.sharding import PartitionSpec as P

KT = 16
CT = 8
SLOT = 2
GROUPS = 4
META = 8


def pack_kernel(reader_ref, k_ref, column_ref, tiles_ref, out_ref, count_ref):
    count, height, _ = tiles_ref.shape
    targets = out_ref.shape[0]
    me = lax.axis_index("bulk")
    out_ref[:, SLOT * height :, :] = jnp.full((targets, META, out_ref.shape[2]), -1.0, jnp.float32)
    for target in range(targets):
        count_ref[target] = 0
    lane = lax.broadcasted_iota(jnp.int32, (META, out_ref.shape[2]), 1)

    def place(j, carry):
        target = jnp.bitwise_xor(reader_ref[j, 0], me)
        slot = count_ref[target]
        count_ref[target] = slot + 1
        out_ref[target, pl.ds(pl.multiple_of(slot * height, height), height), :] = tiles_ref[j]
        code = (k_ref[j] * CT + column_ref[j]).astype(jnp.float32)
        codes = out_ref[target, SLOT * height :, :]
        out_ref[target, SLOT * height :, :] = jnp.where(lane == slot, code, codes)
        return carry

    lax.fori_loop(0, count, place, 0)


def pack(tiles, readers, tile_k, tile_column, targets):
    _, height, width = tiles.shape
    smem = pl.BlockSpec(memory_space=pltpu.SMEM)
    vmem = pl.BlockSpec(memory_space=pltpu.VMEM)
    return pl.pallas_call(
        pack_kernel,
        out_shape=jax.ShapeDtypeStruct((targets, SLOT * height + META, width), jnp.float32),
        in_specs=[smem, smem, smem, vmem],
        out_specs=vmem,
        scratch_shapes=[pltpu.SMEM((targets,), jnp.int32)],
        cost_estimate=pl.CostEstimate(flops=0, bytes_accessed=4 * tiles.size * 3, transcendentals=0),
    )(readers, tile_k, tile_column, tiles)


def contract_kernel(positions, groups_count, parts_count, *refs):
    pieces = refs[: len(positions)]
    end = len(positions) + groups_count * parts_count
    groups = [
        refs[len(positions) + g * parts_count : len(positions) + (g + 1) * parts_count]
        for g in range(groups_count)
    ]
    residual_ref, out_ref, split_ref = refs[end : end + 3]
    codes = refs[end + 3 : end + 3 + groups_count]
    sem = refs[-1]
    height = (groups[0][0].shape[1] - META) // SLOT
    width = groups[0][0].shape[2]
    row = lax.axis_index("row")
    me = lax.axis_index("bulk")
    fetches = [
        pltpu.make_async_copy(parts[0].at[:, pl.ds(SLOT * height, META), :], codes[g], sem.at[g])
        for g, parts in enumerate(groups)
    ]
    for fetch in fetches:
        fetch.start()
    for piece, held in zip(pieces, positions):
        for at, position in enumerate(held):
            block = piece[at]
            high = block.astype(jnp.bfloat16)
            low = (block - high.astype(jnp.float32)).astype(jnp.bfloat16)
            k = at if position is None else jnp.bitwise_xor(me, position)
            split_ref[k] = jnp.concatenate([high, low], axis=1)
    out_ref[...] = residual_ref[...]
    for fetch in fetches:
        fetch.wait()

    def add_group(parts, codes_ref):
        def add(owner, carry):
            for slot in range(SLOT):
                code = codes_ref[owner, 0, slot].astype(jnp.int32)

                @pl.when(code >= 0)
                def _():
                    k = code // CT
                    column = code - k * CT
                    ordered = []
                    for place in range(parts_count):
                        piece = parts[0][owner, slot * height : (slot + 1) * height, :]
                        for q in range(1, parts_count):
                            other = parts[q][owner, slot * height : (slot + 1) * height, :]
                            piece = jnp.where(lax.rem(place + q, parts_count) == row, other, piece)
                        ordered.append(piece)
                    tile = jnp.concatenate(ordered, axis=0)
                    high = tile.astype(jnp.bfloat16)
                    low = (tile - high.astype(jnp.float32)).astype(jnp.bfloat16)
                    both = jnp.concatenate([high, low], axis=1)
                    weights = jnp.concatenate([both, both], axis=0)
                    product = jnp.dot(split_ref[k], weights, preferred_element_type=jnp.float32)
                    lanes = pl.ds(pl.multiple_of(column * width, width), width)
                    out_ref[:, lanes] += product[:, :width] + product[:, width:]

            return carry

        lax.fori_loop(0, parts[0].shape[0], add, 0)

    for parts, codes_ref in zip(groups, codes):
        add_group(parts, codes_ref)


def contract(pieces, positions, groups, residual):
    rows = residual.shape[0]
    width = groups[0][0].shape[2]
    vmem = pl.BlockSpec(memory_space=pltpu.VMEM)
    arrays = [*pieces, *[part for parts in groups for part in parts], residual]
    return pl.pallas_call(
        functools.partial(contract_kernel, positions, len(groups), len(groups[0])),
        out_shape=jax.ShapeDtypeStruct(residual.shape, jnp.float32),
        in_specs=[vmem] * len(arrays),
        out_specs=vmem,
        scratch_shapes=[
            pltpu.VMEM((KT, rows, 2 * width), jnp.bfloat16),
            *[pltpu.SMEM((parts[0].shape[0], META, width), jnp.float32) for parts in groups],
            pltpu.SemaphoreType.DMA((len(groups),)),
        ],
        compiler_params=pltpu.CompilerParams(vmem_limit_bytes=40 * 1024 * 1024),
    )(*arrays)


def send(x, axis, partner):
    size = lax.axis_size(axis)
    return lax.ppermute(x, axis, [(i, partner(i)) for i in range(size)])


def gather(block, axis):
    size = lax.axis_size(axis)
    held, at = block[None], [0]
    bit = size // 2
    while bit > 2:
        come = send(held, axis, lambda i, b=bit: i ^ b)
        if bit > 4:
            held, at = jnp.concatenate([held, come], axis=0), at + [p ^ bit for p in at]
        else:
            late, late_at = come, [p ^ bit for p in at]
        bit //= 2
    out, out_at = [], []
    for part, part_at, first, second in ((held, at, 2, 1), (late, late_at, 1, 2)):
        come = send(part, axis, lambda i: i ^ first)
        whole, whole_at = jnp.concatenate([part, come], axis=0), part_at + [p ^ first for p in part_at]
        out += [whole, send(whole, axis, lambda i: i ^ second)]
        out_at += [tuple(whole_at), tuple(p ^ second for p in whole_at)]
    return out, out_at


def local(residual_in, amplitudes, integral_tiles, tile_reader, tile_k, tile_column):
    targets = lax.axis_size("bulk")
    rows_axis = lax.axis_size("row")
    width = integral_tiles.shape[2]
    outgoing = pack(integral_tiles, tile_reader, tile_k, tile_column, targets)
    pieces, positions = gather(amplitudes, "bulk")
    half = targets // 2
    order = [p for near in range(half) for p in (near + half, near) if p]
    arrived = {0: outgoing[0]}
    for p in order:
        arrived[p] = send(outgoing[p], "bulk", lambda i: i ^ p)
    members = [0] + order
    size = targets // GROUPS
    groups = []
    for g in range(GROUPS):
        mine = jnp.stack([arrived[p] for p in members[g * size : (g + 1) * size]])
        groups.append(
            [mine] + [send(mine, "row", lambda i: (i + q) % rows_axis) for q in range(1, rows_axis)]
        )
    if amplitudes.shape[1] != width:
        stacked = jnp.concatenate(pieces, axis=0)
        listed = [p for held in positions for p in held]
        place = jnp.asarray([listed.index(p) for p in range(targets)], jnp.int32)
        wanted = jnp.bitwise_xor(jnp.arange(targets, dtype=jnp.int32), lax.axis_index("bulk"))
        stacked = stacked[place[wanted]]
        stacked = stacked.transpose(1, 0, 2).reshape(amplitudes.shape[0], KT, width).transpose(1, 0, 2)
        pieces, positions = [stacked], [(None,) * KT]
    return contract(pieces, positions, groups, residual_in)


def solution(mesh):
    placed = (
        P("row", "bulk"),
        P("row", "bulk"),
        P("bulk", "row", None),
        P("bulk", None),
        P("bulk"),
        P("bulk"),
    )
    return jax.shard_map(
        local, mesh=mesh, in_specs=placed, out_specs=P("row", "bulk"), check_vma=False
    )
```

profile of v0, /device:TPU:0, one launch (start us, length us, event | category | flops | bytes accessed | tf_op | source)
XLA Modules:
  0.0 69.9 jit_solution(11015488312648469904)
XLA Ops:
  0.0 0.0 copy-start.1
  0.0 4.0 %collective-permute-start = (f32[1,256,128]{2,1,0:T(8,128)}, f32[1,256,128]{2,1,0:T(8,128)S(1)}, u32[]{:S(2)}, u32[]{:S(2)}) collective-permute-start(f32[1,256,128]{2,1,0:T(8,128)} %bitcast.46), channel_id=1, source_target_pairs={{0,8},{1,9},{2,10},{3,11},{4,12},{5,13},{6,14},{7,15},{8,0},{9,1},... | collective-permute-start | bytes 393224 | tf_op jit(solution)/shard_map/ppermute | solution.py:138
  4.0 1.3 %copy.7.reader_ref = s32[16,1]{1,0:T(8,128)} copy(s32[16,1]{0,1:T(1,128)} %param.9) | data formatting | bytes 128 | tf_op args[3]
  5.4 2.3 %shard_map.64 = f32[16,136,128]{2,1,0:T(8,128)} custom-call(s32[16,1]{1,0:T(8,128)} %copy.7.reader_ref, s32[16]{0:T(128)} %k_ref.1, s32[16]{0:T(128)} %column_ref.1, f32[16,64,128]{2,1,0:T(8,128)} %tiles_ref.1), custom_call_target="tpu_custom_call" | custom-call | bytes 1572864 | tf_op jit(solution)/shard_map/pallas_call | solution.py:43
  7.7 2.9 %collective-permute-done = f32[1,256,128]{2,1,0:T(8,128)S(1)} collective-permute-done((f32[1,256,128]{2,1,0:T(8,128)}, f32[1,256,128]{2,1,0:T(8,128)S(1)}, u32[]{:S(2)}, u32[]{:S(2)}) %collective-permute-start) | collective-permute-done | bytes 131104 | tf_op jit(solution)/shard_map/ppermute | solution.py:138
  10.6 0.0 copy-done.1
  10.6 0.8 %collective-permute-start.3 = (f32[2,256,128]{2,1,0:T(8,128)S(1)}, f32[2,256,128]{2,1,0:T(8,128)S(1)}, u32[]{:S(2)}, u32[]{:S(2)}) collective-permute-start(f32[2,256,128]{2,1,0:T(8,128)S(1)} %pad_maximum_fusion.5), channel_id=1, source_target_pairs={{0,4},{1,5},{2,6},{3,7},{4,0},{5,1},{6,2},{7,3},{8,12},{9,13},{10,... | collective-permute-start | bytes 786440 | tf_op jit(solution)/shard_map/ppermute | solution.py:138
  11.5 1.5 %collective-permute-start.1 = (f32[2,256,128]{2,1,0:T(8,128)S(1)}, f32[2,256,128]{2,1,0:T(8,128)S(1)}, u32[]{:S(2)}, u32[]{:S(2)}) collective-permute-start(f32[2,256,128]{2,1,0:T(8,128)S(1)} %pad_maximum_fusion.5), channel_id=1, source_target_pairs={{0,2},{1,3},{2,0},{3,1},{4,6},{5,7},{6,4},{7,5},{8,10},{9,11},{10,... | collective-permute-start | bytes 786440 | tf_op jit(solution)/shard_map/ppermute | solution.py:138
  13.0 1.4 %slice_bitcast_fusion.3 = (f32[136,128]{1,0:T(8,128)S(1)}, f32[136,128]{1,0:T(8,128)S(1)}, f32[136,128]{1,0:T(8,128)S(1)}, f32[136,128]{1,0:T(8,128)S(1)}, f32[1...) fusion(f32[16,136,128]{2,1,0:T(8,128)} %shard_map.64), kind=kLoop, calls=%fused_computation.9 | loop fusion | bytes 2228224 | tf_op jit(solution)/shard_map/squeeze | solution.py:171
  14.4 1.6 %collective-permute-start.8 = (f32[136,128]{1,0:T(8,128)S(1)}, f32[136,128]{1,0:T(8,128)S(1)}, u32[]{:S(2)}, u32[]{:S(2)}) collective-permute-start(f32[136,128]{1,0:T(8,128)S(1)} %get-tuple-element.17), channel_id=1, source_target_pairs={{0,1},{1,0},{2,3},{3,2},{4,5},{5,4},{6,7},{7,6},{8,9},{9,8},{10,11... | collective-permute-start | bytes 208904 | tf_op jit(solution)/shard_map/ppermute | solution.py:138
  15.9 3.2 %collective-permute-start.7 = (f32[136,128]{1,0:T(8,128)S(1)}, f32[136,128]{1,0:T(8,128)S(1)}, u32[]{:S(2)}, u32[]{:S(2)}) collective-permute-start(f32[136,128]{1,0:T(8,128)S(1)} %get-tuple-element.18), channel_id=1, source_target_pairs={{0,9},{1,8},{2,11},{3,10},{4,13},{5,12},{6,15},{7,14},{8,1},{9,0},... | collective-permute-start | bytes 208904 | tf_op jit(solution)/shard_map/ppermute | solution.py:138
  19.2 0.0 collective-permute-start.6
  19.2 0.0 collective-permute-done.8
  19.2 2.4 %collective-permute-start.20 = (f32[136,128]{1,0:T(8,128)S(1)}, f32[136,128]{1,0:T(8,128)S(1)}, u32[]{:S(2)}, u32[]{:S(2)}) collective-permute-start(f32[136,128]{1,0:T(8,128)S(1)} %get-tuple-element.5), channel_id=1, source_target_pairs={{0,14},{1,15},{2,12},{3,13},{4,10},{5,11},{6,8},{7,9},{8,6},{9,7},... | collective-permute-start | bytes 208904 | tf_op jit(solution)/shard_map/ppermute | solution.py:138
  21.6 5.0 %collective-permute-done.7 = f32[136,128]{1,0:T(8,128)S(1)} collective-permute-done((f32[136,128]{1,0:T(8,128)S(1)}, f32[136,128]{1,0:T(8,128)S(1)}, u32[]{:S(2)}, u32[]{:S(2)}) %collective-permute-start.7) | collective-permute-done | bytes 69664 | tf_op jit(solution)/shard_map/ppermute | solution.py:138
  26.6 0.0 collective-permute-start.23
  26.6 0.9 %collective-permute-done.6 = f32[136,128]{1,0:T(8,128)S(1)} collective-permute-done((f32[136,128]{1,0:T(8,128)S(1)}, f32[136,128]{1,0:T(8,128)S(1)}, u32[]{:S(2)}, u32[]{:S(2)}) %collective-permute-start.6) | collective-permute-done | bytes 69664 | tf_op jit(solution)/shard_map/ppermute | solution.py:138
  27.6 0.4 collective-permute-start.18
  28.0 0.0 collective-permute-done.3
  28.0 0.6 collective-permute-start.4
  28.6 0.0 collective-permute-done.1
  28.7 5.5 %collective-permute-start.17 = (f32[136,128]{1,0:T(8,128)S(1)}, f32[136,128]{1,0:T(8,128)S(1)}, u32[]{:S(2)}, u32[]{:S(2)}) collective-permute-start(f32[136,128]{1,0:T(8,128)S(1)} %get-tuple-element.10), channel_id=1, source_target_pairs={{0,13},{1,12},{2,15},{3,14},{4,9},{5,8},{6,11},{7,10},{8,5},{9,4},... | collective-permute-start | bytes 208904 | tf_op jit(solution)/shard_map/ppermute | solution.py:138
  34.1 0.1 pad_maximum_fusion.refs_0_
  34.2 0.0 collective-permute-done.20
  34.2 0.1 collective-permute-start.16
  34.3 0.0 collective-permute-done.23
  34.3 2.6 %collective-permute-start.15 = (f32[136,128]{1,0:T(8,128)S(1)}, f32[136,128]{1,0:T(8,128)S(1)}, u32[]{:S(2)}, u32[]{:S(2)}) collective-permute-start(f32[136,128]{1,0:T(8,128)S(1)} %get-tuple-element.12), channel_id=1, source_target_pairs={{0,12},{1,13},{2,14},{3,15},{4,8},{5,9},{6,10},{7,11},{8,4},{9,5},... | collective-permute-start | bytes 208904 | tf_op jit(solution)/shard_map/ppermute | solution.py:138
  36.9 0.0 collective-permute-done.18
  36.9 0.0 copy-start
  36.9 0.1 collective-permute-start.13
  37.0 1.8 %collective-permute-done.4 = f32[2,256,128]{2,1,0:T(8,128)S(1)} collective-permute-done((f32[2,256,128]{2,1,0:T(8,128)S(1)}, f32[2,256,128]{2,1,0:T(8,128)S(1)}, u32[]{:S(2)}, u32[]{:S(2)}) %collective-permute-start.4) | collective-permute-done | bytes 262176 | tf_op jit(solution)/shard_map/ppermute | solution.py:138
  38.8 2.0 %collective-permute-start.12 = (f32[136,128]{1,0:T(8,128)S(1)}, f32[136,128]{1,0:T(8,128)S(1)}, u32[]{:S(2)}, u32[]{:S(2)}) collective-permute-start(f32[136,128]{1,0:T(8,128)S(1)} %get-tuple-element.14), channel_id=1, source_target_pairs={{0,11},{1,10},{2,9},{3,8},{4,15},{5,14},{6,13},{7,12},{8,3},{9,2},... | collective-permute-start | bytes 208904 | tf_op jit(solution)/shard_map/ppermute | solution.py:138
  40.9 0.0 collective-permute-done.17
  40.9 2.6 %collective-permute-start.11 = (f32[136,128]{1,0:T(8,128)S(1)}, f32[136,128]{1,0:T(8,128)S(1)}, u32[]{:S(2)}, u32[]{:S(2)}) collective-permute-start(f32[136,128]{1,0:T(8,128)S(1)} %get-tuple-element.15), channel_id=1, source_target_pairs={{0,2},{1,3},{2,0},{3,1},{4,6},{5,7},{6,4},{7,5},{8,10},{9,11},{10,... | collective-permute-start | bytes 208904 | tf_op jit(solution)/shard_map/ppermute | solution.py:138
  43.5 0.0 collective-permute-done.16
  43.5 1.4 %collective-permute-start.10 = (f32[136,128]{1,0:T(8,128)S(1)}, f32[136,128]{1,0:T(8,128)S(1)}, u32[]{:S(2)}, u32[]{:S(2)}) collective-permute-start(f32[136,128]{1,0:T(8,128)S(1)} %get-tuple-element.16), channel_id=1, source_target_pairs={{0,10},{1,11},{2,8},{3,9},{4,14},{5,15},{6,12},{7,13},{8,2},{9,3},... | collective-permute-start | bytes 208904 | tf_op jit(solution)/shard_map/ppermute | solution.py:138
  44.9 0.0 collective-permute-done.15
  44.9 0.0 collective-permute-start.9
  44.9 0.0 collective-permute-done.13
  44.9 1.1 %collective-permute-start.2 = (f32[4,256,128]{2,1,0:T(8,128)S(1)}, f32[4,256,128]{2,1,0:T(8,128)S(1)}, u32[]{:S(2)}, u32[]{:S(2)}) collective-permute-start(f32[4,256,128]{2,1,0:T(8,128)S(1)} %pad_maximum_fusion.refs_0_), channel_id=1, source_target_pairs={{0,1},{1,0},{2,3},{3,2},{4,5},{5,4},{6,7},{7,6},{8,9},{9,8},{10,11... | collective-permute-start | bytes 1572872 | tf_op jit(solution)/shard_map/ppermute | solution.py:138
  46.0 1.8 %collective-permute-done.12 = f32[136,128]{1,0:T(8,128)S(1)} collective-permute-done((f32[136,128]{1,0:T(8,128)S(1)}, f32[136,128]{1,0:T(8,128)S(1)}, u32[]{:S(2)}, u32[]{:S(2)}) %collective-permute-start.12) | collective-permute-done | bytes 69664 | tf_op jit(solution)/shard_map/ppermute | solution.py:138
  47.8 0.9 %collective-permute-start.5 = (f32[4,256,128]{2,1,0:T(8,128)S(1)}, f32[4,256,128]{2,1,0:T(8,128)S(1)}, u32[]{:S(2)}, u32[]{:S(2)}) collective-permute-start(f32[4,256,128]{2,1,0:T(8,128)S(1)} %constant_dynamic-update-slice_fusion.refs_2_), channel_id=1, source_target_pairs={{0,2},{1,3},{2,0},{3,1},{4,6},{5,7},{6,4},{7,5},{8,10},{9,11},{10,... | collective-permute-start | bytes 1572872 | tf_op jit(solution)/shard_map/ppermute | solution.py:138
  48.7 0.0 collective-permute-done.11
  48.7 3.3 %collective-permute-start.22 = (f32[136,128]{1,0:T(8,128)S(1)}, f32[136,128]{1,0:T(8,128)S(1)}, u32[]{:S(2)}, u32[]{:S(2)}) collective-permute-start(f32[136,128]{1,0:T(8,128)S(1)} %get-tuple-element.7), channel_id=1, source_target_pairs={{0,15},{1,14},{2,13},{3,12},{4,11},{5,10},{6,9},{7,8},{8,7},{9,6},... | collective-permute-start | bytes 208904 | tf_op jit(solution)/shard_map/ppermute | solution.py:138
  52.1 0.0 collective-permute-done.10
  52.1 0.0 collective-permute-start.21
  52.1 5.0 %collective-permute-done.22 = f32[136,128]{1,0:T(8,128)S(1)} collective-permute-done((f32[136,128]{1,0:T(8,128)S(1)}, f32[136,128]{1,0:T(8,128)S(1)}, u32[]{:S(2)}, u32[]{:S(2)}) %collective-permute-start.22) | collective-permute-done | bytes 69664 | tf_op jit(solution)/shard_map/ppermute | solution.py:138
  57.1 0.0 collective-permute-start.14
  57.1 0.5 collective-permute-done.21
  57.6 0.0 collective-permute-start.19
  57.6 0.0 collective-permute-done.9.refs_5_
  57.6 0.6 collective-permute-start.24
  58.2 0.4 collective-permute-done.14.refs_7_
  58.6 0.5 collective-permute-done.19.refs_9_
  59.2 0.4 collective-permute-done.24.refs_11_
  59.6 1.2 %collective-permute-done.2.refs_1_ = f32[4,256,128]{2,1,0:T(8,128)S(1)} collective-permute-done((f32[4,256,128]{2,1,0:T(8,128)S(1)}, f32[4,256,128]{2,1,0:T(8,128)S(1)}, u32[]{:S(2)}, u32[]{:S(2)}) %collective-permute-start.2) | collective-permute-done | bytes 524320 | tf_op jit(solution)/shard_map/ppermute | solution.py:138
  60.8 3.0 %collective-permute-done.5.refs_3_ = f32[4,256,128]{2,1,0:T(8,128)S(1)} collective-permute-done((f32[4,256,128]{2,1,0:T(8,128)S(1)}, f32[4,256,128]{2,1,0:T(8,128)S(1)}, u32[]{:S(2)}, u32[]{:S(2)}) %collective-permute-start.5) | collective-permute-done | bytes 524320 | tf_op jit(solution)/shard_map/ppermute | solution.py:138
  63.7 0.0 copy-done
  63.7 6.2 %shard_map.65 = f32[256,1024]{1,0:T(8,128)} custom-call(f32[4,256,128]{2,1,0:T(8,128)S(1)} %pad_maximum_fusion.refs_0_, f32[4,256,128]{2,1,0:T(8,128)S(1)} %collective-permute-done.2.refs_1_, f32[4,256,128]{2,1,0:T(8,128)S(1)} %constant_dynamic-update-slice_fusion.refs_2_, f32[4,256,128]{2,1,0:T(8,128)S(1)} %collective-permute-done.5.refs_3_, ...), custom_call_target="tpu_custom_call" | custom-call | tf_op jit(solution)/shard_map/pallas_call | solution.py:122
  (7 shorter events, 0.1 us)
Async XLA Ops:
  0.0 10.6 %copy-start.1 = (f32[256,128]{1,0:T(8,128)S(1)}, f32[256,128]{1,0:T(8,128)}, u32[]{:S(2)}) copy-start(f32[256,128]{1,0:T(8,128)} %param.7) | copy-start | bytes 393220
  0.0 10.6 %collective-permute-start = (f32[1,256,128]{2,1,0:T(8,128)}, f32[1,256,128]{2,1,0:T(8,128)S(1)}, u32[]{:S(2)}, u32[]{:S(2)}) collective-permute-start(f32[1,256,128]{2,1,0:T(8,128)} %bitcast.46), channel_id=1, source_target_pairs={{0,8},{1,9},{2,10},{3,11},{4,12},{5,13},{6,14},{7,15},{8,0},{9,1},... | collective-permute-start | bytes 393224 | tf_op jit(solution)/shard_map/ppermute | solution.py:138
  10.6 17.4 %collective-permute-start.3 = (f32[2,256,128]{2,1,0:T(8,128)S(1)}, f32[2,256,128]{2,1,0:T(8,128)S(1)}, u32[]{:S(2)}, u32[]{:S(2)}) collective-permute-start(f32[2,256,128]{2,1,0:T(8,128)S(1)} %pad_maximum_fusion.5), channel_id=1, source_target_pairs={{0,4},{1,5},{2,6},{3,7},{4,0},{5,1},{6,2},{7,3},{8,12},{9,13},{10,... | collective-permute-start | bytes 786440 | tf_op jit(solution)/shard_map/ppermute | solution.py:138
  11.5 17.2 %collective-permute-start.1 = (f32[2,256,128]{2,1,0:T(8,128)S(1)}, f32[2,256,128]{2,1,0:T(8,128)S(1)}, u32[]{:S(2)}, u32[]{:S(2)}) collective-permute-start(f32[2,256,128]{2,1,0:T(8,128)S(1)} %pad_maximum_fusion.5), channel_id=1, source_target_pairs={{0,2},{1,3},{2,0},{3,1},{4,6},{5,7},{6,4},{7,5},{8,10},{9,11},{10,... | collective-permute-start | bytes 786440 | tf_op jit(solution)/shard_map/ppermute | solution.py:138
  14.4 4.8 %collective-permute-start.8 = (f32[136,128]{1,0:T(8,128)S(1)}, f32[136,128]{1,0:T(8,128)S(1)}, u32[]{:S(2)}, u32[]{:S(2)}) collective-permute-start(f32[136,128]{1,0:T(8,128)S(1)} %get-tuple-element.17), channel_id=1, source_target_pairs={{0,1},{1,0},{2,3},{3,2},{4,5},{5,4},{6,7},{7,6},{8,9},{9,8},{10,11... | collective-permute-start | bytes 208904 | tf_op jit(solution)/shard_map/ppermute | solution.py:138
  15.9 10.7 %collective-permute-start.7 = (f32[136,128]{1,0:T(8,128)S(1)}, f32[136,128]{1,0:T(8,128)S(1)}, u32[]{:S(2)}, u32[]{:S(2)}) collective-permute-start(f32[136,128]{1,0:T(8,128)S(1)} %get-tuple-element.18), channel_id=1, source_target_pairs={{0,9},{1,8},{2,11},{3,10},{4,13},{5,12},{6,15},{7,14},{8,1},{9,0},... | collective-permute-start | bytes 208904 | tf_op jit(solution)/shard_map/ppermute | solution.py:138
  19.2 8.4 %collective-permute-start.6 = (f32[136,128]{1,0:T(8,128)S(1)}, f32[136,128]{1,0:T(8,128)S(1)}, u32[]{:S(2)}, u32[]{:S(2)}) collective-permute-start(f32[136,128]{1,0:T(8,128)S(1)} %get-tuple-element.19), channel_id=1, source_target_pairs={{0,8},{1,9},{2,10},{3,11},{4,12},{5,13},{6,14},{7,15},{8,0},{9,1},... | collective-permute-start | bytes 208904 | tf_op jit(solution)/shard_map/ppermute | solution.py:138
  19.2 15.0 %collective-permute-start.20 = (f32[136,128]{1,0:T(8,128)S(1)}, f32[136,128]{1,0:T(8,128)S(1)}, u32[]{:S(2)}, u32[]{:S(2)}) collective-permute-start(f32[136,128]{1,0:T(8,128)S(1)} %get-tuple-element.5), channel_id=1, source_target_pairs={{0,14},{1,15},{2,12},{3,13},{4,10},{5,11},{6,8},{7,9},{8,6},{9,7},... | collective-permute-start | bytes 208904 | tf_op jit(solution)/shard_map/ppermute | solution.py:138
  26.6 7.7 %collective-permute-start.23 = (f32[136,128]{1,0:T(8,128)S(1)}, f32[136,128]{1,0:T(8,128)S(1)}, u32[]{:S(2)}, u32[]{:S(2)}) collective-permute-start(f32[136,128]{1,0:T(8,128)S(1)} %get-tuple-element.6), channel_id=1, source_target_pairs={{0,7},{1,6},{2,5},{3,4},{4,3},{5,2},{6,1},{7,0},{8,15},{9,14},{10,... | collective-permute-start | bytes 208904 | tf_op jit(solution)/shard_map/ppermute | solution.py:138
  27.6 9.4 %collective-permute-start.18 = (f32[136,128]{1,0:T(8,128)S(1)}, f32[136,128]{1,0:T(8,128)S(1)}, u32[]{:S(2)}, u32[]{:S(2)}) collective-permute-start(f32[136,128]{1,0:T(8,128)S(1)} %get-tuple-element.9), channel_id=1, source_target_pairs={{0,5},{1,4},{2,7},{3,6},{4,1},{5,0},{6,3},{7,2},{8,13},{9,12},{10,... | collective-permute-start | bytes 208904 | tf_op jit(solution)/shard_map/ppermute | solution.py:138
  28.0 10.8 %collective-permute-start.4 = (f32[2,256,128]{2,1,0:T(8,128)S(1)}, f32[2,256,128]{2,1,0:T(8,128)S(1)}, u32[]{:S(2)}, u32[]{:S(2)}) collective-permute-start(f32[2,256,128]{2,1,0:T(8,128)S(1)} %collective-permute-done.3), channel_id=1, source_target_pairs={{0,1},{1,0},{2,3},{3,2},{4,5},{5,4},{6,7},{7,6},{8,9},{9,8},{10,11... | collective-permute-start | bytes 786440 | tf_op jit(solution)/shard_map/ppermute | solution.py:138
  28.7 12.2 %collective-permute-start.17 = (f32[136,128]{1,0:T(8,128)S(1)}, f32[136,128]{1,0:T(8,128)S(1)}, u32[]{:S(2)}, u32[]{:S(2)}) collective-permute-start(f32[136,128]{1,0:T(8,128)S(1)} %get-tuple-element.10), channel_id=1, source_target_pairs={{0,13},{1,12},{2,15},{3,14},{4,9},{5,8},{6,11},{7,10},{8,5},{9,4},... | collective-permute-start | bytes 208904 | tf_op jit(solution)/shard_map/ppermute | solution.py:138
  34.2 9.3 %collective-permute-start.16 = (f32[136,128]{1,0:T(8,128)S(1)}, f32[136,128]{1,0:T(8,128)S(1)}, u32[]{:S(2)}, u32[]{:S(2)}) collective-permute-start(f32[136,128]{1,0:T(8,128)S(1)} %get-tuple-element.11), channel_id=1, source_target_pairs={{0,4},{1,5},{2,6},{3,7},{4,0},{5,1},{6,2},{7,3},{8,12},{9,13},{10,... | collective-permute-start | bytes 208904 | tf_op jit(solution)/shard_map/ppermute | solution.py:138
  34.3 10.6 %collective-permute-start.15 = (f32[136,128]{1,0:T(8,128)S(1)}, f32[136,128]{1,0:T(8,128)S(1)}, u32[]{:S(2)}, u32[]{:S(2)}) collective-permute-start(f32[136,128]{1,0:T(8,128)S(1)} %get-tuple-element.12), channel_id=1, source_target_pairs={{0,12},{1,13},{2,14},{3,15},{4,8},{5,9},{6,10},{7,11},{8,4},{9,5},... | collective-permute-start | bytes 208904 | tf_op jit(solution)/shard_map/ppermute | solution.py:138
  36.9 26.8 %copy-start = (f32[256,1024]{1,0:T(8,128)S(1)}, f32[256,1024]{1,0:T(8,128)}, u32[]{:S(2)}) copy-start(f32[256,1024]{1,0:T(8,128)} %refs_12_.1) | copy-start | bytes 3145732
  36.9 8.0 %collective-permute-start.13 = (f32[136,128]{1,0:T(8,128)S(1)}, f32[136,128]{1,0:T(8,128)S(1)}, u32[]{:S(2)}, u32[]{:S(2)}) collective-permute-start(f32[136,128]{1,0:T(8,128)S(1)} %get-tuple-element.13), channel_id=1, source_target_pairs={{0,3},{1,2},{2,1},{3,0},{4,7},{5,6},{6,5},{7,4},{8,11},{9,10},{10,... | collective-permute-start | bytes 208904 | tf_op jit(solution)/shard_map/ppermute | solution.py:138
  38.8 8.9 %collective-permute-start.12 = (f32[136,128]{1,0:T(8,128)S(1)}, f32[136,128]{1,0:T(8,128)S(1)}, u32[]{:S(2)}, u32[]{:S(2)}) collective-permute-start(f32[136,128]{1,0:T(8,128)S(1)} %get-tuple-element.14), channel_id=1, source_target_pairs={{0,11},{1,10},{2,9},{3,8},{4,15},{5,14},{6,13},{7,12},{8,3},{9,2},... | collective-permute-start | bytes 208904 | tf_op jit(solution)/shard_map/ppermute | solution.py:138
  40.9 7.8 %collective-permute-start.11 = (f32[136,128]{1,0:T(8,128)S(1)}, f32[136,128]{1,0:T(8,128)S(1)}, u32[]{:S(2)}, u32[]{:S(2)}) collective-permute-start(f32[136,128]{1,0:T(8,128)S(1)} %get-tuple-element.15), channel_id=1, source_target_pairs={{0,2},{1,3},{2,0},{3,1},{4,6},{5,7},{6,4},{7,5},{8,10},{9,11},{10,... | collective-permute-start | bytes 208904 | tf_op jit(solution)/shard_map/ppermute | solution.py:138
  43.5 8.5 %collective-permute-start.10 = (f32[136,128]{1,0:T(8,128)S(1)}, f32[136,128]{1,0:T(8,128)S(1)}, u32[]{:S(2)}, u32[]{:S(2)}) collective-permute-start(f32[136,128]{1,0:T(8,128)S(1)} %get-tuple-element.16), channel_id=1, source_target_pairs={{0,10},{1,11},{2,8},{3,9},{4,14},{5,15},{6,12},{7,13},{8,2},{9,3},... | collective-permute-start | bytes 208904 | tf_op jit(solution)/shard_map/ppermute | solution.py:138
  44.9 12.7 %collective-permute-start.9 = (f32[4,136,128]{2,1,0:T(8,128)S(1)}, f32[4,136,128]{2,1,0:T(8,128)S(1)}, u32[]{:S(2)}, u32[]{:S(2)}) collective-permute-start(f32[4,136,128]{2,1,0:T(8,128)S(1)} %pad_maximum_fusion.1.refs_4_), channel_id=1, source_target_pairs={{0,16},{16,0},{1,17},{17,1},{2,18},{18,2},{3,19},{19,3},{4,20},{20... | collective-permute-start | bytes 835592 | tf_op jit(solution)/shard_map/ppermute | solution.py:138
  44.9 15.8 %collective-permute-start.2 = (f32[4,256,128]{2,1,0:T(8,128)S(1)}, f32[4,256,128]{2,1,0:T(8,128)S(1)}, u32[]{:S(2)}, u32[]{:S(2)}) collective-permute-start(f32[4,256,128]{2,1,0:T(8,128)S(1)} %pad_maximum_fusion.refs_0_), channel_id=1, source_target_pairs={{0,1},{1,0},{2,3},{3,2},{4,5},{5,4},{6,7},{7,6},{8,9},{9,8},{10,11... | collective-permute-start | bytes 1572872 | tf_op jit(solution)/shard_map/ppermute | solution.py:138
  47.8 16.0 %collective-permute-start.5 = (f32[4,256,128]{2,1,0:T(8,128)S(1)}, f32[4,256,128]{2,1,0:T(8,128)S(1)}, u32[]{:S(2)}, u32[]{:S(2)}) collective-permute-start(f32[4,256,128]{2,1,0:T(8,128)S(1)} %constant_dynamic-update-slice_fusion.refs_2_), channel_id=1, source_target_pairs={{0,2},{1,3},{2,0},{3,1},{4,6},{5,7},{6,4},{7,5},{8,10},{9,11},{10,... | collective-permute-start | bytes 1572872 | tf_op jit(solution)/shard_map/ppermute | solution.py:138
  48.7 8.3 %collective-permute-start.22 = (f32[136,128]{1,0:T(8,128)S(1)}, f32[136,128]{1,0:T(8,128)S(1)}, u32[]{:S(2)}, u32[]{:S(2)}) collective-permute-start(f32[136,128]{1,0:T(8,128)S(1)} %get-tuple-element.7), channel_id=1, source_target_pairs={{0,15},{1,14},{2,13},{3,12},{4,11},{5,10},{6,9},{7,8},{8,7},{9,6},... | collective-permute-start | bytes 208904 | tf_op jit(solution)/shard_map/ppermute | solution.py:138
  52.1 5.5 %collective-permute-start.21 = (f32[136,128]{1,0:T(8,128)S(1)}, f32[136,128]{1,0:T(8,128)S(1)}, u32[]{:S(2)}, u32[]{:S(2)}) collective-permute-start(f32[136,128]{1,0:T(8,128)S(1)} %get-tuple-element.8), channel_id=1, source_target_pairs={{0,6},{1,7},{2,4},{3,5},{4,2},{5,3},{6,0},{7,1},{8,14},{9,15},{10,... | collective-permute-start | bytes 208904 | tf_op jit(solution)/shard_map/ppermute | solution.py:138
  57.1 1.6 %collective-permute-start.14 = (f32[4,136,128]{2,1,0:T(8,128)S(1)}, f32[4,136,128]{2,1,0:T(8,128)S(1)}, u32[]{:S(2)}, u32[]{:S(2)}) collective-permute-start(f32[4,136,128]{2,1,0:T(8,128)S(1)} %pad_maximum_fusion.2.refs_6_), channel_id=1, source_target_pairs={{0,16},{16,0},{1,17},{17,1},{2,18},{18,2},{3,19},{19,3},{4,20},{20... | collective-permute-start | bytes 835592 | tf_op jit(solution)/shard_map/ppermute | solution.py:138
  57.6 1.6 %collective-permute-start.19 = (f32[4,136,128]{2,1,0:T(8,128)S(1)}, f32[4,136,128]{2,1,0:T(8,128)S(1)}, u32[]{:S(2)}, u32[]{:S(2)}) collective-permute-start(f32[4,136,128]{2,1,0:T(8,128)S(1)} %pad_maximum_fusion.3.refs_8_), channel_id=1, source_target_pairs={{0,16},{16,0},{1,17},{17,1},{2,18},{18,2},{3,19},{19,3},{4,20},{20... | collective-permute-start | bytes 835592 | tf_op jit(solution)/shard_map/ppermute | solution.py:138
  57.6 1.9 %collective-permute-start.24 = (f32[4,136,128]{2,1,0:T(8,128)S(1)}, f32[4,136,128]{2,1,0:T(8,128)S(1)}, u32[]{:S(2)}, u32[]{:S(2)}) collective-permute-start(f32[4,136,128]{2,1,0:T(8,128)S(1)} %pad_maximum_fusion.4.refs_10_), channel_id=1, source_target_pairs={{0,16},{16,0},{1,17},{17,1},{2,18},{18,2},{3,19},{19,3},{4,20},{20... | collective-permute-start | bytes 835592 | tf_op jit(solution)/shard_map/ppermute | solution.py:138
where the time goes:
time: 70.1 us; the launch traced here: 69.9 us
  starting transfers between devices  34.9 us (50%)
  waiting for transfers between devices  23.5 us (34%)
  Pallas kernels  8.49 us (12%)
  local copies, waits for them, and re-layouts  2.75 us (4%)
    ppermute x25, starting transfers between devices, send(): return lax.ppermute(x, axis, [(i, partner(i)) for i in range(size)])  34.9 us
    ppermute x25, waiting for transfers between devices, send(): return lax.ppermute(x, axis, [(i, partner(i)) for i in range(size)])  23.5 us
    pallas_call x1, Pallas kernels, contract(): pl.pallas_call(functools.partial(contract_kernel, positions, len(groups),...  6.18 us
    pallas_call x1, Pallas kernels, pack(): pl.pallas_call(pack_kernel, out_shape=jax.ShapeDtypeStruct((targets, SLOT...  2.32 us
  transfers between devices with their start and end apart: 25, of which 12 were waited for; matrix products, arithmetic and copies ran while one was open for 4% of the time, Pallas kernels for 3%

commit v1 on v0

v1 whole, which is shorter than its diff:
```python
import functools

import jax
import jax.numpy as jnp
from jax import lax
from jax.experimental import pallas as pl
from jax.experimental.pallas import tpu as pltpu
from jax.sharding import PartitionSpec as P

KT = 16
CT = 8
META = 8


def pack_kernel(slot, reader_ref, k_ref, column_ref, tiles_ref, *refs):
    out_ref, count_ref = refs[-2:]
    count, height, width = tiles_ref.shape
    targets = out_ref.shape[0]
    out_ref[:, height:, :] = jnp.full((targets, META, width), -1.0, jnp.float32)
    for target in range(targets):
        count_ref[target] = 0

    def place(j, carry):
        target = reader_ref[j]
        seen = count_ref[target]
        count_ref[target] = seen + 1

        @pl.when(seen == slot)
        def _():
            out_ref[target, :height, :] = tiles_ref[j]
            code = (k_ref[j] * CT + column_ref[j]).astype(jnp.float32)
            out_ref[target, height:, :] = jnp.full((META, width), code, jnp.float32)

        return carry

    lax.fori_loop(0, count, place, 0)


def pack(slot, tiles, readers, tile_k, tile_column, targets, after):
    _, height, width = tiles.shape
    smem = pl.BlockSpec(memory_space=pltpu.SMEM)
    vmem = pl.BlockSpec(memory_space=pltpu.VMEM)
    return pl.pallas_call(
        functools.partial(pack_kernel, slot),
        out_shape=jax.ShapeDtypeStruct((targets, height + META, width), jnp.float32),
        in_specs=[smem, smem, smem, vmem] + [pl.BlockSpec(memory_space=pl.ANY)] * len(after),
        out_specs=vmem,
        scratch_shapes=[pltpu.SMEM((targets,), jnp.int32)],
        cost_estimate=pl.CostEstimate(flops=0, bytes_accessed=4 * tiles.size * 3, transcendentals=0),
    )(readers.reshape(-1), tile_k, tile_column, tiles, *after)


def contract_kernel(positions, groups_count, parts_count, *refs):
    pieces = refs[: len(positions)]
    end = len(positions) + groups_count * parts_count
    groups = [
        refs[len(positions) + g * parts_count : len(positions) + (g + 1) * parts_count]
        for g in range(groups_count)
    ]
    residual_ref, out_ref, split_ref = refs[end : end + 3]
    codes = refs[end + 3 : end + 3 + groups_count]
    sem = refs[-1]
    height = groups[0][0].shape[1] - META
    width = groups[0][0].shape[2]
    row = lax.axis_index("row")
    me = lax.axis_index("bulk")
    fetches = [
        pltpu.make_async_copy(parts[0].at[:, pl.ds(height, META), :], codes[g], sem.at[g])
        for g, parts in enumerate(groups)
    ]
    for fetch in fetches:
        fetch.start()
    for piece, held in zip(pieces, positions):
        for at, position in enumerate(held):
            block = piece[at]
            high = block.astype(jnp.bfloat16)
            low = (block - high.astype(jnp.float32)).astype(jnp.bfloat16)
            k = at if position is None else jnp.bitwise_xor(me, position)
            split_ref[k] = jnp.concatenate([high, low], axis=1)
    out_ref[...] = residual_ref[...]
    for fetch in fetches:
        fetch.wait()

    def add_group(parts, codes_ref):
        def add(owner, carry):
            code = codes_ref[owner, 0, 0].astype(jnp.int32)

            @pl.when(code >= 0)
            def _():
                k = code // CT
                column = code - k * CT
                ordered = []
                for place in range(parts_count):
                    piece = parts[0][owner, :height, :]
                    for q in range(1, parts_count):
                        other = parts[q][owner, :height, :]
                        piece = jnp.where(lax.rem(place + q, parts_count) == row, other, piece)
                    ordered.append(piece)
                tile = jnp.concatenate(ordered, axis=0)
                high = tile.astype(jnp.bfloat16)
                low = (tile - high.astype(jnp.float32)).astype(jnp.bfloat16)
                both = jnp.concatenate([high, low], axis=1)
                weights = jnp.concatenate([both, both], axis=0)
                product = jnp.dot(split_ref[k], weights, preferred_element_type=jnp.float32)
                lanes = pl.ds(pl.multiple_of(column * width, width), width)
                out_ref[:, lanes] += product[:, :width] + product[:, width:]

            return carry

        lax.fori_loop(0, parts[0].shape[0], add, 0)

    for parts, codes_ref in zip(groups, codes):
        add_group(parts, codes_ref)


def contract(pieces, positions, groups, residual):
    rows = residual.shape[0]
    width = groups[0][0].shape[2]
    vmem = pl.BlockSpec(memory_space=pltpu.VMEM)
    arrays = [*pieces, *[part for parts in groups for part in parts], residual]
    return pl.pallas_call(
        functools.partial(contract_kernel, positions, len(groups), len(groups[0])),
        out_shape=jax.ShapeDtypeStruct(residual.shape, jnp.float32),
        in_specs=[vmem] * len(arrays),
        out_specs=vmem,
        scratch_shapes=[
            pltpu.VMEM((KT, rows, 2 * width), jnp.bfloat16),
            *[pltpu.SMEM((parts[0].shape[0], META, width), jnp.float32) for parts in groups],
            pltpu.SemaphoreType.DMA((len(groups),)),
        ],
        compiler_params=pltpu.CompilerParams(vmem_limit_bytes=40 * 1024 * 1024),
    )(*arrays)


def send(x, axis, partner):
    size = lax.axis_size(axis)
    return lax.ppermute(x, axis, [(i, partner(i)) for i in range(size)])


def gather(block, axis):
    held, at = block[None], (0,)
    bit = lax.axis_size(axis) // 2
    while bit > 4:
        come = send(held, axis, lambda i: i ^ bit)
        held, at = jnp.concatenate([held, come], axis=0), at + tuple(p ^ bit for p in at)
        bit //= 2
    hop = lambda x, step: send(x, axis, lambda i: i ^ step)
    pieces = {0: held}
    pieces[4] = hop(held, 4)
    pieces[2] = hop(held, 2)
    pieces[1] = hop(held, 1)
    pieces[5] = hop(pieces[4], 1)
    pieces[6] = hop(pieces[4], 2)
    pieces[3] = hop(pieces[2], 1)
    pieces[7] = hop(pieces[5], 2)
    return list(pieces.values()), [tuple(p ^ step for p in at) for step in pieces], [pieces[step] for step in (4, 2, 1)]


def local(residual_in, amplitudes, integral_tiles, tile_reader, tile_k, tile_column):
    targets = lax.axis_size("bulk")
    rows_axis = lax.axis_size("row")
    width = integral_tiles.shape[2]
    pieces, positions, near = gather(amplitudes, "bulk")
    groups = []
    for slot, after in enumerate(([], near)):
        outgoing = pack(slot, integral_tiles, tile_reader, tile_k, tile_column, targets, after)
        mine = lax.all_to_all(outgoing, "bulk", split_axis=0, concat_axis=0, tiled=True)
        groups.append(
            [mine] + [send(mine, "row", lambda i: (i + q) % rows_axis) for q in range(1, rows_axis)]
        )
    if amplitudes.shape[1] != width:
        stacked = jnp.concatenate(pieces, axis=0)
        listed = [p for held in positions for p in held]
        place = jnp.asarray([listed.index(p) for p in range(targets)], jnp.int32)
        wanted = jnp.bitwise_xor(jnp.arange(targets, dtype=jnp.int32), lax.axis_index("bulk"))
        stacked = stacked[place[wanted]]
        stacked = stacked.transpose(1, 0, 2).reshape(amplitudes.shape[0], KT, width).transpose(1, 0, 2)
        pieces, positions = [stacked], [(None,) * KT]
    return contract(pieces, positions, groups, residual_in)


def solution(mesh):
    placed = (
        P("row", "bulk"),
        P("row", "bulk"),
        P("bulk", "row", None),
        P("bulk", None),
        P("bulk"),
        P("bulk"),
    )
    return jax.shard_map(
        local, mesh=mesh, in_specs=placed, out_specs=P("row", "bulk"), check_vma=False
    )
```

time: 70.1 us -> 91.1 us (1.30)
  waiting for transfers between devices: 23.5 us -> 53.1 us
  starting transfers between devices: 34.9 us -> 22.2 us
  Pallas kernels: 8.49 us -> 11.7 us
    ppermute x25 -> x10, starting transfers between devices: 34.9 us -> 9.9 us  [send(): return lax.ppermute(x, axis, [(i, partner(i)) for i in range(size)])]
    all_to_all x0 -> x2, waiting for transfers between devices: none -> 15 us  [local(): lax.all_to_all(outgoing, 'bulk', split_axis=0, concat_axis=0, tiled=True)]
    ppermute x25 -> x10, waiting for transfers between devices: 23.5 us -> 38.1 us  [send(): return lax.ppermute(x, axis, [(i, partner(i)) for i in range(size)])]
    all_to_all x0 -> x2, starting transfers between devices: none -> 12.3 us  [local(): lax.all_to_all(outgoing, 'bulk', split_axis=0, concat_axis=0, tiled=True)]
    unnamed x6 -> x16, local copies, waits for them, and re-layouts: 1.35 us -> 3.55 us
    pallas_call x1 -> x2, Pallas kernels: 2.32 us -> 4.35 us  [pack(): pl.pallas_call(functools.partial(pack_kernel, slot), out_shape=jax.ShapeD...]
    squeeze x1 -> x0, local copies, waits for them, and re-layouts: 1.38 us -> none  [local(): arrived[p] = send(outgoing[p], 'bulk', lambda i: i ^ p)]
    pallas_call x1, Pallas kernels: 6.18 us -> 7.31 us  [contract(): pl.pallas_call(functools.partial(contract_kernel, positions, len(groups),...]
  transfers between devices with their start and end apart: 25 -> 12, of which waited for: 12 -> 8; matrix products, arithmetic and copies ran while one was open for 4% -> 0% of each run, Pallas kernels for 3% -> 2%
where the time goes in v1:
time: 91.1 us; the launch traced here: 90.7 us
  waiting for transfers between devices  53.1 us (58%)
  starting transfers between devices  22.2 us (24%)
  Pallas kernels  11.7 us (13%)
  local copies, waits for them, and re-layouts  3.55 us (4%)
    ppermute x10, waiting for transfers between devices, send(): return lax.ppermute(x, axis, [(i, partner(i)) for i in range(size)])  38.1 us
    all_to_all x2, waiting for transfers between devices, local(): lax.all_to_all(outgoing, 'bulk', split_axis=0, concat_axis=0, tiled=True)  15 us
    all_to_all x2, starting transfers between devices, local(): lax.all_to_all(outgoing, 'bulk', split_axis=0, concat_axis=0, tiled=True)  12.3 us
    ppermute x10, starting transfers between devices, send(): return lax.ppermute(x, axis, [(i, partner(i)) for i in range(size)])  9.9 us
    pallas_call x1, Pallas kernels, contract(): pl.pallas_call(functools.partial(contract_kernel, positions, len(groups),...  7.31 us
    pallas_call x2, Pallas kernels, pack(): pl.pallas_call(functools.partial(pack_kernel, slot), out_shape=jax.ShapeD...  4.35 us
    unnamed x16, local copies, waits for them, and re-layouts  3.55 us
  transfers between devices with their start and end apart: 12, of which 8 were waited for; matrix products, arithmetic and copies ran while one was open for 0% of the time, Pallas kernels for 2%

profile of v1, /device:TPU:0, one launch (start us, length us, event | category | flops | bytes accessed | tf_op | source)
XLA Modules:
  0.0 90.7 jit_solution(11813520836022759322)
XLA Ops:
  0.0 2.2 %shard_map.64 = f32[16,72,128]{2,1,0:T(8,128)} custom-call(s32[16]{0:T(128)} %bitcast.4, s32[16]{0:T(128)} %k_ref.3, s32[16]{0:T(128)} %column_ref.3, f32[16,64,128]{2,1,0:T(8,128)} %tiles_ref.3), custom_call_target="tpu_custom_call" | custom-call | bytes 1572864 | tf_op jit(solution)/shard_map/pallas_call | solution.py:43
  2.2 0.0 copy-start.7
  2.2 8.4 %all-to-all-start = ((f32[16,72,128]{2,1,0:T(8,128)}), f32[16,72,128]{2,1,0:T(8,128)S(1)}, u32[]{:S(2)}, u32[]{:S(2)}) async-start(f32[16,72,128]{2,1,0:T(8,128)} %shard_map.64), calls=%async_computation | async-start | bytes 1179648 | tf_op jit(solution)/shard_map/all_to_all | solution.py:167
  10.6 0.0 copy-done.7
  10.7 2.9 %collective-permute-start = (f32[1,256,128]{2,1,0:T(8,128)S(1)}, f32[1,256,128]{2,1,0:T(8,128)S(1)}, u32[]{:S(2)}, u32[]{:S(2)}) collective-permute-start(f32[1,256,128]{2,1,0:T(8,128)S(1)} %bitcast.2), channel_id=1, source_target_pairs={{0,8},{1,9},{2,10},{3,11},{4,12},{5,13},{6,14},{7,15},{8,0},{9,1},... | collective-permute-start | bytes 393224 | tf_op jit(solution)/shard_map/ppermute | solution.py:137
  13.5 18.5 %collective-permute-done = f32[1,256,128]{2,1,0:T(8,128)S(1)} collective-permute-done((f32[1,256,128]{2,1,0:T(8,128)S(1)}, f32[1,256,128]{2,1,0:T(8,128)S(1)}, u32[]{:S(2)}, u32[]{:S(2)}) %collective-permute-start) | collective-permute-done | bytes 131104 | tf_op jit(solution)/shard_map/ppermute | solution.py:137
  32.1 1.5 %collective-permute-start.3 = (f32[2,256,128]{2,1,0:T(8,128)S(1)}, f32[2,256,128]{2,1,0:T(8,128)S(1)}, u32[]{:S(2)}, u32[]{:S(2)}) collective-permute-start(f32[2,256,128]{2,1,0:T(8,128)S(1)} %pad_maximum_fusion.refs_0_), channel_id=1, source_target_pairs={{0,1},{1,0},{2,3},{3,2},{4,5},{5,4},{6,7},{7,6},{8,9},{9,8},{10,11... | collective-permute-start | bytes 786440 | tf_op jit(solution)/shard_map/ppermute | solution.py:137
  33.6 1.5 %collective-permute-start.2 = (f32[2,256,128]{2,1,0:T(8,128)S(1)}, f32[2,256,128]{2,1,0:T(8,128)S(1)}, u32[]{:S(2)}, u32[]{:S(2)}) collective-permute-start(f32[2,256,128]{2,1,0:T(8,128)S(1)} %pad_maximum_fusion.refs_0_), channel_id=1, source_target_pairs={{0,2},{1,3},{2,0},{3,1},{4,6},{5,7},{6,4},{7,5},{8,10},{9,11},{10,... | collective-permute-start | bytes 786440 | tf_op jit(solution)/shard_map/ppermute | solution.py:137
  35.1 0.0 collective-permute-start.1
  35.1 4.3 %collective-permute-done.3.refs_2_.refs_3_ = f32[2,256,128]{2,1,0:T(8,128)S(1)} collective-permute-done((f32[2,256,128]{2,1,0:T(8,128)S(1)}, f32[2,256,128]{2,1,0:T(8,128)S(1)}, u32[]{:S(2)}, u32[]{:S(2)}) %collective-permute-start.3) | collective-permute-done | bytes 262176 | tf_op jit(solution)/shard_map/ppermute | solution.py:137
  39.4 0.0 copy-start.1
  39.4 1.2 %collective-permute-done.2.refs_1_.refs_2_ = f32[2,256,128]{2,1,0:T(8,128)S(1)} collective-permute-done((f32[2,256,128]{2,1,0:T(8,128)S(1)}, f32[2,256,128]{2,1,0:T(8,128)S(1)}, u32[]{:S(2)}, u32[]{:S(2)}) %collective-permute-start.2) | collective-permute-done | bytes 262176 | tf_op jit(solution)/shard_map/ppermute | solution.py:137
  40.6 0.0 copy-start.3
  40.6 1.2 %collective-permute-done.1.refs_0_.refs_1_ = f32[2,256,128]{2,1,0:T(8,128)S(1)} collective-permute-done((f32[2,256,128]{2,1,0:T(8,128)S(1)}, f32[2,256,128]{2,1,0:T(8,128)S(1)}, u32[]{:S(2)}, u32[]{:S(2)}) %collective-permute-start.1) | collective-permute-done | bytes 262176 | tf_op jit(solution)/shard_map/ppermute | solution.py:137
  41.8 0.0 copy-done.1
  41.8 0.0 copy-done.3
  41.8 0.0 copy-start.5
  41.8 0.7 copy-done.5
  42.5 2.2 %shard_map.65 = f32[16,72,128]{2,1,0:T(8,128)} custom-call(s32[16]{0:T(128)} %bitcast.5, s32[16]{0:T(128)} %k_ref.3, s32[16]{0:T(128)} %column_ref.3, f32[16,64,128]{2,1,0:T(8,128)} %tiles_ref.3, f32[2,256,128]{2,1,0:T(8,128)} %copy-done.5, f32[2,256,128]{2,1,0:T(8,128)} %copy-done.3, f32[2,256,128]{2,1,0:T(8,128)} %copy-done.1), custom_call_target="tpu_custom_call" | custom-call | bytes 1572864 | tf_op jit(solution)/shard_map/pallas_call | solution.py:43
  44.6 0.0 copy-start
  44.6 0.0 all-to-all-done.refs_8_
  44.7 3.9 %all-to-all-start.1 = ((f32[16,72,128]{2,1,0:T(8,128)}), f32[16,72,128]{2,1,0:T(8,128)S(1)}, u32[]{:S(2)}, u32[]{:S(2)}) async-start(f32[16,72,128]{2,1,0:T(8,128)} %shard_map.65), calls=%async_computation.1 | async-start | bytes 1179648 | tf_op jit(solution)/shard_map/all_to_all | solution.py:167
  48.6 0.1 collective-permute-start.8
  48.6 15.0 %all-to-all-done.1.refs_10_ = f32[16,72,128]{2,1,0:T(8,128)S(1)} async-done(((f32[16,72,128]{2,1,0:T(8,128)}), f32[16,72,128]{2,1,0:T(8,128)S(1)}, u32[]{:S(2)}, u32[]{:S(2)}) %all-to-all-start.1) | async-done | bytes 589856 | tf_op jit(solution)/shard_map/all_to_all | solution.py:167
  63.6 0.0 collective-permute-start.9
  63.6 0.6 collective-permute-start.4
  64.2 1.5 %collective-permute-start.6 = (f32[2,256,128]{2,1,0:T(8,128)}, f32[2,256,128]{2,1,0:T(8,128)S(1)}, u32[]{:S(2)}, u32[]{:S(2)}) collective-permute-start(f32[2,256,128]{2,1,0:T(8,128)} %copy-done.3), channel_id=1, source_target_pairs={{0,1},{1,0},{2,3},{3,2},{4,5},{5,4},{6,7},{7,6},{8,9},{9,8},{10,11... | collective-permute-start | bytes 786440 | tf_op jit(solution)/shard_map/ppermute | solution.py:137
  65.7 1.0 %collective-permute-start.5 = (f32[2,256,128]{2,1,0:T(8,128)}, f32[2,256,128]{2,1,0:T(8,128)S(1)}, u32[]{:S(2)}, u32[]{:S(2)}) collective-permute-start(f32[2,256,128]{2,1,0:T(8,128)} %copy-done.5), channel_id=1, source_target_pairs={{0,2},{1,3},{2,0},{3,1},{4,6},{5,7},{6,4},{7,5},{8,10},{9,11},{10,... | collective-permute-start | bytes 786440 | tf_op jit(solution)/shard_map/ppermute | solution.py:137
  66.6 6.3 %collective-permute-done.4.refs_4_ = f32[2,256,128]{2,1,0:T(8,128)S(1)} collective-permute-done((f32[2,256,128]{2,1,0:T(8,128)}, f32[2,256,128]{2,1,0:T(8,128)S(1)}, u32[]{:S(2)}, u32[]{:S(2)}) %collective-permute-start.4) | collective-permute-done | bytes 262176 | tf_op jit(solution)/shard_map/ppermute | solution.py:137
  73.0 1.0 %collective-permute-start.7 = (f32[2,256,128]{2,1,0:T(8,128)S(1)}, f32[2,256,128]{2,1,0:T(8,128)S(1)}, u32[]{:S(2)}, u32[]{:S(2)}) collective-permute-start(f32[2,256,128]{2,1,0:T(8,128)S(1)} %collective-permute-done.4.refs_4_), channel_id=1, source_target_pairs={{0,2},{1,3},{2,0},{3,1},{4,6},{5,7},{6,4},{7,5},{8,10},{9,11},{10,... | collective-permute-start | bytes 786440 | tf_op jit(solution)/shard_map/ppermute | solution.py:137
  73.9 4.3 %collective-permute-done.6.refs_6_ = f32[2,256,128]{2,1,0:T(8,128)S(1)} collective-permute-done((f32[2,256,128]{2,1,0:T(8,128)}, f32[2,256,128]{2,1,0:T(8,128)S(1)}, u32[]{:S(2)}, u32[]{:S(2)}) %collective-permute-start.6) | collective-permute-done | bytes 262176 | tf_op jit(solution)/shard_map/ppermute | solution.py:137
  78.2 0.0 collective-permute-done.5.refs_5_
  78.2 2.3 %collective-permute-done.7.refs_7_ = f32[2,256,128]{2,1,0:T(8,128)S(1)} collective-permute-done((f32[2,256,128]{2,1,0:T(8,128)S(1)}, f32[2,256,128]{2,1,0:T(8,128)S(1)}, u32[]{:S(2)}, u32[]{:S(2)}) %collective-permute-start.7) | collective-permute-done | bytes 262176 | tf_op jit(solution)/shard_map/ppermute | solution.py:137
  80.5 0.0 collective-permute-done.8.refs_9_
  80.5 0.0 collective-permute-done.9.refs_11_
  80.5 0.0 copy-done
  80.5 0.0 copy-start.2
  80.5 0.9 %copy-done.2 = f32[2,256,128]{2,1,0:T(8,128)S(1)} copy-done((f32[2,256,128]{2,1,0:T(8,128)S(1)}, f32[2,256,128]{2,1,0:T(8,128)}, u32[]{:S(2)}) %copy-start.2) | copy-done | bytes 262168
  81.5 0.0 copy-start.4
  81.5 0.9 %copy-done.4 = f32[2,256,128]{2,1,0:T(8,128)S(1)} copy-done((f32[2,256,128]{2,1,0:T(8,128)S(1)}, f32[2,256,128]{2,1,0:T(8,128)}, u32[]{:S(2)}) %copy-start.4) | copy-done | bytes 262168
  82.4 0.0 copy-start.6
  82.4 0.9 %copy-done.6 = f32[2,256,128]{2,1,0:T(8,128)S(1)} copy-done((f32[2,256,128]{2,1,0:T(8,128)S(1)}, f32[2,256,128]{2,1,0:T(8,128)}, u32[]{:S(2)}) %copy-start.6) | copy-done | bytes 262168
  83.4 7.3 %shard_map.66 = f32[256,1024]{1,0:T(8,128)} custom-call(f32[2,256,128]{2,1,0:T(8,128)S(1)} %pad_maximum_fusion.refs_0_, f32[2,256,128]{2,1,0:T(8,128)S(1)} %copy-done.6, f32[2,256,128]{2,1,0:T(8,128)S(1)} %copy-done.4, f32[2,256,128]{2,1,0:T(8,128)S(1)} %copy-done.2, f32[2,256,128]{2,1,0:T(8,128)S(1)} %collective-permute-done.4.refs_4_, ...), custom_call_target="tpu_custom_call" | custom-call | tf_op jit(solution)/shard_map/pallas_call | solution.py:121
  (1 shorter events, 0.0 us)
Async XLA Ops:
  2.2 8.5 %copy-start.7 = (f32[256,128]{1,0:T(8,128)S(1)}, f32[256,128]{1,0:T(8,128)}, u32[]{:S(2)}) copy-start(f32[256,128]{1,0:T(8,128)} %param.7) | copy-start | bytes 393220
  2.2 42.5 %all-to-all-start = ((f32[16,72,128]{2,1,0:T(8,128)}), f32[16,72,128]{2,1,0:T(8,128)S(1)}, u32[]{:S(2)}, u32[]{:S(2)}) async-start(f32[16,72,128]{2,1,0:T(8,128)} %shard_map.64), calls=%async_computation | async-start | bytes 1179648 | tf_op jit(solution)/shard_map/all_to_all | solution.py:167
  10.7 21.4 %collective-permute-start = (f32[1,256,128]{2,1,0:T(8,128)S(1)}, f32[1,256,128]{2,1,0:T(8,128)S(1)}, u32[]{:S(2)}, u32[]{:S(2)}) collective-permute-start(f32[1,256,128]{2,1,0:T(8,128)S(1)} %bitcast.2), channel_id=1, source_target_pairs={{0,8},{1,9},{2,10},{3,11},{4,12},{5,13},{6,14},{7,15},{8,0},{9,1},... | collective-permute-start | bytes 393224 | tf_op jit(solution)/shard_map/ppermute | solution.py:137
  32.1 7.3 %collective-permute-start.3 = (f32[2,256,128]{2,1,0:T(8,128)S(1)}, f32[2,256,128]{2,1,0:T(8,128)S(1)}, u32[]{:S(2)}, u32[]{:S(2)}) collective-permute-start(f32[2,256,128]{2,1,0:T(8,128)S(1)} %pad_maximum_fusion.refs_0_), channel_id=1, source_target_pairs={{0,1},{1,0},{2,3},{3,2},{4,5},{5,4},{6,7},{7,6},{8,9},{9,8},{10,11... | collective-permute-start | bytes 786440 | tf_op jit(solution)/shard_map/ppermute | solution.py:137
  33.6 7.0 %collective-permute-start.2 = (f32[2,256,128]{2,1,0:T(8,128)S(1)}, f32[2,256,128]{2,1,0:T(8,128)S(1)}, u32[]{:S(2)}, u32[]{:S(2)}) collective-permute-start(f32[2,256,128]{2,1,0:T(8,128)S(1)} %pad_maximum_fusion.refs_0_), channel_id=1, source_target_pairs={{0,2},{1,3},{2,0},{3,1},{4,6},{5,7},{6,4},{7,5},{8,10},{9,11},{10,... | collective-permute-start | bytes 786440 | tf_op jit(solution)/shard_map/ppermute | solution.py:137
  35.1 6.7 %collective-permute-start.1 = (f32[2,256,128]{2,1,0:T(8,128)S(1)}, f32[2,256,128]{2,1,0:T(8,128)S(1)}, u32[]{:S(2)}, u32[]{:S(2)}) collective-permute-start(f32[2,256,128]{2,1,0:T(8,128)S(1)} %pad_maximum_fusion.refs_0_), channel_id=1, source_target_pairs={{0,4},{1,5},{2,6},{3,7},{4,0},{5,1},{6,2},{7,3},{8,12},{9,13},{10,... | collective-permute-start | bytes 786440 | tf_op jit(solution)/shard_map/ppermute | solution.py:137
  39.4 2.4 %copy-start.1 = (f32[2,256,128]{2,1,0:T(8,128)}, f32[2,256,128]{2,1,0:T(8,128)S(1)}, u32[]{:S(2)}) copy-start(f32[2,256,128]{2,1,0:T(8,128)S(1)} %collective-permute-done.3.refs_2_.refs_3_) | copy-start | bytes 786436
  40.6 1.2 %copy-start.3 = (f32[2,256,128]{2,1,0:T(8,128)}, f32[2,256,128]{2,1,0:T(8,128)S(1)}, u32[]{:S(2)}) copy-start(f32[2,256,128]{2,1,0:T(8,128)S(1)} %collective-permute-done.2.refs_1_.refs_2_) | copy-start | bytes 786436
  41.8 0.7 copy-start.5
  44.6 35.9 %copy-start = (f32[256,1024]{1,0:T(8,128)S(1)}, f32[256,1024]{1,0:T(8,128)}, u32[]{:S(2)}) copy-start(f32[256,1024]{1,0:T(8,128)} %refs_12_.1) | copy-start | bytes 3145732
  44.7 19.0 %all-to-all-start.1 = ((f32[16,72,128]{2,1,0:T(8,128)}), f32[16,72,128]{2,1,0:T(8,128)S(1)}, u32[]{:S(2)}, u32[]{:S(2)}) async-start(f32[16,72,128]{2,1,0:T(8,128)} %shard_map.65), calls=%async_computation.1 | async-start | bytes 1179648 | tf_op jit(solution)/shard_map/all_to_all | solution.py:167
  48.6 32.0 %collective-permute-start.8 = (f32[16,72,128]{2,1,0:T(8,128)S(1)}, f32[16,72,128]{2,1,0:T(8,128)S(1)}, u32[]{:S(2)}, u32[]{:S(2)}) collective-permute-start(f32[16,72,128]{2,1,0:T(8,128)S(1)} %all-to-all-done.refs_8_), channel_id=1, source_target_pairs={{0,16},{16,0},{1,17},{17,1},{2,18},{18,2},{3,19},{19,3},{4,20},{20... | collective-permute-start | bytes 1769480 | tf_op jit(solution)/shard_map/ppermute | solution.py:137
  63.6 16.9 %collective-permute-start.9 = (f32[16,72,128]{2,1,0:T(8,128)S(1)}, f32[16,72,128]{2,1,0:T(8,128)S(1)}, u32[]{:S(2)}, u32[]{:S(2)}) collective-permute-start(f32[16,72,128]{2,1,0:T(8,128)S(1)} %all-to-all-done.1.refs_10_), channel_id=1, source_target_pairs={{0,16},{16,0},{1,17},{17,1},{2,18},{18,2},{3,19},{19,3},{4,20},{20... | collective-permute-start | bytes 1769480 | tf_op jit(solution)/shard_map/ppermute | solution.py:137
  63.6 9.3 %collective-permute-start.4 = (f32[2,256,128]{2,1,0:T(8,128)}, f32[2,256,128]{2,1,0:T(8,128)S(1)}, u32[]{:S(2)}, u32[]{:S(2)}) collective-permute-start(f32[2,256,128]{2,1,0:T(8,128)} %copy-done.5), channel_id=1, source_target_pairs={{0,1},{1,0},{2,3},{3,2},{4,5},{5,4},{6,7},{7,6},{8,9},{9,8},{10,11... | collective-permute-start | bytes 786440 | tf_op jit(solution)/shard_map/ppermute | solution.py:137
  64.2 14.0 %collective-permute-start.6 = (f32[2,256,128]{2,1,0:T(8,128)}, f32[2,256,128]{2,1,0:T(8,128)S(1)}, u32[]{:S(2)}, u32[]{:S(2)}) collective-permute-start(f32[2,256,128]{2,1,0:T(8,128)} %copy-done.3), channel_id=1, source_target_pairs={{0,1},{1,0},{2,3},{3,2},{4,5},{5,4},{6,7},{7,6},{8,9},{9,8},{10,11... | collective-permute-start | bytes 786440 | tf_op jit(solution)/shard_map/ppermute | solution.py:137
  65.7 12.5 %collective-permute-start.5 = (f32[2,256,128]{2,1,0:T(8,128)}, f32[2,256,128]{2,1,0:T(8,128)S(1)}, u32[]{:S(2)}, u32[]{:S(2)}) collective-permute-start(f32[2,256,128]{2,1,0:T(8,128)} %copy-done.5), channel_id=1, source_target_pairs={{0,2},{1,3},{2,0},{3,1},{4,6},{5,7},{6,4},{7,5},{8,10},{9,11},{10,... | collective-permute-start | bytes 786440 | tf_op jit(solution)/shard_map/ppermute | solution.py:137
  73.0 7.6 %collective-permute-start.7 = (f32[2,256,128]{2,1,0:T(8,128)S(1)}, f32[2,256,128]{2,1,0:T(8,128)S(1)}, u32[]{:S(2)}, u32[]{:S(2)}) collective-permute-start(f32[2,256,128]{2,1,0:T(8,128)S(1)} %collective-permute-done.4.refs_4_), channel_id=1, source_target_pairs={{0,2},{1,3},{2,0},{3,1},{4,6},{5,7},{6,4},{7,5},{8,10},{9,11},{10,... | collective-permute-start | bytes 786440 | tf_op jit(solution)/shard_map/ppermute | solution.py:137
  80.5 1.0 %copy-start.2 = (f32[2,256,128]{2,1,0:T(8,128)S(1)}, f32[2,256,128]{2,1,0:T(8,128)}, u32[]{:S(2)}) copy-start(f32[2,256,128]{2,1,0:T(8,128)} %copy-done.1) | copy-start | bytes 786436
  81.5 0.9 %copy-start.4 = (f32[2,256,128]{2,1,0:T(8,128)S(1)}, f32[2,256,128]{2,1,0:T(8,128)}, u32[]{:S(2)}) copy-start(f32[2,256,128]{2,1,0:T(8,128)} %copy-done.3) | copy-start | bytes 786436
  82.4 0.9 %copy-start.6 = (f32[2,256,128]{2,1,0:T(8,128)S(1)}, f32[2,256,128]{2,1,0:T(8,128)}, u32[]{:S(2)}) copy-start(f32[2,256,128]{2,1,0:T(8,128)} %copy-done.5) | copy-start | bytes 786436

commit v2 on v0

v2 whole, which is shorter than its diff:
```python
import functools

import jax
import jax.numpy as jnp
from jax import lax
from jax.experimental import pallas as pl
from jax.experimental.pallas import tpu as pltpu
from jax.sharding import PartitionSpec as P

KT = 16
CT = 8
SLOT = 2
GROUPS = 4
META = 8


def pack_kernel(reader_ref, k_ref, column_ref, tiles_ref, *refs):
    out_ref, count_ref = refs[-2:]
    count, height, _ = tiles_ref.shape
    targets = out_ref.shape[0]
    out_ref[:, SLOT * height :, :] = jnp.full((targets, META, out_ref.shape[2]), -1.0, jnp.float32)
    for target in range(targets):
        count_ref[target] = 0
    lane = lax.broadcasted_iota(jnp.int32, (META, out_ref.shape[2]), 1)

    def place(j, carry):
        target = reader_ref[j]
        slot = count_ref[target]
        count_ref[target] = slot + 1
        out_ref[target, pl.ds(pl.multiple_of(slot * height, height), height), :] = tiles_ref[j]
        code = (k_ref[j] * CT + column_ref[j]).astype(jnp.float32)
        codes = out_ref[target, SLOT * height :, :]
        out_ref[target, SLOT * height :, :] = jnp.where(lane == slot, code, codes)
        return carry

    lax.fori_loop(0, count, place, 0)


def pack(tiles, readers, tile_k, tile_column, targets, after):
    _, height, width = tiles.shape
    smem = pl.BlockSpec(memory_space=pltpu.SMEM)
    vmem = pl.BlockSpec(memory_space=pltpu.VMEM)
    return pl.pallas_call(
        pack_kernel,
        out_shape=jax.ShapeDtypeStruct((targets, SLOT * height + META, width), jnp.float32),
        in_specs=[smem, smem, smem, vmem] + [vmem] * len(after),
        out_specs=vmem,
        scratch_shapes=[pltpu.SMEM((targets,), jnp.int32)],
        cost_estimate=pl.CostEstimate(flops=0, bytes_accessed=4 * tiles.size * 3, transcendentals=0),
    )(readers.reshape(-1), tile_k, tile_column, tiles, *after)


def split_kernel(positions, *refs):
    pieces, split_ref = refs[:-1], refs[-1]
    me = lax.axis_index("bulk")
    for piece, held in zip(pieces, positions):
        for at, position in enumerate(held):
            block = piece[at]
            high = block.astype(jnp.bfloat16)
            low = (block - high.astype(jnp.float32)).astype(jnp.bfloat16)
            k = at if position is None else jnp.bitwise_xor(me, position)
            split_ref[k] = jnp.concatenate([high, low], axis=1)


def split(pieces, positions):
    _, rows, width = pieces[0].shape
    vmem = pl.BlockSpec(memory_space=pltpu.VMEM)
    return pl.pallas_call(
        functools.partial(split_kernel, positions),
        out_shape=jax.ShapeDtypeStruct((KT, rows, 2 * width), jnp.bfloat16),
        in_specs=[vmem] * len(pieces),
        out_specs=vmem,
        compiler_params=pltpu.CompilerParams(vmem_limit_bytes=24 * 1024 * 1024),
    )(*pieces)


def contract_kernel(groups_count, parts_count, split_ref, *refs):
    end = groups_count * parts_count
    groups = [refs[g * parts_count : (g + 1) * parts_count] for g in range(groups_count)]
    residual_ref, out_ref = refs[end : end + 2]
    codes = refs[end + 2 : end + 2 + groups_count]
    sem = refs[-1]
    height = (groups[0][0].shape[1] - META) // SLOT
    width = groups[0][0].shape[2]
    row = lax.axis_index("row")
    fetches = [
        pltpu.make_async_copy(parts[0].at[:, pl.ds(SLOT * height, META), :], codes[g], sem.at[g])
        for g, parts in enumerate(groups)
    ]
    for fetch in fetches:
        fetch.start()
    out_ref[...] = residual_ref[...]
    for fetch in fetches:
        fetch.wait()

    def add_group(parts, codes_ref):
        def add(owner, carry):
            for slot in range(SLOT):
                code = codes_ref[owner, 0, slot].astype(jnp.int32)

                @pl.when(code >= 0)
                def _():
                    k = code // CT
                    column = code - k * CT
                    ordered = []
                    for place in range(parts_count):
                        piece = parts[0][owner, slot * height : (slot + 1) * height, :]
                        for q in range(1, parts_count):
                            other = parts[q][owner, slot * height : (slot + 1) * height, :]
                            piece = jnp.where(lax.rem(place + q, parts_count) == row, other, piece)
                        ordered.append(piece)
                    tile = jnp.concatenate(ordered, axis=0)
                    high = tile.astype(jnp.bfloat16)
                    low = (tile - high.astype(jnp.float32)).astype(jnp.bfloat16)
                    both = jnp.concatenate([high, low], axis=1)
                    weights = jnp.concatenate([both, both], axis=0)
                    product = jnp.dot(split_ref[k], weights, preferred_element_type=jnp.float32)
                    lanes = pl.ds(pl.multiple_of(column * width, width), width)
                    out_ref[:, lanes] += product[:, :width] + product[:, width:]

            return carry

        lax.fori_loop(0, parts[0].shape[0], add, 0)

    for parts, codes_ref in zip(groups, codes):
        add_group(parts, codes_ref)


def contract(split_amplitudes, groups, residual):
    width = groups[0][0].shape[2]
    vmem = pl.BlockSpec(memory_space=pltpu.VMEM)
    arrays = [split_amplitudes, *[part for parts in groups for part in parts], residual]
    return pl.pallas_call(
        functools.partial(contract_kernel, len(groups), len(groups[0])),
        out_shape=jax.ShapeDtypeStruct(residual.shape, jnp.float32),
        in_specs=[vmem] * len(arrays),
        out_specs=vmem,
        scratch_shapes=[
            *[pltpu.SMEM((parts[0].shape[0], META, width), jnp.float32) for parts in groups],
            pltpu.SemaphoreType.DMA((len(groups),)),
        ],
        compiler_params=pltpu.CompilerParams(vmem_limit_bytes=40 * 1024 * 1024),
    )(*arrays)


def send(x, axis, partner):
    size = lax.axis_size(axis)
    return lax.ppermute(x, axis, [(i, partner(i)) for i in range(size)])


def gather(block, axis):
    own = block[None]
    hop = lambda x, step: send(x, axis, lambda i: i ^ step)
    far_at = tuple(range(4, lax.axis_size(axis), 4))
    come = [hop(own, p) for p in far_at]
    pieces = [(own, (0,)), (hop(own, 1), (1,)), (hop(own, 2), (2,))]
    far = jnp.concatenate(come, axis=0)
    far_one, far_two = hop(far, 1), hop(far, 2)
    cut = 2 * len(far_at) // 3
    pieces += [
        (hop(pieces[2][0], 1), (3,)),
        (far, far_at),
        (far_one, tuple(p + 1 for p in far_at)),
        (far_two, tuple(p + 2 for p in far_at)),
        (hop(far_one[:cut], 2), tuple(p + 3 for p in far_at[:cut])),
        (hop(far_two[cut:], 1), tuple(p + 3 for p in far_at[cut:])),
    ]
    return [piece for piece, _ in pieces], [held for _, held in pieces], come


def local(residual_in, amplitudes, integral_tiles, tile_reader, tile_k, tile_column):
    targets = lax.axis_size("bulk")
    rows_axis = lax.axis_size("row")
    width = integral_tiles.shape[2]
    pieces, positions, far = gather(amplitudes, "bulk")
    outgoing = pack(integral_tiles, tile_reader, tile_k, tile_column, targets, far)
    arrived = lax.all_to_all(outgoing, "bulk", split_axis=0, concat_axis=0, tiled=True)
    size = targets // GROUPS
    groups = []
    for g in range(GROUPS):
        mine = arrived[g * size : (g + 1) * size]
        groups.append(
            [mine] + [send(mine, "row", lambda i: (i + q) % rows_axis) for q in range(1, rows_axis)]
        )
    if amplitudes.shape[1] != width:
        stacked = jnp.concatenate(pieces, axis=0)
        listed = [p for held in positions for p in held]
        place = jnp.asarray([listed.index(p) for p in range(targets)], jnp.int32)
        wanted = jnp.bitwise_xor(jnp.arange(targets, dtype=jnp.int32), lax.axis_index("bulk"))
        stacked = stacked[place[wanted]]
        stacked = stacked.transpose(1, 0, 2).reshape(amplitudes.shape[0], KT, width).transpose(1, 0, 2)
        pieces, positions = [stacked], [(None,) * KT]
    return contract(split(pieces, positions), groups, residual_in)


def solution(mesh):
    placed = (
        P("row", "bulk"),
        P("row", "bulk"),
        P("bulk", "row", None),
        P("bulk", None),
        P("bulk"),
        P("bulk"),
    )
    return jax.shard_map(
        local, mesh=mesh, in_specs=placed, out_specs=P("row", "bulk"), check_vma=False
    )
```

time: 70.1 us -> 70.9 us (1.011)
  waiting for transfers between devices: 23.5 us -> 41.4 us
  starting transfers between devices: 34.9 us -> 19.4 us
  local copies, waits for them, and re-layouts: 2.75 us -> 0.85 us
    ppermute x25 -> x14, starting transfers between devices: 34.9 us -> 13.5 us  [send(): return lax.ppermute(x, axis, [(i, partner(i)) for i in range(size)])]
    ppermute x25 -> x14, waiting for transfers between devices: 23.5 us -> 41.4 us  [send(): return lax.ppermute(x, axis, [(i, partner(i)) for i in range(size)])]
    all_to_all x0 -> x1, starting transfers between devices: none -> 5.88 us  [local(): lax.all_to_all(outgoing, 'bulk', split_axis=0, concat_axis=0, tiled=True)]
    squeeze x1 -> x0, local copies, waits for them, and re-layouts: 1.38 us -> none  [local(): arrived[p] = send(outgoing[p], 'bulk', lambda i: i ^ p)]
    pallas_call x1 -> x2, Pallas kernels: 6.18 us -> 6.37 us  [the longest x1 6.12 us: contract(): pl.pallas_call(functools.partial(contract_kernel, len(groups), len(groups...]
  transfers between devices with their start and end apart: 25 -> 15, of which waited for: 12 -> 6; matrix products, arithmetic and copies ran while one was open for 4% -> 0% of each run, Pallas kernels for 3% -> 0%
where the time goes in v2:
time: 70.9 us; the launch traced here: 70.6 us
  waiting for transfers between devices  41.4 us (58%)
  starting transfers between devices  19.4 us (27%)
  Pallas kernels  8.81 us (12%)
  local copies, waits for them, and re-layouts  0.85 us (1%)
    ppermute x14, waiting for transfers between devices, send(): return lax.ppermute(x, axis, [(i, partner(i)) for i in range(size)])  41.4 us
    ppermute x14, starting transfers between devices, send(): return lax.ppermute(x, axis, [(i, partner(i)) for i in range(size)])  13.5 us
    pallas_call x1, Pallas kernels, contract(): pl.pallas_call(functools.partial(contract_kernel, len(groups), len(groups...  6.12 us
    all_to_all x1, starting transfers between devices, local(): lax.all_to_all(outgoing, 'bulk', split_axis=0, concat_axis=0, tiled=True)  5.88 us
    pallas_call x1, Pallas kernels, pack(): pl.pallas_call(pack_kernel, out_shape=jax.ShapeDtypeStruct((targets, SLOT...  2.44 us
  transfers between devices with their start and end apart: 15, of which 6 were waited for; matrix products, arithmetic and copies ran while one was open for 0% of the time, Pallas kernels for 0%

profile of v2, /device:TPU:0, one launch (start us, length us, event | category | flops | bytes accessed | tf_op | source)
XLA Modules:
  0.0 70.6 jit_solution(9683475294887589254)
XLA Ops:
  0.0 5.0 %collective-permute-start.5 = (f32[1,256,128]{2,1,0:T(8,128)}, f32[1,256,128]{2,1,0:T(8,128)S(1)}, u32[]{:S(2)}, u32[]{:S(2)}) collective-permute-start(f32[1,256,128]{2,1,0:T(8,128)} %bitcast.2), channel_id=1, source_target_pairs={{0,12},{1,13},{2,14},{3,15},{4,8},{5,9},{6,10},{7,11},{8,4},{9,5},... | collective-permute-start | bytes 393224 | tf_op jit(solution)/shard_map/ppermute | solution.py:148
  5.0 0.0 collective-permute-start.4
  5.1 0.6 collective-permute-start.3
  5.6 4.1 %collective-permute-done.5.refs_2_ = f32[1,256,128]{2,1,0:T(8,128)S(1)} collective-permute-done((f32[1,256,128]{2,1,0:T(8,128)}, f32[1,256,128]{2,1,0:T(8,128)S(1)}, u32[]{:S(2)}, u32[]{:S(2)}) %collective-permute-start.5) | collective-permute-done | bytes 131104 | tf_op jit(solution)/shard_map/ppermute | solution.py:148
  9.7 0.0 copy-start.2
  9.7 6.6 %collective-permute-done.4.refs_1_ = f32[1,256,128]{2,1,0:T(8,128)S(1)} collective-permute-done((f32[1,256,128]{2,1,0:T(8,128)}, f32[1,256,128]{2,1,0:T(8,128)S(1)}, u32[]{:S(2)}, u32[]{:S(2)}) %collective-permute-start.4) | collective-permute-done | bytes 131104 | tf_op jit(solution)/shard_map/ppermute | solution.py:148
  16.3 0.0 copy-start.4
  16.3 0.0 collective-permute-done.3.refs_0_
  16.3 0.0 copy-start.6
  16.3 0.0 copy-done.2
  16.3 0.6 copy-done.4
  17.0 0.0 copy-done.6
  17.0 2.4 %shard_map.65 = f32[16,136,128]{2,1,0:T(8,128)} custom-call(s32[16]{0:T(128)} %bitcast.8, s32[16]{0:T(128)} %k_ref.1, s32[16]{0:T(128)} %column_ref.1, f32[16,64,128]{2,1,0:T(8,128)} %tiles_ref.1, f32[1,256,128]{2,1,0:T(8,128)} %copy-done.6, f32[1,256,128]{2,1,0:T(8,128)} %copy-done.4, f32[1,256,128]{2,1,0:T(8,128)} %copy-done.2), custom_call_target="tpu_custom_call" | custom-call | bytes 1572864 | tf_op jit(solution)/shard_map/pallas_call | solution.py:43
  19.5 0.0 copy-start.7
  19.5 0.0 copy-start.5
  19.5 0.0 copy-start.3
  19.5 0.0 copy-start.1
  19.5 5.9 %all-to-all-start = ((f32[16,136,128]{2,1,0:T(8,128)}), f32[16,136,128]{2,1,0:T(8,128)S(1)}, u32[]{:S(2)}, u32[]{:S(2)}) async-start(f32[16,136,128]{2,1,0:T(8,128)} %shard_map.65), calls=%async_computation | async-start | bytes 2228224 | tf_op jit(solution)/shard_map/all_to_all | solution.py:177
  25.4 0.0 copy-done.7
  25.4 0.0 copy-done.5
  25.4 0.0 copy-done.3
  25.5 2.0 %collective-permute-start.7 = (f32[3,256,128]{2,1,0:T(8,128)S(1)}, f32[3,256,128]{2,1,0:T(8,128)S(1)}, u32[]{:S(2)}, u32[]{:S(2)}) collective-permute-start(f32[3,256,128]{2,1,0:T(8,128)S(1)} %constant_dynamic-update-slice_fusion.refs_4_), channel_id=1, source_target_pairs={{0,2},{1,3},{2,0},{3,1},{4,6},{5,7},{6,4},{7,5},{8,10},{9,11},{10,... | collective-permute-start | bytes 1179656 | tf_op jit(solution)/shard_map/ppermute | solution.py:148
  27.5 1.5 %collective-permute-start.6 = (f32[3,256,128]{2,1,0:T(8,128)S(1)}, f32[3,256,128]{2,1,0:T(8,128)S(1)}, u32[]{:S(2)}, u32[]{:S(2)}) collective-permute-start(f32[3,256,128]{2,1,0:T(8,128)S(1)} %constant_dynamic-update-slice_fusion.refs_4_), channel_id=1, source_target_pairs={{0,1},{1,0},{2,3},{3,2},{4,5},{5,4},{6,7},{7,6},{8,9},{9,8},{10,11... | collective-permute-start | bytes 1179656 | tf_op jit(solution)/shard_map/ppermute | solution.py:148
  28.9 0.0 copy-done.1
  28.9 0.6 collective-permute-start.1
  29.5 0.1 collective-permute-start
  29.6 19.9 %collective-permute-done.1.refs_2_ = f32[1,256,128]{2,1,0:T(8,128)S(1)} collective-permute-done((f32[1,256,128]{2,1,0:T(8,128)S(1)}, f32[1,256,128]{2,1,0:T(8,128)S(1)}, u32[]{:S(2)}, u32[]{:S(2)}) %collective-permute-start.1) | collective-permute-done | bytes 131104 | tf_op jit(solution)/shard_map/ppermute | solution.py:148
  49.5 1.9 %collective-permute-start.2 = (f32[1,256,128]{2,1,0:T(8,128)S(1)}, f32[1,256,128]{2,1,0:T(8,128)S(1)}, u32[]{:S(2)}, u32[]{:S(2)}) collective-permute-start(f32[1,256,128]{2,1,0:T(8,128)S(1)} %collective-permute-done.1.refs_2_), channel_id=1, source_target_pairs={{0,1},{1,0},{2,3},{3,2},{4,5},{5,4},{6,7},{7,6},{8,9},{9,8},{10,11... | collective-permute-start | bytes 393224 | tf_op jit(solution)/shard_map/ppermute | solution.py:148
  51.4 0.0 collective-permute-done.7.refs_6_
  51.4 0.2 collective-permute-start.9
  51.6 0.0 all-to-all-done
  51.6 0.1 fusion
  51.7 0.1 collective-permute-start.13
  51.7 0.0 collective-permute-done.refs_1_
  51.8 0.5 collective-permute-start.12
  52.2 3.1 %collective-permute-done.2.refs_3_ = f32[1,256,128]{2,1,0:T(8,128)S(1)} collective-permute-done((f32[1,256,128]{2,1,0:T(8,128)S(1)}, f32[1,256,128]{2,1,0:T(8,128)S(1)}, u32[]{:S(2)}, u32[]{:S(2)}) %collective-permute-start.2) | collective-permute-done | bytes 131104 | tf_op jit(solution)/shard_map/ppermute | solution.py:148
  55.3 0.0 collective-permute-start.11
  55.3 0.0 collective-permute-done.6.refs_5_
  55.3 0.5 collective-permute-start.10
  55.9 0.0 copy-start
  55.9 0.9 %collective-permute-done.9.refs_8_ = f32[1,256,128]{2,1,0:T(8,128)S(1)} collective-permute-done((f32[1,256,128]{2,1,0:T(8,128)S(1)}, f32[1,256,128]{2,1,0:T(8,128)S(1)}, u32[]{:S(2)}, u32[]{:S(2)}) %collective-permute-start.9) | collective-permute-done | bytes 131104 | tf_op jit(solution)/shard_map/ppermute | solution.py:148
  56.7 0.6 collective-permute-start.8
  57.3 6.8 %collective-permute-done.8.refs_7_ = f32[2,256,128]{2,1,0:T(8,128)S(1)} collective-permute-done((f32[2,256,128]{2,1,0:T(8,128)S(1)}, f32[2,256,128]{2,1,0:T(8,128)S(1)}, u32[]{:S(2)}, u32[]{:S(2)}) %collective-permute-start.8) | collective-permute-done | bytes 262176 | tf_op jit(solution)/shard_map/ppermute | solution.py:148
  64.2 0.3 shard_map.64.split_ref
  64.4 0.0 collective-permute-done.13.refs_7_
  64.4 0.0 collective-permute-done.12.refs_5_
  64.5 0.0 collective-permute-done.11.refs_3_
  64.5 0.0 collective-permute-done.10.refs_1_
  64.5 0.0 copy-done
  64.5 6.1 %shard_map.66 = f32[256,1024]{1,0:T(8,128)} custom-call(bf16[16,256,256]{2,1,0:T(8,128)(2,1)S(1)} %shard_map.64.split_ref, f32[4,136,128]{2,1,0:T(8,128)S(1)} %get-tuple-element.8.refs_0_, f32[4,136,128]{2,1,0:T(8,128)S(1)} %collective-permute-done.10.refs_1_, f32[4,136,128]{2,1,0:T(8,128)S(1)} %get-tuple-element.7.refs_2_, ...), custom_call_target="tpu_custom_call" | custom-call | tf_op jit(solution)/shard_map/pallas_call | solution.py:133
  (5 shorter events, 0.1 us)
Async XLA Ops:
  0.0 9.7 %collective-permute-start.5 = (f32[1,256,128]{2,1,0:T(8,128)}, f32[1,256,128]{2,1,0:T(8,128)S(1)}, u32[]{:S(2)}, u32[]{:S(2)}) collective-permute-start(f32[1,256,128]{2,1,0:T(8,128)} %bitcast.2), channel_id=1, source_target_pairs={{0,12},{1,13},{2,14},{3,15},{4,8},{5,9},{6,10},{7,11},{8,4},{9,5},... | collective-permute-start | bytes 393224 | tf_op jit(solution)/shard_map/ppermute | solution.py:148
  5.0 11.3 %collective-permute-start.4 = (f32[1,256,128]{2,1,0:T(8,128)}, f32[1,256,128]{2,1,0:T(8,128)S(1)}, u32[]{:S(2)}, u32[]{:S(2)}) collective-permute-start(f32[1,256,128]{2,1,0:T(8,128)} %bitcast.3), channel_id=1, source_target_pairs={{0,8},{1,9},{2,10},{3,11},{4,12},{5,13},{6,14},{7,15},{8,0},{9,1},... | collective-permute-start | bytes 393224 | tf_op jit(solution)/shard_map/ppermute | solution.py:148
  5.1 11.3 %collective-permute-start.3 = (f32[1,256,128]{2,1,0:T(8,128)}, f32[1,256,128]{2,1,0:T(8,128)S(1)}, u32[]{:S(2)}, u32[]{:S(2)}) collective-permute-start(f32[1,256,128]{2,1,0:T(8,128)} %bitcast.4), channel_id=1, source_target_pairs={{0,4},{1,5},{2,6},{3,7},{4,0},{5,1},{6,2},{7,3},{8,12},{9,13},{10,... | collective-permute-start | bytes 393224 | tf_op jit(solution)/shard_map/ppermute | solution.py:148
  9.7 6.7 %copy-start.2 = (f32[1,256,128]{2,1,0:T(8,128)}, f32[1,256,128]{2,1,0:T(8,128)S(1)}, u32[]{:S(2)}) copy-start(f32[1,256,128]{2,1,0:T(8,128)S(1)} %collective-permute-done.5.refs_2_) | copy-start | bytes 393220
  16.3 0.7 copy-start.4
  16.3 0.7 copy-start.6
  19.5 5.9 %copy-start.7 = (f32[1,256,128]{2,1,0:T(8,128)S(1)}, f32[1,256,128]{2,1,0:T(8,128)}, u32[]{:S(2)}) copy-start(f32[1,256,128]{2,1,0:T(8,128)} %copy-done.6) | copy-start | bytes 393220
  19.5 5.9 %copy-start.5 = (f32[1,256,128]{2,1,0:T(8,128)S(1)}, f32[1,256,128]{2,1,0:T(8,128)}, u32[]{:S(2)}) copy-start(f32[1,256,128]{2,1,0:T(8,128)} %copy-done.4) | copy-start | bytes 393220
  19.5 6.0 %copy-start.3 = (f32[1,256,128]{2,1,0:T(8,128)S(1)}, f32[1,256,128]{2,1,0:T(8,128)}, u32[]{:S(2)}) copy-start(f32[1,256,128]{2,1,0:T(8,128)} %copy-done.2) | copy-start | bytes 393220
  19.5 9.4 %copy-start.1 = (f32[256,128]{1,0:T(8,128)S(1)}, f32[256,128]{1,0:T(8,128)}, u32[]{:S(2)}) copy-start(f32[256,128]{1,0:T(8,128)} %param.7) | copy-start | bytes 393220
  19.5 32.1 %all-to-all-start = ((f32[16,136,128]{2,1,0:T(8,128)}), f32[16,136,128]{2,1,0:T(8,128)S(1)}, u32[]{:S(2)}, u32[]{:S(2)}) async-start(f32[16,136,128]{2,1,0:T(8,128)} %shard_map.65), calls=%async_computation | async-start | bytes 2228224 | tf_op jit(solution)/shard_map/all_to_all | solution.py:177
  25.5 25.9 %collective-permute-start.7 = (f32[3,256,128]{2,1,0:T(8,128)S(1)}, f32[3,256,128]{2,1,0:T(8,128)S(1)}, u32[]{:S(2)}, u32[]{:S(2)}) collective-permute-start(f32[3,256,128]{2,1,0:T(8,128)S(1)} %constant_dynamic-update-slice_fusion.refs_4_), channel_id=1, source_target_pairs={{0,2},{1,3},{2,0},{3,1},{4,6},{5,7},{6,4},{7,5},{8,10},{9,11},{10,... | collective-permute-start | bytes 1179656 | tf_op jit(solution)/shard_map/ppermute | solution.py:148
  27.5 27.9 %collective-permute-start.6 = (f32[3,256,128]{2,1,0:T(8,128)S(1)}, f32[3,256,128]{2,1,0:T(8,128)S(1)}, u32[]{:S(2)}, u32[]{:S(2)}) collective-permute-start(f32[3,256,128]{2,1,0:T(8,128)S(1)} %constant_dynamic-update-slice_fusion.refs_4_), channel_id=1, source_target_pairs={{0,1},{1,0},{2,3},{3,2},{4,5},{5,4},{6,7},{7,6},{8,9},{9,8},{10,11... | collective-permute-start | bytes 1179656 | tf_op jit(solution)/shard_map/ppermute | solution.py:148
  28.9 20.5 %collective-permute-start.1 = (f32[1,256,128]{2,1,0:T(8,128)S(1)}, f32[1,256,128]{2,1,0:T(8,128)S(1)}, u32[]{:S(2)}, u32[]{:S(2)}) collective-permute-start(f32[1,256,128]{2,1,0:T(8,128)S(1)} %bitcast.5), channel_id=1, source_target_pairs={{0,2},{1,3},{2,0},{3,1},{4,6},{5,7},{6,4},{7,5},{8,10},{9,11},{10,... | collective-permute-start | bytes 393224 | tf_op jit(solution)/shard_map/ppermute | solution.py:148
  29.5 22.3 %collective-permute-start = (f32[1,256,128]{2,1,0:T(8,128)S(1)}, f32[1,256,128]{2,1,0:T(8,128)S(1)}, u32[]{:S(2)}, u32[]{:S(2)}) collective-permute-start(f32[1,256,128]{2,1,0:T(8,128)S(1)} %bitcast.6), channel_id=1, source_target_pairs={{0,1},{1,0},{2,3},{3,2},{4,5},{5,4},{6,7},{7,6},{8,9},{9,8},{10,11... | collective-permute-start | bytes 393224 | tf_op jit(solution)/shard_map/ppermute | solution.py:148
  49.5 5.9 %collective-permute-start.2 = (f32[1,256,128]{2,1,0:T(8,128)S(1)}, f32[1,256,128]{2,1,0:T(8,128)S(1)}, u32[]{:S(2)}, u32[]{:S(2)}) collective-permute-start(f32[1,256,128]{2,1,0:T(8,128)S(1)} %collective-permute-done.1.refs_2_), channel_id=1, source_target_pairs={{0,1},{1,0},{2,3},{3,2},{4,5},{5,4},{6,7},{7,6},{8,9},{9,8},{10,11... | collective-permute-start | bytes 393224 | tf_op jit(solution)/shard_map/ppermute | solution.py:148
  51.4 5.3 %collective-permute-start.9 = (f32[1,256,128]{2,1,0:T(8,128)S(1)}, f32[1,256,128]{2,1,0:T(8,128)S(1)}, u32[]{:S(2)}, u32[]{:S(2)}) collective-permute-start(f32[1,256,128]{2,1,0:T(8,128)S(1)} %slice.25), channel_id=1, source_target_pairs={{0,1},{1,0},{2,3},{3,2},{4,5},{5,4},{6,7},{7,6},{8,9},{9,8},{10,11... | collective-permute-start | bytes 393224 | tf_op jit(solution)/shard_map/ppermute | solution.py:148
  51.7 12.8 %collective-permute-start.13 = (f32[4,136,128]{2,1,0:T(8,128)S(1)}, f32[4,136,128]{2,1,0:T(8,128)S(1)}, u32[]{:S(2)}, u32[]{:S(2)}) collective-permute-start(f32[4,136,128]{2,1,0:T(8,128)S(1)} %get-tuple-element.5.refs_6_), channel_id=1, source_target_pairs={{0,16},{16,0},{1,17},{17,1},{2,18},{18,2},{3,19},{19,3},{4,20},{20... | collective-permute-start | bytes 835592 | tf_op jit(solution)/shard_map/ppermute | solution.py:148
  51.8 12.7 %collective-permute-start.12 = (f32[4,136,128]{2,1,0:T(8,128)S(1)}, f32[4,136,128]{2,1,0:T(8,128)S(1)}, u32[]{:S(2)}, u32[]{:S(2)}) collective-permute-start(f32[4,136,128]{2,1,0:T(8,128)S(1)} %get-tuple-element.6.refs_4_), channel_id=1, source_target_pairs={{0,16},{16,0},{1,17},{17,1},{2,18},{18,2},{3,19},{19,3},{4,20},{20... | collective-permute-start | bytes 835592 | tf_op jit(solution)/shard_map/ppermute | solution.py:148
  55.3 9.1 %collective-permute-start.11 = (f32[4,136,128]{2,1,0:T(8,128)S(1)}, f32[4,136,128]{2,1,0:T(8,128)S(1)}, u32[]{:S(2)}, u32[]{:S(2)}) collective-permute-start(f32[4,136,128]{2,1,0:T(8,128)S(1)} %get-tuple-element.7.refs_2_), channel_id=1, source_target_pairs={{0,16},{16,0},{1,17},{17,1},{2,18},{18,2},{3,19},{19,3},{4,20},{20... | collective-permute-start | bytes 835592 | tf_op jit(solution)/shard_map/ppermute | solution.py:148
  55.3 9.1 %collective-permute-start.10 = (f32[4,136,128]{2,1,0:T(8,128)S(1)}, f32[4,136,128]{2,1,0:T(8,128)S(1)}, u32[]{:S(2)}, u32[]{:S(2)}) collective-permute-start(f32[4,136,128]{2,1,0:T(8,128)S(1)} %get-tuple-element.8.refs_0_), channel_id=1, source_target_pairs={{0,16},{16,0},{1,17},{17,1},{2,18},{18,2},{3,19},{19,3},{4,20},{20... | collective-permute-start | bytes 835592 | tf_op jit(solution)/shard_map/ppermute | solution.py:148
  55.9 8.6 %copy-start = (f32[256,1024]{1,0:T(8,128)S(1)}, f32[256,1024]{1,0:T(8,128)}, u32[]{:S(2)}) copy-start(f32[256,1024]{1,0:T(8,128)} %refs_8_.1) | copy-start | bytes 3145732
  56.7 7.4 %collective-permute-start.8 = (f32[2,256,128]{2,1,0:T(8,128)S(1)}, f32[2,256,128]{2,1,0:T(8,128)S(1)}, u32[]{:S(2)}, u32[]{:S(2)}) collective-permute-start(f32[2,256,128]{2,1,0:T(8,128)S(1)} %slice.24), channel_id=1, source_target_pairs={{0,2},{1,3},{2,0},{3,1},{4,6},{5,7},{6,4},{7,5},{8,10},{9,11},{10,... | collective-permute-start | bytes 786440 | tf_op jit(solution)/shard_map/ppermute | solution.py:148

commit v3 on v2

--- a/solution.py
+++ b/solution.py
@@ -15,39 +15,53 @@
 
 
 def pack_kernel(reader_ref, k_ref, column_ref, tiles_ref, *refs):
-    out_ref, count_ref = refs[-2:]
-    count, height, _ = tiles_ref.shape
-    targets = out_ref.shape[0]
-    out_ref[:, SLOT * height :, :] = jnp.full((targets, META, out_ref.shape[2]), -1.0, jnp.float32)
+    outs, count_ref = refs[:-1], refs[-1]
+    count, height, width = tiles_ref.shape
+    half = outs[0].shape[0] // 2
+    targets = 8 * half
+    me = lax.axis_index("bulk")
+    for out_ref in outs:
+        out_ref[:, SLOT * height :, :] = jnp.full((2 * half, META, width), -1.0, jnp.float32)
     for target in range(targets):
         count_ref[target] = 0
-    lane = lax.broadcasted_iota(jnp.int32, (META, out_ref.shape[2]), 1)
+    lane = lax.broadcasted_iota(jnp.int32, (META, width), 1)
 
     def place(j, carry):
-        target = reader_ref[j]
-        slot = count_ref[target]
-        count_ref[target] = slot + 1
-        out_ref[target, pl.ds(pl.multiple_of(slot * height, height), height), :] = tiles_ref[j]
+        position = jnp.bitwise_xor(reader_ref[j], me)
+        slot = count_ref[position]
+        count_ref[position] = slot + 1
         code = (k_ref[j] * CT + column_ref[j]).astype(jnp.float32)
-        codes = out_ref[target, SLOT * height :, :]
-        out_ref[target, SLOT * height :, :] = jnp.where(lane == slot, code, codes)
+        x, y, z = position % 2, position // 2 % 2, position // 4
+        far = z >= half
+        first, second = jnp.where(far, y, x), jnp.where(far, x, y)
+        which = 2 * far.astype(jnp.int32) + first
+        at = second * half + jnp.where(far, z - half, z)
+        for number, out_ref in enumerate(outs):
+
+            @pl.when(which == number)
+            def _():
+                out_ref[at, pl.ds(pl.multiple_of(slot * height, height), height), :] = tiles_ref[j]
+                codes = out_ref[at, SLOT * height :, :]
+                out_ref[at, SLOT * height :, :] = jnp.where(lane == slot, code, codes)
+
         return carry
 
     lax.fori_loop(0, count, place, 0)
 
 
-def pack(tiles, readers, tile_k, tile_column, targets, after):
+def pack(tiles, readers, tile_k, tile_column, targets):
     _, height, width = tiles.shape
     smem = pl.BlockSpec(memory_space=pltpu.SMEM)
     vmem = pl.BlockSpec(memory_space=pltpu.VMEM)
+    out = jax.ShapeDtypeStruct((targets // 4, SLOT * height + META, width), jnp.float32)
     return pl.pallas_call(
         pack_kernel,
-        out_shape=jax.ShapeDtypeStruct((targets, SLOT * height + META, width), jnp.float32),
-        in_specs=[smem, smem, smem, vmem] + [vmem] * len(after),
-        out_specs=vmem,
+        out_shape=[out] * 4,
+        in_specs=[smem, smem, smem, vmem],
+        out_specs=[vmem] * 4,
         scratch_shapes=[pltpu.SMEM((targets,), jnp.int32)],
         cost_estimate=pl.CostEstimate(flops=0, bytes_accessed=4 * tiles.size * 3, transcendentals=0),
-    )(readers.reshape(-1), tile_k, tile_column, tiles, *after)
+    )(readers.reshape(-1), tile_k, tile_column, tiles)
 
 
 def split_kernel(positions, *refs):
@@ -148,37 +162,49 @@
     return lax.ppermute(x, axis, [(i, partner(i)) for i in range(size)])
 
 
-def gather(block, axis):
-    own = block[None]
-    hop = lambda x, step: send(x, axis, lambda i: i ^ step)
-    far_at = tuple(range(4, lax.axis_size(axis), 4))
-    come = [hop(own, p) for p in far_at]
-    pieces = [(own, (0,)), (hop(own, 1), (1,)), (hop(own, 2), (2,))]
-    far = jnp.concatenate(come, axis=0)
-    far_one, far_two = hop(far, 1), hop(far, 2)
-    cut = 2 * len(far_at) // 3
-    pieces += [
-        (hop(pieces[2][0], 1), (3,)),
-        (far, far_at),
-        (far_one, tuple(p + 1 for p in far_at)),
-        (far_two, tuple(p + 2 for p in far_at)),
-        (hop(far_one[:cut], 2), tuple(p + 3 for p in far_at[:cut])),
-        (hop(far_two[cut:], 1), tuple(p + 3 for p in far_at[cut:])),
-    ]
-    return [piece for piece, _ in pieces], [held for _, held in pieces], come
+def hop(x, step):
+    return send(x, "bulk", lambda i: i ^ step)
+
+
+def gather(block, size):
+    held, at = block[None], (0,)
+    bit = size // 2
+    while bit > 4:
+        held, at = jnp.concatenate([held, hop(held, bit)], axis=0), at + tuple(p ^ bit for p in at)
+        bit //= 2
+    late, late_at = hop(held, 4), tuple(p ^ 4 for p in at)
+    out, out_at = [], []
+    for part, part_at, first, second in ((held, at, 2, 1), (late, late_at, 1, 2)):
+        whole = jnp.concatenate([part, hop(part, first)], axis=0)
+        whole_at = part_at + tuple(p ^ first for p in part_at)
+        out += [whole, hop(whole, second)]
+        out_at += [whole_at, tuple(p ^ second for p in whole_at)]
+    return out, out_at
+
+
+def across(kept, sent, first, second):
+    half = kept.shape[0] // 2
+    come = hop(sent, first)
+    last = hop(jnp.concatenate([kept[half:], come[half:]], axis=0), second)
+    return [jnp.stack([kept[z], come[z], last[z], last[half + z]]) for z in range(half)]
 
 
 def local(residual_in, amplitudes, integral_tiles, tile_reader, tile_k, tile_column):
     targets = lax.axis_size("bulk")
     rows_axis = lax.axis_size("row")
     width = integral_tiles.shape[2]
-    pieces, positions, far = gather(amplitudes, "bulk")
-    outgoing = pack(integral_tiles, tile_reader, tile_k, tile_column, targets, far)
-    arrived = lax.all_to_all(outgoing, "bulk", split_axis=0, concat_axis=0, tiled=True)
-    size = targets // GROUPS
+    pieces, positions = gather(amplitudes, targets)
+    near_kept, near_sent, far_kept, far_sent = pack(
+        integral_tiles, tile_reader, tile_k, tile_column, targets
+    )
+    far = across(far_kept, far_sent, 2, 1)
+    near = across(near_kept, near_sent, 1, 2)
+    planes = near + far
+    planes = [planes[0]] + [hop(plane, 4 * z) for z, plane in enumerate(planes) if z]
+    size = len(planes) // GROUPS
     groups = []
     for g in range(GROUPS):
-        mine = arrived[g * size : (g + 1) * size]
+        mine = jnp.concatenate(planes[g * size : (g + 1) * size], axis=0)
         groups.append(
             [mine] + [send(mine, "row", lambda i: (i + q) % rows_axis) for q in range(1, rows_axis)]
         )

time: 70.9 us -> 61.7 us (0.87); the launches traced: 70.6 us -> 60.5 us
  waiting for transfers between devices: 41.4 us -> 27.1 us
  local copies, waits for them, and re-layouts: 0.85 us -> 2.97 us
  other arithmetic: 0 us -> 1.11 us
    ppermute x14 -> x17, waiting for transfers between devices: 41.4 us -> 27.1 us  [send(): return lax.ppermute(x, axis, [(i, partner(i)) for i in range(size)])]
    ppermute x14 -> x17, starting transfers between devices: 13.5 us -> 20.1 us  [send(): return lax.ppermute(x, axis, [(i, partner(i)) for i in range(size)])]
    all_to_all x1 -> x0, starting transfers between devices: 5.88 us -> none  [local(): lax.all_to_all(outgoing, 'bulk', split_axis=0, concat_axis=0, tiled=True)]
    slice x3 -> x9, local copies, waits for them, and re-layouts: 0.1 us -> 2.92 us  [the longest x4 1.86 us: across(): last = hop(jnp.concatenate([kept[half:], come[half:]], axis=0), second)]
    concatenate x0 -> x4, other arithmetic: none -> 1.02 us  [the longest x1 0.93 us: gather(): jnp.concatenate([held, hop(held, bit)], axis=0)]
  transfers between devices with their start and end apart: 15 -> 17, of which waited for: 6 -> 7; matrix products, arithmetic and copies ran while one was open for 0% -> 7% of each run, Pallas kernels for 0% -> 5%
where the time goes in v3:
time: 61.7 us; the launch traced here: 60.5 us
  waiting for transfers between devices  27.1 us (44%)
  starting transfers between devices  20.1 us (33%)
  Pallas kernels  9.04 us (15%)
  local copies, waits for them, and re-layouts  2.97 us (5%)
  other arithmetic  1.11 us (2%)
    ppermute x17, waiting for transfers between devices, send(): return lax.ppermute(x, axis, [(i, partner(i)) for i in range(size)])  27.1 us
    ppermute x17, starting transfers between devices, send(): return lax.ppermute(x, axis, [(i, partner(i)) for i in range(size)])  20.1 us
    pallas_call x1, Pallas kernels, contract(): pl.pallas_call(functools.partial(contract_kernel, len(groups), len(groups...  5.92 us
    pallas_call x1, Pallas kernels, pack(): pl.pallas_call(pack_kernel, out_shape=[out] * 4, in_specs=[smem, smem, sm...  2.87 us
    slice x4, local copies, waits for them, and re-layouts, across(): last = hop(jnp.concatenate([kept[half:], come[half:]], axis=0), second)  1.86 us
  transfers between devices with their start and end apart: 17, of which 7 were waited for; matrix products, arithmetic and copies ran while one was open for 7% of the time, Pallas kernels for 5%

profile of v3, /device:TPU:0, one launch (start us, length us, event | category | flops | bytes accessed | tf_op | source)
XLA Modules:
  0.0 60.5 jit_solution(13767806843875617281)
XLA Ops:
  0.0 4.0 %collective-permute-start = (f32[1,256,128]{2,1,0:T(8,128)}, f32[1,256,128]{2,1,0:T(8,128)S(1)}, u32[]{:S(2)}, u32[]{:S(2)}) collective-permute-start(f32[1,256,128]{2,1,0:T(8,128)} %bitcast.2), channel_id=1, source_target_pairs={{0,8},{1,9},{2,10},{3,11},{4,12},{5,13},{6,14},{7,15},{8,0},{9,1},... | collective-permute-start | bytes 393224 | tf_op jit(solution)/shard_map/ppermute | solution.py:162
  4.0 0.0 copy-start.1
  4.0 2.9 %shard_map.65 = (f32[4,136,128]{2,1,0:T(8,128)}, f32[4,136,128]{2,1,0:T(8,128)}, f32[4,136,128]{2,1,0:T(8,128)}, f32[4,136,128]{2,1,0:T(8,128)}) custom-call(s32[16]{0:T(128)} %bitcast.5, s32[16]{0:T(128)} %k_ref.1, s32[16]{0:T(128)} %column_ref.1, f32[16,64,128]{2,1,0:T(8,128)} %tiles_ref.1), custom_call_target="tpu_custom_call" | custom-call | bytes 1572864 | tf_op jit(solution)/shard_map/pallas_call | solution.py:57
  6.9 1.5 %collective-permute-start.6 = (f32[4,136,128]{2,1,0:T(8,128)}, f32[4,136,128]{2,1,0:T(8,128)S(1)}, u32[]{:S(2)}, u32[]{:S(2)}) collective-permute-start(f32[4,136,128]{2,1,0:T(8,128)} %get-tuple-element.10), channel_id=1, source_target_pairs={{0,1},{1,0},{2,3},{3,2},{4,5},{5,4},{6,7},{7,6},{8,9},{9,8},{10,11... | collective-permute-start | bytes 835592 | tf_op jit(solution)/shard_map/ppermute | solution.py:162
  8.4 1.5 %collective-permute-start.11 = (f32[4,136,128]{2,1,0:T(8,128)}, f32[4,136,128]{2,1,0:T(8,128)S(1)}, u32[]{:S(2)}, u32[]{:S(2)}) collective-permute-start(f32[4,136,128]{2,1,0:T(8,128)} %get-tuple-element.12), channel_id=1, source_target_pairs={{0,2},{1,3},{2,0},{3,1},{4,6},{5,7},{6,4},{7,5},{8,10},{9,11},{10,... | collective-permute-start | bytes 835592 | tf_op jit(solution)/shard_map/ppermute | solution.py:162
  9.9 1.0 %fusion = (f32[1,136,128]{2,1,0:T(8,128)S(1)}, f32[1,136,128]{2,1,0:T(8,128)S(1)}, f32[1,136,128]{2,1,0:T(8,128)S(1)}, f32[1,136,128]{2,1,0:T(8,128)S(1)}) fusion(f32[4,136,128]{2,1,0:T(8,128)} %get-tuple-element.11, f32[4,136,128]{2,1,0:T(8,128)} %get-tuple-element.9), kind=kLoop, calls=%fused_computation.10 | loop fusion | bytes 557056 | tf_op jit(solution)/shard_map/slice | solution.py:189
  10.9 0.9 %slice.62 = f32[2,136,128]{2,1,0:T(8,128)S(1)} slice(f32[4,136,128]{2,1,0:T(8,128)} %get-tuple-element.9), slice={[2:4], [0:136], [0:128]} | slice | bytes 278528 | tf_op jit(solution)/shard_map/slice | solution.py:188
  11.8 0.9 %slice.72 = f32[2,136,128]{2,1,0:T(8,128)S(1)} slice(f32[4,136,128]{2,1,0:T(8,128)} %get-tuple-element.11), slice={[2:4], [0:136], [0:128]} | slice | bytes 278528 | tf_op jit(solution)/shard_map/slice | solution.py:188
  12.8 0.0 collective-permute-done
  12.8 0.9 %pad_maximum_fusion.7 = f32[2,256,128]{2,1,0:T(8,128)S(1)} fusion(f32[1,256,128]{2,1,0:T(8,128)S(1)} %collective-permute-done, f32[1,256,128]{2,1,0:T(8,128)} %bitcast.3), kind=kLoop, calls=%fused_computation.7 | loop fusion | flops 65536 | bytes 524288 | tf_op jit(solution)/shard_map/concatenate | solution.py:173
  13.7 1.6 %collective-permute-start.3 = (f32[2,256,128]{2,1,0:T(8,128)S(1)}, f32[2,256,128]{2,1,0:T(8,128)S(1)}, u32[]{:S(2)}, u32[]{:S(2)}) collective-permute-start(f32[2,256,128]{2,1,0:T(8,128)S(1)} %pad_maximum_fusion.7), channel_id=1, source_target_pairs={{0,4},{1,5},{2,6},{3,7},{4,0},{5,1},{6,2},{7,3},{8,12},{9,13},{10,... | collective-permute-start | bytes 786440 | tf_op jit(solution)/shard_map/ppermute | solution.py:162
  15.4 0.5 collective-permute-start.1
  15.9 0.0 collective-permute-done.6
  15.9 1.6 %collective-permute-start.7 = (f32[4,136,128]{2,1,0:T(8,128)S(1)}, f32[4,136,128]{2,1,0:T(8,128)S(1)}, u32[]{:S(2)}, u32[]{:S(2)}) collective-permute-start(f32[4,136,128]{2,1,0:T(8,128)S(1)} %pad_maximum_fusion.1), channel_id=1, source_target_pairs={{0,2},{1,3},{2,0},{3,1},{4,6},{5,7},{6,4},{7,5},{8,10},{9,11},{10,... | collective-permute-start | bytes 835592 | tf_op jit(solution)/shard_map/ppermute | solution.py:162
  17.5 0.0 collective-permute-done.11
  17.5 0.9 %collective-permute-start.12 = (f32[4,136,128]{2,1,0:T(8,128)S(1)}, f32[4,136,128]{2,1,0:T(8,128)S(1)}, u32[]{:S(2)}, u32[]{:S(2)}) collective-permute-start(f32[4,136,128]{2,1,0:T(8,128)S(1)} %pad_maximum_fusion.4), channel_id=1, source_target_pairs={{0,1},{1,0},{2,3},{3,2},{4,5},{5,4},{6,7},{7,6},{8,9},{9,8},{10,11... | collective-permute-start | bytes 835592 | tf_op jit(solution)/shard_map/ppermute | solution.py:162
  18.5 6.1 %collective-permute-done.1 = f32[2,256,128]{2,1,0:T(8,128)S(1)} collective-permute-done((f32[2,256,128]{2,1,0:T(8,128)S(1)}, f32[2,256,128]{2,1,0:T(8,128)S(1)}, u32[]{:S(2)}, u32[]{:S(2)}) %collective-permute-start.1) | collective-permute-done | bytes 262176 | tf_op jit(solution)/shard_map/ppermute | solution.py:162
  24.6 0.0 copy-done.1
  24.6 0.1 pad_maximum_fusion.refs_0_
  24.7 0.6 collective-permute-start.2
  25.3 0.0 collective-permute-done.3
  25.3 1.5 %collective-permute-start.4 = (f32[2,256,128]{2,1,0:T(8,128)S(1)}, f32[2,256,128]{2,1,0:T(8,128)S(1)}, u32[]{:S(2)}, u32[]{:S(2)}) collective-permute-start(f32[2,256,128]{2,1,0:T(8,128)S(1)} %collective-permute-done.3), channel_id=1, source_target_pairs={{0,1},{1,0},{2,3},{3,2},{4,5},{5,4},{6,7},{7,6},{8,9},{9,8},{10,11... | collective-permute-start | bytes 786440 | tf_op jit(solution)/shard_map/ppermute | solution.py:162
  26.8 1.5 %collective-permute-done.7 = f32[4,136,128]{2,1,0:T(8,128)S(1)} collective-permute-done((f32[4,136,128]{2,1,0:T(8,128)S(1)}, f32[4,136,128]{2,1,0:T(8,128)S(1)}, u32[]{:S(2)}, u32[]{:S(2)}) %collective-permute-start.7) | collective-permute-done | bytes 278560 | tf_op jit(solution)/shard_map/ppermute | solution.py:162
  28.3 1.4 %collective-permute-start.9 = (f32[4,136,128]{2,1,0:T(8,128)S(1)}, f32[4,136,128]{2,1,0:T(8,128)S(1)}, u32[]{:S(2)}, u32[]{:S(2)}) collective-permute-start(f32[4,136,128]{2,1,0:T(8,128)S(1)} %pad_maximum_fusion.3), channel_id=1, source_target_pairs={{0,4},{1,5},{2,6},{3,7},{4,0},{5,1},{6,2},{7,3},{8,12},{9,13},{10,... | collective-permute-start | bytes 835592 | tf_op jit(solution)/shard_map/ppermute | solution.py:162
  29.7 0.0 collective-permute-done.12
  29.8 0.4 collective-permute-start.13
  30.2 2.7 %collective-permute-start.15 = (f32[4,136,128]{2,1,0:T(8,128)S(1)}, f32[4,136,128]{2,1,0:T(8,128)S(1)}, u32[]{:S(2)}, u32[]{:S(2)}) collective-permute-start(f32[4,136,128]{2,1,0:T(8,128)S(1)} %pad_maximum_fusion.6), channel_id=1, source_target_pairs={{0,12},{1,13},{2,14},{3,15},{4,8},{5,9},{6,10},{7,11},{8,4},{9,5},... | collective-permute-start | bytes 835592 | tf_op jit(solution)/shard_map/ppermute | solution.py:162
  33.0 8.2 %collective-permute-done.4 = f32[2,256,128]{2,1,0:T(8,128)S(1)} collective-permute-done((f32[2,256,128]{2,1,0:T(8,128)S(1)}, f32[2,256,128]{2,1,0:T(8,128)S(1)}, u32[]{:S(2)}, u32[]{:S(2)}) %collective-permute-start.4) | collective-permute-done | bytes 262176 | tf_op jit(solution)/shard_map/ppermute | solution.py:162
  41.2 1.1 %collective-permute-start.5 = (f32[4,256,128]{2,1,0:T(8,128)S(1)}, f32[4,256,128]{2,1,0:T(8,128)S(1)}, u32[]{:S(2)}, u32[]{:S(2)}) collective-permute-start(f32[4,256,128]{2,1,0:T(8,128)S(1)} %constant_dynamic-update-slice_fusion.refs_2_), channel_id=1, source_target_pairs={{0,2},{1,3},{2,0},{3,1},{4,6},{5,7},{6,4},{7,5},{8,10},{9,11},{10,... | collective-permute-start | bytes 1572872 | tf_op jit(solution)/shard_map/ppermute | solution.py:162
  42.3 0.0 copy-start
  42.3 0.0 collective-permute-done.9.refs_2_
  42.3 0.1 collective-permute-start.8
  42.4 9.8 %collective-permute-done.13.refs_4_ = f32[4,136,128]{2,1,0:T(8,128)S(1)} collective-permute-done((f32[4,136,128]{2,1,0:T(8,128)S(1)}, f32[4,136,128]{2,1,0:T(8,128)S(1)}, u32[]{:S(2)}, u32[]{:S(2)}) %collective-permute-start.13) | collective-permute-done | bytes 278560 | tf_op jit(solution)/shard_map/ppermute | solution.py:162
  52.2 0.0 collective-permute-start.10
  52.3 0.0 collective-permute-done.15.refs_6_
  52.3 0.5 collective-permute-start.14
  52.8 0.0 collective-permute-done.2.refs_1_
  52.8 0.1 collective-permute-start.16
  52.8 0.0 collective-permute-done.5.refs_3_
  52.8 0.3 shard_map.64.split_ref
  53.1 0.0 collective-permute-done.8.refs_1_
  53.1 0.7 %collective-permute-done.10.refs_3_ = f32[4,136,128]{2,1,0:T(8,128)S(1)} collective-permute-done((f32[4,136,128]{2,1,0:T(8,128)S(1)}, f32[4,136,128]{2,1,0:T(8,128)S(1)}, u32[]{:S(2)}, u32[]{:S(2)}) %collective-permute-start.10) | collective-permute-done | bytes 278560 | tf_op jit(solution)/shard_map/ppermute | solution.py:162
  53.8 0.4 collective-permute-done.14.refs_5_
  54.2 0.4 collective-permute-done.16.refs_7_
  54.6 0.0 copy-done
  54.6 5.9 %shard_map.66 = f32[256,1024]{1,0:T(8,128)} custom-call(bf16[16,256,256]{2,1,0:T(8,128)(2,1)S(1)} %shard_map.64.split_ref, f32[4,136,128]{2,1,0:T(8,128)S(1)} %pad_maximum_fusion.2.refs_0_, f32[4,136,128]{2,1,0:T(8,128)S(1)} %collective-permute-done.8.refs_1_, f32[4,136,128]{2,1,0:T(8,128)S(1)} %collective-permute-done.9.refs_2_, ...), custom_call_target="tpu_custom_call" | custom-call | tf_op jit(solution)/shard_map/pallas_call | solution.py:147
  (14 shorter events, 0.3 us)
Async XLA Ops:
  0.0 12.8 %collective-permute-start = (f32[1,256,128]{2,1,0:T(8,128)}, f32[1,256,128]{2,1,0:T(8,128)S(1)}, u32[]{:S(2)}, u32[]{:S(2)}) collective-permute-start(f32[1,256,128]{2,1,0:T(8,128)} %bitcast.2), channel_id=1, source_target_pairs={{0,8},{1,9},{2,10},{3,11},{4,12},{5,13},{6,14},{7,15},{8,0},{9,1},... | collective-permute-start | bytes 393224 | tf_op jit(solution)/shard_map/ppermute | solution.py:162
  4.0 20.6 %copy-start.1 = (f32[256,128]{1,0:T(8,128)S(1)}, f32[256,128]{1,0:T(8,128)}, u32[]{:S(2)}) copy-start(f32[256,128]{1,0:T(8,128)} %param.7) | copy-start | bytes 393220
  6.9 9.0 %collective-permute-start.6 = (f32[4,136,128]{2,1,0:T(8,128)}, f32[4,136,128]{2,1,0:T(8,128)S(1)}, u32[]{:S(2)}, u32[]{:S(2)}) collective-permute-start(f32[4,136,128]{2,1,0:T(8,128)} %get-tuple-element.10), channel_id=1, source_target_pairs={{0,1},{1,0},{2,3},{3,2},{4,5},{5,4},{6,7},{7,6},{8,9},{9,8},{10,11... | collective-permute-start | bytes 835592 | tf_op jit(solution)/shard_map/ppermute | solution.py:162
  8.4 9.1 %collective-permute-start.11 = (f32[4,136,128]{2,1,0:T(8,128)}, f32[4,136,128]{2,1,0:T(8,128)S(1)}, u32[]{:S(2)}, u32[]{:S(2)}) collective-permute-start(f32[4,136,128]{2,1,0:T(8,128)} %get-tuple-element.12), channel_id=1, source_target_pairs={{0,2},{1,3},{2,0},{3,1},{4,6},{5,7},{6,4},{7,5},{8,10},{9,11},{10,... | collective-permute-start | bytes 835592 | tf_op jit(solution)/shard_map/ppermute | solution.py:162
  13.7 11.5 %collective-permute-start.3 = (f32[2,256,128]{2,1,0:T(8,128)S(1)}, f32[2,256,128]{2,1,0:T(8,128)S(1)}, u32[]{:S(2)}, u32[]{:S(2)}) collective-permute-start(f32[2,256,128]{2,1,0:T(8,128)S(1)} %pad_maximum_fusion.7), channel_id=1, source_target_pairs={{0,4},{1,5},{2,6},{3,7},{4,0},{5,1},{6,2},{7,3},{8,12},{9,13},{10,... | collective-permute-start | bytes 786440 | tf_op jit(solution)/shard_map/ppermute | solution.py:162
  15.4 9.2 %collective-permute-start.1 = (f32[2,256,128]{2,1,0:T(8,128)S(1)}, f32[2,256,128]{2,1,0:T(8,128)S(1)}, u32[]{:S(2)}, u32[]{:S(2)}) collective-permute-start(f32[2,256,128]{2,1,0:T(8,128)S(1)} %pad_maximum_fusion.7), channel_id=1, source_target_pairs={{0,2},{1,3},{2,0},{3,1},{4,6},{5,7},{6,4},{7,5},{8,10},{9,11},{10,... | collective-permute-start | bytes 786440 | tf_op jit(solution)/shard_map/ppermute | solution.py:162
  15.9 12.3 %collective-permute-start.7 = (f32[4,136,128]{2,1,0:T(8,128)S(1)}, f32[4,136,128]{2,1,0:T(8,128)S(1)}, u32[]{:S(2)}, u32[]{:S(2)}) collective-permute-start(f32[4,136,128]{2,1,0:T(8,128)S(1)} %pad_maximum_fusion.1), channel_id=1, source_target_pairs={{0,2},{1,3},{2,0},{3,1},{4,6},{5,7},{6,4},{7,5},{8,10},{9,11},{10,... | collective-permute-start | bytes 835592 | tf_op jit(solution)/shard_map/ppermute | solution.py:162
  17.5 12.2 %collective-permute-start.12 = (f32[4,136,128]{2,1,0:T(8,128)S(1)}, f32[4,136,128]{2,1,0:T(8,128)S(1)}, u32[]{:S(2)}, u32[]{:S(2)}) collective-permute-start(f32[4,136,128]{2,1,0:T(8,128)S(1)} %pad_maximum_fusion.4), channel_id=1, source_target_pairs={{0,1},{1,0},{2,3},{3,2},{4,5},{5,4},{6,7},{7,6},{8,9},{9,8},{10,11... | collective-permute-start | bytes 835592 | tf_op jit(solution)/shard_map/ppermute | solution.py:162
  24.7 28.1 %collective-permute-start.2 = (f32[4,256,128]{2,1,0:T(8,128)S(1)}, f32[4,256,128]{2,1,0:T(8,128)S(1)}, u32[]{:S(2)}, u32[]{:S(2)}) collective-permute-start(f32[4,256,128]{2,1,0:T(8,128)S(1)} %pad_maximum_fusion.refs_0_), channel_id=1, source_target_pairs={{0,1},{1,0},{2,3},{3,2},{4,5},{5,4},{6,7},{7,6},{8,9},{9,8},{10,11... | collective-permute-start | bytes 1572872 | tf_op jit(solution)/shard_map/ppermute | solution.py:162
  25.3 15.9 %collective-permute-start.4 = (f32[2,256,128]{2,1,0:T(8,128)S(1)}, f32[2,256,128]{2,1,0:T(8,128)S(1)}, u32[]{:S(2)}, u32[]{:S(2)}) collective-permute-start(f32[2,256,128]{2,1,0:T(8,128)S(1)} %collective-permute-done.3), channel_id=1, source_target_pairs={{0,1},{1,0},{2,3},{3,2},{4,5},{5,4},{6,7},{7,6},{8,9},{9,8},{10,11... | collective-permute-start | bytes 786440 | tf_op jit(solution)/shard_map/ppermute | solution.py:162
  28.3 14.0 %collective-permute-start.9 = (f32[4,136,128]{2,1,0:T(8,128)S(1)}, f32[4,136,128]{2,1,0:T(8,128)S(1)}, u32[]{:S(2)}, u32[]{:S(2)}) collective-permute-start(f32[4,136,128]{2,1,0:T(8,128)S(1)} %pad_maximum_fusion.3), channel_id=1, source_target_pairs={{0,4},{1,5},{2,6},{3,7},{4,0},{5,1},{6,2},{7,3},{8,12},{9,13},{10,... | collective-permute-start | bytes 835592 | tf_op jit(solution)/shard_map/ppermute | solution.py:162
  29.8 22.5 %collective-permute-start.13 = (f32[4,136,128]{2,1,0:T(8,128)S(1)}, f32[4,136,128]{2,1,0:T(8,128)S(1)}, u32[]{:S(2)}, u32[]{:S(2)}) collective-permute-start(f32[4,136,128]{2,1,0:T(8,128)S(1)} %pad_maximum_fusion.5), channel_id=1, source_target_pairs={{0,8},{1,9},{2,10},{3,11},{4,12},{5,13},{6,14},{7,15},{8,0},{9,1},... | collective-permute-start | bytes 835592 | tf_op jit(solution)/shard_map/ppermute | solution.py:162
  30.2 22.0 %collective-permute-start.15 = (f32[4,136,128]{2,1,0:T(8,128)S(1)}, f32[4,136,128]{2,1,0:T(8,128)S(1)}, u32[]{:S(2)}, u32[]{:S(2)}) collective-permute-start(f32[4,136,128]{2,1,0:T(8,128)S(1)} %pad_maximum_fusion.6), channel_id=1, source_target_pairs={{0,12},{1,13},{2,14},{3,15},{4,8},{5,9},{6,10},{7,11},{8,4},{9,5},... | collective-permute-start | bytes 835592 | tf_op jit(solution)/shard_map/ppermute | solution.py:162
  41.2 11.6 %collective-permute-start.5 = (f32[4,256,128]{2,1,0:T(8,128)S(1)}, f32[4,256,128]{2,1,0:T(8,128)S(1)}, u32[]{:S(2)}, u32[]{:S(2)}) collective-permute-start(f32[4,256,128]{2,1,0:T(8,128)S(1)} %constant_dynamic-update-slice_fusion.refs_2_), channel_id=1, source_target_pairs={{0,2},{1,3},{2,0},{3,1},{4,6},{5,7},{6,4},{7,5},{8,10},{9,11},{10,... | collective-permute-start | bytes 1572872 | tf_op jit(solution)/shard_map/ppermute | solution.py:162
  42.3 12.3 %copy-start = (f32[256,1024]{1,0:T(8,128)S(1)}, f32[256,1024]{1,0:T(8,128)}, u32[]{:S(2)}) copy-start(f32[256,1024]{1,0:T(8,128)} %refs_8_.1) | copy-start | bytes 3145732
  42.3 10.8 %collective-permute-start.8 = (f32[4,136,128]{2,1,0:T(8,128)S(1)}, f32[4,136,128]{2,1,0:T(8,128)S(1)}, u32[]{:S(2)}, u32[]{:S(2)}) collective-permute-start(f32[4,136,128]{2,1,0:T(8,128)S(1)} %pad_maximum_fusion.2.refs_0_), channel_id=1, source_target_pairs={{0,16},{16,0},{1,17},{17,1},{2,18},{18,2},{3,19},{19,3},{4,20},{20... | collective-permute-start | bytes 835592 | tf_op jit(solution)/shard_map/ppermute | solution.py:162
  52.2 1.6 %collective-permute-start.10 = (f32[4,136,128]{2,1,0:T(8,128)S(1)}, f32[4,136,128]{2,1,0:T(8,128)S(1)}, u32[]{:S(2)}, u32[]{:S(2)}) collective-permute-start(f32[4,136,128]{2,1,0:T(8,128)S(1)} %collective-permute-done.9.refs_2_), channel_id=1, source_target_pairs={{0,16},{16,0},{1,17},{17,1},{2,18},{18,2},{3,19},{19,3},{4,20},{20... | collective-permute-start | bytes 835592 | tf_op jit(solution)/shard_map/ppermute | solution.py:162
  52.3 2.0 %collective-permute-start.14 = (f32[4,136,128]{2,1,0:T(8,128)S(1)}, f32[4,136,128]{2,1,0:T(8,128)S(1)}, u32[]{:S(2)}, u32[]{:S(2)}) collective-permute-start(f32[4,136,128]{2,1,0:T(8,128)S(1)} %collective-permute-done.13.refs_4_), channel_id=1, source_target_pairs={{0,16},{16,0},{1,17},{17,1},{2,18},{18,2},{3,19},{19,3},{4,20},{20... | collective-permute-start | bytes 835592 | tf_op jit(solution)/shard_map/ppermute | solution.py:162
  52.8 1.8 %collective-permute-start.16 = (f32[4,136,128]{2,1,0:T(8,128)S(1)}, f32[4,136,128]{2,1,0:T(8,128)S(1)}, u32[]{:S(2)}, u32[]{:S(2)}) collective-permute-start(f32[4,136,128]{2,1,0:T(8,128)S(1)} %collective-permute-done.15.refs_6_), channel_id=1, source_target_pairs={{0,16},{16,0},{1,17},{17,1},{2,18},{18,2},{3,19},{19,3},{4,20},{20... | collective-permute-start | bytes 835592 | tf_op jit(solution)/shard_map/ppermute | solution.py:162

commit v4 on v3

--- a/solution.py
+++ b/solution.py
@@ -14,8 +14,9 @@
 META = 8
 
 
-def pack_kernel(reader_ref, k_ref, column_ref, tiles_ref, *refs):
-    outs, count_ref = refs[:-1], refs[-1]
+def pack_kernel(reader_ref, k_ref, column_ref, tiles_ref, block_ref, *refs):
+    copy_ref, outs, count_ref = refs[0], refs[1:-1], refs[-1]
+    copy_ref[0] = block_ref[...]
     count, height, width = tiles_ref.shape
     half = outs[0].shape[0] // 2
     targets = 8 * half
@@ -32,10 +33,10 @@
         count_ref[position] = slot + 1
         code = (k_ref[j] * CT + column_ref[j]).astype(jnp.float32)
         x, y, z = position % 2, position // 2 % 2, position // 4
-        far = z >= half
-        first, second = jnp.where(far, y, x), jnp.where(far, x, y)
-        which = 2 * far.astype(jnp.int32) + first
-        at = second * half + jnp.where(far, z - half, z)
+        odd = z % 2
+        first, second = jnp.where(odd == 1, y, x), jnp.where(odd == 1, x, y)
+        which = 2 * odd + first
+        at = second * half + z // 2
         for number, out_ref in enumerate(outs):
 
             @pl.when(which == number)
@@ -49,19 +50,20 @@
     lax.fori_loop(0, count, place, 0)
 
 
-def pack(tiles, readers, tile_k, tile_column, targets):
+def pack(tiles, readers, tile_k, tile_column, block, targets):
     _, height, width = tiles.shape
     smem = pl.BlockSpec(memory_space=pltpu.SMEM)
     vmem = pl.BlockSpec(memory_space=pltpu.VMEM)
     out = jax.ShapeDtypeStruct((targets // 4, SLOT * height + META, width), jnp.float32)
     return pl.pallas_call(
         pack_kernel,
-        out_shape=[out] * 4,
-        in_specs=[smem, smem, smem, vmem],
-        out_specs=[vmem] * 4,
+        out_shape=[jax.ShapeDtypeStruct((1, *block.shape), block.dtype)] + [out] * 4,
+        in_specs=[smem, smem, smem, vmem, vmem],
+        out_specs=[vmem] * 5,
         scratch_shapes=[pltpu.SMEM((targets,), jnp.int32)],
         cost_estimate=pl.CostEstimate(flops=0, bytes_accessed=4 * tiles.size * 3, transcendentals=0),
-    )(readers.reshape(-1), tile_k, tile_column, tiles)
+        compiler_params=pltpu.CompilerParams(vmem_limit_bytes=8 * 1024 * 1024),
+    )(readers.reshape(-1), tile_k, tile_column, tiles, block)
 
 
 def split_kernel(positions, *refs):
@@ -84,7 +86,7 @@
         out_shape=jax.ShapeDtypeStruct((KT, rows, 2 * width), jnp.bfloat16),
         in_specs=[vmem] * len(pieces),
         out_specs=vmem,
-        compiler_params=pltpu.CompilerParams(vmem_limit_bytes=24 * 1024 * 1024),
+        compiler_params=pltpu.CompilerParams(vmem_limit_bytes=16 * 1024 * 1024),
     )(*pieces)
 
 
@@ -107,34 +109,51 @@
     for fetch in fetches:
         fetch.wait()
 
+    def whole(parts, owner, slot, code):
+        k = code // CT
+        column = code - k * CT
+        ordered = []
+        for place in range(parts_count):
+            piece = parts[0][owner, slot * height : (slot + 1) * height, :]
+            for q in range(1, parts_count):
+                other = parts[q][owner, slot * height : (slot + 1) * height, :]
+                piece = jnp.where(lax.rem(place + q, parts_count) == row, other, piece)
+            ordered.append(piece)
+        return jnp.concatenate(ordered, axis=0), k, column
+
+    def multiply(tile, k, column):
+        high = tile.astype(jnp.bfloat16)
+        low = (tile - high.astype(jnp.float32)).astype(jnp.bfloat16)
+        both = jnp.concatenate([high, low], axis=1)
+        weights = jnp.concatenate([both, both], axis=0)
+        product = jnp.dot(split_ref[k], weights, preferred_element_type=jnp.float32)
+        lanes = pl.ds(pl.multiple_of(column * width, width), width)
+        out_ref[:, lanes] += product[:, :width] + product[:, width:]
+
     def add_group(parts, codes_ref):
-        def add(owner, carry):
-            for slot in range(SLOT):
-                code = codes_ref[owner, 0, slot].astype(jnp.int32)
-
-                @pl.when(code >= 0)
-                def _():
-                    k = code // CT
-                    column = code - k * CT
-                    ordered = []
-                    for place in range(parts_count):
-                        piece = parts[0][owner, slot * height : (slot + 1) * height, :]
-                        for q in range(1, parts_count):
-                            other = parts[q][owner, slot * height : (slot + 1) * height, :]
-                            piece = jnp.where(lax.rem(place + q, parts_count) == row, other, piece)
-                        ordered.append(piece)
-                    tile = jnp.concatenate(ordered, axis=0)
-                    high = tile.astype(jnp.bfloat16)
-                    low = (tile - high.astype(jnp.float32)).astype(jnp.bfloat16)
-                    both = jnp.concatenate([high, low], axis=1)
-                    weights = jnp.concatenate([both, both], axis=0)
-                    product = jnp.dot(split_ref[k], weights, preferred_element_type=jnp.float32)
-                    lanes = pl.ds(pl.multiple_of(column * width, width), width)
-                    out_ref[:, lanes] += product[:, :width] + product[:, width:]
-
+        owners = parts[0].shape[0]
+
+        def first(owner):
+            code = codes_ref[owner, 0, 0].astype(jnp.int32)
+            tile, k, column = whole(parts, owner, 0, jnp.maximum(code, 0))
+            multiply(jnp.where(code >= 0, tile, 0.0), k, column)
+
+        def later(owner, slot):
+            code = codes_ref[owner, 0, slot].astype(jnp.int32)
+
+            @pl.when(code >= 0)
+            def _():
+                multiply(*whole(parts, owner, slot, code))
+
+        def four(step, carry):
+            for i in range(4):
+                first(4 * step + i)
+            for i in range(4):
+                for slot in range(1, SLOT):
+                    later(4 * step + i, slot)
             return carry
 
-        lax.fori_loop(0, parts[0].shape[0], add, 0)
+        lax.fori_loop(0, owners // 4, four, 0)
 
     for parts, codes_ref in zip(groups, codes):
         add_group(parts, codes_ref)
@@ -153,7 +172,7 @@
             *[pltpu.SMEM((parts[0].shape[0], META, width), jnp.float32) for parts in groups],
             pltpu.SemaphoreType.DMA((len(groups),)),
         ],
-        compiler_params=pltpu.CompilerParams(vmem_limit_bytes=40 * 1024 * 1024),
+        compiler_params=pltpu.CompilerParams(vmem_limit_bytes=24 * 1024 * 1024),
     )(*arrays)
 
 
@@ -167,19 +186,17 @@
 
 
 def gather(block, size):
-    held, at = block[None], (0,)
+    held, at = block, (0,)
     bit = size // 2
-    while bit > 4:
+    while bit > 2:
         held, at = jnp.concatenate([held, hop(held, bit)], axis=0), at + tuple(p ^ bit for p in at)
         bit //= 2
-    late, late_at = hop(held, 4), tuple(p ^ 4 for p in at)
-    out, out_at = [], []
-    for part, part_at, first, second in ((held, at, 2, 1), (late, late_at, 1, 2)):
-        whole = jnp.concatenate([part, hop(part, first)], axis=0)
-        whole_at = part_at + tuple(p ^ first for p in part_at)
-        out += [whole, hop(whole, second)]
-        out_at += [whole_at, tuple(p ^ second for p in whole_at)]
-    return out, out_at
+    over_x, over_y = hop(held, 1), hop(held, 2)
+    cut = len(at) // 2
+    pieces = [held, over_x, over_y, hop(over_x[:cut], 2), hop(over_y[cut:], 1)]
+    positions = [at] + [tuple(p ^ step for p in at) for step in (1, 2)]
+    positions += [tuple(p ^ 3 for p in at[:cut]), tuple(p ^ 3 for p in at[cut:])]
+    return pieces, positions
 
 
 def across(kept, sent, first, second):
@@ -193,13 +210,13 @@
     targets = lax.axis_size("bulk")
     rows_axis = lax.axis_size("row")
     width = integral_tiles.shape[2]
-    pieces, positions = gather(amplitudes, targets)
-    near_kept, near_sent, far_kept, far_sent = pack(
-        integral_tiles, tile_reader, tile_k, tile_column, targets
+    block, even_kept, even_sent, odd_kept, odd_sent = pack(
+        integral_tiles, tile_reader, tile_k, tile_column, amplitudes, targets
     )
-    far = across(far_kept, far_sent, 2, 1)
-    near = across(near_kept, near_sent, 1, 2)
-    planes = near + far
+    pieces, positions = gather(block, targets)
+    odd = across(odd_kept, odd_sent, 2, 1)
+    even = across(even_kept, even_sent, 1, 2)
+    planes = [plane for pair in zip(even, odd) for plane in pair]
     planes = [planes[0]] + [hop(plane, 4 * z) for z, plane in enumerate(planes) if z]
     size = len(planes) // GROUPS
     groups = []

time: 61.7 us -> 65.9 us (1.068)
  the two profiles are of different devices: /device:TPU:0 before, /device:TPU:16 now
where the time goes in v4:
time: 65.9 us; the launch traced here: 65.7 us
  waiting for transfers between devices  36.3 us (55%)
  starting transfers between devices  19.1 us (29%)
  Pallas kernels  5.8 us (9%)
  local copies, waits for them, and re-layouts  4.11 us (6%)
    ppermute x17, waiting for transfers between devices, send(): return lax.ppermute(x, axis, [(i, partner(i)) for i in range(size)])  36.3 us
    ppermute x17, starting transfers between devices, send(): return lax.ppermute(x, axis, [(i, partner(i)) for i in range(size)])  19.1 us
    pallas_call x1, Pallas kernels, contract(): pl.pallas_call(functools.partial(contract_kernel, len(groups), len(groups...  4.15 us
    unnamed x14, local copies, waits for them, and re-layouts  3.94 us
    pallas_call x1, Pallas kernels, pack(): pl.pallas_call(pack_kernel, out_shape=[jax.ShapeDtypeStruct((1, *block.sh...  1.4 us
  transfers between devices with their start and end apart: 17, of which 7 were waited for; matrix products, arithmetic and copies ran while one was open for 1% of the time, Pallas kernels for 0%

profile of v4, /device:TPU:16, one launch (start us, length us, event | category | flops | bytes accessed | tf_op | source)
XLA Modules:
  0.0 65.7 jit_solution(7559679646412185612)
XLA Ops:
  0.0 0.0 copy-start.1
  0.0 1.0 %copy-done.1 = f32[16,64,128]{2,1,0:T(8,128)S(1)} copy-done((f32[16,64,128]{2,1,0:T(8,128)S(1)}, f32[16,64,128]{2,1,0:T(8,128)}, u32[]{:S(2)}) %copy-start.1) | copy-done | bytes 524312
  1.0 0.0 copy-start.2
  1.0 0.9 %copy-done.2 = f32[256,128]{1,0:T(8,128)S(1)} copy-done((f32[256,128]{1,0:T(8,128)S(1)}, f32[256,128]{1,0:T(8,128)}, u32[]{:S(2)}) %copy-start.2) | copy-done | bytes 131096
  1.9 0.0 copy-start.3
  1.9 0.7 copy-done.3
  2.6 0.0 copy-start.4
  2.6 0.7 copy-done.4
  3.3 0.0 copy-start.5
  3.3 0.7 copy-done.5
  3.9 1.4 %shard_map.64 = (f32[1,256,128]{2,1,0:T(8,128)S(1)}, f32[4,136,128]{2,1,0:T(8,128)S(1)}, f32[4,136,128]{2,1,0:T(8,128)S(1)}, f32[4,136,128]{2,1,0:T(8,128)S(1)}, f32[4,136,128]{2,1,0:T(8,128)S(1)}) custom-call(s32[16]{0:T(128)S(1)} %bitcast.1, s32[16]{0:T(128)S(1)} %copy-done.4, s32[16]{0:T(128)S(1)} %copy-done.5, f32[16,64,128]{2,1,0:T(8,128)S(1)} %copy-done.1, ...), custom_call_target="tpu_custom_call" | custom-call | bytes 1572864 | tf_op jit(solution)/shard_map/pallas_call | solution.py:58
  5.3 0.1 collective-permute-start
  5.4 1.8 %collective-permute-start.6 = (f32[4,136,128]{2,1,0:T(8,128)S(1)}, f32[4,136,128]{2,1,0:T(8,128)S(1)}, u32[]{:S(2)}, u32[]{:S(2)}) collective-permute-start(f32[4,136,128]{2,1,0:T(8,128)S(1)} %get-tuple-element.12), channel_id=1, source_target_pairs={{0,1},{1,0},{2,3},{3,2},{4,5},{5,4},{6,7},{7,6},{8,9},{9,8},{10,11... | collective-permute-start | bytes 835592 | tf_op jit(solution)/shard_map/ppermute | solution.py:181
  7.2 1.5 %collective-permute-start.9 = (f32[4,136,128]{2,1,0:T(8,128)S(1)}, f32[4,136,128]{2,1,0:T(8,128)S(1)}, u32[]{:S(2)}, u32[]{:S(2)}) collective-permute-start(f32[4,136,128]{2,1,0:T(8,128)S(1)} %get-tuple-element.14), channel_id=1, source_target_pairs={{0,2},{1,3},{2,0},{3,1},{4,6},{5,7},{6,4},{7,5},{8,10},{9,11},{10,... | collective-permute-start | bytes 835592 | tf_op jit(solution)/shard_map/ppermute | solution.py:181
  8.8 2.8 %collective-permute-done = f32[1,256,128]{2,1,0:T(8,128)S(1)} collective-permute-done((f32[1,256,128]{2,1,0:T(8,128)S(1)}, f32[1,256,128]{2,1,0:T(8,128)S(1)}, u32[]{:S(2)}, u32[]{:S(2)}) %collective-permute-start) | collective-permute-done | bytes 131104 | tf_op jit(solution)/shard_map/ppermute | solution.py:181
  11.6 4.2 %collective-permute-start.1 = (f32[2,256,128]{2,1,0:T(8,128)S(1)}, f32[2,256,128]{2,1,0:T(8,128)S(1)}, u32[]{:S(2)}, u32[]{:S(2)}) collective-permute-start(f32[2,256,128]{2,1,0:T(8,128)S(1)} %pad_maximum_fusion.6), channel_id=1, source_target_pairs={{0,4},{1,5},{2,6},{3,7},{4,0},{5,1},{6,2},{7,3},{8,12},{9,13},{10,... | collective-permute-start | bytes 786440 | tf_op jit(solution)/shard_map/ppermute | solution.py:181
  15.9 0.0 collective-permute-done.6
  16.0 1.6 %collective-permute-start.7 = (f32[4,136,128]{2,1,0:T(8,128)S(1)}, f32[4,136,128]{2,1,0:T(8,128)S(1)}, u32[]{:S(2)}, u32[]{:S(2)}) collective-permute-start(f32[4,136,128]{2,1,0:T(8,128)S(1)} %pad_maximum_fusion), channel_id=1, source_target_pairs={{0,2},{1,3},{2,0},{3,1},{4,6},{5,7},{6,4},{7,5},{8,10},{9,11},{10,... | collective-permute-start | bytes 835592 | tf_op jit(solution)/shard_map/ppermute | solution.py:181
  17.5 0.0 collective-permute-done.9
  17.6 1.6 %collective-permute-start.10 = (f32[4,136,128]{2,1,0:T(8,128)S(1)}, f32[4,136,128]{2,1,0:T(8,128)S(1)}, u32[]{:S(2)}, u32[]{:S(2)}) collective-permute-start(f32[4,136,128]{2,1,0:T(8,128)S(1)} %pad_maximum_fusion.2), channel_id=1, source_target_pairs={{0,1},{1,0},{2,3},{3,2},{4,5},{5,4},{6,7},{7,6},{8,9},{9,8},{10,11... | collective-permute-start | bytes 835592 | tf_op jit(solution)/shard_map/ppermute | solution.py:181
  19.2 3.2 %collective-permute-done.1 = f32[2,256,128]{2,1,0:T(8,128)S(1)} collective-permute-done((f32[2,256,128]{2,1,0:T(8,128)S(1)}, f32[2,256,128]{2,1,0:T(8,128)S(1)}, u32[]{:S(2)}, u32[]{:S(2)}) %collective-permute-start.1) | collective-permute-done | bytes 262176 | tf_op jit(solution)/shard_map/ppermute | solution.py:181
  22.4 1.6 %collective-permute-start.2 = (f32[4,256,128]{2,1,0:T(8,128)S(1)}, f32[4,256,128]{2,1,0:T(8,128)S(1)}, u32[]{:S(2)}, u32[]{:S(2)}) collective-permute-start(f32[4,256,128]{2,1,0:T(8,128)S(1)} %constant_dynamic-update-slice_fusion.refs_0_), channel_id=1, source_target_pairs={{0,1},{1,0},{2,3},{3,2},{4,5},{5,4},{6,7},{7,6},{8,9},{9,8},{10,11... | collective-permute-start | bytes 1572872 | tf_op jit(solution)/shard_map/ppermute | solution.py:181
  23.9 1.5 %collective-permute-start.3 = (f32[4,256,128]{2,1,0:T(8,128)S(1)}, f32[4,256,128]{2,1,0:T(8,128)S(1)}, u32[]{:S(2)}, u32[]{:S(2)}) collective-permute-start(f32[4,256,128]{2,1,0:T(8,128)S(1)} %constant_dynamic-update-slice_fusion.refs_0_), channel_id=1, source_target_pairs={{0,2},{1,3},{2,0},{3,1},{4,6},{5,7},{6,4},{7,5},{8,10},{9,11},{10,... | collective-permute-start | bytes 1572872 | tf_op jit(solution)/shard_map/ppermute | solution.py:181
  25.5 0.0 collective-permute-done.7
  25.5 0.1 collective-permute-start.13
  25.6 1.1 %collective-permute-done.10 = f32[4,136,128]{2,1,0:T(8,128)S(1)} collective-permute-done((f32[4,136,128]{2,1,0:T(8,128)S(1)}, f32[4,136,128]{2,1,0:T(8,128)S(1)}, u32[]{:S(2)}, u32[]{:S(2)}) %collective-permute-start.10) | collective-permute-done | bytes 278560 | tf_op jit(solution)/shard_map/ppermute | solution.py:181
  26.8 2.1 %collective-permute-start.15 = (f32[4,136,128]{2,1,0:T(8,128)S(1)}, f32[4,136,128]{2,1,0:T(8,128)S(1)}, u32[]{:S(2)}, u32[]{:S(2)}) collective-permute-start(f32[4,136,128]{2,1,0:T(8,128)S(1)} %pad_maximum_fusion.5), channel_id=1, source_target_pairs={{0,12},{1,13},{2,14},{3,15},{4,8},{5,9},{6,10},{7,11},{8,4},{9,5},... | collective-permute-start | bytes 835592 | tf_op jit(solution)/shard_map/ppermute | solution.py:181
  28.9 1.3 %collective-permute-start.11 = (f32[4,136,128]{2,1,0:T(8,128)S(1)}, f32[4,136,128]{2,1,0:T(8,128)S(1)}, u32[]{:S(2)}, u32[]{:S(2)}) collective-permute-start(f32[4,136,128]{2,1,0:T(8,128)S(1)} %pad_maximum_fusion.3), channel_id=1, source_target_pairs={{0,4},{1,5},{2,6},{3,7},{4,0},{5,1},{6,2},{7,3},{8,12},{9,13},{10,... | collective-permute-start | bytes 835592 | tf_op jit(solution)/shard_map/ppermute | solution.py:181
  30.2 6.7 %collective-permute-done.2.refs_1_ = f32[4,256,128]{2,1,0:T(8,128)S(1)} collective-permute-done((f32[4,256,128]{2,1,0:T(8,128)S(1)}, f32[4,256,128]{2,1,0:T(8,128)S(1)}, u32[]{:S(2)}, u32[]{:S(2)}) %collective-permute-start.2) | collective-permute-done | bytes 524320 | tf_op jit(solution)/shard_map/ppermute | solution.py:181
  36.9 0.6 collective-permute-start.4
  37.5 6.4 %collective-permute-done.13.refs_4_ = f32[4,136,128]{2,1,0:T(8,128)S(1)} collective-permute-done((f32[4,136,128]{2,1,0:T(8,128)S(1)}, f32[4,136,128]{2,1,0:T(8,128)S(1)}, u32[]{:S(2)}, u32[]{:S(2)}) %collective-permute-start.13) | collective-permute-done | bytes 278560 | tf_op jit(solution)/shard_map/ppermute | solution.py:181
  43.9 0.0 collective-permute-start.8
  43.9 8.0 %collective-permute-done.15.refs_6_ = f32[4,136,128]{2,1,0:T(8,128)S(1)} collective-permute-done((f32[4,136,128]{2,1,0:T(8,128)S(1)}, f32[4,136,128]{2,1,0:T(8,128)S(1)}, u32[]{:S(2)}, u32[]{:S(2)}) %collective-permute-start.15) | collective-permute-done | bytes 278560 | tf_op jit(solution)/shard_map/ppermute | solution.py:181
  51.9 0.0 collective-permute-start.14
  51.9 0.0 collective-permute-done.11.refs_2_
  51.9 0.5 collective-permute-start.16
  52.4 0.0 collective-permute-done.3.refs_2_
  52.4 0.1 collective-permute-start.12
  52.5 0.0 copy-start
  52.5 0.0 collective-permute-done.4.refs_3_
  52.5 0.6 collective-permute-start.5
  53.1 8.1 %collective-permute-done.5.refs_4_ = f32[2,256,128]{2,1,0:T(8,128)S(1)} collective-permute-done((f32[2,256,128]{2,1,0:T(8,128)S(1)}, f32[2,256,128]{2,1,0:T(8,128)S(1)}, u32[]{:S(2)}, u32[]{:S(2)}) %collective-permute-start.5) | collective-permute-done | bytes 262176 | tf_op jit(solution)/shard_map/ppermute | solution.py:181
  61.2 0.3 shard_map.65.split_ref
  61.5 0.0 collective-permute-done.8.refs_1_
  61.5 0.0 collective-permute-done.14.refs_5_
  61.5 0.0 collective-permute-done.16.refs_7_
  61.5 0.0 collective-permute-done.12.refs_3_
  61.5 0.0 copy-done
  61.6 4.1 %shard_map.66 = f32[256,1024]{1,0:T(8,128)} custom-call(bf16[16,256,256]{2,1,0:T(8,128)(2,1)S(1)} %shard_map.65.split_ref, f32[4,136,128]{2,1,0:T(8,128)S(1)} %pad_maximum_fusion.1.refs_0_, f32[4,136,128]{2,1,0:T(8,128)S(1)} %collective-permute-done.8.refs_1_, f32[4,136,128]{2,1,0:T(8,128)S(1)} %collective-permute-done.11.refs_2_, ...), custom_call_target="tpu_custom_call" | custom-call | tf_op jit(solution)/shard_map/pallas_call | solution.py:166
  (21 shorter events, 0.4 us)
Async XLA Ops:
  0.0 1.0 %copy-start.1 = (f32[16,64,128]{2,1,0:T(8,128)S(1)}, f32[16,64,128]{2,1,0:T(8,128)}, u32[]{:S(2)}) copy-start(f32[16,64,128]{2,1,0:T(8,128)} %tiles_ref.1) | copy-start | bytes 1572868
  1.0 0.9 %copy-start.2 = (f32[256,128]{1,0:T(8,128)S(1)}, f32[256,128]{1,0:T(8,128)}, u32[]{:S(2)}) copy-start(f32[256,128]{1,0:T(8,128)} %block_ref.1) | copy-start | bytes 393220
  1.9 0.7 copy-start.3
  2.6 0.7 copy-start.4
  3.3 0.7 copy-start.5
  5.3 6.3 %collective-permute-start = (f32[1,256,128]{2,1,0:T(8,128)S(1)}, f32[1,256,128]{2,1,0:T(8,128)S(1)}, u32[]{:S(2)}, u32[]{:S(2)}) collective-permute-start(f32[1,256,128]{2,1,0:T(8,128)S(1)} %get-tuple-element.10), channel_id=1, source_target_pairs={{0,8},{1,9},{2,10},{3,11},{4,12},{5,13},{6,14},{7,15},{8,0},{9,1},... | collective-permute-start | bytes 393224 | tf_op jit(solution)/shard_map/ppermute | solution.py:181
  5.4 10.5 %collective-permute-start.6 = (f32[4,136,128]{2,1,0:T(8,128)S(1)}, f32[4,136,128]{2,1,0:T(8,128)S(1)}, u32[]{:S(2)}, u32[]{:S(2)}) collective-permute-start(f32[4,136,128]{2,1,0:T(8,128)S(1)} %get-tuple-element.12), channel_id=1, source_target_pairs={{0,1},{1,0},{2,3},{3,2},{4,5},{5,4},{6,7},{7,6},{8,9},{9,8},{10,11... | collective-permute-start | bytes 835592 | tf_op jit(solution)/shard_map/ppermute | solution.py:181
  7.2 10.3 %collective-permute-start.9 = (f32[4,136,128]{2,1,0:T(8,128)S(1)}, f32[4,136,128]{2,1,0:T(8,128)S(1)}, u32[]{:S(2)}, u32[]{:S(2)}) collective-permute-start(f32[4,136,128]{2,1,0:T(8,128)S(1)} %get-tuple-element.14), channel_id=1, source_target_pairs={{0,2},{1,3},{2,0},{3,1},{4,6},{5,7},{6,4},{7,5},{8,10},{9,11},{10,... | collective-permute-start | bytes 835592 | tf_op jit(solution)/shard_map/ppermute | solution.py:181
  11.6 10.7 %collective-permute-start.1 = (f32[2,256,128]{2,1,0:T(8,128)S(1)}, f32[2,256,128]{2,1,0:T(8,128)S(1)}, u32[]{:S(2)}, u32[]{:S(2)}) collective-permute-start(f32[2,256,128]{2,1,0:T(8,128)S(1)} %pad_maximum_fusion.6), channel_id=1, source_target_pairs={{0,4},{1,5},{2,6},{3,7},{4,0},{5,1},{6,2},{7,3},{8,12},{9,13},{10,... | collective-permute-start | bytes 786440 | tf_op jit(solution)/shard_map/ppermute | solution.py:181
  16.0 9.5 %collective-permute-start.7 = (f32[4,136,128]{2,1,0:T(8,128)S(1)}, f32[4,136,128]{2,1,0:T(8,128)S(1)}, u32[]{:S(2)}, u32[]{:S(2)}) collective-permute-start(f32[4,136,128]{2,1,0:T(8,128)S(1)} %pad_maximum_fusion), channel_id=1, source_target_pairs={{0,2},{1,3},{2,0},{3,1},{4,6},{5,7},{6,4},{7,5},{8,10},{9,11},{10,... | collective-permute-start | bytes 835592 | tf_op jit(solution)/shard_map/ppermute | solution.py:181
  17.6 9.1 %collective-permute-start.10 = (f32[4,136,128]{2,1,0:T(8,128)S(1)}, f32[4,136,128]{2,1,0:T(8,128)S(1)}, u32[]{:S(2)}, u32[]{:S(2)}) collective-permute-start(f32[4,136,128]{2,1,0:T(8,128)S(1)} %pad_maximum_fusion.2), channel_id=1, source_target_pairs={{0,1},{1,0},{2,3},{3,2},{4,5},{5,4},{6,7},{7,6},{8,9},{9,8},{10,11... | collective-permute-start | bytes 835592 | tf_op jit(solution)/shard_map/ppermute | solution.py:181
  22.4 14.5 %collective-permute-start.2 = (f32[4,256,128]{2,1,0:T(8,128)S(1)}, f32[4,256,128]{2,1,0:T(8,128)S(1)}, u32[]{:S(2)}, u32[]{:S(2)}) collective-permute-start(f32[4,256,128]{2,1,0:T(8,128)S(1)} %constant_dynamic-update-slice_fusion.refs_0_), channel_id=1, source_target_pairs={{0,1},{1,0},{2,3},{3,2},{4,5},{5,4},{6,7},{7,6},{8,9},{9,8},{10,11... | collective-permute-start | bytes 1572872 | tf_op jit(solution)/shard_map/ppermute | solution.py:181
  23.9 28.5 %collective-permute-start.3 = (f32[4,256,128]{2,1,0:T(8,128)S(1)}, f32[4,256,128]{2,1,0:T(8,128)S(1)}, u32[]{:S(2)}, u32[]{:S(2)}) collective-permute-start(f32[4,256,128]{2,1,0:T(8,128)S(1)} %constant_dynamic-update-slice_fusion.refs_0_), channel_id=1, source_target_pairs={{0,2},{1,3},{2,0},{3,1},{4,6},{5,7},{6,4},{7,5},{8,10},{9,11},{10,... | collective-permute-start | bytes 1572872 | tf_op jit(solution)/shard_map/ppermute | solution.py:181
  25.5 18.4 %collective-permute-start.13 = (f32[4,136,128]{2,1,0:T(8,128)S(1)}, f32[4,136,128]{2,1,0:T(8,128)S(1)}, u32[]{:S(2)}, u32[]{:S(2)}) collective-permute-start(f32[4,136,128]{2,1,0:T(8,128)S(1)} %pad_maximum_fusion.4), channel_id=1, source_target_pairs={{0,8},{1,9},{2,10},{3,11},{4,12},{5,13},{6,14},{7,15},{8,0},{9,1},... | collective-permute-start | bytes 835592 | tf_op jit(solution)/shard_map/ppermute | solution.py:181
  26.8 25.1 %collective-permute-start.15 = (f32[4,136,128]{2,1,0:T(8,128)S(1)}, f32[4,136,128]{2,1,0:T(8,128)S(1)}, u32[]{:S(2)}, u32[]{:S(2)}) collective-permute-start(f32[4,136,128]{2,1,0:T(8,128)S(1)} %pad_maximum_fusion.5), channel_id=1, source_target_pairs={{0,12},{1,13},{2,14},{3,15},{4,8},{5,9},{6,10},{7,11},{8,4},{9,5},... | collective-permute-start | bytes 835592 | tf_op jit(solution)/shard_map/ppermute | solution.py:181
  28.9 23.0 %collective-permute-start.11 = (f32[4,136,128]{2,1,0:T(8,128)S(1)}, f32[4,136,128]{2,1,0:T(8,128)S(1)}, u32[]{:S(2)}, u32[]{:S(2)}) collective-permute-start(f32[4,136,128]{2,1,0:T(8,128)S(1)} %pad_maximum_fusion.3), channel_id=1, source_target_pairs={{0,4},{1,5},{2,6},{3,7},{4,0},{5,1},{6,2},{7,3},{8,12},{9,13},{10,... | collective-permute-start | bytes 835592 | tf_op jit(solution)/shard_map/ppermute | solution.py:181
  36.9 15.6 %collective-permute-start.4 = (f32[2,256,128]{2,1,0:T(8,128)S(1)}, f32[2,256,128]{2,1,0:T(8,128)S(1)}, u32[]{:S(2)}, u32[]{:S(2)}) collective-permute-start(f32[2,256,128]{2,1,0:T(8,128)S(1)} %slice.88), channel_id=1, source_target_pairs={{0,2},{1,3},{2,0},{3,1},{4,6},{5,7},{6,4},{7,5},{8,10},{9,11},{10,... | collective-permute-start | bytes 786440 | tf_op jit(solution)/shard_map/ppermute | solution.py:181
  43.9 17.6 %collective-permute-start.8 = (f32[4,136,128]{2,1,0:T(8,128)S(1)}, f32[4,136,128]{2,1,0:T(8,128)S(1)}, u32[]{:S(2)}, u32[]{:S(2)}) collective-permute-start(f32[4,136,128]{2,1,0:T(8,128)S(1)} %pad_maximum_fusion.1.refs_0_), channel_id=1, source_target_pairs={{0,16},{16,0},{1,17},{17,1},{2,18},{18,2},{3,19},{19,3},{4,20},{20... | collective-permute-start | bytes 835592 | tf_op jit(solution)/shard_map/ppermute | solution.py:181
  51.9 9.6 %collective-permute-start.14 = (f32[4,136,128]{2,1,0:T(8,128)S(1)}, f32[4,136,128]{2,1,0:T(8,128)S(1)}, u32[]{:S(2)}, u32[]{:S(2)}) collective-permute-start(f32[4,136,128]{2,1,0:T(8,128)S(1)} %collective-permute-done.13.refs_4_), channel_id=1, source_target_pairs={{0,16},{16,0},{1,17},{17,1},{2,18},{18,2},{3,19},{19,3},{4,20},{20... | collective-permute-start | bytes 835592 | tf_op jit(solution)/shard_map/ppermute | solution.py:181
  51.9 9.6 %collective-permute-start.16 = (f32[4,136,128]{2,1,0:T(8,128)S(1)}, f32[4,136,128]{2,1,0:T(8,128)S(1)}, u32[]{:S(2)}, u32[]{:S(2)}) collective-permute-start(f32[4,136,128]{2,1,0:T(8,128)S(1)} %collective-permute-done.15.refs_6_), channel_id=1, source_target_pairs={{0,16},{16,0},{1,17},{17,1},{2,18},{18,2},{3,19},{19,3},{4,20},{20... | collective-permute-start | bytes 835592 | tf_op jit(solution)/shard_map/ppermute | solution.py:181
  52.4 9.1 %collective-permute-start.12 = (f32[4,136,128]{2,1,0:T(8,128)S(1)}, f32[4,136,128]{2,1,0:T(8,128)S(1)}, u32[]{:S(2)}, u32[]{:S(2)}) collective-permute-start(f32[4,136,128]{2,1,0:T(8,128)S(1)} %collective-permute-done.11.refs_2_), channel_id=1, source_target_pairs={{0,16},{16,0},{1,17},{17,1},{2,18},{18,2},{3,19},{19,3},{4,20},{20... | collective-permute-start | bytes 835592 | tf_op jit(solution)/shard_map/ppermute | solution.py:181
  52.5 9.0 %copy-start = (f32[256,1024]{1,0:T(8,128)S(1)}, f32[256,1024]{1,0:T(8,128)}, u32[]{:S(2)}) copy-start(f32[256,1024]{1,0:T(8,128)} %refs_8_.1) | copy-start | bytes 3145732
  52.5 8.7 %collective-permute-start.5 = (f32[2,256,128]{2,1,0:T(8,128)S(1)}, f32[2,256,128]{2,1,0:T(8,128)S(1)}, u32[]{:S(2)}, u32[]{:S(2)}) collective-permute-start(f32[2,256,128]{2,1,0:T(8,128)S(1)} %slice.89), channel_id=1, source_target_pairs={{0,1},{1,0},{2,3},{3,2},{4,5},{5,4},{6,7},{7,6},{8,9},{9,8},{10,11... | collective-permute-start | bytes 786440 | tf_op jit(solution)/shard_map/ppermute | solution.py:181

commit v5 on v4

--- a/solution.py
+++ b/solution.py
@@ -10,13 +10,26 @@
 KT = 16
 CT = 8
 SLOT = 2
-GROUPS = 4
+HINT = 32 * 1024 * 1024
 META = 8
 
 
-def pack_kernel(reader_ref, k_ref, column_ref, tiles_ref, block_ref, *refs):
-    copy_ref, outs, count_ref = refs[0], refs[1:-1], refs[-1]
-    copy_ref[0] = block_ref[...]
+def pack_kernel(reader_any, k_any, column_any, tiles_any, *refs):
+    outs = refs[:4]
+    reader_ref, k_ref, column_ref, tiles_ref, count_ref, sem = refs[4:]
+    fetches = [
+        pltpu.make_async_copy(*pair, sem.at[number])
+        for number, pair in enumerate(
+            (
+                (tiles_any, tiles_ref),
+                (reader_any, reader_ref),
+                (k_any, k_ref),
+                (column_any, column_ref),
+            )
+        )
+    ]
+    for fetch in fetches:
+        fetch.start()
     count, height, width = tiles_ref.shape
     half = outs[0].shape[0] // 2
     targets = 8 * half
@@ -26,6 +39,8 @@
     for target in range(targets):
         count_ref[target] = 0
     lane = lax.broadcasted_iota(jnp.int32, (META, width), 1)
+    for fetch in fetches:
+        fetch.wait()
 
     def place(j, carry):
         position = jnp.bitwise_xor(reader_ref[j], me)
@@ -50,20 +65,23 @@
     lax.fori_loop(0, count, place, 0)
 
 
-def pack(tiles, readers, tile_k, tile_column, block, targets):
-    _, height, width = tiles.shape
-    smem = pl.BlockSpec(memory_space=pltpu.SMEM)
-    vmem = pl.BlockSpec(memory_space=pltpu.VMEM)
+def pack(tiles, readers, tile_k, tile_column, targets):
+    count, height, width = tiles.shape
     out = jax.ShapeDtypeStruct((targets // 4, SLOT * height + META, width), jnp.float32)
     return pl.pallas_call(
         pack_kernel,
-        out_shape=[jax.ShapeDtypeStruct((1, *block.shape), block.dtype)] + [out] * 4,
-        in_specs=[smem, smem, smem, vmem, vmem],
-        out_specs=[vmem] * 5,
-        scratch_shapes=[pltpu.SMEM((targets,), jnp.int32)],
+        out_shape=[out] * 4,
+        in_specs=[pl.BlockSpec(memory_space=pltpu.HBM)] * 4,
+        out_specs=[pl.BlockSpec(memory_space=pltpu.VMEM)] * 4,
+        scratch_shapes=[
+            *[pltpu.SMEM((count,), jnp.int32)] * 3,
+            pltpu.VMEM(tiles.shape, tiles.dtype),
+            pltpu.SMEM((targets,), jnp.int32),
+            pltpu.SemaphoreType.DMA((4,)),
+        ],
         cost_estimate=pl.CostEstimate(flops=0, bytes_accessed=4 * tiles.size * 3, transcendentals=0),
         compiler_params=pltpu.CompilerParams(vmem_limit_bytes=8 * 1024 * 1024),
-    )(readers.reshape(-1), tile_k, tile_column, tiles, block)
+    )(readers.reshape(-1), tile_k, tile_column, tiles)
 
 
 def split_kernel(positions, *refs):
@@ -86,6 +104,7 @@
         out_shape=jax.ShapeDtypeStruct((KT, rows, 2 * width), jnp.bfloat16),
         in_specs=[vmem] * len(pieces),
         out_specs=vmem,
+        cost_estimate=pl.CostEstimate(flops=0, bytes_accessed=HINT, transcendentals=0),
         compiler_params=pltpu.CompilerParams(vmem_limit_bytes=16 * 1024 * 1024),
     )(*pieces)
 
@@ -145,15 +164,17 @@
             def _():
                 multiply(*whole(parts, owner, slot, code))
 
-        def four(step, carry):
-            for i in range(4):
-                first(4 * step + i)
-            for i in range(4):
+        unroll = min(4, owners)
+
+        def some(step, carry):
+            for i in range(unroll):
+                first(unroll * step + i)
+            for i in range(unroll):
                 for slot in range(1, SLOT):
-                    later(4 * step + i, slot)
+                    later(unroll * step + i, slot)
             return carry
 
-        lax.fori_loop(0, owners // 4, four, 0)
+        lax.fori_loop(0, owners // unroll, some, 0)
 
     for parts, codes_ref in zip(groups, codes):
         add_group(parts, codes_ref)
@@ -186,7 +207,7 @@
 
 
 def gather(block, size):
-    held, at = block, (0,)
+    held, at = block[None], (0,)
     bit = size // 2
     while bit > 2:
         held, at = jnp.concatenate([held, hop(held, bit)], axis=0), at + tuple(p ^ bit for p in at)
@@ -203,25 +224,33 @@
     half = kept.shape[0] // 2
     come = hop(sent, first)
     last = hop(jnp.concatenate([kept[half:], come[half:]], axis=0), second)
-    return [jnp.stack([kept[z], come[z], last[z], last[half + z]]) for z in range(half)]
+    return (
+        [jnp.stack([kept[z], come[z]]) for z in range(half)],
+        [jnp.stack([last[z], last[half + z]]) for z in range(half)],
+    )
 
 
 def local(residual_in, amplitudes, integral_tiles, tile_reader, tile_k, tile_column):
     targets = lax.axis_size("bulk")
     rows_axis = lax.axis_size("row")
     width = integral_tiles.shape[2]
-    block, even_kept, even_sent, odd_kept, odd_sent = pack(
-        integral_tiles, tile_reader, tile_k, tile_column, amplitudes, targets
-    )
-    pieces, positions = gather(block, targets)
+    pieces, positions = gather(amplitudes, targets)
+    even_kept, even_sent, odd_kept, odd_sent = pack(
+        integral_tiles, tile_reader, tile_k, tile_column, targets
+    )
     odd = across(odd_kept, odd_sent, 2, 1)
     even = across(even_kept, even_sent, 1, 2)
-    planes = [plane for pair in zip(even, odd) for plane in pair]
-    planes = [planes[0]] + [hop(plane, 4 * z) for z, plane in enumerate(planes) if z]
-    size = len(planes) // GROUPS
+    waves = [[plane for pair in zip(even[w], odd[w]) for plane in pair] for w in range(2)]
+    waves = [[wave[0]] + [hop(plane, 4 * z) for z, plane in enumerate(wave) if z] for wave in waves]
+    quarter = targets // 16
     groups = []
-    for g in range(GROUPS):
-        mine = jnp.concatenate(planes[g * size : (g + 1) * size], axis=0)
+    for planes in (
+        waves[0],
+        waves[1][: 2 * quarter],
+        waves[1][2 * quarter : 3 * quarter],
+        waves[1][3 * quarter :],
+    ):
+        mine = jnp.concatenate(planes, axis=0)
         groups.append(
             [mine] + [send(mine, "row", lambda i: (i + q) % rows_axis) for q in range(1, rows_axis)]
         )

time: 65.9 us -> 59.2 us (0.90)
  the two profiles are of different devices: /device:TPU:16 before, /device:TPU:0 now
where the time goes in v5:
time: 59.2 us; the launch traced here: 59 us
  starting transfers between devices  29.8 us (50%)
  waiting for transfers between devices  18.6 us (31%)
  Pallas kernels  6.04 us (10%)
  local copies, waits for them, and re-layouts  3.21 us (5%)
  other arithmetic  1.14 us (2%)
    ppermute x20, starting transfers between devices, send(): return lax.ppermute(x, axis, [(i, partner(i)) for i in range(size)])  29.8 us
    ppermute x20, waiting for transfers between devices, send(): return lax.ppermute(x, axis, [(i, partner(i)) for i in range(size)])  18.6 us
    pallas_call x1, Pallas kernels, contract(): pl.pallas_call(functools.partial(contract_kernel, len(groups), len(groups...  4.33 us
    unnamed x14, local copies, waits for them, and re-layouts  3.04 us
    pallas_call x1, Pallas kernels, pack(): pl.pallas_call(pack_kernel, out_shape=[out] * 4, in_specs=[pl.BlockSpec(m...  1.46 us
  transfers between devices with their start and end apart: 20, of which 8 were waited for; matrix products, arithmetic and copies ran while one was open for 2% of the time, Pallas kernels for 3%

profile of v5, /device:TPU:0, one launch (start us, length us, event | category | flops | bytes accessed | tf_op | source)
XLA Modules:
  0.0 59.0 jit_solution(14242024434989588252)
XLA Ops:
  0.0 4.0 %collective-permute-start = (f32[1,256,128]{2,1,0:T(8,128)}, f32[1,256,128]{2,1,0:T(8,128)S(1)}, u32[]{:S(2)}, u32[]{:S(2)}) collective-permute-start(f32[1,256,128]{2,1,0:T(8,128)} %bitcast.3), channel_id=1, source_target_pairs={{0,8},{1,9},{2,10},{3,11},{4,12},{5,13},{6,14},{7,15},{8,0},{9,1},... | collective-permute-start | bytes 393224 | tf_op jit(solution)/shard_map/ppermute | solution.py:202
  4.0 0.0 copy-start.1
  4.0 1.0 %copy-done.1 = f32[16,64,128]{2,1,0:T(8,128)S(1)} copy-done((f32[16,64,128]{2,1,0:T(8,128)S(1)}, f32[16,64,128]{2,1,0:T(8,128)}, u32[]{:S(2)}) %copy-start.1) | copy-done | bytes 524312
  5.1 0.0 copy-start.2
  5.1 0.7 %copy-done.2 = s32[16,1]{0,1:T(1,128)S(1)} copy-done((s32[16,1]{0,1:T(1,128)S(1)}, s32[16,1]{0,1:T(1,128)}, u32[]{:S(2)}) %copy-start.2) | copy-done | bytes 88
  5.7 0.0 copy-start.3
  5.7 0.7 %copy-done.3 = s32[16]{0:T(128)S(1)} copy-done((s32[16]{0:T(128)S(1)}, s32[16]{0:T(128)}, u32[]{:S(2)}) %copy-start.3) | copy-done | bytes 88
  6.4 0.0 copy-start.4
  6.4 0.7 %copy-done.4 = s32[16]{0:T(128)S(1)} copy-done((s32[16]{0:T(128)S(1)}, s32[16]{0:T(128)}, u32[]{:S(2)}) %copy-start.4) | copy-done | bytes 88
  7.0 1.5 %shard_map.65 = (f32[4,136,128]{2,1,0:T(8,128)S(1)}, f32[4,136,128]{2,1,0:T(8,128)S(1)}, f32[4,136,128]{2,1,0:T(8,128)S(1)}, f32[4,136,128]{2,1,0:T(8,128)S(1)}) custom-call(s32[16]{0:T(128)S(1)} %bitcast.2, s32[16]{0:T(128)S(1)} %copy-done.3, s32[16]{0:T(128)S(1)} %copy-done.4, f32[16,64,128]{2,1,0:T(8,128)S(1)} %copy-done.1), custom_call_target="tpu_custom_call" | custom-call | bytes 1572864 | tf_op jit(solution)/shard_map/pallas_call | solution.py:71
  8.5 1.6 %collective-permute-start.6 = (f32[4,136,128]{2,1,0:T(8,128)S(1)}, f32[4,136,128]{2,1,0:T(8,128)S(1)}, u32[]{:S(2)}, u32[]{:S(2)}) collective-permute-start(f32[4,136,128]{2,1,0:T(8,128)S(1)} %get-tuple-element.10), channel_id=1, source_target_pairs={{0,1},{1,0},{2,3},{3,2},{4,5},{5,4},{6,7},{7,6},{8,9},{9,8},{10,11... | collective-permute-start | bytes 835592 | tf_op jit(solution)/shard_map/ppermute | solution.py:202
  10.1 1.5 %collective-permute-start.7 = (f32[4,136,128]{2,1,0:T(8,128)S(1)}, f32[4,136,128]{2,1,0:T(8,128)S(1)}, u32[]{:S(2)}, u32[]{:S(2)}) collective-permute-start(f32[4,136,128]{2,1,0:T(8,128)S(1)} %get-tuple-element.12), channel_id=1, source_target_pairs={{0,2},{1,3},{2,0},{3,1},{4,6},{5,7},{6,4},{7,5},{8,10},{9,11},{10,... | collective-permute-start | bytes 835592 | tf_op jit(solution)/shard_map/ppermute | solution.py:202
  11.6 0.0 copy-start.5
  11.7 0.0 collective-permute-done
  11.7 1.0 %pad_maximum_fusion.4 = f32[2,256,128]{2,1,0:T(8,128)S(1)} fusion(f32[1,256,128]{2,1,0:T(8,128)S(1)} %collective-permute-done, f32[1,256,128]{2,1,0:T(8,128)} %bitcast.4), kind=kLoop, calls=%fused_computation.4 | loop fusion | flops 65536 | bytes 524288 | tf_op jit(solution)/shard_map/concatenate | solution.py:213
  12.6 1.6 %collective-permute-start.1 = (f32[2,256,128]{2,1,0:T(8,128)S(1)}, f32[2,256,128]{2,1,0:T(8,128)S(1)}, u32[]{:S(2)}, u32[]{:S(2)}) collective-permute-start(f32[2,256,128]{2,1,0:T(8,128)S(1)} %pad_maximum_fusion.4), channel_id=1, source_target_pairs={{0,4},{1,5},{2,6},{3,7},{4,0},{5,1},{6,2},{7,3},{8,12},{9,13},{10,... | collective-permute-start | bytes 786440 | tf_op jit(solution)/shard_map/ppermute | solution.py:202
  14.3 2.4 %collective-permute-done.6 = f32[4,136,128]{2,1,0:T(8,128)S(1)} collective-permute-done((f32[4,136,128]{2,1,0:T(8,128)S(1)}, f32[4,136,128]{2,1,0:T(8,128)S(1)}, u32[]{:S(2)}, u32[]{:S(2)}) %collective-permute-start.6) | collective-permute-done | bytes 278560 | tf_op jit(solution)/shard_map/ppermute | solution.py:202
  16.7 0.3 collective-permute-start.9
  17.1 1.6 %collective-permute-start.12 = (f32[4,136,128]{2,1,0:T(8,128)S(1)}, f32[4,136,128]{2,1,0:T(8,128)S(1)}, u32[]{:S(2)}, u32[]{:S(2)}) collective-permute-start(f32[4,136,128]{2,1,0:T(8,128)S(1)} %pad_maximum_fusion.1), channel_id=1, source_target_pairs={{0,2},{1,3},{2,0},{3,1},{4,6},{5,7},{6,4},{7,5},{8,10},{9,11},{10,... | collective-permute-start | bytes 835592 | tf_op jit(solution)/shard_map/ppermute | solution.py:202
  18.8 0.0 collective-permute-done.7
  18.8 1.6 %collective-permute-start.8 = (f32[2,136,128]{2,1,0:T(8,128)S(1)}, f32[2,136,128]{2,1,0:T(8,128)S(1)}, u32[]{:S(2)}, u32[]{:S(2)}) collective-permute-start(f32[2,136,128]{2,1,0:T(8,128)S(1)} %pad_maximum_fusion.5), channel_id=1, source_target_pairs={{0,4},{1,5},{2,6},{3,7},{4,0},{5,1},{6,2},{7,3},{8,12},{9,13},{10,... | collective-permute-start | bytes 417800 | tf_op jit(solution)/shard_map/ppermute | solution.py:202
  20.4 2.5 %collective-permute-start.10 = (f32[2,136,128]{2,1,0:T(8,128)S(1)}, f32[2,136,128]{2,1,0:T(8,128)S(1)}, u32[]{:S(2)}, u32[]{:S(2)}) collective-permute-start(f32[2,136,128]{2,1,0:T(8,128)S(1)} %pad_maximum_fusion.7), channel_id=1, source_target_pairs={{0,12},{1,13},{2,14},{3,15},{4,8},{5,9},{6,10},{7,11},{8,4},{9,5},... | collective-permute-start | bytes 417800 | tf_op jit(solution)/shard_map/ppermute | solution.py:202
  23.0 0.0 collective-permute-done.1
  23.0 1.6 %collective-permute-start.13 = (f32[4,136,128]{2,1,0:T(8,128)S(1)}, f32[4,136,128]{2,1,0:T(8,128)S(1)}, u32[]{:S(2)}, u32[]{:S(2)}) collective-permute-start(f32[4,136,128]{2,1,0:T(8,128)S(1)} %pad_maximum_fusion.2), channel_id=1, source_target_pairs={{0,1},{1,0},{2,3},{3,2},{4,5},{5,4},{6,7},{7,6},{8,9},{9,8},{10,11... | collective-permute-start | bytes 835592 | tf_op jit(solution)/shard_map/ppermute | solution.py:202
  24.6 0.0 copy-done.5
  24.6 1.9 %collective-permute-done.8 = f32[2,136,128]{2,1,0:T(8,128)S(1)} collective-permute-done((f32[2,136,128]{2,1,0:T(8,128)S(1)}, f32[2,136,128]{2,1,0:T(8,128)S(1)}, u32[]{:S(2)}, u32[]{:S(2)}) %collective-permute-start.8) | collective-permute-done | bytes 139296 | tf_op jit(solution)/shard_map/ppermute | solution.py:202
  26.5 0.6 %collective-permute-start.3 = (f32[4,256,128]{2,1,0:T(8,128)S(1)}, f32[4,256,128]{2,1,0:T(8,128)S(1)}, u32[]{:S(2)}, u32[]{:S(2)}) collective-permute-start(f32[4,256,128]{2,1,0:T(8,128)S(1)} %pad_maximum_fusion.refs_0_), channel_id=1, source_target_pairs={{0,2},{1,3},{2,0},{3,1},{4,6},{5,7},{6,4},{7,5},{8,10},{9,11},{10,... | collective-permute-start | bytes 1572872 | tf_op jit(solution)/shard_map/ppermute | solution.py:202
  27.1 0.0 collective-permute-done.9
  27.1 1.2 %collective-permute-start.2 = (f32[4,256,128]{2,1,0:T(8,128)S(1)}, f32[4,256,128]{2,1,0:T(8,128)S(1)}, u32[]{:S(2)}, u32[]{:S(2)}) collective-permute-start(f32[4,256,128]{2,1,0:T(8,128)S(1)} %pad_maximum_fusion.refs_0_), channel_id=1, source_target_pairs={{0,1},{1,0},{2,3},{3,2},{4,5},{5,4},{6,7},{7,6},{8,9},{9,8},{10,11... | collective-permute-start | bytes 1572872 | tf_op jit(solution)/shard_map/ppermute | solution.py:202
  28.3 2.4 %collective-permute-done.10 = f32[2,136,128]{2,1,0:T(8,128)S(1)} collective-permute-done((f32[2,136,128]{2,1,0:T(8,128)S(1)}, f32[2,136,128]{2,1,0:T(8,128)S(1)}, u32[]{:S(2)}, u32[]{:S(2)}) %collective-permute-start.10) | collective-permute-done | bytes 139296 | tf_op jit(solution)/shard_map/ppermute | solution.py:202
  30.7 0.1 collective-permute-start.11
  30.8 1.5 %collective-permute-done.13 = f32[4,136,128]{2,1,0:T(8,128)S(1)} collective-permute-done((f32[4,136,128]{2,1,0:T(8,128)S(1)}, f32[4,136,128]{2,1,0:T(8,128)S(1)}, u32[]{:S(2)}, u32[]{:S(2)}) %collective-permute-start.13) | collective-permute-done | bytes 278560 | tf_op jit(solution)/shard_map/ppermute | solution.py:202
  32.4 0.1 collective-permute-start.14
  32.4 0.0 collective-permute-done.12
  32.5 3.8 %collective-permute-start.16 = (f32[2,136,128]{2,1,0:T(8,128)S(1)}, f32[2,136,128]{2,1,0:T(8,128)S(1)}, u32[]{:S(2)}, u32[]{:S(2)}) collective-permute-start(f32[2,136,128]{2,1,0:T(8,128)S(1)} %pad_maximum_fusion.9), channel_id=1, source_target_pairs={{0,8},{1,9},{2,10},{3,11},{4,12},{5,13},{6,14},{7,15},{8,0},{9,1},... | collective-permute-start | bytes 417800 | tf_op jit(solution)/shard_map/ppermute | solution.py:202
  36.3 1.6 %collective-permute-done.3.refs_2_ = f32[4,256,128]{2,1,0:T(8,128)S(1)} collective-permute-done((f32[4,256,128]{2,1,0:T(8,128)S(1)}, f32[4,256,128]{2,1,0:T(8,128)S(1)}, u32[]{:S(2)}, u32[]{:S(2)}) %collective-permute-start.3) | collective-permute-done | bytes 524320 | tf_op jit(solution)/shard_map/ppermute | solution.py:202
  38.0 0.5 collective-permute-start.5
  38.5 1.4 %collective-permute-done.14 = f32[2,136,128]{2,1,0:T(8,128)S(1)} collective-permute-done((f32[2,136,128]{2,1,0:T(8,128)S(1)}, f32[2,136,128]{2,1,0:T(8,128)S(1)}, u32[]{:S(2)}, u32[]{:S(2)}) %collective-permute-start.14) | collective-permute-done | bytes 139296 | tf_op jit(solution)/shard_map/ppermute | solution.py:202
  39.9 5.5 %collective-permute-start.18 = (f32[2,136,128]{2,1,0:T(8,128)S(1)}, f32[2,136,128]{2,1,0:T(8,128)S(1)}, u32[]{:S(2)}, u32[]{:S(2)}) collective-permute-start(f32[2,136,128]{2,1,0:T(8,128)S(1)} %pad_maximum_fusion.10), channel_id=1, source_target_pairs={{0,12},{1,13},{2,14},{3,15},{4,8},{5,9},{6,10},{7,11},{8,4},{9,5},... | collective-permute-start | bytes 417800 | tf_op jit(solution)/shard_map/ppermute | solution.py:202
  45.5 0.0 collective-permute-done.2.refs_1_
  45.5 0.1 collective-permute-start.15
  45.6 0.0 copy-start
  45.6 0.0 collective-permute-done.16.refs_4_
  45.6 0.9 %collective-permute-start.4 = (f32[2,256,128]{2,1,0:T(8,128)S(1)}, f32[2,256,128]{2,1,0:T(8,128)S(1)}, u32[]{:S(2)}, u32[]{:S(2)}) collective-permute-start(f32[2,256,128]{2,1,0:T(8,128)S(1)} %slice.88), channel_id=1, source_target_pairs={{0,2},{1,3},{2,0},{3,1},{4,6},{5,7},{6,4},{7,5},{8,10},{9,11},{10,... | collective-permute-start | bytes 786440 | tf_op jit(solution)/shard_map/ppermute | solution.py:202
  46.6 2.0 %collective-permute-done.18.refs_6_ = f32[2,136,128]{2,1,0:T(8,128)S(1)} collective-permute-done((f32[2,136,128]{2,1,0:T(8,128)S(1)}, f32[2,136,128]{2,1,0:T(8,128)S(1)}, u32[]{:S(2)}, u32[]{:S(2)}) %collective-permute-start.18) | collective-permute-done | bytes 139296 | tf_op jit(solution)/shard_map/ppermute | solution.py:202
  48.6 0.0 collective-permute-start.17
  48.6 0.0 collective-permute-done.5.refs_4_
  48.6 0.5 collective-permute-start.19
  49.1 5.3 %collective-permute-done.4.refs_3_ = f32[2,256,128]{2,1,0:T(8,128)S(1)} collective-permute-done((f32[2,256,128]{2,1,0:T(8,128)S(1)}, f32[2,256,128]{2,1,0:T(8,128)S(1)}, u32[]{:S(2)}, u32[]{:S(2)}) %collective-permute-start.4) | collective-permute-done | bytes 262176 | tf_op jit(solution)/shard_map/ppermute | solution.py:202
  54.4 0.3 shard_map.64.split_ref
  54.6 0.0 collective-permute-done.17.refs_5_
  54.6 0.0 collective-permute-done.19.refs_7_
  54.7 0.0 collective-permute-done.11.refs_1_
  54.7 0.0 collective-permute-done.15.refs_3_
  54.7 0.0 copy-done
  54.7 4.3 %shard_map.66 = f32[256,1024]{1,0:T(8,128)} custom-call(bf16[16,256,256]{2,1,0:T(8,128)(2,1)S(1)} %shard_map.64.split_ref, f32[8,136,128]{2,1,0:T(8,128)S(1)} %constant_dynamic-update-slice_fusion.refs_0_, f32[8,136,128]{2,1,0:T(8,128)S(1)} %collective-permute-done.11.refs_1_, f32[4,136,128]{2,1,0:T(8,128)S(1)} %pad_maximum_fusion.3.refs_2_, ...), custom_call_target="tpu_custom_call" | custom-call | tf_op jit(solution)/shard_map/pallas_call | solution.py:187
  (24 shorter events, 0.4 us)
Async XLA Ops:
  0.0 11.7 %collective-permute-start = (f32[1,256,128]{2,1,0:T(8,128)}, f32[1,256,128]{2,1,0:T(8,128)S(1)}, u32[]{:S(2)}, u32[]{:S(2)}) collective-permute-start(f32[1,256,128]{2,1,0:T(8,128)} %bitcast.3), channel_id=1, source_target_pairs={{0,8},{1,9},{2,10},{3,11},{4,12},{5,13},{6,14},{7,15},{8,0},{9,1},... | collective-permute-start | bytes 393224 | tf_op jit(solution)/shard_map/ppermute | solution.py:202
  4.0 1.0 %copy-start.1 = (f32[16,64,128]{2,1,0:T(8,128)S(1)}, f32[16,64,128]{2,1,0:T(8,128)}, u32[]{:S(2)}) copy-start(f32[16,64,128]{2,1,0:T(8,128)} %tiles_any.1) | copy-start | bytes 1572868
  5.1 0.7 %copy-start.2 = (s32[16,1]{0,1:T(1,128)S(1)}, s32[16,1]{0,1:T(1,128)}, u32[]{:S(2)}) copy-start(s32[16,1]{0,1:T(1,128)} %param.9) | copy-start | bytes 196
  5.7 0.7 %copy-start.3 = (s32[16]{0:T(128)S(1)}, s32[16]{0:T(128)}, u32[]{:S(2)}) copy-start(s32[16]{0:T(128)} %k_any.1) | copy-start | bytes 196
  6.4 0.7 %copy-start.4 = (s32[16]{0:T(128)S(1)}, s32[16]{0:T(128)}, u32[]{:S(2)}) copy-start(s32[16]{0:T(128)} %column_any.1) | copy-start | bytes 196
  8.5 8.2 %collective-permute-start.6 = (f32[4,136,128]{2,1,0:T(8,128)S(1)}, f32[4,136,128]{2,1,0:T(8,128)S(1)}, u32[]{:S(2)}, u32[]{:S(2)}) collective-permute-start(f32[4,136,128]{2,1,0:T(8,128)S(1)} %get-tuple-element.10), channel_id=1, source_target_pairs={{0,1},{1,0},{2,3},{3,2},{4,5},{5,4},{6,7},{7,6},{8,9},{9,8},{10,11... | collective-permute-start | bytes 835592 | tf_op jit(solution)/shard_map/ppermute | solution.py:202
  10.1 8.7 %collective-permute-start.7 = (f32[4,136,128]{2,1,0:T(8,128)S(1)}, f32[4,136,128]{2,1,0:T(8,128)S(1)}, u32[]{:S(2)}, u32[]{:S(2)}) collective-permute-start(f32[4,136,128]{2,1,0:T(8,128)S(1)} %get-tuple-element.12), channel_id=1, source_target_pairs={{0,2},{1,3},{2,0},{3,1},{4,6},{5,7},{6,4},{7,5},{8,10},{9,11},{10,... | collective-permute-start | bytes 835592 | tf_op jit(solution)/shard_map/ppermute | solution.py:202
  11.6 13.0 %copy-start.5 = (f32[256,128]{1,0:T(8,128)S(1)}, f32[256,128]{1,0:T(8,128)}, u32[]{:S(2)}) copy-start(f32[256,128]{1,0:T(8,128)} %param.7) | copy-start | bytes 393220
  12.6 10.4 %collective-permute-start.1 = (f32[2,256,128]{2,1,0:T(8,128)S(1)}, f32[2,256,128]{2,1,0:T(8,128)S(1)}, u32[]{:S(2)}, u32[]{:S(2)}) collective-permute-start(f32[2,256,128]{2,1,0:T(8,128)S(1)} %pad_maximum_fusion.4), channel_id=1, source_target_pairs={{0,4},{1,5},{2,6},{3,7},{4,0},{5,1},{6,2},{7,3},{8,12},{9,13},{10,... | collective-permute-start | bytes 786440 | tf_op jit(solution)/shard_map/ppermute | solution.py:202
  16.7 10.4 %collective-permute-start.9 = (f32[2,136,128]{2,1,0:T(8,128)S(1)}, f32[2,136,128]{2,1,0:T(8,128)S(1)}, u32[]{:S(2)}, u32[]{:S(2)}) collective-permute-start(f32[2,136,128]{2,1,0:T(8,128)S(1)} %pad_maximum_fusion.6), channel_id=1, source_target_pairs={{0,8},{1,9},{2,10},{3,11},{4,12},{5,13},{6,14},{7,15},{8,0},{9,1},... | collective-permute-start | bytes 417800 | tf_op jit(solution)/shard_map/ppermute | solution.py:202
  17.1 15.3 %collective-permute-start.12 = (f32[4,136,128]{2,1,0:T(8,128)S(1)}, f32[4,136,128]{2,1,0:T(8,128)S(1)}, u32[]{:S(2)}, u32[]{:S(2)}) collective-permute-start(f32[4,136,128]{2,1,0:T(8,128)S(1)} %pad_maximum_fusion.1), channel_id=1, source_target_pairs={{0,2},{1,3},{2,0},{3,1},{4,6},{5,7},{6,4},{7,5},{8,10},{9,11},{10,... | collective-permute-start | bytes 835592 | tf_op jit(solution)/shard_map/ppermute | solution.py:202
  18.8 7.7 %collective-permute-start.8 = (f32[2,136,128]{2,1,0:T(8,128)S(1)}, f32[2,136,128]{2,1,0:T(8,128)S(1)}, u32[]{:S(2)}, u32[]{:S(2)}) collective-permute-start(f32[2,136,128]{2,1,0:T(8,128)S(1)} %pad_maximum_fusion.5), channel_id=1, source_target_pairs={{0,4},{1,5},{2,6},{3,7},{4,0},{5,1},{6,2},{7,3},{8,12},{9,13},{10,... | collective-permute-start | bytes 417800 | tf_op jit(solution)/shard_map/ppermute | solution.py:202
  20.4 10.2 %collective-permute-start.10 = (f32[2,136,128]{2,1,0:T(8,128)S(1)}, f32[2,136,128]{2,1,0:T(8,128)S(1)}, u32[]{:S(2)}, u32[]{:S(2)}) collective-permute-start(f32[2,136,128]{2,1,0:T(8,128)S(1)} %pad_maximum_fusion.7), channel_id=1, source_target_pairs={{0,12},{1,13},{2,14},{3,15},{4,8},{5,9},{6,10},{7,11},{8,4},{9,5},... | collective-permute-start | bytes 417800 | tf_op jit(solution)/shard_map/ppermute | solution.py:202
  23.0 9.3 %collective-permute-start.13 = (f32[4,136,128]{2,1,0:T(8,128)S(1)}, f32[4,136,128]{2,1,0:T(8,128)S(1)}, u32[]{:S(2)}, u32[]{:S(2)}) collective-permute-start(f32[4,136,128]{2,1,0:T(8,128)S(1)} %pad_maximum_fusion.2), channel_id=1, source_target_pairs={{0,1},{1,0},{2,3},{3,2},{4,5},{5,4},{6,7},{7,6},{8,9},{9,8},{10,11... | collective-permute-start | bytes 835592 | tf_op jit(solution)/shard_map/ppermute | solution.py:202
  26.5 11.4 %collective-permute-start.3 = (f32[4,256,128]{2,1,0:T(8,128)S(1)}, f32[4,256,128]{2,1,0:T(8,128)S(1)}, u32[]{:S(2)}, u32[]{:S(2)}) collective-permute-start(f32[4,256,128]{2,1,0:T(8,128)S(1)} %pad_maximum_fusion.refs_0_), channel_id=1, source_target_pairs={{0,2},{1,3},{2,0},{3,1},{4,6},{5,7},{6,4},{7,5},{8,10},{9,11},{10,... | collective-permute-start | bytes 1572872 | tf_op jit(solution)/shard_map/ppermute | solution.py:202
  27.1 18.3 %collective-permute-start.2 = (f32[4,256,128]{2,1,0:T(8,128)S(1)}, f32[4,256,128]{2,1,0:T(8,128)S(1)}, u32[]{:S(2)}, u32[]{:S(2)}) collective-permute-start(f32[4,256,128]{2,1,0:T(8,128)S(1)} %pad_maximum_fusion.refs_0_), channel_id=1, source_target_pairs={{0,1},{1,0},{2,3},{3,2},{4,5},{5,4},{6,7},{7,6},{8,9},{9,8},{10,11... | collective-permute-start | bytes 1572872 | tf_op jit(solution)/shard_map/ppermute | solution.py:202
  30.7 24.0 %collective-permute-start.11 = (f32[8,136,128]{2,1,0:T(8,128)S(1)}, f32[8,136,128]{2,1,0:T(8,128)S(1)}, u32[]{:S(2)}, u32[]{:S(2)}) collective-permute-start(f32[8,136,128]{2,1,0:T(8,128)S(1)} %constant_dynamic-update-slice_fusion.refs_0_), channel_id=1, source_target_pairs={{0,16},{16,0},{1,17},{17,1},{2,18},{18,2},{3,19},{19,3},{4,20},{20... | collective-permute-start | bytes 1671176 | tf_op jit(solution)/shard_map/ppermute | solution.py:202
  32.4 7.5 %collective-permute-start.14 = (f32[2,136,128]{2,1,0:T(8,128)S(1)}, f32[2,136,128]{2,1,0:T(8,128)S(1)}, u32[]{:S(2)}, u32[]{:S(2)}) collective-permute-start(f32[2,136,128]{2,1,0:T(8,128)S(1)} %pad_maximum_fusion.8), channel_id=1, source_target_pairs={{0,4},{1,5},{2,6},{3,7},{4,0},{5,1},{6,2},{7,3},{8,12},{9,13},{10,... | collective-permute-start | bytes 417800 | tf_op jit(solution)/shard_map/ppermute | solution.py:202
  32.5 13.1 %collective-permute-start.16 = (f32[2,136,128]{2,1,0:T(8,128)S(1)}, f32[2,136,128]{2,1,0:T(8,128)S(1)}, u32[]{:S(2)}, u32[]{:S(2)}) collective-permute-start(f32[2,136,128]{2,1,0:T(8,128)S(1)} %pad_maximum_fusion.9), channel_id=1, source_target_pairs={{0,8},{1,9},{2,10},{3,11},{4,12},{5,13},{6,14},{7,15},{8,0},{9,1},... | collective-permute-start | bytes 417800 | tf_op jit(solution)/shard_map/ppermute | solution.py:202
  38.0 10.6 %collective-permute-start.5 = (f32[2,256,128]{2,1,0:T(8,128)S(1)}, f32[2,256,128]{2,1,0:T(8,128)S(1)}, u32[]{:S(2)}, u32[]{:S(2)}) collective-permute-start(f32[2,256,128]{2,1,0:T(8,128)S(1)} %slice.89), channel_id=1, source_target_pairs={{0,1},{1,0},{2,3},{3,2},{4,5},{5,4},{6,7},{7,6},{8,9},{9,8},{10,11... | collective-permute-start | bytes 786440 | tf_op jit(solution)/shard_map/ppermute | solution.py:202
  39.9 8.7 %collective-permute-start.18 = (f32[2,136,128]{2,1,0:T(8,128)S(1)}, f32[2,136,128]{2,1,0:T(8,128)S(1)}, u32[]{:S(2)}, u32[]{:S(2)}) collective-permute-start(f32[2,136,128]{2,1,0:T(8,128)S(1)} %pad_maximum_fusion.10), channel_id=1, source_target_pairs={{0,12},{1,13},{2,14},{3,15},{4,8},{5,9},{6,10},{7,11},{8,4},{9,5},... | collective-permute-start | bytes 417800 | tf_op jit(solution)/shard_map/ppermute | solution.py:202
  45.5 9.2 %collective-permute-start.15 = (f32[4,136,128]{2,1,0:T(8,128)S(1)}, f32[4,136,128]{2,1,0:T(8,128)S(1)}, u32[]{:S(2)}, u32[]{:S(2)}) collective-permute-start(f32[4,136,128]{2,1,0:T(8,128)S(1)} %pad_maximum_fusion.3.refs_2_), channel_id=1, source_target_pairs={{0,16},{16,0},{1,17},{17,1},{2,18},{18,2},{3,19},{19,3},{4,20},{20... | collective-permute-start | bytes 835592 | tf_op jit(solution)/shard_map/ppermute | solution.py:202
  45.6 9.1 %copy-start = (f32[256,1024]{1,0:T(8,128)S(1)}, f32[256,1024]{1,0:T(8,128)}, u32[]{:S(2)}) copy-start(f32[256,1024]{1,0:T(8,128)} %refs_8_.1) | copy-start | bytes 3145732
  45.6 8.8 %collective-permute-start.4 = (f32[2,256,128]{2,1,0:T(8,128)S(1)}, f32[2,256,128]{2,1,0:T(8,128)S(1)}, u32[]{:S(2)}, u32[]{:S(2)}) collective-permute-start(f32[2,256,128]{2,1,0:T(8,128)S(1)} %slice.88), channel_id=1, source_target_pairs={{0,2},{1,3},{2,0},{3,1},{4,6},{5,7},{6,4},{7,5},{8,10},{9,11},{10,... | collective-permute-start | bytes 786440 | tf_op jit(solution)/shard_map/ppermute | solution.py:202
  48.6 6.1 %collective-permute-start.17 = (f32[2,136,128]{2,1,0:T(8,128)S(1)}, f32[2,136,128]{2,1,0:T(8,128)S(1)}, u32[]{:S(2)}, u32[]{:S(2)}) collective-permute-start(f32[2,136,128]{2,1,0:T(8,128)S(1)} %collective-permute-done.16.refs_4_), channel_id=1, source_target_pairs={{0,16},{16,0},{1,17},{17,1},{2,18},{18,2},{3,19},{19,3},{4,20},{20... | collective-permute-start | bytes 417800 | tf_op jit(solution)/shard_map/ppermute | solution.py:202
  48.6 6.1 %collective-permute-start.19 = (f32[2,136,128]{2,1,0:T(8,128)S(1)}, f32[2,136,128]{2,1,0:T(8,128)S(1)}, u32[]{:S(2)}, u32[]{:S(2)}) collective-permute-start(f32[2,136,128]{2,1,0:T(8,128)S(1)} %collective-permute-done.18.refs_6_), channel_id=1, source_target_pairs={{0,16},{16,0},{1,17},{17,1},{2,18},{18,2},{3,19},{19,3},{4,20},{20... | collective-permute-start | bytes 417800 | tf_op jit(solution)/shard_map/ppermute | solution.py:202

commit v6 on v5

--- a/solution.py
+++ b/solution.py
@@ -14,22 +14,8 @@
 META = 8
 
 
-def pack_kernel(reader_any, k_any, column_any, tiles_any, *refs):
-    outs = refs[:4]
-    reader_ref, k_ref, column_ref, tiles_ref, count_ref, sem = refs[4:]
-    fetches = [
-        pltpu.make_async_copy(*pair, sem.at[number])
-        for number, pair in enumerate(
-            (
-                (tiles_any, tiles_ref),
-                (reader_any, reader_ref),
-                (k_any, k_ref),
-                (column_any, column_ref),
-            )
-        )
-    ]
-    for fetch in fetches:
-        fetch.start()
+def pack_kernel(words_ref, tiles_ref, *refs):
+    outs, count_ref = refs[:4], refs[4]
     count, height, width = tiles_ref.shape
     half = outs[0].shape[0] // 2
     targets = 8 * half
@@ -39,14 +25,14 @@
     for target in range(targets):
         count_ref[target] = 0
     lane = lax.broadcasted_iota(jnp.int32, (META, width), 1)
-    for fetch in fetches:
-        fetch.wait()
 
     def place(j, carry):
-        position = jnp.bitwise_xor(reader_ref[j], me)
+        word = words_ref[j]
+        reader = word // (KT * CT)
+        position = jnp.bitwise_xor(reader, me)
         slot = count_ref[position]
         count_ref[position] = slot + 1
-        code = (k_ref[j] * CT + column_ref[j]).astype(jnp.float32)
+        code = (word - reader * (KT * CT)).astype(jnp.float32)
         x, y, z = position % 2, position // 2 % 2, position // 4
         odd = z % 2
         first, second = jnp.where(odd == 1, y, x), jnp.where(odd == 1, x, y)
@@ -66,22 +52,21 @@
 
 
 def pack(tiles, readers, tile_k, tile_column, targets):
-    count, height, width = tiles.shape
+    _, height, width = tiles.shape
+    vmem = pl.BlockSpec(memory_space=pltpu.VMEM)
+    words = (readers.reshape(-1) * KT + tile_k) * CT + tile_column
     out = jax.ShapeDtypeStruct((targets // 4, SLOT * height + META, width), jnp.float32)
     return pl.pallas_call(
         pack_kernel,
         out_shape=[out] * 4,
-        in_specs=[pl.BlockSpec(memory_space=pltpu.HBM)] * 4,
-        out_specs=[pl.BlockSpec(memory_space=pltpu.VMEM)] * 4,
+        in_specs=[pl.BlockSpec(memory_space=pltpu.SMEM), vmem],
+        out_specs=[vmem] * 4,
         scratch_shapes=[
-            *[pltpu.SMEM((count,), jnp.int32)] * 3,
-            pltpu.VMEM(tiles.shape, tiles.dtype),
             pltpu.SMEM((targets,), jnp.int32),
-            pltpu.SemaphoreType.DMA((4,)),
         ],
         cost_estimate=pl.CostEstimate(flops=0, bytes_accessed=4 * tiles.size * 3, transcendentals=0),
         compiler_params=pltpu.CompilerParams(vmem_limit_bytes=8 * 1024 * 1024),
-    )(readers.reshape(-1), tile_k, tile_column, tiles)
+    )(words, tiles)
 
 
 def split_kernel(positions, *refs):
@@ -209,15 +194,15 @@
 def gather(block, size):
     held, at = block[None], (0,)
     bit = size // 2
-    while bit > 2:
+    while bit > 4:
         held, at = jnp.concatenate([held, hop(held, bit)], axis=0), at + tuple(p ^ bit for p in at)
         bit //= 2
-    over_x, over_y = hop(held, 1), hop(held, 2)
-    cut = len(at) // 2
-    pieces = [held, over_x, over_y, hop(over_x[:cut], 2), hop(over_y[cut:], 1)]
-    positions = [at] + [tuple(p ^ step for p in at) for step in (1, 2)]
-    positions += [tuple(p ^ 3 for p in at[:cut]), tuple(p ^ 3 for p in at[cut:])]
-    return pieces, positions
+    pieces = {0: held, 4: hop(held, 4), 1: hop(held, 1), 2: hop(held, 2)}
+    pieces[5] = hop(pieces[4], 1)
+    pieces[6] = hop(pieces[4], 2)
+    pieces[3] = hop(pieces[2], 1)
+    pieces[7] = hop(pieces[5], 2)
+    return list(pieces.values()), [tuple(p ^ step for p in at) for step in pieces]
 
 
 def across(kept, sent, first, second):

time: 59.2 us -> 70.9 us (1.20)
  waiting for transfers between devices: 18.6 us -> 35.1 us
  starting transfers between devices: 29.8 us -> 25.9 us
  local copies, waits for them, and re-layouts: 3.21 us -> 1.2 us
    ppermute x20 -> x22, waiting for transfers between devices: 18.6 us -> 35.1 us  [send(): return lax.ppermute(x, axis, [(i, partner(i)) for i in range(size)])]
    ppermute x20 -> x22, starting transfers between devices: 29.8 us -> 25.9 us  [send(): return lax.ppermute(x, axis, [(i, partner(i)) for i in range(size)])]
    unnamed x14 -> x6, local copies, waits for them, and re-layouts: 3.04 us -> 1.07 us
  transfers between devices with their start and end apart: 20 -> 22, of which waited for: 8 -> 10; matrix products, arithmetic and copies ran while one was open for 2% -> 3% of each run, Pallas kernels for 3% -> 2%
where the time goes in v6:
time: 70.9 us; the launch traced here: 70.2 us
  waiting for transfers between devices  35.1 us (50%)
  starting transfers between devices  25.9 us (37%)
  Pallas kernels  6.05 us (9%)
  other arithmetic  1.77 us (2%)
  local copies, waits for them, and re-layouts  1.2 us (2%)
    ppermute x22, waiting for transfers between devices, send(): return lax.ppermute(x, axis, [(i, partner(i)) for i in range(size)])  35.1 us
    ppermute x22, starting transfers between devices, send(): return lax.ppermute(x, axis, [(i, partner(i)) for i in range(size)])  25.9 us
    pallas_call x1, Pallas kernels, contract(): pl.pallas_call(functools.partial(contract_kernel, len(groups), len(groups...  4.32 us
    pallas_call x1, Pallas kernels, pack(): pl.pallas_call(pack_kernel, out_shape=[out] * 4, in_specs=[pl.BlockSpec(m...  1.48 us
  transfers between devices with their start and end apart: 22, of which 10 were waited for; matrix products, arithmetic and copies ran while one was open for 3% of the time, Pallas kernels for 2%

profile of v6, /device:TPU:0, one launch (start us, length us, event | category | flops | bytes accessed | tf_op | source)
XLA Modules:
  0.0 70.2 jit_solution(10459558914019105989)
XLA Ops:
  0.0 4.0 %collective-permute-start = (f32[1,256,128]{2,1,0:T(8,128)}, f32[1,256,128]{2,1,0:T(8,128)S(1)}, u32[]{:S(2)}, u32[]{:S(2)}) collective-permute-start(f32[1,256,128]{2,1,0:T(8,128)} %bitcast.7), channel_id=1, source_target_pairs={{0,8},{1,9},{2,10},{3,11},{4,12},{5,13},{6,14},{7,15},{8,0},{9,1},... | collective-permute-start | bytes 393224 | tf_op jit(solution)/shard_map/ppermute | solution.py:187
  4.0 0.7 fusion.1.words_ref
  4.7 0.0 copy-start.1
  4.7 1.0 %copy-done.1 = f32[16,64,128]{2,1,0:T(8,128)S(1)} copy-done((f32[16,64,128]{2,1,0:T(8,128)S(1)}, f32[16,64,128]{2,1,0:T(8,128)}, u32[]{:S(2)}) %copy-start.1) | copy-done | bytes 524312
  5.8 1.5 %shard_map.65 = (f32[4,136,128]{2,1,0:T(8,128)S(1)}, f32[4,136,128]{2,1,0:T(8,128)S(1)}, f32[4,136,128]{2,1,0:T(8,128)S(1)}, f32[4,136,128]{2,1,0:T(8,128)S(1)}) custom-call(s32[16]{0:T(128)S(1)} %fusion.1.words_ref, f32[16,64,128]{2,1,0:T(8,128)S(1)} %copy-done.1), custom_call_target="tpu_custom_call" | custom-call | bytes 1572864 | tf_op jit(solution)/shard_map/pallas_call | solution.py:59
  7.3 1.6 %collective-permute-start.8 = (f32[4,136,128]{2,1,0:T(8,128)S(1)}, f32[4,136,128]{2,1,0:T(8,128)S(1)}, u32[]{:S(2)}, u32[]{:S(2)}) collective-permute-start(f32[4,136,128]{2,1,0:T(8,128)S(1)} %get-tuple-element.10), channel_id=1, source_target_pairs={{0,1},{1,0},{2,3},{3,2},{4,5},{5,4},{6,7},{7,6},{8,9},{9,8},{10,11... | collective-permute-start | bytes 835592 | tf_op jit(solution)/shard_map/ppermute | solution.py:187
  8.8 1.5 %collective-permute-start.9 = (f32[4,136,128]{2,1,0:T(8,128)S(1)}, f32[4,136,128]{2,1,0:T(8,128)S(1)}, u32[]{:S(2)}, u32[]{:S(2)}) collective-permute-start(f32[4,136,128]{2,1,0:T(8,128)S(1)} %get-tuple-element.12), channel_id=1, source_target_pairs={{0,2},{1,3},{2,0},{3,1},{4,6},{5,7},{6,4},{7,5},{8,10},{9,11},{10,... | collective-permute-start | bytes 835592 | tf_op jit(solution)/shard_map/ppermute | solution.py:187
  10.4 0.2 collective-permute-done
  10.6 0.9 %pad_maximum_fusion.3.refs_0_ = f32[2,256,128]{2,1,0:T(8,128)S(1)} fusion(f32[1,256,128]{2,1,0:T(8,128)S(1)} %collective-permute-done, f32[1,256,128]{2,1,0:T(8,128)} %bitcast.8), kind=kLoop, calls=%fused_computation.3 | loop fusion | flops 65536 | bytes 524288 | tf_op jit(solution)/shard_map/concatenate | solution.py:198
  11.5 1.6 %collective-permute-start.3 = (f32[2,256,128]{2,1,0:T(8,128)S(1)}, f32[2,256,128]{2,1,0:T(8,128)S(1)}, u32[]{:S(2)}, u32[]{:S(2)}) collective-permute-start(f32[2,256,128]{2,1,0:T(8,128)S(1)} %pad_maximum_fusion.3.refs_0_), channel_id=1, source_target_pairs={{0,2},{1,3},{2,0},{3,1},{4,6},{5,7},{6,4},{7,5},{8,10},{9,11},{10,... | collective-permute-start | bytes 786440 | tf_op jit(solution)/shard_map/ppermute | solution.py:187
  13.1 0.8 %collective-permute-start.1 = (f32[2,256,128]{2,1,0:T(8,128)S(1)}, f32[2,256,128]{2,1,0:T(8,128)S(1)}, u32[]{:S(2)}, u32[]{:S(2)}) collective-permute-start(f32[2,256,128]{2,1,0:T(8,128)S(1)} %pad_maximum_fusion.3.refs_0_), channel_id=1, source_target_pairs={{0,4},{1,5},{2,6},{3,7},{4,0},{5,1},{6,2},{7,3},{8,12},{9,13},{10,... | collective-permute-start | bytes 786440 | tf_op jit(solution)/shard_map/ppermute | solution.py:187
  13.9 1.5 %collective-permute-done.8 = f32[4,136,128]{2,1,0:T(8,128)S(1)} collective-permute-done((f32[4,136,128]{2,1,0:T(8,128)S(1)}, f32[4,136,128]{2,1,0:T(8,128)S(1)}, u32[]{:S(2)}, u32[]{:S(2)}) %collective-permute-start.8) | collective-permute-done | bytes 278560 | tf_op jit(solution)/shard_map/ppermute | solution.py:187
  15.5 1.8 %collective-permute-start.11 = (f32[2,136,128]{2,1,0:T(8,128)S(1)}, f32[2,136,128]{2,1,0:T(8,128)S(1)}, u32[]{:S(2)}, u32[]{:S(2)}) collective-permute-start(f32[2,136,128]{2,1,0:T(8,128)S(1)} %pad_maximum_fusion.5), channel_id=1, source_target_pairs={{0,8},{1,9},{2,10},{3,11},{4,12},{5,13},{6,14},{7,15},{8,0},{9,1},... | collective-permute-start | bytes 417800 | tf_op jit(solution)/shard_map/ppermute | solution.py:187
  17.3 0.6 collective-permute-start.14
  17.9 0.5 collective-permute-done.9
  18.4 1.6 %collective-permute-start.10 = (f32[2,136,128]{2,1,0:T(8,128)S(1)}, f32[2,136,128]{2,1,0:T(8,128)S(1)}, u32[]{:S(2)}, u32[]{:S(2)}) collective-permute-start(f32[2,136,128]{2,1,0:T(8,128)S(1)} %pad_maximum_fusion.4), channel_id=1, source_target_pairs={{0,4},{1,5},{2,6},{3,7},{4,0},{5,1},{6,2},{7,3},{8,12},{9,13},{10,... | collective-permute-start | bytes 417800 | tf_op jit(solution)/shard_map/ppermute | solution.py:187
  20.1 5.9 %collective-permute-done.10 = f32[2,136,128]{2,1,0:T(8,128)S(1)} collective-permute-done((f32[2,136,128]{2,1,0:T(8,128)S(1)}, f32[2,136,128]{2,1,0:T(8,128)S(1)}, u32[]{:S(2)}, u32[]{:S(2)}) %collective-permute-start.10) | collective-permute-done | bytes 139296 | tf_op jit(solution)/shard_map/ppermute | solution.py:187
  26.1 4.5 %collective-permute-start.12 = (f32[2,136,128]{2,1,0:T(8,128)S(1)}, f32[2,136,128]{2,1,0:T(8,128)S(1)}, u32[]{:S(2)}, u32[]{:S(2)}) collective-permute-start(f32[2,136,128]{2,1,0:T(8,128)S(1)} %pad_maximum_fusion.6), channel_id=1, source_target_pairs={{0,12},{1,13},{2,14},{3,15},{4,8},{5,9},{6,10},{7,11},{8,4},{9,5},... | collective-permute-start | bytes 417800 | tf_op jit(solution)/shard_map/ppermute | solution.py:187
  30.5 0.0 collective-permute-done.11
  30.5 1.6 %collective-permute-start.2 = (f32[2,256,128]{2,1,0:T(8,128)S(1)}, f32[2,256,128]{2,1,0:T(8,128)S(1)}, u32[]{:S(2)}, u32[]{:S(2)}) collective-permute-start(f32[2,256,128]{2,1,0:T(8,128)S(1)} %pad_maximum_fusion.3.refs_0_), channel_id=1, source_target_pairs={{0,1},{1,0},{2,3},{3,2},{4,5},{5,4},{6,7},{7,6},{8,9},{9,8},{10,11... | collective-permute-start | bytes 786440 | tf_op jit(solution)/shard_map/ppermute | solution.py:187
  32.1 0.0 collective-permute-done.1.refs_1_
  32.1 0.6 collective-permute-start.15
  32.7 0.9 %collective-permute-done.12 = f32[2,136,128]{2,1,0:T(8,128)S(1)} collective-permute-done((f32[2,136,128]{2,1,0:T(8,128)S(1)}, f32[2,136,128]{2,1,0:T(8,128)S(1)}, u32[]{:S(2)}, u32[]{:S(2)}) %collective-permute-start.12) | collective-permute-done | bytes 139296 | tf_op jit(solution)/shard_map/ppermute | solution.py:187
  33.6 0.5 collective-permute-start.5
  34.1 0.0 collective-permute-done.3.refs_3_
  34.1 1.6 %collective-permute-start.4 = (f32[2,256,128]{2,1,0:T(8,128)S(1)}, f32[2,256,128]{2,1,0:T(8,128)S(1)}, u32[]{:S(2)}, u32[]{:S(2)}) collective-permute-start(f32[2,256,128]{2,1,0:T(8,128)S(1)} %collective-permute-done.1.refs_1_), channel_id=1, source_target_pairs={{0,1},{1,0},{2,3},{3,2},{4,5},{5,4},{6,7},{7,6},{8,9},{9,8},{10,11... | collective-permute-start | bytes 786440 | tf_op jit(solution)/shard_map/ppermute | solution.py:187
  35.7 0.0 collective-permute-done.14
  35.7 0.5 collective-permute-start.6
  36.3 9.6 %collective-permute-done.15 = f32[4,136,128]{2,1,0:T(8,128)S(1)} collective-permute-done((f32[4,136,128]{2,1,0:T(8,128)S(1)}, f32[4,136,128]{2,1,0:T(8,128)S(1)}, u32[]{:S(2)}, u32[]{:S(2)}) %collective-permute-start.15) | collective-permute-done | bytes 278560 | tf_op jit(solution)/shard_map/ppermute | solution.py:187
  45.8 0.0 collective-permute-start.13
  45.9 0.0 collective-permute-done.2.refs_2_
  45.9 0.1 collective-permute-start.16
  46.0 8.7 %collective-permute-done.6.refs_6_ = f32[2,256,128]{2,1,0:T(8,128)S(1)} collective-permute-done((f32[2,256,128]{2,1,0:T(8,128)S(1)}, f32[2,256,128]{2,1,0:T(8,128)S(1)}, u32[]{:S(2)}, u32[]{:S(2)}) %collective-permute-start.6) | collective-permute-done | bytes 262176 | tf_op jit(solution)/shard_map/ppermute | solution.py:187
  54.7 0.0 collective-permute-start.18
  54.7 0.0 collective-permute-done.16
  54.7 1.9 %collective-permute-start.20 = (f32[2,136,128]{2,1,0:T(8,128)S(1)}, f32[2,136,128]{2,1,0:T(8,128)S(1)}, u32[]{:S(2)}, u32[]{:S(2)}) collective-permute-start(f32[2,136,128]{2,1,0:T(8,128)S(1)} %pad_maximum_fusion.9), channel_id=1, source_target_pairs={{0,12},{1,13},{2,14},{3,15},{4,8},{5,9},{6,10},{7,11},{8,4},{9,5},... | collective-permute-start | bytes 417800 | tf_op jit(solution)/shard_map/ppermute | solution.py:187
  56.7 0.0 copy-start
  56.7 0.0 collective-permute-done.5.refs_5_
  56.7 0.1 collective-permute-start.17
  56.8 0.0 collective-permute-done.4.refs_4_
  56.8 0.6 collective-permute-start.7
  57.4 7.0 %collective-permute-done.18.refs_4_ = f32[2,136,128]{2,1,0:T(8,128)S(1)} collective-permute-done((f32[2,136,128]{2,1,0:T(8,128)S(1)}, f32[2,136,128]{2,1,0:T(8,128)S(1)}, u32[]{:S(2)}, u32[]{:S(2)}) %collective-permute-start.18) | collective-permute-done | bytes 139296 | tf_op jit(solution)/shard_map/ppermute | solution.py:187
  64.4 0.0 collective-permute-start.19
  64.4 0.0 collective-permute-done.20.refs_6_
  64.4 0.5 collective-permute-start.21
  64.9 0.7 collective-permute-done.7.refs_7_
  65.5 0.3 shard_map.64.split_ref
  65.8 0.0 collective-permute-done.19.refs_5_
  65.8 0.1 collective-permute-done.21.refs_7_
  65.9 0.0 collective-permute-done.13.refs_1_
  65.9 0.0 collective-permute-done.17.refs_3_
  65.9 0.0 copy-done
  65.9 4.3 %shard_map.66 = f32[256,1024]{1,0:T(8,128)} custom-call(bf16[16,256,256]{2,1,0:T(8,128)(2,1)S(1)} %shard_map.64.split_ref, f32[8,136,128]{2,1,0:T(8,128)S(1)} %constant_dynamic-update-slice_fusion.refs_0_, f32[8,136,128]{2,1,0:T(8,128)S(1)} %collective-permute-done.13.refs_1_, f32[4,136,128]{2,1,0:T(8,128)S(1)} %pad_maximum_fusion.2.refs_2_, ...), custom_call_target="tpu_custom_call" | custom-call | tf_op jit(solution)/shard_map/pallas_call | solution.py:172
  (21 shorter events, 0.3 us)
Async XLA Ops:
  0.0 10.5 %collective-permute-start = (f32[1,256,128]{2,1,0:T(8,128)}, f32[1,256,128]{2,1,0:T(8,128)S(1)}, u32[]{:S(2)}, u32[]{:S(2)}) collective-permute-start(f32[1,256,128]{2,1,0:T(8,128)} %bitcast.7), channel_id=1, source_target_pairs={{0,8},{1,9},{2,10},{3,11},{4,12},{5,13},{6,14},{7,15},{8,0},{9,1},... | collective-permute-start | bytes 393224 | tf_op jit(solution)/shard_map/ppermute | solution.py:187
  4.7 1.0 %copy-start.1 = (f32[16,64,128]{2,1,0:T(8,128)S(1)}, f32[16,64,128]{2,1,0:T(8,128)}, u32[]{:S(2)}) copy-start(f32[16,64,128]{2,1,0:T(8,128)} %tiles_ref.1) | copy-start | bytes 1572868
  7.3 8.2 %collective-permute-start.8 = (f32[4,136,128]{2,1,0:T(8,128)S(1)}, f32[4,136,128]{2,1,0:T(8,128)S(1)}, u32[]{:S(2)}, u32[]{:S(2)}) collective-permute-start(f32[4,136,128]{2,1,0:T(8,128)S(1)} %get-tuple-element.10), channel_id=1, source_target_pairs={{0,1},{1,0},{2,3},{3,2},{4,5},{5,4},{6,7},{7,6},{8,9},{9,8},{10,11... | collective-permute-start | bytes 835592 | tf_op jit(solution)/shard_map/ppermute | solution.py:187
  8.8 9.6 %collective-permute-start.9 = (f32[4,136,128]{2,1,0:T(8,128)S(1)}, f32[4,136,128]{2,1,0:T(8,128)S(1)}, u32[]{:S(2)}, u32[]{:S(2)}) collective-permute-start(f32[4,136,128]{2,1,0:T(8,128)S(1)} %get-tuple-element.12), channel_id=1, source_target_pairs={{0,2},{1,3},{2,0},{3,1},{4,6},{5,7},{6,4},{7,5},{8,10},{9,11},{10,... | collective-permute-start | bytes 835592 | tf_op jit(solution)/shard_map/ppermute | solution.py:187
  11.5 22.7 %collective-permute-start.3 = (f32[2,256,128]{2,1,0:T(8,128)S(1)}, f32[2,256,128]{2,1,0:T(8,128)S(1)}, u32[]{:S(2)}, u32[]{:S(2)}) collective-permute-start(f32[2,256,128]{2,1,0:T(8,128)S(1)} %pad_maximum_fusion.3.refs_0_), channel_id=1, source_target_pairs={{0,2},{1,3},{2,0},{3,1},{4,6},{5,7},{6,4},{7,5},{8,10},{9,11},{10,... | collective-permute-start | bytes 786440 | tf_op jit(solution)/shard_map/ppermute | solution.py:187
  13.1 19.0 %collective-permute-start.1 = (f32[2,256,128]{2,1,0:T(8,128)S(1)}, f32[2,256,128]{2,1,0:T(8,128)S(1)}, u32[]{:S(2)}, u32[]{:S(2)}) collective-permute-start(f32[2,256,128]{2,1,0:T(8,128)S(1)} %pad_maximum_fusion.3.refs_0_), channel_id=1, source_target_pairs={{0,4},{1,5},{2,6},{3,7},{4,0},{5,1},{6,2},{7,3},{8,12},{9,13},{10,... | collective-permute-start | bytes 786440 | tf_op jit(solution)/shard_map/ppermute | solution.py:187
  15.5 15.1 %collective-permute-start.11 = (f32[2,136,128]{2,1,0:T(8,128)S(1)}, f32[2,136,128]{2,1,0:T(8,128)S(1)}, u32[]{:S(2)}, u32[]{:S(2)}) collective-permute-start(f32[2,136,128]{2,1,0:T(8,128)S(1)} %pad_maximum_fusion.5), channel_id=1, source_target_pairs={{0,8},{1,9},{2,10},{3,11},{4,12},{5,13},{6,14},{7,15},{8,0},{9,1},... | collective-permute-start | bytes 417800 | tf_op jit(solution)/shard_map/ppermute | solution.py:187
  17.3 18.4 %collective-permute-start.14 = (f32[4,136,128]{2,1,0:T(8,128)S(1)}, f32[4,136,128]{2,1,0:T(8,128)S(1)}, u32[]{:S(2)}, u32[]{:S(2)}) collective-permute-start(f32[4,136,128]{2,1,0:T(8,128)S(1)} %pad_maximum_fusion), channel_id=1, source_target_pairs={{0,2},{1,3},{2,0},{3,1},{4,6},{5,7},{6,4},{7,5},{8,10},{9,11},{10,... | collective-permute-start | bytes 835592 | tf_op jit(solution)/shard_map/ppermute | solution.py:187
  18.4 7.6 %collective-permute-start.10 = (f32[2,136,128]{2,1,0:T(8,128)S(1)}, f32[2,136,128]{2,1,0:T(8,128)S(1)}, u32[]{:S(2)}, u32[]{:S(2)}) collective-permute-start(f32[2,136,128]{2,1,0:T(8,128)S(1)} %pad_maximum_fusion.4), channel_id=1, source_target_pairs={{0,4},{1,5},{2,6},{3,7},{4,0},{5,1},{6,2},{7,3},{8,12},{9,13},{10,... | collective-permute-start | bytes 417800 | tf_op jit(solution)/shard_map/ppermute | solution.py:187
  26.1 7.5 %collective-permute-start.12 = (f32[2,136,128]{2,1,0:T(8,128)S(1)}, f32[2,136,128]{2,1,0:T(8,128)S(1)}, u32[]{:S(2)}, u32[]{:S(2)}) collective-permute-start(f32[2,136,128]{2,1,0:T(8,128)S(1)} %pad_maximum_fusion.6), channel_id=1, source_target_pairs={{0,12},{1,13},{2,14},{3,15},{4,8},{5,9},{6,10},{7,11},{8,4},{9,5},... | collective-permute-start | bytes 417800 | tf_op jit(solution)/shard_map/ppermute | solution.py:187
  30.5 15.3 %collective-permute-start.2 = (f32[2,256,128]{2,1,0:T(8,128)S(1)}, f32[2,256,128]{2,1,0:T(8,128)S(1)}, u32[]{:S(2)}, u32[]{:S(2)}) collective-permute-start(f32[2,256,128]{2,1,0:T(8,128)S(1)} %pad_maximum_fusion.3.refs_0_), channel_id=1, source_target_pairs={{0,1},{1,0},{2,3},{3,2},{4,5},{5,4},{6,7},{7,6},{8,9},{9,8},{10,11... | collective-permute-start | bytes 786440 | tf_op jit(solution)/shard_map/ppermute | solution.py:187
  32.1 13.7 %collective-permute-start.15 = (f32[4,136,128]{2,1,0:T(8,128)S(1)}, f32[4,136,128]{2,1,0:T(8,128)S(1)}, u32[]{:S(2)}, u32[]{:S(2)}) collective-permute-start(f32[4,136,128]{2,1,0:T(8,128)S(1)} %pad_maximum_fusion.1), channel_id=1, source_target_pairs={{0,1},{1,0},{2,3},{3,2},{4,5},{5,4},{6,7},{7,6},{8,9},{9,8},{10,11... | collective-permute-start | bytes 835592 | tf_op jit(solution)/shard_map/ppermute | solution.py:187
  33.6 23.1 %collective-permute-start.5 = (f32[2,256,128]{2,1,0:T(8,128)S(1)}, f32[2,256,128]{2,1,0:T(8,128)S(1)}, u32[]{:S(2)}, u32[]{:S(2)}) collective-permute-start(f32[2,256,128]{2,1,0:T(8,128)S(1)} %collective-permute-done.1.refs_1_), channel_id=1, source_target_pairs={{0,2},{1,3},{2,0},{3,1},{4,6},{5,7},{6,4},{7,5},{8,10},{9,11},{10,... | collective-permute-start | bytes 786440 | tf_op jit(solution)/shard_map/ppermute | solution.py:187
  34.1 22.7 %collective-permute-start.4 = (f32[2,256,128]{2,1,0:T(8,128)S(1)}, f32[2,256,128]{2,1,0:T(8,128)S(1)}, u32[]{:S(2)}, u32[]{:S(2)}) collective-permute-start(f32[2,256,128]{2,1,0:T(8,128)S(1)} %collective-permute-done.1.refs_1_), channel_id=1, source_target_pairs={{0,1},{1,0},{2,3},{3,2},{4,5},{5,4},{6,7},{7,6},{8,9},{9,8},{10,11... | collective-permute-start | bytes 786440 | tf_op jit(solution)/shard_map/ppermute | solution.py:187
  35.7 19.0 %collective-permute-start.6 = (f32[2,256,128]{2,1,0:T(8,128)S(1)}, f32[2,256,128]{2,1,0:T(8,128)S(1)}, u32[]{:S(2)}, u32[]{:S(2)}) collective-permute-start(f32[2,256,128]{2,1,0:T(8,128)S(1)} %collective-permute-done.3.refs_3_), channel_id=1, source_target_pairs={{0,1},{1,0},{2,3},{3,2},{4,5},{5,4},{6,7},{7,6},{8,9},{9,8},{10,11... | collective-permute-start | bytes 786440 | tf_op jit(solution)/shard_map/ppermute | solution.py:187
  45.8 20.1 %collective-permute-start.13 = (f32[8,136,128]{2,1,0:T(8,128)S(1)}, f32[8,136,128]{2,1,0:T(8,128)S(1)}, u32[]{:S(2)}, u32[]{:S(2)}) collective-permute-start(f32[8,136,128]{2,1,0:T(8,128)S(1)} %constant_dynamic-update-slice_fusion.refs_0_), channel_id=1, source_target_pairs={{0,16},{16,0},{1,17},{17,1},{2,18},{18,2},{3,19},{19,3},{4,20},{20... | collective-permute-start | bytes 1671176 | tf_op jit(solution)/shard_map/ppermute | solution.py:187
  45.9 8.8 %collective-permute-start.16 = (f32[2,136,128]{2,1,0:T(8,128)S(1)}, f32[2,136,128]{2,1,0:T(8,128)S(1)}, u32[]{:S(2)}, u32[]{:S(2)}) collective-permute-start(f32[2,136,128]{2,1,0:T(8,128)S(1)} %pad_maximum_fusion.7), channel_id=1, source_target_pairs={{0,4},{1,5},{2,6},{3,7},{4,0},{5,1},{6,2},{7,3},{8,12},{9,13},{10,... | collective-permute-start | bytes 417800 | tf_op jit(solution)/shard_map/ppermute | solution.py:187
  54.7 9.6 %collective-permute-start.18 = (f32[2,136,128]{2,1,0:T(8,128)S(1)}, f32[2,136,128]{2,1,0:T(8,128)S(1)}, u32[]{:S(2)}, u32[]{:S(2)}) collective-permute-start(f32[2,136,128]{2,1,0:T(8,128)S(1)} %pad_maximum_fusion.8), channel_id=1, source_target_pairs={{0,8},{1,9},{2,10},{3,11},{4,12},{5,13},{6,14},{7,15},{8,0},{9,1},... | collective-permute-start | bytes 417800 | tf_op jit(solution)/shard_map/ppermute | solution.py:187
  54.7 9.6 %collective-permute-start.20 = (f32[2,136,128]{2,1,0:T(8,128)S(1)}, f32[2,136,128]{2,1,0:T(8,128)S(1)}, u32[]{:S(2)}, u32[]{:S(2)}) collective-permute-start(f32[2,136,128]{2,1,0:T(8,128)S(1)} %pad_maximum_fusion.9), channel_id=1, source_target_pairs={{0,12},{1,13},{2,14},{3,15},{4,8},{5,9},{6,10},{7,11},{8,4},{9,5},... | collective-permute-start | bytes 417800 | tf_op jit(solution)/shard_map/ppermute | solution.py:187
  56.7 9.2 %copy-start = (f32[256,1024]{1,0:T(8,128)S(1)}, f32[256,1024]{1,0:T(8,128)}, u32[]{:S(2)}) copy-start(f32[256,1024]{1,0:T(8,128)} %refs_8_.1) | copy-start | bytes 3145732
  56.7 9.2 %collective-permute-start.17 = (f32[4,136,128]{2,1,0:T(8,128)S(1)}, f32[4,136,128]{2,1,0:T(8,128)S(1)}, u32[]{:S(2)}, u32[]{:S(2)}) collective-permute-start(f32[4,136,128]{2,1,0:T(8,128)S(1)} %pad_maximum_fusion.2.refs_2_), channel_id=1, source_target_pairs={{0,16},{16,0},{1,17},{17,1},{2,18},{18,2},{3,19},{19,3},{4,20},{20... | collective-permute-start | bytes 835592 | tf_op jit(solution)/shard_map/ppermute | solution.py:187
  56.8 8.7 %collective-permute-start.7 = (f32[2,256,128]{2,1,0:T(8,128)S(1)}, f32[2,256,128]{2,1,0:T(8,128)S(1)}, u32[]{:S(2)}, u32[]{:S(2)}) collective-permute-start(f32[2,256,128]{2,1,0:T(8,128)S(1)} %collective-permute-done.4.refs_4_), channel_id=1, source_target_pairs={{0,2},{1,3},{2,0},{3,1},{4,6},{5,7},{6,4},{7,5},{8,10},{9,11},{10,... | collective-permute-start | bytes 786440 | tf_op jit(solution)/shard_map/ppermute | solution.py:187
  64.4 1.4 %collective-permute-start.19 = (f32[2,136,128]{2,1,0:T(8,128)S(1)}, f32[2,136,128]{2,1,0:T(8,128)S(1)}, u32[]{:S(2)}, u32[]{:S(2)}) collective-permute-start(f32[2,136,128]{2,1,0:T(8,128)S(1)} %collective-permute-done.18.refs_4_), channel_id=1, source_target_pairs={{0,16},{16,0},{1,17},{17,1},{2,18},{18,2},{3,19},{19,3},{4,20},{20... | collective-permute-start | bytes 417800 | tf_op jit(solution)/shard_map/ppermute | solution.py:187
  64.4 1.6 %collective-permute-start.21 = (f32[2,136,128]{2,1,0:T(8,128)S(1)}, f32[2,136,128]{2,1,0:T(8,128)S(1)}, u32[]{:S(2)}, u32[]{:S(2)}) collective-permute-start(f32[2,136,128]{2,1,0:T(8,128)S(1)} %collective-permute-done.20.refs_6_), channel_id=1, source_target_pairs={{0,16},{16,0},{1,17},{17,1},{2,18},{18,2},{3,19},{19,3},{4,20},{20... | collective-permute-start | bytes 417800 | tf_op jit(solution)/shard_map/ppermute | solution.py:187

commit v7 on v6

--- a/solution.py
+++ b/solution.py
@@ -191,50 +191,50 @@
     return send(x, "bulk", lambda i: i ^ step)
 
 
-def gather(block, size):
-    held, at = block[None], (0,)
-    bit = size // 2
-    while bit > 4:
-        held, at = jnp.concatenate([held, hop(held, bit)], axis=0), at + tuple(p ^ bit for p in at)
-        bit //= 2
-    pieces = {0: held, 4: hop(held, 4), 1: hop(held, 1), 2: hop(held, 2)}
-    pieces[5] = hop(pieces[4], 1)
-    pieces[6] = hop(pieces[4], 2)
-    pieces[3] = hop(pieces[2], 1)
-    pieces[7] = hop(pieces[5], 2)
-    return list(pieces.values()), [tuple(p ^ step for p in at) for step in pieces]
-
-
-def across(kept, sent, first, second):
-    half = kept.shape[0] // 2
-    come = hop(sent, first)
-    last = hop(jnp.concatenate([kept[half:], come[half:]], axis=0), second)
-    return (
-        [jnp.stack([kept[z], come[z]]) for z in range(half)],
-        [jnp.stack([last[z], last[half + z]]) for z in range(half)],
-    )
+def hop(x, step):
+    return send(x, "bulk", lambda i: i ^ step)
+
+
+def hop_both(blocks, other, step):
+    count, height, width = blocks.shape
+    flat = jnp.concatenate([blocks.reshape(-1, width), other.reshape(-1, width)], axis=0)
+    come = hop(flat, step)
+    return come[: count * height].reshape(blocks.shape), come[count * height :].reshape(other.shape)
 
 
 def local(residual_in, amplitudes, integral_tiles, tile_reader, tile_k, tile_column):
     targets = lax.axis_size("bulk")
     rows_axis = lax.axis_size("row")
     width = integral_tiles.shape[2]
-    pieces, positions = gather(amplitudes, targets)
+    held, at = amplitudes[None], (0,)
+    bit = targets // 2
+    while bit > 4:
+        held, at = jnp.concatenate([held, hop(held, bit)], axis=0), at + tuple(p ^ bit for p in at)
+        bit //= 2
     even_kept, even_sent, odd_kept, odd_sent = pack(
         integral_tiles, tile_reader, tile_k, tile_column, targets
     )
-    odd = across(odd_kept, odd_sent, 2, 1)
-    even = across(even_kept, even_sent, 1, 2)
-    waves = [[plane for pair in zip(even[w], odd[w]) for plane in pair] for w in range(2)]
-    waves = [[wave[0]] + [hop(plane, 4 * z) for z, plane in enumerate(wave) if z] for wave in waves]
-    quarter = targets // 16
+    half = targets // 8
+    even_come, odd_come = hop(even_sent, 1), hop(odd_sent, 2)
+    late = hop(held, 4)
+    first = [jnp.stack([even_kept[z], even_come[z]]) for z in range(half)]
+    first = [plane for z in range(half) for plane in (first[z], jnp.stack([odd_kept[z], odd_come[z]]))]
+    far_first = [hop(first[z], 4 * z) for z in range(half, 2 * half)]
+    even_last, over_y = hop_both(jnp.concatenate([even_kept[half:], even_come[half:]]), held, 2)
+    odd_last, over_x = hop_both(jnp.concatenate([odd_kept[half:], odd_come[half:]]), held, 1)
+    last = [
+        jnp.stack([come[z], come[half + z]]) for z in range(half) for come in (even_last, odd_last)
+    ]
+    near = [jnp.concatenate([first[z], last[z]]) for z in range(half)]
+    near = [near[0]] + [hop(plane, 4 * z) for z, plane in enumerate(near) if z]
+    far_last = [hop(last[z], 4 * z) for z in range(half, 2 * half)]
+    late_x, late_y = hop(late, 1), hop(late, 2)
+    pieces = {0: held, 4: late, 1: over_x, 2: over_y, 5: late_x, 6: late_y}
+    pieces[3], pieces[7] = hop(over_y, 1), hop(late_x, 2)
+    positions = [tuple(p ^ step for p in at) for step in pieces]
+    pieces = list(pieces.values())
     groups = []
-    for planes in (
-        waves[0],
-        waves[1][: 2 * quarter],
-        waves[1][2 * quarter : 3 * quarter],
-        waves[1][3 * quarter :],
-    ):
+    for planes in (near[:1] + far_first, near[1:], far_last[: half // 2], far_last[half // 2 :]):
         mine = jnp.concatenate(planes, axis=0)
         groups.append(
             [mine] + [send(mine, "row", lambda i: (i + q) % rows_axis) for q in range(1, rows_axis)]

time: 70.9 us -> 60.4 us (0.85)
  waiting for transfers between devices: 35.1 us -> 24.6 us
  local copies, waits for them, and re-layouts: 1.2 us -> 2.15 us
    ppermute x22 -> x19, waiting for transfers between devices: 35.1 us -> 24.6 us  [send(): return lax.ppermute(x, axis, [(i, partner(i)) for i in range(size)])]
    unnamed x6 -> x7, local copies, waits for them, and re-layouts: 1.07 us -> 1.99 us
    ppermute x22 -> x19, starting transfers between devices: 25.9 us -> 25.2 us  [send(): return lax.ppermute(x, axis, [(i, partner(i)) for i in range(size)])]
  transfers between devices with their start and end apart: 22 -> 19, of which waited for: 10 -> 9; matrix products, arithmetic and copies ran while one was open for 3% -> 3% of each run, Pallas kernels for 2% -> 3%
where the time goes in v7:
time: 60.4 us; the launch traced here: 60.1 us
  starting transfers between devices  25.2 us (42%)
  waiting for transfers between devices  24.6 us (41%)
  Pallas kernels  6.06 us (10%)
  local copies, waits for them, and re-layouts  2.15 us (4%)
  other arithmetic  1.79 us (3%)
    ppermute x19, starting transfers between devices, send(): return lax.ppermute(x, axis, [(i, partner(i)) for i in range(size)])  25.2 us
    ppermute x19, waiting for transfers between devices, send(): return lax.ppermute(x, axis, [(i, partner(i)) for i in range(size)])  24.6 us
    pallas_call x1, Pallas kernels, contract(): pl.pallas_call(functools.partial(contract_kernel, len(groups), len(groups...  4.33 us
    unnamed x7, local copies, waits for them, and re-layouts  1.99 us
    pallas_call x1, Pallas kernels, pack(): pl.pallas_call(pack_kernel, out_shape=[out] * 4, in_specs=[pl.BlockSpec(m...  1.48 us
  transfers between devices with their start and end apart: 19, of which 9 were waited for; matrix products, arithmetic and copies ran while one was open for 3% of the time, Pallas kernels for 3%

profile of v7, /device:TPU:0, one launch (start us, length us, event | category | flops | bytes accessed | tf_op | source)
XLA Modules:
  0.0 60.1 jit_solution(18280813271159092105)
XLA Ops:
  0.0 4.0 %collective-permute-start = (f32[1,256,128]{2,1,0:T(8,128)}, f32[1,256,128]{2,1,0:T(8,128)S(1)}, u32[]{:S(2)}, u32[]{:S(2)}) collective-permute-start(f32[1,256,128]{2,1,0:T(8,128)} %bitcast.38), channel_id=1, source_target_pairs={{0,8},{1,9},{2,10},{3,11},{4,12},{5,13},{6,14},{7,15},{8,0},{9,1},... | collective-permute-start | bytes 393224 | tf_op jit(solution)/shard_map/ppermute | solution.py:187
  4.0 0.7 %fusion.3.words_ref = s32[16]{0:T(128)S(1)} fusion(s32[16]{0:T(128)} %param.11, s32[16]{0:T(128)} %param.10, s32[16,1]{0,1:T(1,128)} %param.9), kind=kLoop, calls=%fused_computation.26 | loop fusion | flops 64 | bytes 256 | tf_op jit(solution)/shard_map/add | solution.py:57
  4.7 0.0 copy-start.1
  4.7 1.0 %copy-done.1 = f32[16,64,128]{2,1,0:T(8,128)S(1)} copy-done((f32[16,64,128]{2,1,0:T(8,128)S(1)}, f32[16,64,128]{2,1,0:T(8,128)}, u32[]{:S(2)}) %copy-start.1) | copy-done | bytes 524312
  5.8 1.5 %shard_map.64 = (f32[4,136,128]{2,1,0:T(8,128)S(1)}, f32[4,136,128]{2,1,0:T(8,128)S(1)}, f32[4,136,128]{2,1,0:T(8,128)S(1)}, f32[4,136,128]{2,1,0:T(8,128)S(1)}) custom-call(s32[16]{0:T(128)S(1)} %fusion.3.words_ref, f32[16,64,128]{2,1,0:T(8,128)S(1)} %copy-done.1), custom_call_target="tpu_custom_call" | custom-call | bytes 1572864 | tf_op jit(solution)/shard_map/pallas_call | solution.py:59
  7.3 1.6 %collective-permute-start.2 = (f32[4,136,128]{2,1,0:T(8,128)S(1)}, f32[4,136,128]{2,1,0:T(8,128)S(1)}, u32[]{:S(2)}, u32[]{:S(2)}) collective-permute-start(f32[4,136,128]{2,1,0:T(8,128)S(1)} %get-tuple-element.10), channel_id=1, source_target_pairs={{0,2},{1,3},{2,0},{3,1},{4,6},{5,7},{6,4},{7,5},{8,10},{9,11},{10,... | collective-permute-start | bytes 835592 | tf_op jit(solution)/shard_map/ppermute | solution.py:187
  8.8 1.5 %collective-permute-start.4 = (f32[4,136,128]{2,1,0:T(8,128)S(1)}, f32[4,136,128]{2,1,0:T(8,128)S(1)}, u32[]{:S(2)}, u32[]{:S(2)}) collective-permute-start(f32[4,136,128]{2,1,0:T(8,128)S(1)} %get-tuple-element.12), channel_id=1, source_target_pairs={{0,1},{1,0},{2,3},{3,2},{4,5},{5,4},{6,7},{7,6},{8,9},{9,8},{10,11... | collective-permute-start | bytes 835592 | tf_op jit(solution)/shard_map/ppermute | solution.py:187
  10.4 0.1 collective-permute-done
  10.6 0.9 %pad_maximum_fusion.5.refs_0_ = f32[2,256,128]{2,1,0:T(8,128)S(1)} fusion(f32[1,256,128]{2,1,0:T(8,128)S(1)} %collective-permute-done, f32[1,256,128]{2,1,0:T(8,128)} %bitcast.39), kind=kLoop, calls=%fused_computation.5 | loop fusion | flops 65536 | bytes 524288 | tf_op jit(solution)/shard_map/concatenate | solution.py:212
  11.5 1.5 %collective-permute-start.1 = (f32[2,256,128]{2,1,0:T(8,128)S(1)}, f32[2,256,128]{2,1,0:T(8,128)S(1)}, u32[]{:S(2)}, u32[]{:S(2)}) collective-permute-start(f32[2,256,128]{2,1,0:T(8,128)S(1)} %pad_maximum_fusion.5.refs_0_), channel_id=1, source_target_pairs={{0,4},{1,5},{2,6},{3,7},{4,0},{5,1},{6,2},{7,3},{8,12},{9,13},{10,... | collective-permute-start | bytes 786440 | tf_op jit(solution)/shard_map/ppermute | solution.py:187
  13.0 2.5 %collective-permute-done.2 = f32[4,136,128]{2,1,0:T(8,128)S(1)} collective-permute-done((f32[4,136,128]{2,1,0:T(8,128)S(1)}, f32[4,136,128]{2,1,0:T(8,128)S(1)}, u32[]{:S(2)}, u32[]{:S(2)}) %collective-permute-start.2) | collective-permute-done | bytes 278560 | tf_op jit(solution)/shard_map/ppermute | solution.py:187
  15.5 1.2 %collective-permute-done.4 = f32[4,136,128]{2,1,0:T(8,128)S(1)} collective-permute-done((f32[4,136,128]{2,1,0:T(8,128)S(1)}, f32[4,136,128]{2,1,0:T(8,128)S(1)}, u32[]{:S(2)}, u32[]{:S(2)}) %collective-permute-start.4) | collective-permute-done | bytes 278560 | tf_op jit(solution)/shard_map/ppermute | solution.py:187
  16.7 0.1 pad_maximum_fusion
  16.8 1.6 %collective-permute-start.3 = (f32[1056,128]{1,0:T(8,128)S(1)}, f32[1056,128]{1,0:T(8,128)S(1)}, u32[]{:S(2)}, u32[]{:S(2)}) collective-permute-start(f32[1056,128]{1,0:T(8,128)S(1)} %get-tuple-element.28), channel_id=1, source_target_pairs={{0,1},{1,0},{2,3},{3,2},{4,5},{5,4},{6,7},{7,6},{8,9},{9,8},{10,11... | collective-permute-start | bytes 1622024 | tf_op jit(solution)/shard_map/ppermute | solution.py:187
  18.4 1.4 %collective-permute-start.11 = (f32[2,136,128]{2,1,0:T(8,128)S(1)}, f32[2,136,128]{2,1,0:T(8,128)S(1)}, u32[]{:S(2)}, u32[]{:S(2)}) collective-permute-start(f32[2,136,128]{2,1,0:T(8,128)S(1)} %pad_maximum_fusion.7), channel_id=1, source_target_pairs={{0,12},{1,13},{2,14},{3,15},{4,8},{5,9},{6,10},{7,11},{8,4},{9,5},... | collective-permute-start | bytes 417800 | tf_op jit(solution)/shard_map/ppermute | solution.py:187
  19.8 0.5 collective-permute-start.5
  20.3 0.0 collective-permute-done.1.refs_1_
  20.3 0.5 collective-permute-start.6
  20.9 5.1 %collective-permute-start.10 = (f32[2,136,128]{2,1,0:T(8,128)S(1)}, f32[2,136,128]{2,1,0:T(8,128)S(1)}, u32[]{:S(2)}, u32[]{:S(2)}) collective-permute-start(f32[2,136,128]{2,1,0:T(8,128)S(1)} %pad_maximum_fusion.6), channel_id=1, source_target_pairs={{0,8},{1,9},{2,10},{3,11},{4,12},{5,13},{6,14},{7,15},{8,0},{9,1},... | collective-permute-start | bytes 417800 | tf_op jit(solution)/shard_map/ppermute | solution.py:187
  26.0 9.0 %collective-permute-done.6.refs_4_ = f32[2,256,128]{2,1,0:T(8,128)S(1)} collective-permute-done((f32[2,256,128]{2,1,0:T(8,128)S(1)}, f32[2,256,128]{2,1,0:T(8,128)S(1)}, u32[]{:S(2)}, u32[]{:S(2)}) %collective-permute-start.6) | collective-permute-done | bytes 262176 | tf_op jit(solution)/shard_map/ppermute | solution.py:187
  35.0 0.6 %collective-permute-start.7 = (f32[2,256,128]{2,1,0:T(8,128)S(1)}, f32[2,256,128]{2,1,0:T(8,128)S(1)}, u32[]{:S(2)}, u32[]{:S(2)}) collective-permute-start(f32[2,256,128]{2,1,0:T(8,128)S(1)} %collective-permute-done.1.refs_1_), channel_id=1, source_target_pairs={{0,2},{1,3},{2,0},{3,1},{4,6},{5,7},{6,4},{7,5},{8,10},{9,11},{10,... | collective-permute-start | bytes 786440 | tf_op jit(solution)/shard_map/ppermute | solution.py:187
  35.6 0.0 collective-permute-done.3
  35.7 1.4 %collective-permute-start.9 = (f32[2,256,128]{2,1,0:T(8,128)S(1)}, f32[2,256,128]{2,1,0:T(8,128)S(1)}, u32[]{:S(2)}, u32[]{:S(2)}) collective-permute-start(f32[2,256,128]{2,1,0:T(8,128)S(1)} %collective-permute-done.6.refs_4_), channel_id=1, source_target_pairs={{0,2},{1,3},{2,0},{3,1},{4,6},{5,7},{6,4},{7,5},{8,10},{9,11},{10,... | collective-permute-start | bytes 786440 | tf_op jit(solution)/shard_map/ppermute | solution.py:187
  37.1 0.0 collective-permute-done.5
  37.1 1.6 %collective-permute-start.13 = (f32[4,136,128]{2,1,0:T(8,128)S(1)}, f32[4,136,128]{2,1,0:T(8,128)S(1)}, u32[]{:S(2)}, u32[]{:S(2)}) collective-permute-start(f32[4,136,128]{2,1,0:T(8,128)S(1)} %pad_maximum_fusion.4), channel_id=1, source_target_pairs={{0,4},{1,5},{2,6},{3,7},{4,0},{5,1},{6,2},{7,3},{8,12},{9,13},{10,... | collective-permute-start | bytes 835592 | tf_op jit(solution)/shard_map/ppermute | solution.py:187
  38.8 0.0 collective-permute-done.10
  38.8 0.0 collective-permute-done.11
  38.8 0.1 collective-permute-start.12
  38.9 0.4 collective-permute-start.15
  39.4 4.1 %collective-permute-done.7.refs_5_ = f32[2,256,128]{2,1,0:T(8,128)S(1)} collective-permute-done((f32[2,256,128]{2,1,0:T(8,128)S(1)}, f32[2,256,128]{2,1,0:T(8,128)S(1)}, u32[]{:S(2)}, u32[]{:S(2)}) %collective-permute-start.7) | collective-permute-done | bytes 262176 | tf_op jit(solution)/shard_map/ppermute | solution.py:187
  43.5 1.3 %collective-permute-start.17 = (f32[2,136,128]{2,1,0:T(8,128)S(1)}, f32[2,136,128]{2,1,0:T(8,128)S(1)}, u32[]{:S(2)}, u32[]{:S(2)}) collective-permute-start(f32[2,136,128]{2,1,0:T(8,128)S(1)} %pad_maximum_fusion.9), channel_id=1, source_target_pairs={{0,12},{1,13},{2,14},{3,15},{4,8},{5,9},{6,10},{7,11},{8,4},{9,5},... | collective-permute-start | bytes 417800 | tf_op jit(solution)/shard_map/ppermute | solution.py:187
  44.8 0.9 %collective-permute-done.13.refs_2_ = f32[4,136,128]{2,1,0:T(8,128)S(1)} collective-permute-done((f32[4,136,128]{2,1,0:T(8,128)S(1)}, f32[4,136,128]{2,1,0:T(8,128)S(1)}, u32[]{:S(2)}, u32[]{:S(2)}) %collective-permute-start.13) | collective-permute-done | bytes 278560 | tf_op jit(solution)/shard_map/ppermute | solution.py:187
  45.7 0.0 collective-permute-start.14
  45.7 0.6 collective-permute-done.9.refs_7_
  46.3 1.5 %collective-permute-start.8 = (f32[2,256,128]{2,1,0:T(8,128)S(1)}, f32[2,256,128]{2,1,0:T(8,128)S(1)}, u32[]{:S(2)}, u32[]{:S(2)}) collective-permute-start(f32[2,256,128]{2,1,0:T(8,128)S(1)} %bitcast.33), channel_id=1, source_target_pairs={{0,1},{1,0},{2,3},{3,2},{4,5},{5,4},{6,7},{7,6},{8,9},{9,8},{10,11... | collective-permute-start | bytes 786440 | tf_op jit(solution)/shard_map/ppermute | solution.py:187
  47.8 4.4 %collective-permute-done.15.refs_4_ = f32[2,136,128]{2,1,0:T(8,128)S(1)} collective-permute-done((f32[2,136,128]{2,1,0:T(8,128)S(1)}, f32[2,136,128]{2,1,0:T(8,128)S(1)}, u32[]{:S(2)}, u32[]{:S(2)}) %collective-permute-start.15) | collective-permute-done | bytes 139296 | tf_op jit(solution)/shard_map/ppermute | solution.py:187
  52.2 0.0 collective-permute-start.16
  52.2 0.0 collective-permute-done.17.refs_6_
  52.2 0.5 collective-permute-start.18
  52.7 1.8 %collective-permute-done.8.refs_6_ = f32[2,256,128]{2,1,0:T(8,128)S(1)} collective-permute-done((f32[2,256,128]{2,1,0:T(8,128)S(1)}, f32[2,256,128]{2,1,0:T(8,128)S(1)}, u32[]{:S(2)}, u32[]{:S(2)}) %collective-permute-start.8) | collective-permute-done | bytes 262176 | tf_op jit(solution)/shard_map/ppermute | solution.py:187
  54.5 0.0 copy-start
  54.5 0.3 shard_map.65.split_ref
  54.8 0.0 collective-permute-done.16.refs_5_
  54.8 0.0 collective-permute-done.18.refs_7_
  54.8 0.0 collective-permute-done.14.refs_3_
  54.8 0.0 collective-permute-done.12.refs_1_
  54.8 0.9 %copy-done = f32[256,1024]{1,0:T(8,128)S(1)} copy-done((f32[256,1024]{1,0:T(8,128)S(1)}, f32[256,1024]{1,0:T(8,128)}, u32[]{:S(2)}) %copy-start) | copy-done | bytes 1048600
  55.7 4.3 %shard_map.66 = f32[256,1024]{1,0:T(8,128)} custom-call(bf16[16,256,256]{2,1,0:T(8,128)(2,1)S(1)} %shard_map.65.split_ref, f32[8,136,128]{2,1,0:T(8,128)S(1)} %constant_dynamic-update-slice_fusion.refs_0_, f32[8,136,128]{2,1,0:T(8,128)S(1)} %collective-permute-done.12.refs_1_, f32[4,136,128]{2,1,0:T(8,128)S(1)} %collective-permute-done.13.refs_2_, ...), custom_call_target="tpu_custom_call" | custom-call | tf_op jit(solution)/shard_map/pallas_call | solution.py:172
  (23 shorter events, 0.3 us)
Async XLA Ops:
  0.0 10.5 %collective-permute-start = (f32[1,256,128]{2,1,0:T(8,128)}, f32[1,256,128]{2,1,0:T(8,128)S(1)}, u32[]{:S(2)}, u32[]{:S(2)}) collective-permute-start(f32[1,256,128]{2,1,0:T(8,128)} %bitcast.38), channel_id=1, source_target_pairs={{0,8},{1,9},{2,10},{3,11},{4,12},{5,13},{6,14},{7,15},{8,0},{9,1},... | collective-permute-start | bytes 393224 | tf_op jit(solution)/shard_map/ppermute | solution.py:187
  4.7 1.0 %copy-start.1 = (f32[16,64,128]{2,1,0:T(8,128)S(1)}, f32[16,64,128]{2,1,0:T(8,128)}, u32[]{:S(2)}) copy-start(f32[16,64,128]{2,1,0:T(8,128)} %tiles_ref.1) | copy-start | bytes 1572868
  7.3 8.2 %collective-permute-start.2 = (f32[4,136,128]{2,1,0:T(8,128)S(1)}, f32[4,136,128]{2,1,0:T(8,128)S(1)}, u32[]{:S(2)}, u32[]{:S(2)}) collective-permute-start(f32[4,136,128]{2,1,0:T(8,128)S(1)} %get-tuple-element.10), channel_id=1, source_target_pairs={{0,2},{1,3},{2,0},{3,1},{4,6},{5,7},{6,4},{7,5},{8,10},{9,11},{10,... | collective-permute-start | bytes 835592 | tf_op jit(solution)/shard_map/ppermute | solution.py:187
  8.8 7.8 %collective-permute-start.4 = (f32[4,136,128]{2,1,0:T(8,128)S(1)}, f32[4,136,128]{2,1,0:T(8,128)S(1)}, u32[]{:S(2)}, u32[]{:S(2)}) collective-permute-start(f32[4,136,128]{2,1,0:T(8,128)S(1)} %get-tuple-element.12), channel_id=1, source_target_pairs={{0,1},{1,0},{2,3},{3,2},{4,5},{5,4},{6,7},{7,6},{8,9},{9,8},{10,11... | collective-permute-start | bytes 835592 | tf_op jit(solution)/shard_map/ppermute | solution.py:187
  11.5 8.8 %collective-permute-start.1 = (f32[2,256,128]{2,1,0:T(8,128)S(1)}, f32[2,256,128]{2,1,0:T(8,128)S(1)}, u32[]{:S(2)}, u32[]{:S(2)}) collective-permute-start(f32[2,256,128]{2,1,0:T(8,128)S(1)} %pad_maximum_fusion.5.refs_0_), channel_id=1, source_target_pairs={{0,4},{1,5},{2,6},{3,7},{4,0},{5,1},{6,2},{7,3},{8,12},{9,13},{10,... | collective-permute-start | bytes 786440 | tf_op jit(solution)/shard_map/ppermute | solution.py:187
  16.8 18.8 %collective-permute-start.3 = (f32[1056,128]{1,0:T(8,128)S(1)}, f32[1056,128]{1,0:T(8,128)S(1)}, u32[]{:S(2)}, u32[]{:S(2)}) collective-permute-start(f32[1056,128]{1,0:T(8,128)S(1)} %get-tuple-element.28), channel_id=1, source_target_pairs={{0,1},{1,0},{2,3},{3,2},{4,5},{5,4},{6,7},{7,6},{8,9},{9,8},{10,11... | collective-permute-start | bytes 1622024 | tf_op jit(solution)/shard_map/ppermute | solution.py:187
  18.4 20.4 %collective-permute-start.11 = (f32[2,136,128]{2,1,0:T(8,128)S(1)}, f32[2,136,128]{2,1,0:T(8,128)S(1)}, u32[]{:S(2)}, u32[]{:S(2)}) collective-permute-start(f32[2,136,128]{2,1,0:T(8,128)S(1)} %pad_maximum_fusion.7), channel_id=1, source_target_pairs={{0,12},{1,13},{2,14},{3,15},{4,8},{5,9},{6,10},{7,11},{8,4},{9,5},... | collective-permute-start | bytes 417800 | tf_op jit(solution)/shard_map/ppermute | solution.py:187
  19.8 17.3 %collective-permute-start.5 = (f32[1056,128]{1,0:T(8,128)S(1)}, f32[1056,128]{1,0:T(8,128)S(1)}, u32[]{:S(2)}, u32[]{:S(2)}) collective-permute-start(f32[1056,128]{1,0:T(8,128)S(1)} %get-tuple-element.27), channel_id=1, source_target_pairs={{0,2},{1,3},{2,0},{3,1},{4,6},{5,7},{6,4},{7,5},{8,10},{9,11},{10,... | collective-permute-start | bytes 1622024 | tf_op jit(solution)/shard_map/ppermute | solution.py:187
  20.3 14.7 %collective-permute-start.6 = (f32[2,256,128]{2,1,0:T(8,128)S(1)}, f32[2,256,128]{2,1,0:T(8,128)S(1)}, u32[]{:S(2)}, u32[]{:S(2)}) collective-permute-start(f32[2,256,128]{2,1,0:T(8,128)S(1)} %collective-permute-done.1.refs_1_), channel_id=1, source_target_pairs={{0,1},{1,0},{2,3},{3,2},{4,5},{5,4},{6,7},{7,6},{8,9},{9,8},{10,11... | collective-permute-start | bytes 786440 | tf_op jit(solution)/shard_map/ppermute | solution.py:187
  20.9 17.9 %collective-permute-start.10 = (f32[2,136,128]{2,1,0:T(8,128)S(1)}, f32[2,136,128]{2,1,0:T(8,128)S(1)}, u32[]{:S(2)}, u32[]{:S(2)}) collective-permute-start(f32[2,136,128]{2,1,0:T(8,128)S(1)} %pad_maximum_fusion.6), channel_id=1, source_target_pairs={{0,8},{1,9},{2,10},{3,11},{4,12},{5,13},{6,14},{7,15},{8,0},{9,1},... | collective-permute-start | bytes 417800 | tf_op jit(solution)/shard_map/ppermute | solution.py:187
  35.0 8.4 %collective-permute-start.7 = (f32[2,256,128]{2,1,0:T(8,128)S(1)}, f32[2,256,128]{2,1,0:T(8,128)S(1)}, u32[]{:S(2)}, u32[]{:S(2)}) collective-permute-start(f32[2,256,128]{2,1,0:T(8,128)S(1)} %collective-permute-done.1.refs_1_), channel_id=1, source_target_pairs={{0,2},{1,3},{2,0},{3,1},{4,6},{5,7},{6,4},{7,5},{8,10},{9,11},{10,... | collective-permute-start | bytes 786440 | tf_op jit(solution)/shard_map/ppermute | solution.py:187
  35.7 10.6 %collective-permute-start.9 = (f32[2,256,128]{2,1,0:T(8,128)S(1)}, f32[2,256,128]{2,1,0:T(8,128)S(1)}, u32[]{:S(2)}, u32[]{:S(2)}) collective-permute-start(f32[2,256,128]{2,1,0:T(8,128)S(1)} %collective-permute-done.6.refs_4_), channel_id=1, source_target_pairs={{0,2},{1,3},{2,0},{3,1},{4,6},{5,7},{6,4},{7,5},{8,10},{9,11},{10,... | collective-permute-start | bytes 786440 | tf_op jit(solution)/shard_map/ppermute | solution.py:187
  37.1 8.6 %collective-permute-start.13 = (f32[4,136,128]{2,1,0:T(8,128)S(1)}, f32[4,136,128]{2,1,0:T(8,128)S(1)}, u32[]{:S(2)}, u32[]{:S(2)}) collective-permute-start(f32[4,136,128]{2,1,0:T(8,128)S(1)} %pad_maximum_fusion.4), channel_id=1, source_target_pairs={{0,4},{1,5},{2,6},{3,7},{4,0},{5,1},{6,2},{7,3},{8,12},{9,13},{10,... | collective-permute-start | bytes 835592 | tf_op jit(solution)/shard_map/ppermute | solution.py:187
  38.8 16.0 %collective-permute-start.12 = (f32[8,136,128]{2,1,0:T(8,128)S(1)}, f32[8,136,128]{2,1,0:T(8,128)S(1)}, u32[]{:S(2)}, u32[]{:S(2)}) collective-permute-start(f32[8,136,128]{2,1,0:T(8,128)S(1)} %constant_dynamic-update-slice_fusion.refs_0_), channel_id=1, source_target_pairs={{0,16},{16,0},{1,17},{17,1},{2,18},{18,2},{3,19},{19,3},{4,20},{20... | collective-permute-start | bytes 1671176 | tf_op jit(solution)/shard_map/ppermute | solution.py:187
  38.9 13.2 %collective-permute-start.15 = (f32[2,136,128]{2,1,0:T(8,128)S(1)}, f32[2,136,128]{2,1,0:T(8,128)S(1)}, u32[]{:S(2)}, u32[]{:S(2)}) collective-permute-start(f32[2,136,128]{2,1,0:T(8,128)S(1)} %pad_maximum_fusion.8), channel_id=1, source_target_pairs={{0,8},{1,9},{2,10},{3,11},{4,12},{5,13},{6,14},{7,15},{8,0},{9,1},... | collective-permute-start | bytes 417800 | tf_op jit(solution)/shard_map/ppermute | solution.py:187
  43.5 8.7 %collective-permute-start.17 = (f32[2,136,128]{2,1,0:T(8,128)S(1)}, f32[2,136,128]{2,1,0:T(8,128)S(1)}, u32[]{:S(2)}, u32[]{:S(2)}) collective-permute-start(f32[2,136,128]{2,1,0:T(8,128)S(1)} %pad_maximum_fusion.9), channel_id=1, source_target_pairs={{0,12},{1,13},{2,14},{3,15},{4,8},{5,9},{6,10},{7,11},{8,4},{9,5},... | collective-permute-start | bytes 417800 | tf_op jit(solution)/shard_map/ppermute | solution.py:187
  45.7 9.1 %collective-permute-start.14 = (f32[4,136,128]{2,1,0:T(8,128)S(1)}, f32[4,136,128]{2,1,0:T(8,128)S(1)}, u32[]{:S(2)}, u32[]{:S(2)}) collective-permute-start(f32[4,136,128]{2,1,0:T(8,128)S(1)} %collective-permute-done.13.refs_2_), channel_id=1, source_target_pairs={{0,16},{16,0},{1,17},{17,1},{2,18},{18,2},{3,19},{19,3},{4,20},{20... | collective-permute-start | bytes 835592 | tf_op jit(solution)/shard_map/ppermute | solution.py:187
  46.3 8.2 %collective-permute-start.8 = (f32[2,256,128]{2,1,0:T(8,128)S(1)}, f32[2,256,128]{2,1,0:T(8,128)S(1)}, u32[]{:S(2)}, u32[]{:S(2)}) collective-permute-start(f32[2,256,128]{2,1,0:T(8,128)S(1)} %bitcast.33), channel_id=1, source_target_pairs={{0,1},{1,0},{2,3},{3,2},{4,5},{5,4},{6,7},{7,6},{8,9},{9,8},{10,11... | collective-permute-start | bytes 786440 | tf_op jit(solution)/shard_map/ppermute | solution.py:187
  52.2 2.6 %collective-permute-start.16 = (f32[2,136,128]{2,1,0:T(8,128)S(1)}, f32[2,136,128]{2,1,0:T(8,128)S(1)}, u32[]{:S(2)}, u32[]{:S(2)}) collective-permute-start(f32[2,136,128]{2,1,0:T(8,128)S(1)} %collective-permute-done.15.refs_4_), channel_id=1, source_target_pairs={{0,16},{16,0},{1,17},{17,1},{2,18},{18,2},{3,19},{19,3},{4,20},{20... | collective-permute-start | bytes 417800 | tf_op jit(solution)/shard_map/ppermute | solution.py:187
  52.2 2.6 %collective-permute-start.18 = (f32[2,136,128]{2,1,0:T(8,128)S(1)}, f32[2,136,128]{2,1,0:T(8,128)S(1)}, u32[]{:S(2)}, u32[]{:S(2)}) collective-permute-start(f32[2,136,128]{2,1,0:T(8,128)S(1)} %collective-permute-done.17.refs_6_), channel_id=1, source_target_pairs={{0,16},{16,0},{1,17},{17,1},{2,18},{18,2},{3,19},{19,3},{4,20},{20... | collective-permute-start | bytes 417800 | tf_op jit(solution)/shard_map/ppermute | solution.py:187
  54.5 1.2 %copy-start = (f32[256,1024]{1,0:T(8,128)S(1)}, f32[256,1024]{1,0:T(8,128)}, u32[]{:S(2)}) copy-start(f32[256,1024]{1,0:T(8,128)} %refs_8_.1) | copy-start | bytes 3145732

commit v8 on v7

--- a/solution.py
+++ b/solution.py
@@ -185,10 +185,6 @@
 def send(x, axis, partner):
     size = lax.axis_size(axis)
     return lax.ppermute(x, axis, [(i, partner(i)) for i in range(size)])
-
-
-def hop(x, step):
-    return send(x, "bulk", lambda i: i ^ step)
 
 
 def hop(x, step):
@@ -228,13 +224,17 @@
     near = [jnp.concatenate([first[z], last[z]]) for z in range(half)]
     near = [near[0]] + [hop(plane, 4 * z) for z, plane in enumerate(near) if z]
     far_last = [hop(last[z], 4 * z) for z in range(half, 2 * half)]
-    late_x, late_y = hop(late, 1), hop(late, 2)
-    pieces = {0: held, 4: late, 1: over_x, 2: over_y, 5: late_x, 6: late_y}
-    pieces[3], pieces[7] = hop(over_y, 1), hop(late_x, 2)
-    positions = [tuple(p ^ step for p in at) for step in pieces]
-    pieces = list(pieces.values())
+    cut = len(at) // 2
+    come = hop(jnp.concatenate([late, over_y[:cut]]), 1)
+    late_x, diagonal_x = come[: len(at)], come[len(at) :]
+    come = hop(jnp.concatenate([late, over_x[cut:]]), 2)
+    late_y, diagonal_y = come[: len(at)], come[len(at) :]
+    pieces = [held, late, over_x, over_y, late_x, late_y, diagonal_x, diagonal_y]
+    pieces += [hop(late_y[:cut], 1), hop(late_x[cut:], 2)]
+    positions = [tuple(p ^ step for p in at) for step in (0, 4, 1, 2, 5, 6)]
+    positions += [tuple(p ^ step for p in part) for step in (3, 7) for part in (at[:cut], at[cut:])]
     groups = []
-    for planes in (near[:1] + far_first, near[1:], far_last[: half // 2], far_last[half // 2 :]):
+    for planes in (near + far_first, far_last):
         mine = jnp.concatenate(planes, axis=0)
         groups.append(
             [mine] + [send(mine, "row", lambda i: (i + q) % rows_axis) for q in range(1, rows_axis)]

time: 60.4 us -> 68 us (1.13)
  waiting for transfers between devices: 24.6 us -> 35.5 us
  starting transfers between devices: 25.2 us -> 21.9 us
    ppermute x19 -> x17, waiting for transfers between devices: 24.6 us -> 35.5 us  [send(): return lax.ppermute(x, axis, [(i, partner(i)) for i in range(size)])]
    ppermute x19 -> x17, starting transfers between devices: 25.2 us -> 21.9 us  [send(): return lax.ppermute(x, axis, [(i, partner(i)) for i in range(size)])]
    unnamed x7 -> x9, local copies, waits for them, and re-layouts: 1.99 us -> 2.04 us
  transfers between devices with their start and end apart: 19 -> 17, of which waited for: 9 -> 10; matrix products, arithmetic and copies ran while one was open for 3% -> 3% of each run, Pallas kernels for 3% -> 3%
where the time goes in v8:
time: 68 us; the launch traced here: 67.8 us
  waiting for transfers between devices  35.5 us (52%)
  starting transfers between devices  21.9 us (32%)
  Pallas kernels  5.89 us (9%)
  local copies, waits for them, and re-layouts  2.31 us (3%)
  other arithmetic  1.87 us (3%)
    ppermute x17, waiting for transfers between devices, send(): return lax.ppermute(x, axis, [(i, partner(i)) for i in range(size)])  35.5 us
    ppermute x17, starting transfers between devices, send(): return lax.ppermute(x, axis, [(i, partner(i)) for i in range(size)])  21.9 us
    pallas_call x1, Pallas kernels, contract(): pl.pallas_call(functools.partial(contract_kernel, len(groups), len(groups...  4.15 us
    unnamed x9, local copies, waits for them, and re-layouts  2.04 us
    pallas_call x1, Pallas kernels, pack(): pl.pallas_call(pack_kernel, out_shape=[out] * 4, in_specs=[pl.BlockSpec(m...  1.48 us
  transfers between devices with their start and end apart: 17, of which 10 were waited for; matrix products, arithmetic and copies ran while one was open for 3% of the time, Pallas kernels for 3%

profile of v8, /device:TPU:0, one launch (start us, length us, event | category | flops | bytes accessed | tf_op | source)
XLA Modules:
  0.0 67.8 jit_solution(17289108100035920342)
XLA Ops:
  0.0 4.0 %collective-permute-start = (f32[1,256,128]{2,1,0:T(8,128)}, f32[1,256,128]{2,1,0:T(8,128)S(1)}, u32[]{:S(2)}, u32[]{:S(2)}) collective-permute-start(f32[1,256,128]{2,1,0:T(8,128)} %bitcast.41), channel_id=1, source_target_pairs={{0,8},{1,9},{2,10},{3,11},{4,12},{5,13},{6,14},{7,15},{8,0},{9,1},... | collective-permute-start | bytes 393224 | tf_op jit(solution)/shard_map/ppermute | solution.py:187
  4.0 0.7 %fusion.3.words_ref = s32[16]{0:T(128)S(1)} fusion(s32[16]{0:T(128)} %param.11, s32[16]{0:T(128)} %param.10, s32[16,1]{0,1:T(1,128)} %param.9), kind=kLoop, calls=%fused_computation.33 | loop fusion | flops 64 | bytes 256 | tf_op jit(solution)/shard_map/add | solution.py:57
  4.7 0.0 copy-start.1
  4.7 1.0 %copy-done.1 = f32[16,64,128]{2,1,0:T(8,128)S(1)} copy-done((f32[16,64,128]{2,1,0:T(8,128)S(1)}, f32[16,64,128]{2,1,0:T(8,128)}, u32[]{:S(2)}) %copy-start.1) | copy-done | bytes 524312
  5.8 1.5 %shard_map.64 = (f32[4,136,128]{2,1,0:T(8,128)S(1)}, f32[4,136,128]{2,1,0:T(8,128)S(1)}, f32[4,136,128]{2,1,0:T(8,128)S(1)}, f32[4,136,128]{2,1,0:T(8,128)S(1)}) custom-call(s32[16]{0:T(128)S(1)} %fusion.3.words_ref, f32[16,64,128]{2,1,0:T(8,128)S(1)} %copy-done.1), custom_call_target="tpu_custom_call" | custom-call | bytes 1572864 | tf_op jit(solution)/shard_map/pallas_call | solution.py:59
  7.3 1.6 %collective-permute-start.2 = (f32[4,136,128]{2,1,0:T(8,128)S(1)}, f32[4,136,128]{2,1,0:T(8,128)S(1)}, u32[]{:S(2)}, u32[]{:S(2)}) collective-permute-start(f32[4,136,128]{2,1,0:T(8,128)S(1)} %get-tuple-element.10), channel_id=1, source_target_pairs={{0,2},{1,3},{2,0},{3,1},{4,6},{5,7},{6,4},{7,5},{8,10},{9,11},{10,... | collective-permute-start | bytes 835592 | tf_op jit(solution)/shard_map/ppermute | solution.py:187
  8.8 1.5 %collective-permute-start.4 = (f32[4,136,128]{2,1,0:T(8,128)S(1)}, f32[4,136,128]{2,1,0:T(8,128)S(1)}, u32[]{:S(2)}, u32[]{:S(2)}) collective-permute-start(f32[4,136,128]{2,1,0:T(8,128)S(1)} %get-tuple-element.12), channel_id=1, source_target_pairs={{0,1},{1,0},{2,3},{3,2},{4,5},{5,4},{6,7},{7,6},{8,9},{9,8},{10,11... | collective-permute-start | bytes 835592 | tf_op jit(solution)/shard_map/ppermute | solution.py:187
  10.4 0.1 collective-permute-done
  10.6 0.9 %pad_maximum_fusion.7.refs_0_ = f32[2,256,128]{2,1,0:T(8,128)S(1)} fusion(f32[1,256,128]{2,1,0:T(8,128)S(1)} %collective-permute-done, f32[1,256,128]{2,1,0:T(8,128)} %bitcast.42), kind=kLoop, calls=%fused_computation.7 | loop fusion | flops 65536 | bytes 524288 | tf_op jit(solution)/shard_map/concatenate | solution.py:208
  11.5 1.5 %collective-permute-start.1 = (f32[2,256,128]{2,1,0:T(8,128)S(1)}, f32[2,256,128]{2,1,0:T(8,128)S(1)}, u32[]{:S(2)}, u32[]{:S(2)}) collective-permute-start(f32[2,256,128]{2,1,0:T(8,128)S(1)} %pad_maximum_fusion.7.refs_0_), channel_id=1, source_target_pairs={{0,4},{1,5},{2,6},{3,7},{4,0},{5,1},{6,2},{7,3},{8,12},{9,13},{10,... | collective-permute-start | bytes 786440 | tf_op jit(solution)/shard_map/ppermute | solution.py:187
  13.0 2.5 %collective-permute-done.2 = f32[4,136,128]{2,1,0:T(8,128)S(1)} collective-permute-done((f32[4,136,128]{2,1,0:T(8,128)S(1)}, f32[4,136,128]{2,1,0:T(8,128)S(1)}, u32[]{:S(2)}, u32[]{:S(2)}) %collective-permute-start.2) | collective-permute-done | bytes 278560 | tf_op jit(solution)/shard_map/ppermute | solution.py:187
  15.5 1.2 %collective-permute-done.4 = f32[4,136,128]{2,1,0:T(8,128)S(1)} collective-permute-done((f32[4,136,128]{2,1,0:T(8,128)S(1)}, f32[4,136,128]{2,1,0:T(8,128)S(1)}, u32[]{:S(2)}, u32[]{:S(2)}) %collective-permute-start.4) | collective-permute-done | bytes 278560 | tf_op jit(solution)/shard_map/ppermute | solution.py:187
  16.7 0.1 pad_maximum_fusion
  16.8 0.6 collective-permute-start.5
  17.4 1.4 %collective-permute-start.12 = (f32[2,136,128]{2,1,0:T(8,128)S(1)}, f32[2,136,128]{2,1,0:T(8,128)S(1)}, u32[]{:S(2)}, u32[]{:S(2)}) collective-permute-start(f32[2,136,128]{2,1,0:T(8,128)S(1)} %pad_maximum_fusion.9), channel_id=1, source_target_pairs={{0,12},{1,13},{2,14},{3,15},{4,8},{5,9},{6,10},{7,11},{8,4},{9,5},... | collective-permute-start | bytes 417800 | tf_op jit(solution)/shard_map/ppermute | solution.py:187
  18.8 1.5 %collective-permute-start.3 = (f32[1056,128]{1,0:T(8,128)S(1)}, f32[1056,128]{1,0:T(8,128)S(1)}, u32[]{:S(2)}, u32[]{:S(2)}) collective-permute-start(f32[1056,128]{1,0:T(8,128)S(1)} %get-tuple-element.34), channel_id=1, source_target_pairs={{0,1},{1,0},{2,3},{3,2},{4,5},{5,4},{6,7},{7,6},{8,9},{9,8},{10,11... | collective-permute-start | bytes 1622024 | tf_op jit(solution)/shard_map/ppermute | solution.py:187
  20.3 1.8 %collective-permute-start.11 = (f32[2,136,128]{2,1,0:T(8,128)S(1)}, f32[2,136,128]{2,1,0:T(8,128)S(1)}, u32[]{:S(2)}, u32[]{:S(2)}) collective-permute-start(f32[2,136,128]{2,1,0:T(8,128)S(1)} %pad_maximum_fusion.8), channel_id=1, source_target_pairs={{0,8},{1,9},{2,10},{3,11},{4,12},{5,13},{6,14},{7,15},{8,0},{9,1},... | collective-permute-start | bytes 417800 | tf_op jit(solution)/shard_map/ppermute | solution.py:187
  22.1 7.3 %collective-permute-done.5 = f32[1056,128]{1,0:T(8,128)S(1)} collective-permute-done((f32[1056,128]{1,0:T(8,128)S(1)}, f32[1056,128]{1,0:T(8,128)S(1)}, u32[]{:S(2)}, u32[]{:S(2)}) %collective-permute-start.5) | collective-permute-done | bytes 540704 | tf_op jit(solution)/shard_map/ppermute | solution.py:187
  29.4 0.5 collective-permute-start.14
  29.9 1.0 %collective-permute-done.3 = f32[1056,128]{1,0:T(8,128)S(1)} collective-permute-done((f32[1056,128]{1,0:T(8,128)S(1)}, f32[1056,128]{1,0:T(8,128)S(1)}, u32[]{:S(2)}, u32[]{:S(2)}) %collective-permute-start.3) | collective-permute-done | bytes 540704 | tf_op jit(solution)/shard_map/ppermute | solution.py:187
  31.0 0.7 collective-permute-start.10
  31.7 0.0 collective-permute-done.1.refs_1_
  31.7 2.6 %collective-permute-start.15 = (f32[2,136,128]{2,1,0:T(8,128)S(1)}, f32[2,136,128]{2,1,0:T(8,128)S(1)}, u32[]{:S(2)}, u32[]{:S(2)}) collective-permute-start(f32[2,136,128]{2,1,0:T(8,128)S(1)} %pad_maximum_fusion.11), channel_id=1, source_target_pairs={{0,12},{1,13},{2,14},{3,15},{4,8},{5,9},{6,10},{7,11},{8,4},{9,5},... | collective-permute-start | bytes 417800 | tf_op jit(solution)/shard_map/ppermute | solution.py:187
  34.3 0.1 pad_maximum_fusion.2
  34.4 9.2 %collective-permute-done.10 = f32[4,136,128]{2,1,0:T(8,128)S(1)} collective-permute-done((f32[4,136,128]{2,1,0:T(8,128)S(1)}, f32[4,136,128]{2,1,0:T(8,128)S(1)}, u32[]{:S(2)}, u32[]{:S(2)}) %collective-permute-start.10) | collective-permute-done | bytes 278560 | tf_op jit(solution)/shard_map/ppermute | solution.py:187
  43.6 1.6 %collective-permute-start.7 = (f32[3,256,128]{2,1,0:T(8,128)S(1)}, f32[3,256,128]{2,1,0:T(8,128)S(1)}, u32[]{:S(2)}, u32[]{:S(2)}) collective-permute-start(f32[3,256,128]{2,1,0:T(8,128)S(1)} %get-tuple-element.31), channel_id=1, source_target_pairs={{0,2},{1,3},{2,0},{3,1},{4,6},{5,7},{6,4},{7,5},{8,10},{9,11},{10,... | collective-permute-start | bytes 1179656 | tf_op jit(solution)/shard_map/ppermute | solution.py:187
  45.3 0.0 collective-permute-done.11
  45.3 0.0 collective-permute-done.12
  45.3 0.1 collective-permute-start.13
  45.4 1.0 %collective-permute-start.6 = (f32[3,256,128]{2,1,0:T(8,128)S(1)}, f32[3,256,128]{2,1,0:T(8,128)S(1)}, u32[]{:S(2)}, u32[]{:S(2)}) collective-permute-start(f32[3,256,128]{2,1,0:T(8,128)S(1)} %get-tuple-element.32), channel_id=1, source_target_pairs={{0,1},{1,0},{2,3},{3,2},{4,5},{5,4},{6,7},{7,6},{8,9},{9,8},{10,11... | collective-permute-start | bytes 1179656 | tf_op jit(solution)/shard_map/ppermute | solution.py:187
  46.4 0.0 collective-permute-done.14
  46.4 0.0 collective-permute-done.15
  46.4 0.2 collective-permute-start.16
  46.6 5.0 %collective-permute-done.7 = f32[3,256,128]{2,1,0:T(8,128)S(1)} collective-permute-done((f32[3,256,128]{2,1,0:T(8,128)S(1)}, f32[3,256,128]{2,1,0:T(8,128)S(1)}, u32[]{:S(2)}, u32[]{:S(2)}) %collective-permute-start.7) | collective-permute-done | bytes 393248 | tf_op jit(solution)/shard_map/ppermute | solution.py:187
  51.6 1.0 %collective-permute-start.8 = (f32[1,256,128]{2,1,0:T(8,128)S(1)}, f32[1,256,128]{2,1,0:T(8,128)S(1)}, u32[]{:S(2)}, u32[]{:S(2)}) collective-permute-start(f32[1,256,128]{2,1,0:T(8,128)S(1)} %get-tuple-element.21), channel_id=1, source_target_pairs={{0,1},{1,0},{2,3},{3,2},{4,5},{5,4},{6,7},{7,6},{8,9},{9,8},{10,11... | collective-permute-start | bytes 393224 | tf_op jit(solution)/shard_map/ppermute | solution.py:187
  52.6 4.8 %collective-permute-done.6 = f32[3,256,128]{2,1,0:T(8,128)S(1)} collective-permute-done((f32[3,256,128]{2,1,0:T(8,128)S(1)}, f32[3,256,128]{2,1,0:T(8,128)S(1)}, u32[]{:S(2)}, u32[]{:S(2)}) %collective-permute-start.6) | collective-permute-done | bytes 393248 | tf_op jit(solution)/shard_map/ppermute | solution.py:187
  57.4 0.5 collective-permute-start.9
  58.0 1.8 %collective-permute-done.8.refs_8_ = f32[1,256,128]{2,1,0:T(8,128)S(1)} collective-permute-done((f32[1,256,128]{2,1,0:T(8,128)S(1)}, f32[1,256,128]{2,1,0:T(8,128)S(1)}, u32[]{:S(2)}, u32[]{:S(2)}) %collective-permute-start.8) | collective-permute-done | bytes 131104 | tf_op jit(solution)/shard_map/ppermute | solution.py:187
  59.7 2.7 %collective-permute-done.9.refs_9_ = f32[1,256,128]{2,1,0:T(8,128)S(1)} collective-permute-done((f32[1,256,128]{2,1,0:T(8,128)S(1)}, f32[1,256,128]{2,1,0:T(8,128)S(1)}, u32[]{:S(2)}, u32[]{:S(2)}) %collective-permute-start.9) | collective-permute-done | bytes 131104 | tf_op jit(solution)/shard_map/ppermute | solution.py:187
  62.4 0.0 copy-start
  62.4 0.3 shard_map.65.split_ref
  62.7 0.0 collective-permute-done.16.refs_3_
  62.7 0.0 collective-permute-done.13.refs_1_
  62.7 0.9 %copy-done = f32[256,1024]{1,0:T(8,128)S(1)} copy-done((f32[256,1024]{1,0:T(8,128)S(1)}, f32[256,1024]{1,0:T(8,128)}, u32[]{:S(2)}) %copy-start) | copy-done | bytes 1048600
  63.7 4.2 %shard_map.66 = f32[256,1024]{1,0:T(8,128)} custom-call(bf16[16,256,256]{2,1,0:T(8,128)(2,1)S(1)} %shard_map.65.split_ref, f32[12,136,128]{2,1,0:T(8,128)S(1)} %constant_dynamic-update-slice_fusion.refs_0_, f32[12,136,128]{2,1,0:T(8,128)S(1)} %collective-permute-done.13.refs_1_, f32[4,136,128]{2,1,0:T(8,128)S(1)} %constant_dynamic-update-slice_fusion.3.refs_2_, ...), custom_call_target="tpu_custom_call" | custom-call | tf_op jit(solution)/shard_map/pallas_call | solution.py:172
  (32 shorter events, 0.5 us)
Async XLA Ops:
  0.0 10.5 %collective-permute-start = (f32[1,256,128]{2,1,0:T(8,128)}, f32[1,256,128]{2,1,0:T(8,128)S(1)}, u32[]{:S(2)}, u32[]{:S(2)}) collective-permute-start(f32[1,256,128]{2,1,0:T(8,128)} %bitcast.41), channel_id=1, source_target_pairs={{0,8},{1,9},{2,10},{3,11},{4,12},{5,13},{6,14},{7,15},{8,0},{9,1},... | collective-permute-start | bytes 393224 | tf_op jit(solution)/shard_map/ppermute | solution.py:187
  4.7 1.0 %copy-start.1 = (f32[16,64,128]{2,1,0:T(8,128)S(1)}, f32[16,64,128]{2,1,0:T(8,128)}, u32[]{:S(2)}) copy-start(f32[16,64,128]{2,1,0:T(8,128)} %tiles_ref.1) | copy-start | bytes 1572868
  7.3 8.2 %collective-permute-start.2 = (f32[4,136,128]{2,1,0:T(8,128)S(1)}, f32[4,136,128]{2,1,0:T(8,128)S(1)}, u32[]{:S(2)}, u32[]{:S(2)}) collective-permute-start(f32[4,136,128]{2,1,0:T(8,128)S(1)} %get-tuple-element.10), channel_id=1, source_target_pairs={{0,2},{1,3},{2,0},{3,1},{4,6},{5,7},{6,4},{7,5},{8,10},{9,11},{10,... | collective-permute-start | bytes 835592 | tf_op jit(solution)/shard_map/ppermute | solution.py:187
  8.8 7.8 %collective-permute-start.4 = (f32[4,136,128]{2,1,0:T(8,128)S(1)}, f32[4,136,128]{2,1,0:T(8,128)S(1)}, u32[]{:S(2)}, u32[]{:S(2)}) collective-permute-start(f32[4,136,128]{2,1,0:T(8,128)S(1)} %get-tuple-element.12), channel_id=1, source_target_pairs={{0,1},{1,0},{2,3},{3,2},{4,5},{5,4},{6,7},{7,6},{8,9},{9,8},{10,11... | collective-permute-start | bytes 835592 | tf_op jit(solution)/shard_map/ppermute | solution.py:187
  11.5 20.2 %collective-permute-start.1 = (f32[2,256,128]{2,1,0:T(8,128)S(1)}, f32[2,256,128]{2,1,0:T(8,128)S(1)}, u32[]{:S(2)}, u32[]{:S(2)}) collective-permute-start(f32[2,256,128]{2,1,0:T(8,128)S(1)} %pad_maximum_fusion.7.refs_0_), channel_id=1, source_target_pairs={{0,4},{1,5},{2,6},{3,7},{4,0},{5,1},{6,2},{7,3},{8,12},{9,13},{10,... | collective-permute-start | bytes 786440 | tf_op jit(solution)/shard_map/ppermute | solution.py:187
  16.8 12.6 %collective-permute-start.5 = (f32[1056,128]{1,0:T(8,128)S(1)}, f32[1056,128]{1,0:T(8,128)S(1)}, u32[]{:S(2)}, u32[]{:S(2)}) collective-permute-start(f32[1056,128]{1,0:T(8,128)S(1)} %get-tuple-element.33), channel_id=1, source_target_pairs={{0,2},{1,3},{2,0},{3,1},{4,6},{5,7},{6,4},{7,5},{8,10},{9,11},{10,... | collective-permute-start | bytes 1622024 | tf_op jit(solution)/shard_map/ppermute | solution.py:187
  17.4 27.9 %collective-permute-start.12 = (f32[2,136,128]{2,1,0:T(8,128)S(1)}, f32[2,136,128]{2,1,0:T(8,128)S(1)}, u32[]{:S(2)}, u32[]{:S(2)}) collective-permute-start(f32[2,136,128]{2,1,0:T(8,128)S(1)} %pad_maximum_fusion.9), channel_id=1, source_target_pairs={{0,12},{1,13},{2,14},{3,15},{4,8},{5,9},{6,10},{7,11},{8,4},{9,5},... | collective-permute-start | bytes 417800 | tf_op jit(solution)/shard_map/ppermute | solution.py:187
  18.8 12.1 %collective-permute-start.3 = (f32[1056,128]{1,0:T(8,128)S(1)}, f32[1056,128]{1,0:T(8,128)S(1)}, u32[]{:S(2)}, u32[]{:S(2)}) collective-permute-start(f32[1056,128]{1,0:T(8,128)S(1)} %get-tuple-element.34), channel_id=1, source_target_pairs={{0,1},{1,0},{2,3},{3,2},{4,5},{5,4},{6,7},{7,6},{8,9},{9,8},{10,11... | collective-permute-start | bytes 1622024 | tf_op jit(solution)/shard_map/ppermute | solution.py:187
  20.3 24.9 %collective-permute-start.11 = (f32[2,136,128]{2,1,0:T(8,128)S(1)}, f32[2,136,128]{2,1,0:T(8,128)S(1)}, u32[]{:S(2)}, u32[]{:S(2)}) collective-permute-start(f32[2,136,128]{2,1,0:T(8,128)S(1)} %pad_maximum_fusion.8), channel_id=1, source_target_pairs={{0,8},{1,9},{2,10},{3,11},{4,12},{5,13},{6,14},{7,15},{8,0},{9,1},... | collective-permute-start | bytes 417800 | tf_op jit(solution)/shard_map/ppermute | solution.py:187
  29.4 16.9 %collective-permute-start.14 = (f32[2,136,128]{2,1,0:T(8,128)S(1)}, f32[2,136,128]{2,1,0:T(8,128)S(1)}, u32[]{:S(2)}, u32[]{:S(2)}) collective-permute-start(f32[2,136,128]{2,1,0:T(8,128)S(1)} %pad_maximum_fusion.10), channel_id=1, source_target_pairs={{0,8},{1,9},{2,10},{3,11},{4,12},{5,13},{6,14},{7,15},{8,0},{9,1},... | collective-permute-start | bytes 417800 | tf_op jit(solution)/shard_map/ppermute | solution.py:187
  31.0 12.7 %collective-permute-start.10 = (f32[4,136,128]{2,1,0:T(8,128)S(1)}, f32[4,136,128]{2,1,0:T(8,128)S(1)}, u32[]{:S(2)}, u32[]{:S(2)}) collective-permute-start(f32[4,136,128]{2,1,0:T(8,128)S(1)} %pad_maximum_fusion.6), channel_id=1, source_target_pairs={{0,4},{1,5},{2,6},{3,7},{4,0},{5,1},{6,2},{7,3},{8,12},{9,13},{10,... | collective-permute-start | bytes 835592 | tf_op jit(solution)/shard_map/ppermute | solution.py:187
  31.7 14.7 %collective-permute-start.15 = (f32[2,136,128]{2,1,0:T(8,128)S(1)}, f32[2,136,128]{2,1,0:T(8,128)S(1)}, u32[]{:S(2)}, u32[]{:S(2)}) collective-permute-start(f32[2,136,128]{2,1,0:T(8,128)S(1)} %pad_maximum_fusion.11), channel_id=1, source_target_pairs={{0,12},{1,13},{2,14},{3,15},{4,8},{5,9},{6,10},{7,11},{8,4},{9,5},... | collective-permute-start | bytes 417800 | tf_op jit(solution)/shard_map/ppermute | solution.py:187
  43.6 8.0 %collective-permute-start.7 = (f32[3,256,128]{2,1,0:T(8,128)S(1)}, f32[3,256,128]{2,1,0:T(8,128)S(1)}, u32[]{:S(2)}, u32[]{:S(2)}) collective-permute-start(f32[3,256,128]{2,1,0:T(8,128)S(1)} %get-tuple-element.31), channel_id=1, source_target_pairs={{0,2},{1,3},{2,0},{3,1},{4,6},{5,7},{6,4},{7,5},{8,10},{9,11},{10,... | collective-permute-start | bytes 1179656 | tf_op jit(solution)/shard_map/ppermute | solution.py:187
  45.3 17.4 %collective-permute-start.13 = (f32[12,136,128]{2,1,0:T(8,128)S(1)}, f32[12,136,128]{2,1,0:T(8,128)S(1)}, u32[]{:S(2)}, u32[]{:S(2)}) collective-permute-start(f32[12,136,128]{2,1,0:T(8,128)S(1)} %constant_dynamic-update-slice_fusion.refs_0_), channel_id=1, source_target_pairs={{0,16},{16,0},{1,17},{17,1},{2,18},{18,2},{3,19},{19,3},{4,20},{20... | collective-permute-start | bytes 2506760 | tf_op jit(solution)/shard_map/ppermute | solution.py:187
  45.4 12.0 %collective-permute-start.6 = (f32[3,256,128]{2,1,0:T(8,128)S(1)}, f32[3,256,128]{2,1,0:T(8,128)S(1)}, u32[]{:S(2)}, u32[]{:S(2)}) collective-permute-start(f32[3,256,128]{2,1,0:T(8,128)S(1)} %get-tuple-element.32), channel_id=1, source_target_pairs={{0,1},{1,0},{2,3},{3,2},{4,5},{5,4},{6,7},{7,6},{8,9},{9,8},{10,11... | collective-permute-start | bytes 1179656 | tf_op jit(solution)/shard_map/ppermute | solution.py:187
  46.4 16.3 %collective-permute-start.16 = (f32[4,136,128]{2,1,0:T(8,128)S(1)}, f32[4,136,128]{2,1,0:T(8,128)S(1)}, u32[]{:S(2)}, u32[]{:S(2)}) collective-permute-start(f32[4,136,128]{2,1,0:T(8,128)S(1)} %constant_dynamic-update-slice_fusion.3.refs_2_), channel_id=1, source_target_pairs={{0,16},{16,0},{1,17},{17,1},{2,18},{18,2},{3,19},{19,3},{4,20},{20... | collective-permute-start | bytes 835592 | tf_op jit(solution)/shard_map/ppermute | solution.py:187
  51.6 8.1 %collective-permute-start.8 = (f32[1,256,128]{2,1,0:T(8,128)S(1)}, f32[1,256,128]{2,1,0:T(8,128)S(1)}, u32[]{:S(2)}, u32[]{:S(2)}) collective-permute-start(f32[1,256,128]{2,1,0:T(8,128)S(1)} %get-tuple-element.21), channel_id=1, source_target_pairs={{0,1},{1,0},{2,3},{3,2},{4,5},{5,4},{6,7},{7,6},{8,9},{9,8},{10,11... | collective-permute-start | bytes 393224 | tf_op jit(solution)/shard_map/ppermute | solution.py:187
  57.4 5.0 %collective-permute-start.9 = (f32[1,256,128]{2,1,0:T(8,128)S(1)}, f32[1,256,128]{2,1,0:T(8,128)S(1)}, u32[]{:S(2)}, u32[]{:S(2)}) collective-permute-start(f32[1,256,128]{2,1,0:T(8,128)S(1)} %get-tuple-element.19), channel_id=1, source_target_pairs={{0,2},{1,3},{2,0},{3,1},{4,6},{5,7},{6,4},{7,5},{8,10},{9,11},{10,... | collective-permute-start | bytes 393224 | tf_op jit(solution)/shard_map/ppermute | solution.py:187
  62.4 1.2 %copy-start = (f32[256,1024]{1,0:T(8,128)S(1)}, f32[256,1024]{1,0:T(8,128)}, u32[]{:S(2)}) copy-start(f32[256,1024]{1,0:T(8,128)} %refs_4_.1) | copy-start | bytes 3145732

commit v9 on v8

--- a/solution.py
+++ b/solution.py
@@ -10,7 +10,7 @@
 KT = 16
 CT = 8
 SLOT = 2
-HINT = 32 * 1024 * 1024
+HINT = 256 * 1024 * 1024
 META = 8
 
 
@@ -221,9 +221,11 @@
     last = [
         jnp.stack([come[z], come[half + z]]) for z in range(half) for come in (even_last, odd_last)
     ]
+    last, far_first = lax.optimization_barrier((last, far_first))
+    far_last = [hop(last[z], 4 * z) for z in range(half, 2 * half)]
     near = [jnp.concatenate([first[z], last[z]]) for z in range(half)]
+    near, far_last[: half // 2] = lax.optimization_barrier((near, far_last[: half // 2]))
     near = [near[0]] + [hop(plane, 4 * z) for z, plane in enumerate(near) if z]
-    far_last = [hop(last[z], 4 * z) for z in range(half, 2 * half)]
     cut = len(at) // 2
     come = hop(jnp.concatenate([late, over_y[:cut]]), 1)
     late_x, diagonal_x = come[: len(at)], come[len(at) :]
@@ -234,7 +236,7 @@
     positions = [tuple(p ^ step for p in at) for step in (0, 4, 1, 2, 5, 6)]
     positions += [tuple(p ^ step for p in part) for step in (3, 7) for part in (at[:cut], at[cut:])]
     groups = []
-    for planes in (near + far_first, far_last):
+    for planes in (near[:1] + far_first, near[1:] + far_last):
         mine = jnp.concatenate(planes, axis=0)
         groups.append(
             [mine] + [send(mine, "row", lambda i: (i + q) % rows_axis) for q in range(1, rows_axis)]

time: 68 us -> 62.4 us (0.918)
  waiting for transfers between devices: 35.5 us -> 30.4 us
    ppermute x17, waiting for transfers between devices: 35.5 us -> 30.4 us  [send(): return lax.ppermute(x, axis, [(i, partner(i)) for i in range(size)])]
    unnamed x9 -> x8, local copies, waits for them, and re-layouts: 2.04 us -> 2.05 us
  transfers between devices with their start and end apart: 17 -> 17, of which waited for: 10 -> 10; matrix products, arithmetic and copies ran while one was open for 3% -> 4% of each run, Pallas kernels for 3% -> 3%
where the time goes in v9:
time: 62.4 us; the launch traced here: 62.1 us
  waiting for transfers between devices  30.4 us (49%)
  starting transfers between devices  21.3 us (34%)
  Pallas kernels  5.89 us (9%)
  local copies, waits for them, and re-layouts  2.33 us (4%)
  other arithmetic  1.9 us (3%)
    ppermute x17, waiting for transfers between devices, send(): return lax.ppermute(x, axis, [(i, partner(i)) for i in range(size)])  30.4 us
    ppermute x17, starting transfers between devices, send(): return lax.ppermute(x, axis, [(i, partner(i)) for i in range(size)])  21.3 us
    pallas_call x1, Pallas kernels, contract(): pl.pallas_call(functools.partial(contract_kernel, len(groups), len(groups...  4.16 us
    unnamed x8, local copies, waits for them, and re-layouts  2.05 us
    pallas_call x1, Pallas kernels, pack(): pl.pallas_call(pack_kernel, out_shape=[out] * 4, in_specs=[pl.BlockSpec(m...  1.48 us
  transfers between devices with their start and end apart: 17, of which 10 were waited for; matrix products, arithmetic and copies ran while one was open for 4% of the time, Pallas kernels for 3%

profile of v9, /device:TPU:0, one launch (start us, length us, event | category | flops | bytes accessed | tf_op | source)
XLA Modules:
  0.0 62.1 jit_solution(16964685425557210019)
XLA Ops:
  0.0 4.0 %collective-permute-start = (f32[1,256,128]{2,1,0:T(8,128)}, f32[1,256,128]{2,1,0:T(8,128)S(1)}, u32[]{:S(2)}, u32[]{:S(2)}) collective-permute-start(f32[1,256,128]{2,1,0:T(8,128)} %bitcast.37), channel_id=1, source_target_pairs={{0,8},{1,9},{2,10},{3,11},{4,12},{5,13},{6,14},{7,15},{8,0},{9,1},... | collective-permute-start | bytes 393224 | tf_op jit(solution)/shard_map/ppermute | solution.py:187
  4.0 0.7 %fusion.1.words_ref = s32[16]{0:T(128)S(1)} fusion(s32[16]{0:T(128)} %param.11, s32[16]{0:T(128)} %param.10, s32[16,1]{0,1:T(1,128)} %param.9), kind=kLoop, calls=%fused_computation.33 | loop fusion | flops 64 | bytes 256 | tf_op jit(solution)/shard_map/add | solution.py:57
  4.7 0.0 copy-start.1
  4.7 1.0 %copy-done.1 = f32[16,64,128]{2,1,0:T(8,128)S(1)} copy-done((f32[16,64,128]{2,1,0:T(8,128)S(1)}, f32[16,64,128]{2,1,0:T(8,128)}, u32[]{:S(2)}) %copy-start.1) | copy-done | bytes 524312
  5.8 1.5 %shard_map.64 = (f32[4,136,128]{2,1,0:T(8,128)S(1)}, f32[4,136,128]{2,1,0:T(8,128)S(1)}, f32[4,136,128]{2,1,0:T(8,128)S(1)}, f32[4,136,128]{2,1,0:T(8,128)S(1)}) custom-call(s32[16]{0:T(128)S(1)} %fusion.1.words_ref, f32[16,64,128]{2,1,0:T(8,128)S(1)} %copy-done.1), custom_call_target="tpu_custom_call" | custom-call | bytes 1572864 | tf_op jit(solution)/shard_map/pallas_call | solution.py:59
  7.3 1.6 %collective-permute-start.2 = (f32[4,136,128]{2,1,0:T(8,128)S(1)}, f32[4,136,128]{2,1,0:T(8,128)S(1)}, u32[]{:S(2)}, u32[]{:S(2)}) collective-permute-start(f32[4,136,128]{2,1,0:T(8,128)S(1)} %get-tuple-element.19), channel_id=1, source_target_pairs={{0,2},{1,3},{2,0},{3,1},{4,6},{5,7},{6,4},{7,5},{8,10},{9,11},{10,... | collective-permute-start | bytes 835592 | tf_op jit(solution)/shard_map/ppermute | solution.py:187
  8.8 1.5 %collective-permute-start.4 = (f32[4,136,128]{2,1,0:T(8,128)S(1)}, f32[4,136,128]{2,1,0:T(8,128)S(1)}, u32[]{:S(2)}, u32[]{:S(2)}) collective-permute-start(f32[4,136,128]{2,1,0:T(8,128)S(1)} %get-tuple-element.21), channel_id=1, source_target_pairs={{0,1},{1,0},{2,3},{3,2},{4,5},{5,4},{6,7},{7,6},{8,9},{9,8},{10,11... | collective-permute-start | bytes 835592 | tf_op jit(solution)/shard_map/ppermute | solution.py:187
  10.4 0.1 collective-permute-done
  10.6 0.9 %pad_maximum_fusion.8.refs_0_ = f32[2,256,128]{2,1,0:T(8,128)S(1)} fusion(f32[1,256,128]{2,1,0:T(8,128)S(1)} %collective-permute-done, f32[1,256,128]{2,1,0:T(8,128)} %bitcast.38), kind=kLoop, calls=%fused_computation.8 | loop fusion | flops 65536 | bytes 524288 | tf_op jit(solution)/shard_map/concatenate | solution.py:208
  11.5 1.5 %collective-permute-start.1 = (f32[2,256,128]{2,1,0:T(8,128)S(1)}, f32[2,256,128]{2,1,0:T(8,128)S(1)}, u32[]{:S(2)}, u32[]{:S(2)}) collective-permute-start(f32[2,256,128]{2,1,0:T(8,128)S(1)} %pad_maximum_fusion.8.refs_0_), channel_id=1, source_target_pairs={{0,4},{1,5},{2,6},{3,7},{4,0},{5,1},{6,2},{7,3},{8,12},{9,13},{10,... | collective-permute-start | bytes 786440 | tf_op jit(solution)/shard_map/ppermute | solution.py:187
  13.0 2.5 %collective-permute-done.2 = f32[4,136,128]{2,1,0:T(8,128)S(1)} collective-permute-done((f32[4,136,128]{2,1,0:T(8,128)S(1)}, f32[4,136,128]{2,1,0:T(8,128)S(1)}, u32[]{:S(2)}, u32[]{:S(2)}) %collective-permute-start.2) | collective-permute-done | bytes 278560 | tf_op jit(solution)/shard_map/ppermute | solution.py:187
  15.5 1.2 %collective-permute-done.4 = f32[4,136,128]{2,1,0:T(8,128)S(1)} collective-permute-done((f32[4,136,128]{2,1,0:T(8,128)S(1)}, f32[4,136,128]{2,1,0:T(8,128)S(1)}, u32[]{:S(2)}, u32[]{:S(2)}) %collective-permute-start.4) | collective-permute-done | bytes 278560 | tf_op jit(solution)/shard_map/ppermute | solution.py:187
  16.7 0.1 pad_maximum_fusion
  16.8 0.6 collective-permute-start.5
  17.4 1.4 %collective-permute-start.11 = (f32[2,136,128]{2,1,0:T(8,128)S(1)}, f32[2,136,128]{2,1,0:T(8,128)S(1)}, u32[]{:S(2)}, u32[]{:S(2)}) collective-permute-start(f32[2,136,128]{2,1,0:T(8,128)S(1)} %pad_maximum_fusion.14), channel_id=1, source_target_pairs={{0,12},{1,13},{2,14},{3,15},{4,8},{5,9},{6,10},{7,11},{8,4},{9,5},... | collective-permute-start | bytes 417800 | tf_op jit(solution)/shard_map/ppermute | solution.py:187
  18.8 1.5 %collective-permute-start.3 = (f32[1056,128]{1,0:T(8,128)S(1)}, f32[1056,128]{1,0:T(8,128)S(1)}, u32[]{:S(2)}, u32[]{:S(2)}) collective-permute-start(f32[1056,128]{1,0:T(8,128)S(1)} %get-tuple-element.54), channel_id=1, source_target_pairs={{0,1},{1,0},{2,3},{3,2},{4,5},{5,4},{6,7},{7,6},{8,9},{9,8},{10,11... | collective-permute-start | bytes 1622024 | tf_op jit(solution)/shard_map/ppermute | solution.py:187
  20.3 1.8 %collective-permute-start.10 = (f32[2,136,128]{2,1,0:T(8,128)S(1)}, f32[2,136,128]{2,1,0:T(8,128)S(1)}, u32[]{:S(2)}, u32[]{:S(2)}) collective-permute-start(f32[2,136,128]{2,1,0:T(8,128)S(1)} %pad_maximum_fusion.13), channel_id=1, source_target_pairs={{0,8},{1,9},{2,10},{3,11},{4,12},{5,13},{6,14},{7,15},{8,0},{9,1},... | collective-permute-start | bytes 417800 | tf_op jit(solution)/shard_map/ppermute | solution.py:187
  22.1 7.3 %collective-permute-done.5 = f32[1056,128]{1,0:T(8,128)S(1)} collective-permute-done((f32[1056,128]{1,0:T(8,128)S(1)}, f32[1056,128]{1,0:T(8,128)S(1)}, u32[]{:S(2)}, u32[]{:S(2)}) %collective-permute-start.5) | collective-permute-done | bytes 540704 | tf_op jit(solution)/shard_map/ppermute | solution.py:187
  29.4 1.5 %collective-permute-done.3 = f32[1056,128]{1,0:T(8,128)S(1)} collective-permute-done((f32[1056,128]{1,0:T(8,128)S(1)}, f32[1056,128]{1,0:T(8,128)S(1)}, u32[]{:S(2)}, u32[]{:S(2)}) %collective-permute-start.3) | collective-permute-done | bytes 540704 | tf_op jit(solution)/shard_map/ppermute | solution.py:187
  31.0 0.0 collective-permute-done.11
  31.0 0.7 %collective-permute-done.10 = f32[2,136,128]{2,1,0:T(8,128)S(1)} collective-permute-done((f32[2,136,128]{2,1,0:T(8,128)S(1)}, f32[2,136,128]{2,1,0:T(8,128)S(1)}, u32[]{:S(2)}, u32[]{:S(2)}) %collective-permute-start.10) | collective-permute-done | bytes 139296 | tf_op jit(solution)/shard_map/ppermute | solution.py:187
  31.7 1.1 %collective-permute-start.12 = (f32[2,136,128]{2,1,0:T(8,128)S(1)}, f32[2,136,128]{2,1,0:T(8,128)S(1)}, u32[]{:S(2)}, u32[]{:S(2)}) collective-permute-start(f32[2,136,128]{2,1,0:T(8,128)S(1)} %get-tuple-element.24), channel_id=1, source_target_pairs={{0,8},{1,9},{2,10},{3,11},{4,12},{5,13},{6,14},{7,15},{8,0},{9,1},... | collective-permute-start | bytes 417800 | tf_op jit(solution)/shard_map/ppermute | solution.py:187
  32.8 1.3 %collective-permute-start.15 = (f32[2,136,128]{2,1,0:T(8,128)S(1)}, f32[2,136,128]{2,1,0:T(8,128)S(1)}, u32[]{:S(2)}, u32[]{:S(2)}) collective-permute-start(f32[2,136,128]{2,1,0:T(8,128)S(1)} %get-tuple-element.30), channel_id=1, source_target_pairs={{0,12},{1,13},{2,14},{3,15},{4,8},{5,9},{6,10},{7,11},{8,4},{9,5},... | collective-permute-start | bytes 417800 | tf_op jit(solution)/shard_map/ppermute | solution.py:187
  34.1 0.0 collective-permute-done.1.refs_1_
  34.1 0.1 pad_maximum_fusion.2
  34.1 1.5 %collective-permute-start.7 = (f32[3,256,128]{2,1,0:T(8,128)S(1)}, f32[3,256,128]{2,1,0:T(8,128)S(1)}, u32[]{:S(2)}, u32[]{:S(2)}) collective-permute-start(f32[3,256,128]{2,1,0:T(8,128)S(1)} %get-tuple-element.51), channel_id=1, source_target_pairs={{0,2},{1,3},{2,0},{3,1},{4,6},{5,7},{6,4},{7,5},{8,10},{9,11},{10,... | collective-permute-start | bytes 1179656 | tf_op jit(solution)/shard_map/ppermute | solution.py:187
  35.6 1.5 %collective-permute-start.6 = (f32[3,256,128]{2,1,0:T(8,128)S(1)}, f32[3,256,128]{2,1,0:T(8,128)S(1)}, u32[]{:S(2)}, u32[]{:S(2)}) collective-permute-start(f32[3,256,128]{2,1,0:T(8,128)S(1)} %get-tuple-element.52), channel_id=1, source_target_pairs={{0,1},{1,0},{2,3},{3,2},{4,5},{5,4},{6,7},{7,6},{8,9},{9,8},{10,11... | collective-permute-start | bytes 1179656 | tf_op jit(solution)/shard_map/ppermute | solution.py:187
  37.1 4.5 %collective-permute-done.12 = f32[2,136,128]{2,1,0:T(8,128)S(1)} collective-permute-done((f32[2,136,128]{2,1,0:T(8,128)S(1)}, f32[2,136,128]{2,1,0:T(8,128)S(1)}, u32[]{:S(2)}, u32[]{:S(2)}) %collective-permute-start.12) | collective-permute-done | bytes 139296 | tf_op jit(solution)/shard_map/ppermute | solution.py:187
  41.6 0.0 collective-permute-start.14
  41.7 0.1 collective-permute-start.13
  41.8 8.1 %collective-permute-done.14 = f32[4,136,128]{2,1,0:T(8,128)S(1)} collective-permute-done((f32[4,136,128]{2,1,0:T(8,128)S(1)}, f32[4,136,128]{2,1,0:T(8,128)S(1)}, u32[]{:S(2)}, u32[]{:S(2)}) %collective-permute-start.14) | collective-permute-done | bytes 278560 | tf_op jit(solution)/shard_map/ppermute | solution.py:187
  49.9 0.0 collective-permute-done.15
  49.9 0.1 collective-permute-start.16
  50.0 0.0 collective-permute-done.7
  50.0 1.0 %collective-permute-start.8 = (f32[1,256,128]{2,1,0:T(8,128)S(1)}, f32[1,256,128]{2,1,0:T(8,128)S(1)}, u32[]{:S(2)}, u32[]{:S(2)}) collective-permute-start(f32[1,256,128]{2,1,0:T(8,128)S(1)} %get-tuple-element.41), channel_id=1, source_target_pairs={{0,1},{1,0},{2,3},{3,2},{4,5},{5,4},{6,7},{7,6},{8,9},{9,8},{10,11... | collective-permute-start | bytes 393224 | tf_op jit(solution)/shard_map/ppermute | solution.py:187
  51.1 0.0 collective-permute-done.6
  51.1 1.0 %collective-permute-start.9 = (f32[1,256,128]{2,1,0:T(8,128)S(1)}, f32[1,256,128]{2,1,0:T(8,128)S(1)}, u32[]{:S(2)}, u32[]{:S(2)}) collective-permute-start(f32[1,256,128]{2,1,0:T(8,128)S(1)} %get-tuple-element.39), channel_id=1, source_target_pairs={{0,2},{1,3},{2,0},{3,1},{4,6},{5,7},{6,4},{7,5},{8,10},{9,11},{10,... | collective-permute-start | bytes 393224 | tf_op jit(solution)/shard_map/ppermute | solution.py:187
  52.2 3.8 %collective-permute-done.8.refs_8_ = f32[1,256,128]{2,1,0:T(8,128)S(1)} collective-permute-done((f32[1,256,128]{2,1,0:T(8,128)S(1)}, f32[1,256,128]{2,1,0:T(8,128)S(1)}, u32[]{:S(2)}, u32[]{:S(2)}) %collective-permute-start.8) | collective-permute-done | bytes 131104 | tf_op jit(solution)/shard_map/ppermute | solution.py:187
  56.0 0.8 %collective-permute-done.9.refs_9_ = f32[1,256,128]{2,1,0:T(8,128)S(1)} collective-permute-done((f32[1,256,128]{2,1,0:T(8,128)S(1)}, f32[1,256,128]{2,1,0:T(8,128)S(1)}, u32[]{:S(2)}, u32[]{:S(2)}) %collective-permute-start.9) | collective-permute-done | bytes 131104 | tf_op jit(solution)/shard_map/ppermute | solution.py:187
  56.8 0.0 copy-start
  56.8 0.3 shard_map.65.split_ref
  57.0 0.0 collective-permute-done.13.refs_1_
  57.0 0.0 collective-permute-done.16.refs_3_
  57.0 0.9 %copy-done = f32[256,1024]{1,0:T(8,128)S(1)} copy-done((f32[256,1024]{1,0:T(8,128)S(1)}, f32[256,1024]{1,0:T(8,128)}, u32[]{:S(2)}) %copy-start) | copy-done | bytes 1048600
  58.0 4.2 %shard_map.66 = f32[256,1024]{1,0:T(8,128)} custom-call(bf16[16,256,256]{2,1,0:T(8,128)(2,1)S(1)} %shard_map.65.split_ref, f32[8,136,128]{2,1,0:T(8,128)S(1)} %constant_dynamic-update-slice_fusion.refs_0_, f32[8,136,128]{2,1,0:T(8,128)S(1)} %collective-permute-done.13.refs_1_, f32[8,136,128]{2,1,0:T(8,128)S(1)} %constant_dynamic-update-slice_fusion.3.refs_2_, ...), custom_call_target="tpu_custom_call" | custom-call | tf_op jit(solution)/shard_map/pallas_call | solution.py:172
  (32 shorter events, 0.5 us)
Async XLA Ops:
  0.0 10.5 %collective-permute-start = (f32[1,256,128]{2,1,0:T(8,128)}, f32[1,256,128]{2,1,0:T(8,128)S(1)}, u32[]{:S(2)}, u32[]{:S(2)}) collective-permute-start(f32[1,256,128]{2,1,0:T(8,128)} %bitcast.37), channel_id=1, source_target_pairs={{0,8},{1,9},{2,10},{3,11},{4,12},{5,13},{6,14},{7,15},{8,0},{9,1},... | collective-permute-start | bytes 393224 | tf_op jit(solution)/shard_map/ppermute | solution.py:187
  4.7 1.0 %copy-start.1 = (f32[16,64,128]{2,1,0:T(8,128)S(1)}, f32[16,64,128]{2,1,0:T(8,128)}, u32[]{:S(2)}) copy-start(f32[16,64,128]{2,1,0:T(8,128)} %tiles_ref.1) | copy-start | bytes 1572868
  7.3 8.2 %collective-permute-start.2 = (f32[4,136,128]{2,1,0:T(8,128)S(1)}, f32[4,136,128]{2,1,0:T(8,128)S(1)}, u32[]{:S(2)}, u32[]{:S(2)}) collective-permute-start(f32[4,136,128]{2,1,0:T(8,128)S(1)} %get-tuple-element.19), channel_id=1, source_target_pairs={{0,2},{1,3},{2,0},{3,1},{4,6},{5,7},{6,4},{7,5},{8,10},{9,11},{10,... | collective-permute-start | bytes 835592 | tf_op jit(solution)/shard_map/ppermute | solution.py:187
  8.8 7.8 %collective-permute-start.4 = (f32[4,136,128]{2,1,0:T(8,128)S(1)}, f32[4,136,128]{2,1,0:T(8,128)S(1)}, u32[]{:S(2)}, u32[]{:S(2)}) collective-permute-start(f32[4,136,128]{2,1,0:T(8,128)S(1)} %get-tuple-element.21), channel_id=1, source_target_pairs={{0,1},{1,0},{2,3},{3,2},{4,5},{5,4},{6,7},{7,6},{8,9},{9,8},{10,11... | collective-permute-start | bytes 835592 | tf_op jit(solution)/shard_map/ppermute | solution.py:187
  11.5 22.6 %collective-permute-start.1 = (f32[2,256,128]{2,1,0:T(8,128)S(1)}, f32[2,256,128]{2,1,0:T(8,128)S(1)}, u32[]{:S(2)}, u32[]{:S(2)}) collective-permute-start(f32[2,256,128]{2,1,0:T(8,128)S(1)} %pad_maximum_fusion.8.refs_0_), channel_id=1, source_target_pairs={{0,4},{1,5},{2,6},{3,7},{4,0},{5,1},{6,2},{7,3},{8,12},{9,13},{10,... | collective-permute-start | bytes 786440 | tf_op jit(solution)/shard_map/ppermute | solution.py:187
  16.8 12.6 %collective-permute-start.5 = (f32[1056,128]{1,0:T(8,128)S(1)}, f32[1056,128]{1,0:T(8,128)S(1)}, u32[]{:S(2)}, u32[]{:S(2)}) collective-permute-start(f32[1056,128]{1,0:T(8,128)S(1)} %get-tuple-element.53), channel_id=1, source_target_pairs={{0,2},{1,3},{2,0},{3,1},{4,6},{5,7},{6,4},{7,5},{8,10},{9,11},{10,... | collective-permute-start | bytes 1622024 | tf_op jit(solution)/shard_map/ppermute | solution.py:187
  17.4 13.6 %collective-permute-start.11 = (f32[2,136,128]{2,1,0:T(8,128)S(1)}, f32[2,136,128]{2,1,0:T(8,128)S(1)}, u32[]{:S(2)}, u32[]{:S(2)}) collective-permute-start(f32[2,136,128]{2,1,0:T(8,128)S(1)} %pad_maximum_fusion.14), channel_id=1, source_target_pairs={{0,12},{1,13},{2,14},{3,15},{4,8},{5,9},{6,10},{7,11},{8,4},{9,5},... | collective-permute-start | bytes 417800 | tf_op jit(solution)/shard_map/ppermute | solution.py:187
  18.8 12.1 %collective-permute-start.3 = (f32[1056,128]{1,0:T(8,128)S(1)}, f32[1056,128]{1,0:T(8,128)S(1)}, u32[]{:S(2)}, u32[]{:S(2)}) collective-permute-start(f32[1056,128]{1,0:T(8,128)S(1)} %get-tuple-element.54), channel_id=1, source_target_pairs={{0,1},{1,0},{2,3},{3,2},{4,5},{5,4},{6,7},{7,6},{8,9},{9,8},{10,11... | collective-permute-start | bytes 1622024 | tf_op jit(solution)/shard_map/ppermute | solution.py:187
  20.3 11.3 %collective-permute-start.10 = (f32[2,136,128]{2,1,0:T(8,128)S(1)}, f32[2,136,128]{2,1,0:T(8,128)S(1)}, u32[]{:S(2)}, u32[]{:S(2)}) collective-permute-start(f32[2,136,128]{2,1,0:T(8,128)S(1)} %pad_maximum_fusion.13), channel_id=1, source_target_pairs={{0,8},{1,9},{2,10},{3,11},{4,12},{5,13},{6,14},{7,15},{8,0},{9,1},... | collective-permute-start | bytes 417800 | tf_op jit(solution)/shard_map/ppermute | solution.py:187
  31.7 9.9 %collective-permute-start.12 = (f32[2,136,128]{2,1,0:T(8,128)S(1)}, f32[2,136,128]{2,1,0:T(8,128)S(1)}, u32[]{:S(2)}, u32[]{:S(2)}) collective-permute-start(f32[2,136,128]{2,1,0:T(8,128)S(1)} %get-tuple-element.24), channel_id=1, source_target_pairs={{0,8},{1,9},{2,10},{3,11},{4,12},{5,13},{6,14},{7,15},{8,0},{9,1},... | collective-permute-start | bytes 417800 | tf_op jit(solution)/shard_map/ppermute | solution.py:187
  32.8 17.1 %collective-permute-start.15 = (f32[2,136,128]{2,1,0:T(8,128)S(1)}, f32[2,136,128]{2,1,0:T(8,128)S(1)}, u32[]{:S(2)}, u32[]{:S(2)}) collective-permute-start(f32[2,136,128]{2,1,0:T(8,128)S(1)} %get-tuple-element.30), channel_id=1, source_target_pairs={{0,12},{1,13},{2,14},{3,15},{4,8},{5,9},{6,10},{7,11},{8,4},{9,5},... | collective-permute-start | bytes 417800 | tf_op jit(solution)/shard_map/ppermute | solution.py:187
  34.1 15.9 %collective-permute-start.7 = (f32[3,256,128]{2,1,0:T(8,128)S(1)}, f32[3,256,128]{2,1,0:T(8,128)S(1)}, u32[]{:S(2)}, u32[]{:S(2)}) collective-permute-start(f32[3,256,128]{2,1,0:T(8,128)S(1)} %get-tuple-element.51), channel_id=1, source_target_pairs={{0,2},{1,3},{2,0},{3,1},{4,6},{5,7},{6,4},{7,5},{8,10},{9,11},{10,... | collective-permute-start | bytes 1179656 | tf_op jit(solution)/shard_map/ppermute | solution.py:187
  35.6 15.5 %collective-permute-start.6 = (f32[3,256,128]{2,1,0:T(8,128)S(1)}, f32[3,256,128]{2,1,0:T(8,128)S(1)}, u32[]{:S(2)}, u32[]{:S(2)}) collective-permute-start(f32[3,256,128]{2,1,0:T(8,128)S(1)} %get-tuple-element.52), channel_id=1, source_target_pairs={{0,1},{1,0},{2,3},{3,2},{4,5},{5,4},{6,7},{7,6},{8,9},{9,8},{10,11... | collective-permute-start | bytes 1179656 | tf_op jit(solution)/shard_map/ppermute | solution.py:187
  41.6 8.2 %collective-permute-start.14 = (f32[4,136,128]{2,1,0:T(8,128)S(1)}, f32[4,136,128]{2,1,0:T(8,128)S(1)}, u32[]{:S(2)}, u32[]{:S(2)}) collective-permute-start(f32[4,136,128]{2,1,0:T(8,128)S(1)} %pad_maximum_fusion.7), channel_id=1, source_target_pairs={{0,4},{1,5},{2,6},{3,7},{4,0},{5,1},{6,2},{7,3},{8,12},{9,13},{10,... | collective-permute-start | bytes 835592 | tf_op jit(solution)/shard_map/ppermute | solution.py:187
  41.7 15.4 %collective-permute-start.13 = (f32[8,136,128]{2,1,0:T(8,128)S(1)}, f32[8,136,128]{2,1,0:T(8,128)S(1)}, u32[]{:S(2)}, u32[]{:S(2)}) collective-permute-start(f32[8,136,128]{2,1,0:T(8,128)S(1)} %constant_dynamic-update-slice_fusion.refs_0_), channel_id=1, source_target_pairs={{0,16},{16,0},{1,17},{17,1},{2,18},{18,2},{3,19},{19,3},{4,20},{20... | collective-permute-start | bytes 1671176 | tf_op jit(solution)/shard_map/ppermute | solution.py:187
  49.9 7.1 %collective-permute-start.16 = (f32[8,136,128]{2,1,0:T(8,128)S(1)}, f32[8,136,128]{2,1,0:T(8,128)S(1)}, u32[]{:S(2)}, u32[]{:S(2)}) collective-permute-start(f32[8,136,128]{2,1,0:T(8,128)S(1)} %constant_dynamic-update-slice_fusion.3.refs_2_), channel_id=1, source_target_pairs={{0,16},{16,0},{1,17},{17,1},{2,18},{18,2},{3,19},{19,3},{4,20},{20... | collective-permute-start | bytes 1671176 | tf_op jit(solution)/shard_map/ppermute | solution.py:187
  50.0 6.0 %collective-permute-start.8 = (f32[1,256,128]{2,1,0:T(8,128)S(1)}, f32[1,256,128]{2,1,0:T(8,128)S(1)}, u32[]{:S(2)}, u32[]{:S(2)}) collective-permute-start(f32[1,256,128]{2,1,0:T(8,128)S(1)} %get-tuple-element.41), channel_id=1, source_target_pairs={{0,1},{1,0},{2,3},{3,2},{4,5},{5,4},{6,7},{7,6},{8,9},{9,8},{10,11... | collective-permute-start | bytes 393224 | tf_op jit(solution)/shard_map/ppermute | solution.py:187
  51.1 5.7 %collective-permute-start.9 = (f32[1,256,128]{2,1,0:T(8,128)S(1)}, f32[1,256,128]{2,1,0:T(8,128)S(1)}, u32[]{:S(2)}, u32[]{:S(2)}) collective-permute-start(f32[1,256,128]{2,1,0:T(8,128)S(1)} %get-tuple-element.39), channel_id=1, source_target_pairs={{0,2},{1,3},{2,0},{3,1},{4,6},{5,7},{6,4},{7,5},{8,10},{9,11},{10,... | collective-permute-start | bytes 393224 | tf_op jit(solution)/shard_map/ppermute | solution.py:187
  56.8 1.2 %copy-start = (f32[256,1024]{1,0:T(8,128)S(1)}, f32[256,1024]{1,0:T(8,128)}, u32[]{:S(2)}) copy-start(f32[256,1024]{1,0:T(8,128)} %refs_4_.1) | copy-start | bytes 3145732

commit v10 on v9

--- a/solution.py
+++ b/solution.py
@@ -149,7 +149,7 @@
             def _():
                 multiply(*whole(parts, owner, slot, code))
 
-        unroll = min(4, owners)
+        unroll = next(u for u in (5, 4, 3, 2, 1) if owners % u == 0)
 
         def some(step, carry):
             for i in range(unroll):
@@ -180,6 +180,21 @@
         ],
         compiler_params=pltpu.CompilerParams(vmem_limit_bytes=24 * 1024 * 1024),
     )(*arrays)
+
+
+def fetch_kernel(x_ref, out_ref):
+    out_ref[...] = x_ref[...]
+
+
+def fetch(x):
+    vmem = pl.BlockSpec(memory_space=pltpu.VMEM)
+    return pl.pallas_call(
+        fetch_kernel,
+        out_shape=jax.ShapeDtypeStruct(x.shape, x.dtype),
+        in_specs=[vmem],
+        out_specs=vmem,
+        compiler_params=pltpu.CompilerParams(vmem_limit_bytes=8 * 1024 * 1024),
+    )(x)
 
 
 def send(x, axis, partner):
@@ -212,20 +227,18 @@
     )
     half = targets // 8
     even_come, odd_come = hop(even_sent, 1), hop(odd_sent, 2)
-    late = hop(held, 4)
     first = [jnp.stack([even_kept[z], even_come[z]]) for z in range(half)]
     first = [plane for z in range(half) for plane in (first[z], jnp.stack([odd_kept[z], odd_come[z]]))]
-    far_first = [hop(first[z], 4 * z) for z in range(half, 2 * half)]
+    near_come, late = hop_both(first[1], held, 4)
+    come_first = [near_come] + [hop(plane, 4 * z) for z, plane in enumerate(first) if z > 1]
     even_last, over_y = hop_both(jnp.concatenate([even_kept[half:], even_come[half:]]), held, 2)
     odd_last, over_x = hop_both(jnp.concatenate([odd_kept[half:], odd_come[half:]]), held, 1)
     last = [
         jnp.stack([come[z], come[half + z]]) for z in range(half) for come in (even_last, odd_last)
     ]
-    last, far_first = lax.optimization_barrier((last, far_first))
-    far_last = [hop(last[z], 4 * z) for z in range(half, 2 * half)]
-    near = [jnp.concatenate([first[z], last[z]]) for z in range(half)]
-    near, far_last[: half // 2] = lax.optimization_barrier((near, far_last[: half // 2]))
-    near = [near[0]] + [hop(plane, 4 * z) for z, plane in enumerate(near) if z]
+    residual = fetch(residual_in)
+    last, come_first, residual = lax.optimization_barrier((last, come_first, residual))
+    come_last = [hop(plane, 4 * z) for z, plane in enumerate(last) if z]
     cut = len(at) // 2
     come = hop(jnp.concatenate([late, over_y[:cut]]), 1)
     late_x, diagonal_x = come[: len(at)], come[len(at) :]
@@ -236,7 +249,7 @@
     positions = [tuple(p ^ step for p in at) for step in (0, 4, 1, 2, 5, 6)]
     positions += [tuple(p ^ step for p in part) for step in (3, 7) for part in (at[:cut], at[cut:])]
     groups = []
-    for planes in (near[:1] + far_first, near[1:] + far_last):
+    for planes in ([first[0], last[0]] + come_first, come_last):
         mine = jnp.concatenate(planes, axis=0)
         groups.append(
             [mine] + [send(mine, "row", lambda i: (i + q) % rows_axis) for q in range(1, rows_axis)]
@@ -249,7 +262,7 @@
         stacked = stacked[place[wanted]]
         stacked = stacked.transpose(1, 0, 2).reshape(amplitudes.shape[0], KT, width).transpose(1, 0, 2)
         pieces, positions = [stacked], [(None,) * KT]
-    return contract(split(pieces, positions), groups, residual_in)
+    return contract(split(pieces, positions), groups, residual)
 
 
 def solution(mesh):

time: 62.4 us -> 60.4 us (0.968)
  waiting for transfers between devices: 30.4 us -> 27.1 us
  starting transfers between devices: 21.3 us -> 24.4 us
  local copies, waits for them, and re-layouts: 2.33 us -> 1.41 us
  other arithmetic: 1.9 us -> 1 us
    ppermute x17, waiting for transfers between devices: 30.4 us -> 27.1 us  [send(): return lax.ppermute(x, axis, [(i, partner(i)) for i in range(size)])]
    ppermute x17, starting transfers between devices: 21.3 us -> 24.4 us  [send(): return lax.ppermute(x, axis, [(i, partner(i)) for i in range(size)])]
    unnamed x8 -> x11, local copies, waits for them, and re-layouts: 2.05 us -> 1.1 us
    concatenate x1, other arithmetic: 0.92 us -> 0.02 us  [local(): jnp.concatenate([held, hop(held, bit)], axis=0)]
  transfers between devices with their start and end apart: 17 -> 17, of which waited for: 10 -> 9; matrix products, arithmetic and copies ran while one was open for 4% -> 2% of each run, Pallas kernels for 3% -> 3%
where the time goes in v10:
time: 60.4 us; the launch traced here: 60.2 us
  waiting for transfers between devices  27.1 us (45%)
  starting transfers between devices  24.4 us (40%)
  Pallas kernels  5.96 us (10%)
  local copies, waits for them, and re-layouts  1.41 us (2%)
  other arithmetic  1 us (2%)
    ppermute x17, waiting for transfers between devices, send(): return lax.ppermute(x, axis, [(i, partner(i)) for i in range(size)])  27.1 us
    ppermute x17, starting transfers between devices, send(): return lax.ppermute(x, axis, [(i, partner(i)) for i in range(size)])  24.4 us
    pallas_call x1, Pallas kernels, contract(): pl.pallas_call(functools.partial(contract_kernel, len(groups), len(groups...  4.15 us
    pallas_call x1, Pallas kernels, pack(): pl.pallas_call(pack_kernel, out_shape=[out] * 4, in_specs=[pl.BlockSpec(m...  1.48 us
  transfers between devices with their start and end apart: 17, of which 9 were waited for; matrix products, arithmetic and copies ran while one was open for 2% of the time, Pallas kernels for 3%

profile of v10, /device:TPU:0, one launch (start us, length us, event | category | flops | bytes accessed | tf_op | source)
XLA Modules:
  0.0 60.2 jit_solution(15387710296668019123)
XLA Ops:
  0.0 0.0 copy-start
  0.0 4.0 %collective-permute-start = (f32[1,256,128]{2,1,0:T(8,128)}, f32[1,256,128]{2,1,0:T(8,128)S(1)}, u32[]{:S(2)}, u32[]{:S(2)}) collective-permute-start(f32[1,256,128]{2,1,0:T(8,128)} %bitcast.45), channel_id=1, source_target_pairs={{0,8},{1,9},{2,10},{3,11},{4,12},{5,13},{6,14},{7,15},{8,0},{9,1},... | collective-permute-start | bytes 393224 | tf_op jit(solution)/shard_map/ppermute | solution.py:202
  4.0 0.7 %fusion.1.words_ref = s32[16]{0:T(128)S(1)} fusion(s32[16]{0:T(128)} %param.11, s32[16]{0:T(128)} %param.10, s32[16,1]{0,1:T(1,128)} %param.9), kind=kLoop, calls=%fused_computation.36 | loop fusion | flops 64 | bytes 256 | tf_op jit(solution)/shard_map/add | solution.py:57
  4.7 0.0 copy-start.1
  4.7 1.0 %copy-done.1 = f32[16,64,128]{2,1,0:T(8,128)S(1)} copy-done((f32[16,64,128]{2,1,0:T(8,128)S(1)}, f32[16,64,128]{2,1,0:T(8,128)}, u32[]{:S(2)}) %copy-start.1) | copy-done | bytes 524312
  5.8 0.0 copy-start.2
  5.8 1.5 %shard_map.64 = (f32[4,136,128]{2,1,0:T(8,128)S(1)}, f32[4,136,128]{2,1,0:T(8,128)S(1)}, f32[4,136,128]{2,1,0:T(8,128)S(1)}, f32[4,136,128]{2,1,0:T(8,128)S(1)}) custom-call(s32[16]{0:T(128)S(1)} %fusion.1.words_ref, f32[16,64,128]{2,1,0:T(8,128)S(1)} %copy-done.1), custom_call_target="tpu_custom_call" | custom-call | bytes 1572864 | tf_op jit(solution)/shard_map/pallas_call | solution.py:59
  7.3 1.6 %collective-permute-start.1 = (f32[4,136,128]{2,1,0:T(8,128)S(1)}, f32[4,136,128]{2,1,0:T(8,128)S(1)}, u32[]{:S(2)}, u32[]{:S(2)}) collective-permute-start(f32[4,136,128]{2,1,0:T(8,128)S(1)} %get-tuple-element.18), channel_id=1, source_target_pairs={{0,2},{1,3},{2,0},{3,1},{4,6},{5,7},{6,4},{7,5},{8,10},{9,11},{10,... | collective-permute-start | bytes 835592 | tf_op jit(solution)/shard_map/ppermute | solution.py:202
  8.8 1.5 %collective-permute-start.4 = (f32[4,136,128]{2,1,0:T(8,128)S(1)}, f32[4,136,128]{2,1,0:T(8,128)S(1)}, u32[]{:S(2)}, u32[]{:S(2)}) collective-permute-start(f32[4,136,128]{2,1,0:T(8,128)S(1)} %get-tuple-element.20), channel_id=1, source_target_pairs={{0,1},{1,0},{2,3},{3,2},{4,5},{5,4},{6,7},{7,6},{8,9},{9,8},{10,11... | collective-permute-start | bytes 835592 | tf_op jit(solution)/shard_map/ppermute | solution.py:202
  10.4 0.0 copy-done
  10.4 0.1 shard_map.66.refs_4_
  10.5 0.1 collective-permute-done
  10.6 0.0 copy-done.2
  10.6 4.9 %collective-permute-done.1 = f32[4,136,128]{2,1,0:T(8,128)S(1)} collective-permute-done((f32[4,136,128]{2,1,0:T(8,128)S(1)}, f32[4,136,128]{2,1,0:T(8,128)S(1)}, u32[]{:S(2)}, u32[]{:S(2)}) %collective-permute-start.1) | collective-permute-done | bytes 278560 | tf_op jit(solution)/shard_map/ppermute | solution.py:202
  15.5 1.2 %collective-permute-done.4 = f32[4,136,128]{2,1,0:T(8,128)S(1)} collective-permute-done((f32[4,136,128]{2,1,0:T(8,128)S(1)}, f32[4,136,128]{2,1,0:T(8,128)S(1)}, u32[]{:S(2)}, u32[]{:S(2)}) %collective-permute-start.4) | collective-permute-done | bytes 278560 | tf_op jit(solution)/shard_map/ppermute | solution.py:202
  16.7 0.1 pad_maximum_fusion
  16.8 0.6 collective-permute-start.5
  17.4 1.6 %collective-permute-start.2 = (f32[784,128]{1,0:T(8,128)S(1)}, f32[784,128]{1,0:T(8,128)S(1)}, u32[]{:S(2)}, u32[]{:S(2)}) collective-permute-start(f32[784,128]{1,0:T(8,128)S(1)} %pad_maximum_fusion.4), channel_id=1, source_target_pairs={{0,4},{1,5},{2,6},{3,7},{4,0},{5,1},{6,2},{7,3},{8,12},{9,13},{10,... | collective-permute-start | bytes 1204232 | tf_op jit(solution)/shard_map/ppermute | solution.py:202
  19.1 0.3 collective-permute-start.11
  19.4 1.5 %collective-permute-start.3 = (f32[1056,128]{1,0:T(8,128)S(1)}, f32[1056,128]{1,0:T(8,128)S(1)}, u32[]{:S(2)}, u32[]{:S(2)}) collective-permute-start(f32[1056,128]{1,0:T(8,128)S(1)} %get-tuple-element.52), channel_id=1, source_target_pairs={{0,1},{1,0},{2,3},{3,2},{4,5},{5,4},{6,7},{7,6},{8,9},{9,8},{10,11... | collective-permute-start | bytes 1622024 | tf_op jit(solution)/shard_map/ppermute | solution.py:202
  21.0 1.7 %collective-permute-start.10 = (f32[2,136,128]{2,1,0:T(8,128)S(1)}, f32[2,136,128]{2,1,0:T(8,128)S(1)}, u32[]{:S(2)}, u32[]{:S(2)}) collective-permute-start(f32[2,136,128]{2,1,0:T(8,128)S(1)} %pad_maximum_fusion.13), channel_id=1, source_target_pairs={{0,8},{1,9},{2,10},{3,11},{4,12},{5,13},{6,14},{7,15},{8,0},{9,1},... | collective-permute-start | bytes 417800 | tf_op jit(solution)/shard_map/ppermute | solution.py:202
  22.7 11.2 %collective-permute-done.2 = f32[784,128]{1,0:T(8,128)S(1)} collective-permute-done((f32[784,128]{1,0:T(8,128)S(1)}, f32[784,128]{1,0:T(8,128)S(1)}, u32[]{:S(2)}, u32[]{:S(2)}) %collective-permute-start.2) | collective-permute-done | bytes 401440 | tf_op jit(solution)/shard_map/ppermute | solution.py:202
  33.9 0.0 collective-permute-done.5
  33.9 0.0 collective-permute-done.3
  34.0 0.0 collective-permute-done.11
  34.0 0.0 collective-permute-done.10
  34.0 0.1 collective-permute-start.13
  34.1 2.5 %collective-permute-start.14 = (f32[2,136,128]{2,1,0:T(8,128)S(1)}, f32[2,136,128]{2,1,0:T(8,128)S(1)}, u32[]{:S(2)}, u32[]{:S(2)}) collective-permute-start(f32[2,136,128]{2,1,0:T(8,128)S(1)} %get-tuple-element.26), channel_id=1, source_target_pairs={{0,8},{1,9},{2,10},{3,11},{4,12},{5,13},{6,14},{7,15},{8,0},{9,1},... | collective-permute-start | bytes 417800 | tf_op jit(solution)/shard_map/ppermute | solution.py:202
  36.6 1.9 %collective-permute-start.15 = (f32[2,136,128]{2,1,0:T(8,128)S(1)}, f32[2,136,128]{2,1,0:T(8,128)S(1)}, u32[]{:S(2)}, u32[]{:S(2)}) collective-permute-start(f32[2,136,128]{2,1,0:T(8,128)S(1)} %get-tuple-element.27), channel_id=1, source_target_pairs={{0,12},{1,13},{2,14},{3,15},{4,8},{5,9},{6,10},{7,11},{8,4},{9,5},... | collective-permute-start | bytes 417800 | tf_op jit(solution)/shard_map/ppermute | solution.py:202
  38.5 0.1 pad_maximum_fusion.2
  38.6 3.1 %collective-permute-start.7 = (f32[3,256,128]{2,1,0:T(8,128)S(1)}, f32[3,256,128]{2,1,0:T(8,128)S(1)}, u32[]{:S(2)}, u32[]{:S(2)}) collective-permute-start(f32[3,256,128]{2,1,0:T(8,128)S(1)} %get-tuple-element.49), channel_id=1, source_target_pairs={{0,2},{1,3},{2,0},{3,1},{4,6},{5,7},{6,4},{7,5},{8,10},{9,11},{10,... | collective-permute-start | bytes 1179656 | tf_op jit(solution)/shard_map/ppermute | solution.py:202
  41.7 1.5 %collective-permute-start.6 = (f32[3,256,128]{2,1,0:T(8,128)S(1)}, f32[3,256,128]{2,1,0:T(8,128)S(1)}, u32[]{:S(2)}, u32[]{:S(2)}) collective-permute-start(f32[3,256,128]{2,1,0:T(8,128)S(1)} %get-tuple-element.50), channel_id=1, source_target_pairs={{0,1},{1,0},{2,3},{3,2},{4,5},{5,4},{6,7},{7,6},{8,9},{9,8},{10,11... | collective-permute-start | bytes 1179656 | tf_op jit(solution)/shard_map/ppermute | solution.py:202
  43.2 0.0 collective-permute-done.13
  43.2 0.1 collective-permute-start.12
  43.3 1.4 %collective-permute-done.14 = f32[2,136,128]{2,1,0:T(8,128)S(1)} collective-permute-done((f32[2,136,128]{2,1,0:T(8,128)S(1)}, f32[2,136,128]{2,1,0:T(8,128)S(1)}, u32[]{:S(2)}, u32[]{:S(2)}) %collective-permute-start.14) | collective-permute-done | bytes 139296 | tf_op jit(solution)/shard_map/ppermute | solution.py:202
  44.8 0.0 collective-permute-done.15
  44.8 0.1 collective-permute-start.16
  44.9 2.5 %collective-permute-done.7 = f32[3,256,128]{2,1,0:T(8,128)S(1)} collective-permute-done((f32[3,256,128]{2,1,0:T(8,128)S(1)}, f32[3,256,128]{2,1,0:T(8,128)S(1)}, u32[]{:S(2)}, u32[]{:S(2)}) %collective-permute-start.7) | collective-permute-done | bytes 393248 | tf_op jit(solution)/shard_map/ppermute | solution.py:202
  47.4 2.1 %collective-permute-start.8 = (f32[1,256,128]{2,1,0:T(8,128)S(1)}, f32[1,256,128]{2,1,0:T(8,128)S(1)}, u32[]{:S(2)}, u32[]{:S(2)}) collective-permute-start(f32[1,256,128]{2,1,0:T(8,128)S(1)} %get-tuple-element.39), channel_id=1, source_target_pairs={{0,1},{1,0},{2,3},{3,2},{4,5},{5,4},{6,7},{7,6},{8,9},{9,8},{10,11... | collective-permute-start | bytes 393224 | tf_op jit(solution)/shard_map/ppermute | solution.py:202
  49.5 1.2 %collective-permute-done.6 = f32[3,256,128]{2,1,0:T(8,128)S(1)} collective-permute-done((f32[3,256,128]{2,1,0:T(8,128)S(1)}, f32[3,256,128]{2,1,0:T(8,128)S(1)}, u32[]{:S(2)}, u32[]{:S(2)}) %collective-permute-start.6) | collective-permute-done | bytes 393248 | tf_op jit(solution)/shard_map/ppermute | solution.py:202
  50.7 0.4 collective-permute-start.9
  51.2 1.3 %collective-permute-done.8.refs_8_ = f32[1,256,128]{2,1,0:T(8,128)S(1)} collective-permute-done((f32[1,256,128]{2,1,0:T(8,128)S(1)}, f32[1,256,128]{2,1,0:T(8,128)S(1)}, u32[]{:S(2)}, u32[]{:S(2)}) %collective-permute-start.8) | collective-permute-done | bytes 131104 | tf_op jit(solution)/shard_map/ppermute | solution.py:202
  52.5 3.3 %collective-permute-done.9.refs_9_ = f32[1,256,128]{2,1,0:T(8,128)S(1)} collective-permute-done((f32[1,256,128]{2,1,0:T(8,128)S(1)}, f32[1,256,128]{2,1,0:T(8,128)S(1)}, u32[]{:S(2)}, u32[]{:S(2)}) %collective-permute-start.9) | collective-permute-done | bytes 131104 | tf_op jit(solution)/shard_map/ppermute | solution.py:202
  55.8 0.3 shard_map.65.split_ref
  56.0 0.0 collective-permute-done.16.refs_3_
  56.1 0.0 collective-permute-done.12.refs_1_
  56.1 4.2 %shard_map.67 = f32[256,1024]{1,0:T(8,128)} custom-call(bf16[16,256,256]{2,1,0:T(8,128)(2,1)S(1)} %shard_map.65.split_ref, f32[10,136,128]{2,1,0:T(8,128)S(1)} %constant_dynamic-update-slice_fusion.refs_0_, f32[10,136,128]{2,1,0:T(8,128)S(1)} %collective-permute-done.12.refs_1_, f32[6,136,128]{2,1,0:T(8,128)S(1)} %constant_dynamic-update-slice_fusion.4.refs_2_, ...), custom_call_target="tpu_custom_call" | custom-call | tf_op jit(solution)/shard_map/pallas_call | solution.py:172
  (35 shorter events, 0.5 us)
Async XLA Ops:
  0.0 10.4 %copy-start = (f32[256,1024]{1,0:T(8,128)S(1)}, f32[256,1024]{1,0:T(8,128)}, u32[]{:S(2)}) copy-start(f32[256,1024]{1,0:T(8,128)} %x_ref.1) | copy-start | bytes 3145732
  0.0 10.5 %collective-permute-start = (f32[1,256,128]{2,1,0:T(8,128)}, f32[1,256,128]{2,1,0:T(8,128)S(1)}, u32[]{:S(2)}, u32[]{:S(2)}) collective-permute-start(f32[1,256,128]{2,1,0:T(8,128)} %bitcast.45), channel_id=1, source_target_pairs={{0,8},{1,9},{2,10},{3,11},{4,12},{5,13},{6,14},{7,15},{8,0},{9,1},... | collective-permute-start | bytes 393224 | tf_op jit(solution)/shard_map/ppermute | solution.py:202
  4.7 1.0 %copy-start.1 = (f32[16,64,128]{2,1,0:T(8,128)S(1)}, f32[16,64,128]{2,1,0:T(8,128)}, u32[]{:S(2)}) copy-start(f32[16,64,128]{2,1,0:T(8,128)} %tiles_ref.1) | copy-start | bytes 1572868
  5.8 4.8 %copy-start.2 = (f32[256,128]{1,0:T(8,128)S(1)}, f32[256,128]{1,0:T(8,128)}, u32[]{:S(2)}) copy-start(f32[256,128]{1,0:T(8,128)} %param.7) | copy-start | bytes 393220
  7.3 8.2 %collective-permute-start.1 = (f32[4,136,128]{2,1,0:T(8,128)S(1)}, f32[4,136,128]{2,1,0:T(8,128)S(1)}, u32[]{:S(2)}, u32[]{:S(2)}) collective-permute-start(f32[4,136,128]{2,1,0:T(8,128)S(1)} %get-tuple-element.18), channel_id=1, source_target_pairs={{0,2},{1,3},{2,0},{3,1},{4,6},{5,7},{6,4},{7,5},{8,10},{9,11},{10,... | collective-permute-start | bytes 835592 | tf_op jit(solution)/shard_map/ppermute | solution.py:202
  8.8 7.8 %collective-permute-start.4 = (f32[4,136,128]{2,1,0:T(8,128)S(1)}, f32[4,136,128]{2,1,0:T(8,128)S(1)}, u32[]{:S(2)}, u32[]{:S(2)}) collective-permute-start(f32[4,136,128]{2,1,0:T(8,128)S(1)} %get-tuple-element.20), channel_id=1, source_target_pairs={{0,1},{1,0},{2,3},{3,2},{4,5},{5,4},{6,7},{7,6},{8,9},{9,8},{10,11... | collective-permute-start | bytes 835592 | tf_op jit(solution)/shard_map/ppermute | solution.py:202
  16.8 17.1 %collective-permute-start.5 = (f32[1056,128]{1,0:T(8,128)S(1)}, f32[1056,128]{1,0:T(8,128)S(1)}, u32[]{:S(2)}, u32[]{:S(2)}) collective-permute-start(f32[1056,128]{1,0:T(8,128)S(1)} %get-tuple-element.51), channel_id=1, source_target_pairs={{0,2},{1,3},{2,0},{3,1},{4,6},{5,7},{6,4},{7,5},{8,10},{9,11},{10,... | collective-permute-start | bytes 1622024 | tf_op jit(solution)/shard_map/ppermute | solution.py:202
  17.4 16.4 %collective-permute-start.2 = (f32[784,128]{1,0:T(8,128)S(1)}, f32[784,128]{1,0:T(8,128)S(1)}, u32[]{:S(2)}, u32[]{:S(2)}) collective-permute-start(f32[784,128]{1,0:T(8,128)S(1)} %pad_maximum_fusion.4), channel_id=1, source_target_pairs={{0,4},{1,5},{2,6},{3,7},{4,0},{5,1},{6,2},{7,3},{8,12},{9,13},{10,... | collective-permute-start | bytes 1204232 | tf_op jit(solution)/shard_map/ppermute | solution.py:202
  19.1 14.9 %collective-permute-start.11 = (f32[2,136,128]{2,1,0:T(8,128)S(1)}, f32[2,136,128]{2,1,0:T(8,128)S(1)}, u32[]{:S(2)}, u32[]{:S(2)}) collective-permute-start(f32[2,136,128]{2,1,0:T(8,128)S(1)} %pad_maximum_fusion.14), channel_id=1, source_target_pairs={{0,12},{1,13},{2,14},{3,15},{4,8},{5,9},{6,10},{7,11},{8,4},{9,5},... | collective-permute-start | bytes 417800 | tf_op jit(solution)/shard_map/ppermute | solution.py:202
  19.4 14.5 %collective-permute-start.3 = (f32[1056,128]{1,0:T(8,128)S(1)}, f32[1056,128]{1,0:T(8,128)S(1)}, u32[]{:S(2)}, u32[]{:S(2)}) collective-permute-start(f32[1056,128]{1,0:T(8,128)S(1)} %get-tuple-element.52), channel_id=1, source_target_pairs={{0,1},{1,0},{2,3},{3,2},{4,5},{5,4},{6,7},{7,6},{8,9},{9,8},{10,11... | collective-permute-start | bytes 1622024 | tf_op jit(solution)/shard_map/ppermute | solution.py:202
  21.0 13.1 %collective-permute-start.10 = (f32[2,136,128]{2,1,0:T(8,128)S(1)}, f32[2,136,128]{2,1,0:T(8,128)S(1)}, u32[]{:S(2)}, u32[]{:S(2)}) collective-permute-start(f32[2,136,128]{2,1,0:T(8,128)S(1)} %pad_maximum_fusion.13), channel_id=1, source_target_pairs={{0,8},{1,9},{2,10},{3,11},{4,12},{5,13},{6,14},{7,15},{8,0},{9,1},... | collective-permute-start | bytes 417800 | tf_op jit(solution)/shard_map/ppermute | solution.py:202
  34.0 9.2 %collective-permute-start.13 = (f32[2,136,128]{2,1,0:T(8,128)S(1)}, f32[2,136,128]{2,1,0:T(8,128)S(1)}, u32[]{:S(2)}, u32[]{:S(2)}) collective-permute-start(f32[2,136,128]{2,1,0:T(8,128)S(1)} %get-tuple-element.25), channel_id=1, source_target_pairs={{0,4},{1,5},{2,6},{3,7},{4,0},{5,1},{6,2},{7,3},{8,12},{9,13},{10,... | collective-permute-start | bytes 417800 | tf_op jit(solution)/shard_map/ppermute | solution.py:202
  34.1 10.6 %collective-permute-start.14 = (f32[2,136,128]{2,1,0:T(8,128)S(1)}, f32[2,136,128]{2,1,0:T(8,128)S(1)}, u32[]{:S(2)}, u32[]{:S(2)}) collective-permute-start(f32[2,136,128]{2,1,0:T(8,128)S(1)} %get-tuple-element.26), channel_id=1, source_target_pairs={{0,8},{1,9},{2,10},{3,11},{4,12},{5,13},{6,14},{7,15},{8,0},{9,1},... | collective-permute-start | bytes 417800 | tf_op jit(solution)/shard_map/ppermute | solution.py:202
  36.6 8.2 %collective-permute-start.15 = (f32[2,136,128]{2,1,0:T(8,128)S(1)}, f32[2,136,128]{2,1,0:T(8,128)S(1)}, u32[]{:S(2)}, u32[]{:S(2)}) collective-permute-start(f32[2,136,128]{2,1,0:T(8,128)S(1)} %get-tuple-element.27), channel_id=1, source_target_pairs={{0,12},{1,13},{2,14},{3,15},{4,8},{5,9},{6,10},{7,11},{8,4},{9,5},... | collective-permute-start | bytes 417800 | tf_op jit(solution)/shard_map/ppermute | solution.py:202
  38.6 8.8 %collective-permute-start.7 = (f32[3,256,128]{2,1,0:T(8,128)S(1)}, f32[3,256,128]{2,1,0:T(8,128)S(1)}, u32[]{:S(2)}, u32[]{:S(2)}) collective-permute-start(f32[3,256,128]{2,1,0:T(8,128)S(1)} %get-tuple-element.49), channel_id=1, source_target_pairs={{0,2},{1,3},{2,0},{3,1},{4,6},{5,7},{6,4},{7,5},{8,10},{9,11},{10,... | collective-permute-start | bytes 1179656 | tf_op jit(solution)/shard_map/ppermute | solution.py:202
  41.7 9.1 %collective-permute-start.6 = (f32[3,256,128]{2,1,0:T(8,128)S(1)}, f32[3,256,128]{2,1,0:T(8,128)S(1)}, u32[]{:S(2)}, u32[]{:S(2)}) collective-permute-start(f32[3,256,128]{2,1,0:T(8,128)S(1)} %get-tuple-element.50), channel_id=1, source_target_pairs={{0,1},{1,0},{2,3},{3,2},{4,5},{5,4},{6,7},{7,6},{8,9},{9,8},{10,11... | collective-permute-start | bytes 1179656 | tf_op jit(solution)/shard_map/ppermute | solution.py:202
  43.2 12.8 %collective-permute-start.12 = (f32[10,136,128]{2,1,0:T(8,128)S(1)}, f32[10,136,128]{2,1,0:T(8,128)S(1)}, u32[]{:S(2)}, u32[]{:S(2)}) collective-permute-start(f32[10,136,128]{2,1,0:T(8,128)S(1)} %constant_dynamic-update-slice_fusion.refs_0_), channel_id=1, source_target_pairs={{0,16},{16,0},{1,17},{17,1},{2,18},{18,2},{3,19},{19,3},{4,20},{20... | collective-permute-start | bytes 2088968 | tf_op jit(solution)/shard_map/ppermute | solution.py:202
  44.8 11.2 %collective-permute-start.16 = (f32[6,136,128]{2,1,0:T(8,128)S(1)}, f32[6,136,128]{2,1,0:T(8,128)S(1)}, u32[]{:S(2)}, u32[]{:S(2)}) collective-permute-start(f32[6,136,128]{2,1,0:T(8,128)S(1)} %constant_dynamic-update-slice_fusion.4.refs_2_), channel_id=1, source_target_pairs={{0,16},{16,0},{1,17},{17,1},{2,18},{18,2},{3,19},{19,3},{4,20},{20... | collective-permute-start | bytes 1253384 | tf_op jit(solution)/shard_map/ppermute | solution.py:202
  47.4 5.0 %collective-permute-start.8 = (f32[1,256,128]{2,1,0:T(8,128)S(1)}, f32[1,256,128]{2,1,0:T(8,128)S(1)}, u32[]{:S(2)}, u32[]{:S(2)}) collective-permute-start(f32[1,256,128]{2,1,0:T(8,128)S(1)} %get-tuple-element.39), channel_id=1, source_target_pairs={{0,1},{1,0},{2,3},{3,2},{4,5},{5,4},{6,7},{7,6},{8,9},{9,8},{10,11... | collective-permute-start | bytes 393224 | tf_op jit(solution)/shard_map/ppermute | solution.py:202
  50.7 5.0 %collective-permute-start.9 = (f32[1,256,128]{2,1,0:T(8,128)S(1)}, f32[1,256,128]{2,1,0:T(8,128)S(1)}, u32[]{:S(2)}, u32[]{:S(2)}) collective-permute-start(f32[1,256,128]{2,1,0:T(8,128)S(1)} %get-tuple-element.37), channel_id=1, source_target_pairs={{0,2},{1,3},{2,0},{3,1},{4,6},{5,7},{6,4},{7,5},{8,10},{9,11},{10,... | collective-permute-start | bytes 393224 | tf_op jit(solution)/shard_map/ppermute | solution.py:202

commit v11 on v10

--- a/solution.py
+++ b/solution.py
@@ -10,7 +10,6 @@
 KT = 16
 CT = 8
 SLOT = 2
-HINT = 256 * 1024 * 1024
 META = 8
 
 
@@ -89,7 +88,9 @@
         out_shape=jax.ShapeDtypeStruct((KT, rows, 2 * width), jnp.bfloat16),
         in_specs=[vmem] * len(pieces),
         out_specs=vmem,
-        cost_estimate=pl.CostEstimate(flops=0, bytes_accessed=HINT, transcendentals=0),
+        cost_estimate=pl.CostEstimate(
+            flops=0, bytes_accessed=8 * KT * rows * width, transcendentals=0
+        ),
         compiler_params=pltpu.CompilerParams(vmem_limit_bytes=16 * 1024 * 1024),
     )(*pieces)
 
@@ -227,10 +228,10 @@
     )
     half = targets // 8
     even_come, odd_come = hop(even_sent, 1), hop(odd_sent, 2)
+    late = hop(held, 4)
     first = [jnp.stack([even_kept[z], even_come[z]]) for z in range(half)]
     first = [plane for z in range(half) for plane in (first[z], jnp.stack([odd_kept[z], odd_come[z]]))]
-    near_come, late = hop_both(first[1], held, 4)
-    come_first = [near_come] + [hop(plane, 4 * z) for z, plane in enumerate(first) if z > 1]
+    come_first = [hop(plane, 4 * z) for z, plane in enumerate(first) if z >= half]
     even_last, over_y = hop_both(jnp.concatenate([even_kept[half:], even_come[half:]]), held, 2)
     odd_last, over_x = hop_both(jnp.concatenate([odd_kept[half:], odd_come[half:]]), held, 1)
     last = [
@@ -238,7 +239,9 @@
     ]
     residual = fetch(residual_in)
     last, come_first, residual = lax.optimization_barrier((last, come_first, residual))
-    come_last = [hop(plane, 4 * z) for z, plane in enumerate(last) if z]
+    near = [jnp.concatenate([first[z], last[z]]) for z in range(half)]
+    near = [near[0]] + [hop(plane, 4 * z) for z, plane in enumerate(near) if z]
+    come_last = [hop(last[z], 4 * z) for z in range(half, 2 * half)]
     cut = len(at) // 2
     come = hop(jnp.concatenate([late, over_y[:cut]]), 1)
     late_x, diagonal_x = come[: len(at)], come[len(at) :]
@@ -249,7 +252,7 @@
     positions = [tuple(p ^ step for p in at) for step in (0, 4, 1, 2, 5, 6)]
     positions += [tuple(p ^ step for p in part) for step in (3, 7) for part in (at[:cut], at[cut:])]
     groups = []
-    for planes in ([first[0], last[0]] + come_first, come_last):
+    for planes in (near[:1] + come_first, near[1:] + come_last):
         mine = jnp.concatenate(planes, axis=0)
         groups.append(
             [mine] + [send(mine, "row", lambda i: (i + q) % rows_axis) for q in range(1, rows_axis)]

time: 60.4 us -> 57.6 us (0.954)
  waiting for transfers between devices: 27.1 us -> 25.1 us
  starting transfers between devices: 24.4 us -> 23.7 us
    ppermute x17, waiting for transfers between devices: 27.1 us -> 25.1 us  [send(): return lax.ppermute(x, axis, [(i, partner(i)) for i in range(size)])]
    ppermute x17, starting transfers between devices: 24.4 us -> 23.7 us  [send(): return lax.ppermute(x, axis, [(i, partner(i)) for i in range(size)])]
  transfers between devices with their start and end apart: 17 -> 17, of which waited for: 9 -> 8; matrix products, arithmetic and copies ran while one was open for 2% -> 2% of each run, Pallas kernels for 3% -> 3%
where the time goes in v11:
time: 57.6 us; the launch traced here: 57.4 us
  waiting for transfers between devices  25.1 us (44%)
  starting transfers between devices  23.7 us (41%)
  Pallas kernels  5.96 us (10%)
  local copies, waits for them, and re-layouts  1.38 us (2%)
  other arithmetic  0.98 us (2%)
    ppermute x17, waiting for transfers between devices, send(): return lax.ppermute(x, axis, [(i, partner(i)) for i in range(size)])  25.1 us
    ppermute x17, starting transfers between devices, send(): return lax.ppermute(x, axis, [(i, partner(i)) for i in range(size)])  23.7 us
    pallas_call x1, Pallas kernels, contract(): pl.pallas_call(functools.partial(contract_kernel, len(groups), len(groups...  4.16 us
    pallas_call x1, Pallas kernels, pack(): pl.pallas_call(pack_kernel, out_shape=[out] * 4, in_specs=[pl.BlockSpec(m...  1.48 us
  transfers between devices with their start and end apart: 17, of which 8 were waited for; matrix products, arithmetic and copies ran while one was open for 2% of the time, Pallas kernels for 3%

profile of v11, /device:TPU:0, one launch (start us, length us, event | category | flops | bytes accessed | tf_op | source)
XLA Modules:
  0.0 57.4 jit_solution(4393120209861518302)
XLA Ops:
  0.0 0.0 copy-start
  0.0 4.0 %collective-permute-start = (f32[1,256,128]{2,1,0:T(8,128)}, f32[1,256,128]{2,1,0:T(8,128)S(1)}, u32[]{:S(2)}, u32[]{:S(2)}) collective-permute-start(f32[1,256,128]{2,1,0:T(8,128)} %bitcast.37), channel_id=1, source_target_pairs={{0,8},{1,9},{2,10},{3,11},{4,12},{5,13},{6,14},{7,15},{8,0},{9,1},... | collective-permute-start | bytes 393224 | tf_op jit(solution)/shard_map/ppermute | solution.py:203
  4.0 0.7 %fusion.1.words_ref = s32[16]{0:T(128)S(1)} fusion(s32[16]{0:T(128)} %param.11, s32[16]{0:T(128)} %param.10, s32[16,1]{0,1:T(1,128)} %param.9), kind=kLoop, calls=%fused_computation.34 | loop fusion | flops 64 | bytes 256 | tf_op jit(solution)/shard_map/add | solution.py:56
  4.7 0.0 copy-start.1
  4.7 1.0 %copy-done.1 = f32[16,64,128]{2,1,0:T(8,128)S(1)} copy-done((f32[16,64,128]{2,1,0:T(8,128)S(1)}, f32[16,64,128]{2,1,0:T(8,128)}, u32[]{:S(2)}) %copy-start.1) | copy-done | bytes 524312
  5.8 0.0 copy-start.2
  5.8 1.5 %shard_map.64 = (f32[4,136,128]{2,1,0:T(8,128)S(1)}, f32[4,136,128]{2,1,0:T(8,128)S(1)}, f32[4,136,128]{2,1,0:T(8,128)S(1)}, f32[4,136,128]{2,1,0:T(8,128)S(1)}) custom-call(s32[16]{0:T(128)S(1)} %fusion.1.words_ref, f32[16,64,128]{2,1,0:T(8,128)S(1)} %copy-done.1), custom_call_target="tpu_custom_call" | custom-call | bytes 1572864 | tf_op jit(solution)/shard_map/pallas_call | solution.py:58
  7.3 1.6 %collective-permute-start.2 = (f32[4,136,128]{2,1,0:T(8,128)S(1)}, f32[4,136,128]{2,1,0:T(8,128)S(1)}, u32[]{:S(2)}, u32[]{:S(2)}) collective-permute-start(f32[4,136,128]{2,1,0:T(8,128)S(1)} %get-tuple-element.17), channel_id=1, source_target_pairs={{0,2},{1,3},{2,0},{3,1},{4,6},{5,7},{6,4},{7,5},{8,10},{9,11},{10,... | collective-permute-start | bytes 835592 | tf_op jit(solution)/shard_map/ppermute | solution.py:203
  8.8 1.5 %collective-permute-start.4 = (f32[4,136,128]{2,1,0:T(8,128)S(1)}, f32[4,136,128]{2,1,0:T(8,128)S(1)}, u32[]{:S(2)}, u32[]{:S(2)}) collective-permute-start(f32[4,136,128]{2,1,0:T(8,128)S(1)} %get-tuple-element.19), channel_id=1, source_target_pairs={{0,1},{1,0},{2,3},{3,2},{4,5},{5,4},{6,7},{7,6},{8,9},{9,8},{10,11... | collective-permute-start | bytes 835592 | tf_op jit(solution)/shard_map/ppermute | solution.py:203
  10.4 0.0 copy-done
  10.4 0.1 shard_map.66.refs_4_
  10.5 0.1 collective-permute-done
  10.6 0.0 copy-done.2
  10.6 1.6 %collective-permute-start.1 = (f32[2,256,128]{2,1,0:T(8,128)S(1)}, f32[2,256,128]{2,1,0:T(8,128)S(1)}, u32[]{:S(2)}, u32[]{:S(2)}) collective-permute-start(f32[2,256,128]{2,1,0:T(8,128)S(1)} %pad_maximum_fusion.7.refs_0_), channel_id=1, source_target_pairs={{0,4},{1,5},{2,6},{3,7},{4,0},{5,1},{6,2},{7,3},{8,12},{9,13},{10,... | collective-permute-start | bytes 786440 | tf_op jit(solution)/shard_map/ppermute | solution.py:203
  12.2 3.3 %collective-permute-done.2 = f32[4,136,128]{2,1,0:T(8,128)S(1)} collective-permute-done((f32[4,136,128]{2,1,0:T(8,128)S(1)}, f32[4,136,128]{2,1,0:T(8,128)S(1)}, u32[]{:S(2)}, u32[]{:S(2)}) %collective-permute-start.2) | collective-permute-done | bytes 278560 | tf_op jit(solution)/shard_map/ppermute | solution.py:203
  15.5 1.2 %collective-permute-done.4 = f32[4,136,128]{2,1,0:T(8,128)S(1)} collective-permute-done((f32[4,136,128]{2,1,0:T(8,128)S(1)}, f32[4,136,128]{2,1,0:T(8,128)S(1)}, u32[]{:S(2)}, u32[]{:S(2)}) %collective-permute-start.4) | collective-permute-done | bytes 278560 | tf_op jit(solution)/shard_map/ppermute | solution.py:203
  16.7 0.1 pad_maximum_fusion
  16.8 0.6 collective-permute-start.5
  17.4 1.5 %collective-permute-start.11 = (f32[2,136,128]{2,1,0:T(8,128)S(1)}, f32[2,136,128]{2,1,0:T(8,128)S(1)}, u32[]{:S(2)}, u32[]{:S(2)}) collective-permute-start(f32[2,136,128]{2,1,0:T(8,128)S(1)} %pad_maximum_fusion.13), channel_id=1, source_target_pairs={{0,12},{1,13},{2,14},{3,15},{4,8},{5,9},{6,10},{7,11},{8,4},{9,5},... | collective-permute-start | bytes 417800 | tf_op jit(solution)/shard_map/ppermute | solution.py:203
  18.9 1.5 %collective-permute-start.3 = (f32[1056,128]{1,0:T(8,128)S(1)}, f32[1056,128]{1,0:T(8,128)S(1)}, u32[]{:S(2)}, u32[]{:S(2)}) collective-permute-start(f32[1056,128]{1,0:T(8,128)S(1)} %get-tuple-element.50), channel_id=1, source_target_pairs={{0,1},{1,0},{2,3},{3,2},{4,5},{5,4},{6,7},{7,6},{8,9},{9,8},{10,11... | collective-permute-start | bytes 1622024 | tf_op jit(solution)/shard_map/ppermute | solution.py:203
  20.4 1.7 %collective-permute-start.10 = (f32[2,136,128]{2,1,0:T(8,128)S(1)}, f32[2,136,128]{2,1,0:T(8,128)S(1)}, u32[]{:S(2)}, u32[]{:S(2)}) collective-permute-start(f32[2,136,128]{2,1,0:T(8,128)S(1)} %pad_maximum_fusion.12), channel_id=1, source_target_pairs={{0,8},{1,9},{2,10},{3,11},{4,12},{5,13},{6,14},{7,15},{8,0},{9,1},... | collective-permute-start | bytes 417800 | tf_op jit(solution)/shard_map/ppermute | solution.py:203
  22.1 7.3 %collective-permute-done.5 = f32[1056,128]{1,0:T(8,128)S(1)} collective-permute-done((f32[1056,128]{1,0:T(8,128)S(1)}, f32[1056,128]{1,0:T(8,128)S(1)}, u32[]{:S(2)}, u32[]{:S(2)}) %collective-permute-start.5) | collective-permute-done | bytes 540704 | tf_op jit(solution)/shard_map/ppermute | solution.py:203
  29.4 1.7 %collective-permute-done.3 = f32[1056,128]{1,0:T(8,128)S(1)} collective-permute-done((f32[1056,128]{1,0:T(8,128)S(1)}, f32[1056,128]{1,0:T(8,128)S(1)}, u32[]{:S(2)}, u32[]{:S(2)}) %collective-permute-start.3) | collective-permute-done | bytes 540704 | tf_op jit(solution)/shard_map/ppermute | solution.py:203
  31.2 0.0 collective-permute-done.11
  31.2 0.0 collective-permute-done.10
  31.2 1.6 %collective-permute-start.14 = (f32[2,136,128]{2,1,0:T(8,128)S(1)}, f32[2,136,128]{2,1,0:T(8,128)S(1)}, u32[]{:S(2)}, u32[]{:S(2)}) collective-permute-start(f32[2,136,128]{2,1,0:T(8,128)S(1)} %get-tuple-element.24), channel_id=1, source_target_pairs={{0,8},{1,9},{2,10},{3,11},{4,12},{5,13},{6,14},{7,15},{8,0},{9,1},... | collective-permute-start | bytes 417800 | tf_op jit(solution)/shard_map/ppermute | solution.py:203
  32.8 1.3 %collective-permute-start.15 = (f32[2,136,128]{2,1,0:T(8,128)S(1)}, f32[2,136,128]{2,1,0:T(8,128)S(1)}, u32[]{:S(2)}, u32[]{:S(2)}) collective-permute-start(f32[2,136,128]{2,1,0:T(8,128)S(1)} %get-tuple-element.25), channel_id=1, source_target_pairs={{0,12},{1,13},{2,14},{3,15},{4,8},{5,9},{6,10},{7,11},{8,4},{9,5},... | collective-permute-start | bytes 417800 | tf_op jit(solution)/shard_map/ppermute | solution.py:203
  34.1 0.8 %collective-permute-start.13 = (f32[4,136,128]{2,1,0:T(8,128)S(1)}, f32[4,136,128]{2,1,0:T(8,128)S(1)}, u32[]{:S(2)}, u32[]{:S(2)}) collective-permute-start(f32[4,136,128]{2,1,0:T(8,128)S(1)} %pad_maximum_fusion.6), channel_id=1, source_target_pairs={{0,4},{1,5},{2,6},{3,7},{4,0},{5,1},{6,2},{7,3},{8,12},{9,13},{10,... | collective-permute-start | bytes 835592 | tf_op jit(solution)/shard_map/ppermute | solution.py:203
  34.9 0.0 collective-permute-done.1.refs_1_
  34.9 0.1 pad_maximum_fusion.2
  34.9 1.5 %collective-permute-start.7 = (f32[3,256,128]{2,1,0:T(8,128)S(1)}, f32[3,256,128]{2,1,0:T(8,128)S(1)}, u32[]{:S(2)}, u32[]{:S(2)}) collective-permute-start(f32[3,256,128]{2,1,0:T(8,128)S(1)} %get-tuple-element.47), channel_id=1, source_target_pairs={{0,2},{1,3},{2,0},{3,1},{4,6},{5,7},{6,4},{7,5},{8,10},{9,11},{10,... | collective-permute-start | bytes 1179656 | tf_op jit(solution)/shard_map/ppermute | solution.py:203
  36.4 1.5 %collective-permute-start.6 = (f32[3,256,128]{2,1,0:T(8,128)S(1)}, f32[3,256,128]{2,1,0:T(8,128)S(1)}, u32[]{:S(2)}, u32[]{:S(2)}) collective-permute-start(f32[3,256,128]{2,1,0:T(8,128)S(1)} %get-tuple-element.48), channel_id=1, source_target_pairs={{0,1},{1,0},{2,3},{3,2},{4,5},{5,4},{6,7},{7,6},{8,9},{9,8},{10,11... | collective-permute-start | bytes 1179656 | tf_op jit(solution)/shard_map/ppermute | solution.py:203
  37.9 7.9 %collective-permute-done.13 = f32[4,136,128]{2,1,0:T(8,128)S(1)} collective-permute-done((f32[4,136,128]{2,1,0:T(8,128)S(1)}, f32[4,136,128]{2,1,0:T(8,128)S(1)}, u32[]{:S(2)}, u32[]{:S(2)}) %collective-permute-start.13) | collective-permute-done | bytes 278560 | tf_op jit(solution)/shard_map/ppermute | solution.py:203
  45.9 0.0 collective-permute-start.12
  45.9 0.0 collective-permute-done.14
  45.9 0.0 collective-permute-done.15
  45.9 0.6 collective-permute-start.16
  46.5 0.0 collective-permute-done.7
  46.5 1.2 %collective-permute-start.8 = (f32[1,256,128]{2,1,0:T(8,128)S(1)}, f32[1,256,128]{2,1,0:T(8,128)S(1)}, u32[]{:S(2)}, u32[]{:S(2)}) collective-permute-start(f32[1,256,128]{2,1,0:T(8,128)S(1)} %get-tuple-element.37), channel_id=1, source_target_pairs={{0,1},{1,0},{2,3},{3,2},{4,5},{5,4},{6,7},{7,6},{8,9},{9,8},{10,11... | collective-permute-start | bytes 393224 | tf_op jit(solution)/shard_map/ppermute | solution.py:203
  47.8 0.0 collective-permute-done.6
  47.8 1.4 %collective-permute-start.9 = (f32[1,256,128]{2,1,0:T(8,128)S(1)}, f32[1,256,128]{2,1,0:T(8,128)S(1)}, u32[]{:S(2)}, u32[]{:S(2)}) collective-permute-start(f32[1,256,128]{2,1,0:T(8,128)S(1)} %get-tuple-element.35), channel_id=1, source_target_pairs={{0,2},{1,3},{2,0},{3,1},{4,6},{5,7},{6,4},{7,5},{8,10},{9,11},{10,... | collective-permute-start | bytes 393224 | tf_op jit(solution)/shard_map/ppermute | solution.py:203
  49.3 2.7 %collective-permute-done.8.refs_8_ = f32[1,256,128]{2,1,0:T(8,128)S(1)} collective-permute-done((f32[1,256,128]{2,1,0:T(8,128)S(1)}, f32[1,256,128]{2,1,0:T(8,128)S(1)}, u32[]{:S(2)}, u32[]{:S(2)}) %collective-permute-start.8) | collective-permute-done | bytes 131104 | tf_op jit(solution)/shard_map/ppermute | solution.py:203
  52.0 1.0 %collective-permute-done.9.refs_9_ = f32[1,256,128]{2,1,0:T(8,128)S(1)} collective-permute-done((f32[1,256,128]{2,1,0:T(8,128)S(1)}, f32[1,256,128]{2,1,0:T(8,128)S(1)}, u32[]{:S(2)}, u32[]{:S(2)}) %collective-permute-start.9) | collective-permute-done | bytes 131104 | tf_op jit(solution)/shard_map/ppermute | solution.py:203
  53.0 0.3 shard_map.65.split_ref
  53.3 0.0 collective-permute-done.12.refs_1_
  53.3 0.0 collective-permute-done.16.refs_3_
  53.3 4.2 %shard_map.67 = f32[256,1024]{1,0:T(8,128)} custom-call(bf16[16,256,256]{2,1,0:T(8,128)(2,1)S(1)} %shard_map.65.split_ref, f32[8,136,128]{2,1,0:T(8,128)S(1)} %constant_dynamic-update-slice_fusion.refs_0_, f32[8,136,128]{2,1,0:T(8,128)S(1)} %collective-permute-done.12.refs_1_, f32[8,136,128]{2,1,0:T(8,128)S(1)} %constant_dynamic-update-slice_fusion.3.refs_2_, ...), custom_call_target="tpu_custom_call" | custom-call | tf_op jit(solution)/shard_map/pallas_call | solution.py:173
  (32 shorter events, 0.5 us)
Async XLA Ops:
  0.0 10.4 %copy-start = (f32[256,1024]{1,0:T(8,128)S(1)}, f32[256,1024]{1,0:T(8,128)}, u32[]{:S(2)}) copy-start(f32[256,1024]{1,0:T(8,128)} %x_ref.1) | copy-start | bytes 3145732
  0.0 10.5 %collective-permute-start = (f32[1,256,128]{2,1,0:T(8,128)}, f32[1,256,128]{2,1,0:T(8,128)S(1)}, u32[]{:S(2)}, u32[]{:S(2)}) collective-permute-start(f32[1,256,128]{2,1,0:T(8,128)} %bitcast.37), channel_id=1, source_target_pairs={{0,8},{1,9},{2,10},{3,11},{4,12},{5,13},{6,14},{7,15},{8,0},{9,1},... | collective-permute-start | bytes 393224 | tf_op jit(solution)/shard_map/ppermute | solution.py:203
  4.7 1.0 %copy-start.1 = (f32[16,64,128]{2,1,0:T(8,128)S(1)}, f32[16,64,128]{2,1,0:T(8,128)}, u32[]{:S(2)}) copy-start(f32[16,64,128]{2,1,0:T(8,128)} %tiles_ref.1) | copy-start | bytes 1572868
  5.8 4.8 %copy-start.2 = (f32[256,128]{1,0:T(8,128)S(1)}, f32[256,128]{1,0:T(8,128)}, u32[]{:S(2)}) copy-start(f32[256,128]{1,0:T(8,128)} %param.7) | copy-start | bytes 393220
  7.3 8.2 %collective-permute-start.2 = (f32[4,136,128]{2,1,0:T(8,128)S(1)}, f32[4,136,128]{2,1,0:T(8,128)S(1)}, u32[]{:S(2)}, u32[]{:S(2)}) collective-permute-start(f32[4,136,128]{2,1,0:T(8,128)S(1)} %get-tuple-element.17), channel_id=1, source_target_pairs={{0,2},{1,3},{2,0},{3,1},{4,6},{5,7},{6,4},{7,5},{8,10},{9,11},{10,... | collective-permute-start | bytes 835592 | tf_op jit(solution)/shard_map/ppermute | solution.py:203
  8.8 7.8 %collective-permute-start.4 = (f32[4,136,128]{2,1,0:T(8,128)S(1)}, f32[4,136,128]{2,1,0:T(8,128)S(1)}, u32[]{:S(2)}, u32[]{:S(2)}) collective-permute-start(f32[4,136,128]{2,1,0:T(8,128)S(1)} %get-tuple-element.19), channel_id=1, source_target_pairs={{0,1},{1,0},{2,3},{3,2},{4,5},{5,4},{6,7},{7,6},{8,9},{9,8},{10,11... | collective-permute-start | bytes 835592 | tf_op jit(solution)/shard_map/ppermute | solution.py:203
  10.6 24.3 %collective-permute-start.1 = (f32[2,256,128]{2,1,0:T(8,128)S(1)}, f32[2,256,128]{2,1,0:T(8,128)S(1)}, u32[]{:S(2)}, u32[]{:S(2)}) collective-permute-start(f32[2,256,128]{2,1,0:T(8,128)S(1)} %pad_maximum_fusion.7.refs_0_), channel_id=1, source_target_pairs={{0,4},{1,5},{2,6},{3,7},{4,0},{5,1},{6,2},{7,3},{8,12},{9,13},{10,... | collective-permute-start | bytes 786440 | tf_op jit(solution)/shard_map/ppermute | solution.py:203
  16.8 12.6 %collective-permute-start.5 = (f32[1056,128]{1,0:T(8,128)S(1)}, f32[1056,128]{1,0:T(8,128)S(1)}, u32[]{:S(2)}, u32[]{:S(2)}) collective-permute-start(f32[1056,128]{1,0:T(8,128)S(1)} %get-tuple-element.49), channel_id=1, source_target_pairs={{0,2},{1,3},{2,0},{3,1},{4,6},{5,7},{6,4},{7,5},{8,10},{9,11},{10,... | collective-permute-start | bytes 1622024 | tf_op jit(solution)/shard_map/ppermute | solution.py:203
  17.4 13.8 %collective-permute-start.11 = (f32[2,136,128]{2,1,0:T(8,128)S(1)}, f32[2,136,128]{2,1,0:T(8,128)S(1)}, u32[]{:S(2)}, u32[]{:S(2)}) collective-permute-start(f32[2,136,128]{2,1,0:T(8,128)S(1)} %pad_maximum_fusion.13), channel_id=1, source_target_pairs={{0,12},{1,13},{2,14},{3,15},{4,8},{5,9},{6,10},{7,11},{8,4},{9,5},... | collective-permute-start | bytes 417800 | tf_op jit(solution)/shard_map/ppermute | solution.py:203
  18.9 12.2 %collective-permute-start.3 = (f32[1056,128]{1,0:T(8,128)S(1)}, f32[1056,128]{1,0:T(8,128)S(1)}, u32[]{:S(2)}, u32[]{:S(2)}) collective-permute-start(f32[1056,128]{1,0:T(8,128)S(1)} %get-tuple-element.50), channel_id=1, source_target_pairs={{0,1},{1,0},{2,3},{3,2},{4,5},{5,4},{6,7},{7,6},{8,9},{9,8},{10,11... | collective-permute-start | bytes 1622024 | tf_op jit(solution)/shard_map/ppermute | solution.py:203
  20.4 10.8 %collective-permute-start.10 = (f32[2,136,128]{2,1,0:T(8,128)S(1)}, f32[2,136,128]{2,1,0:T(8,128)S(1)}, u32[]{:S(2)}, u32[]{:S(2)}) collective-permute-start(f32[2,136,128]{2,1,0:T(8,128)S(1)} %pad_maximum_fusion.12), channel_id=1, source_target_pairs={{0,8},{1,9},{2,10},{3,11},{4,12},{5,13},{6,14},{7,15},{8,0},{9,1},... | collective-permute-start | bytes 417800 | tf_op jit(solution)/shard_map/ppermute | solution.py:203
  31.2 14.7 %collective-permute-start.14 = (f32[2,136,128]{2,1,0:T(8,128)S(1)}, f32[2,136,128]{2,1,0:T(8,128)S(1)}, u32[]{:S(2)}, u32[]{:S(2)}) collective-permute-start(f32[2,136,128]{2,1,0:T(8,128)S(1)} %get-tuple-element.24), channel_id=1, source_target_pairs={{0,8},{1,9},{2,10},{3,11},{4,12},{5,13},{6,14},{7,15},{8,0},{9,1},... | collective-permute-start | bytes 417800 | tf_op jit(solution)/shard_map/ppermute | solution.py:203
  32.8 13.1 %collective-permute-start.15 = (f32[2,136,128]{2,1,0:T(8,128)S(1)}, f32[2,136,128]{2,1,0:T(8,128)S(1)}, u32[]{:S(2)}, u32[]{:S(2)}) collective-permute-start(f32[2,136,128]{2,1,0:T(8,128)S(1)} %get-tuple-element.25), channel_id=1, source_target_pairs={{0,12},{1,13},{2,14},{3,15},{4,8},{5,9},{6,10},{7,11},{8,4},{9,5},... | collective-permute-start | bytes 417800 | tf_op jit(solution)/shard_map/ppermute | solution.py:203
  34.1 11.8 %collective-permute-start.13 = (f32[4,136,128]{2,1,0:T(8,128)S(1)}, f32[4,136,128]{2,1,0:T(8,128)S(1)}, u32[]{:S(2)}, u32[]{:S(2)}) collective-permute-start(f32[4,136,128]{2,1,0:T(8,128)S(1)} %pad_maximum_fusion.6), channel_id=1, source_target_pairs={{0,4},{1,5},{2,6},{3,7},{4,0},{5,1},{6,2},{7,3},{8,12},{9,13},{10,... | collective-permute-start | bytes 835592 | tf_op jit(solution)/shard_map/ppermute | solution.py:203
  34.9 11.6 %collective-permute-start.7 = (f32[3,256,128]{2,1,0:T(8,128)S(1)}, f32[3,256,128]{2,1,0:T(8,128)S(1)}, u32[]{:S(2)}, u32[]{:S(2)}) collective-permute-start(f32[3,256,128]{2,1,0:T(8,128)S(1)} %get-tuple-element.47), channel_id=1, source_target_pairs={{0,2},{1,3},{2,0},{3,1},{4,6},{5,7},{6,4},{7,5},{8,10},{9,11},{10,... | collective-permute-start | bytes 1179656 | tf_op jit(solution)/shard_map/ppermute | solution.py:203
  36.4 11.4 %collective-permute-start.6 = (f32[3,256,128]{2,1,0:T(8,128)S(1)}, f32[3,256,128]{2,1,0:T(8,128)S(1)}, u32[]{:S(2)}, u32[]{:S(2)}) collective-permute-start(f32[3,256,128]{2,1,0:T(8,128)S(1)} %get-tuple-element.48), channel_id=1, source_target_pairs={{0,1},{1,0},{2,3},{3,2},{4,5},{5,4},{6,7},{7,6},{8,9},{9,8},{10,11... | collective-permute-start | bytes 1179656 | tf_op jit(solution)/shard_map/ppermute | solution.py:203
  45.9 7.4 %collective-permute-start.12 = (f32[8,136,128]{2,1,0:T(8,128)S(1)}, f32[8,136,128]{2,1,0:T(8,128)S(1)}, u32[]{:S(2)}, u32[]{:S(2)}) collective-permute-start(f32[8,136,128]{2,1,0:T(8,128)S(1)} %constant_dynamic-update-slice_fusion.refs_0_), channel_id=1, source_target_pairs={{0,16},{16,0},{1,17},{17,1},{2,18},{18,2},{3,19},{19,3},{4,20},{20... | collective-permute-start | bytes 1671176 | tf_op jit(solution)/shard_map/ppermute | solution.py:203
  45.9 7.3 %collective-permute-start.16 = (f32[8,136,128]{2,1,0:T(8,128)S(1)}, f32[8,136,128]{2,1,0:T(8,128)S(1)}, u32[]{:S(2)}, u32[]{:S(2)}) collective-permute-start(f32[8,136,128]{2,1,0:T(8,128)S(1)} %constant_dynamic-update-slice_fusion.3.refs_2_), channel_id=1, source_target_pairs={{0,16},{16,0},{1,17},{17,1},{2,18},{18,2},{3,19},{19,3},{4,20},{20... | collective-permute-start | bytes 1671176 | tf_op jit(solution)/shard_map/ppermute | solution.py:203
  46.5 5.5 %collective-permute-start.8 = (f32[1,256,128]{2,1,0:T(8,128)S(1)}, f32[1,256,128]{2,1,0:T(8,128)S(1)}, u32[]{:S(2)}, u32[]{:S(2)}) collective-permute-start(f32[1,256,128]{2,1,0:T(8,128)S(1)} %get-tuple-element.37), channel_id=1, source_target_pairs={{0,1},{1,0},{2,3},{3,2},{4,5},{5,4},{6,7},{7,6},{8,9},{9,8},{10,11... | collective-permute-start | bytes 393224 | tf_op jit(solution)/shard_map/ppermute | solution.py:203
  47.8 5.2 %collective-permute-start.9 = (f32[1,256,128]{2,1,0:T(8,128)S(1)}, f32[1,256,128]{2,1,0:T(8,128)S(1)}, u32[]{:S(2)}, u32[]{:S(2)}) collective-permute-start(f32[1,256,128]{2,1,0:T(8,128)S(1)} %get-tuple-element.35), channel_id=1, source_target_pairs={{0,2},{1,3},{2,0},{3,1},{4,6},{5,7},{6,4},{7,5},{8,10},{9,11},{10,... | collective-permute-start | bytes 393224 | tf_op jit(solution)/shard_map/ppermute | solution.py:203

commit v12 on v11

--- a/solution.py
+++ b/solution.py
@@ -232,8 +232,14 @@
     first = [jnp.stack([even_kept[z], even_come[z]]) for z in range(half)]
     first = [plane for z in range(half) for plane in (first[z], jnp.stack([odd_kept[z], odd_come[z]]))]
     come_first = [hop(plane, 4 * z) for z, plane in enumerate(first) if z >= half]
-    even_last, over_y = hop_both(jnp.concatenate([even_kept[half:], even_come[half:]]), held, 2)
-    odd_last, over_x = hop_both(jnp.concatenate([odd_kept[half:], odd_come[half:]]), held, 1)
+    cut = len(at) // 2
+    late_a, late_b = late[:cut], late[cut:]
+    even_last, over_y = hop_both(
+        jnp.concatenate([even_kept[half:], even_come[half:]]), jnp.concatenate([held, late_b]), 2
+    )
+    odd_last, over_x = hop_both(
+        jnp.concatenate([odd_kept[half:], odd_come[half:]]), jnp.concatenate([held, late_a]), 1
+    )
     last = [
         jnp.stack([come[z], come[half + z]]) for z in range(half) for come in (even_last, odd_last)
     ]
@@ -242,15 +248,22 @@
     near = [jnp.concatenate([first[z], last[z]]) for z in range(half)]
     near = [near[0]] + [hop(plane, 4 * z) for z, plane in enumerate(near) if z]
     come_last = [hop(last[z], 4 * z) for z in range(half, 2 * half)]
-    cut = len(at) // 2
-    come = hop(jnp.concatenate([late, over_y[:cut]]), 1)
-    late_x, diagonal_x = come[: len(at)], come[len(at) :]
-    come = hop(jnp.concatenate([late, over_x[cut:]]), 2)
-    late_y, diagonal_y = come[: len(at)], come[len(at) :]
-    pieces = [held, late, over_x, over_y, late_x, late_y, diagonal_x, diagonal_y]
-    pieces += [hop(late_y[:cut], 1), hop(late_x[cut:], 2)]
-    positions = [tuple(p ^ step for p in at) for step in (0, 4, 1, 2, 5, 6)]
-    positions += [tuple(p ^ step for p in part) for step in (3, 7) for part in (at[:cut], at[cut:])]
+    size = len(at)
+    last_x = hop(jnp.concatenate([late_b, over_y[:cut], over_y[size:]]), 1)
+    last_y = hop(jnp.concatenate([late_a, over_x[cut:]]), 2)
+    at_a, at_b = tuple(p ^ 4 for p in at[:cut]), tuple(p ^ 4 for p in at[cut:])
+    places = (
+        (held, 0, at),
+        (late, 0, at_a + at_b),
+        (over_x, 1, at + at_a),
+        (over_y, 2, at + at_b),
+        (last_x[: size - cut], 1, at_b),
+        (last_x[size - cut :], 3, at[:cut] + at_b),
+        (last_y[:cut], 2, at_a),
+        (last_y[cut:], 3, at[cut:] + at_a),
+    )
+    pieces = [piece for piece, _, _ in places]
+    positions = [tuple(p ^ step for p in part) for _, step, part in places]
     groups = []
     for planes in (near[:1] + come_first, near[1:] + come_last):
         mine = jnp.concatenate(planes, axis=0)

time: 57.6 us -> 69.8 us (1.21)
  waiting for transfers between devices: 25.1 us -> 38.1 us
  starting transfers between devices: 23.7 us -> 22.7 us
    ppermute x17 -> x15, waiting for transfers between devices: 25.1 us -> 38.1 us  [send(): return lax.ppermute(x, axis, [(i, partner(i)) for i in range(size)])]
    ppermute x17 -> x15, starting transfers between devices: 23.7 us -> 22.7 us  [send(): return lax.ppermute(x, axis, [(i, partner(i)) for i in range(size)])]
  transfers between devices with their start and end apart: 17 -> 15, of which waited for: 8 -> 10; matrix products, arithmetic and copies ran while one was open for 2% -> 2% of each run, Pallas kernels for 3% -> 3%
where the time goes in v12:
time: 69.8 us; the launch traced here: 69.6 us
  waiting for transfers between devices  38.1 us (55%)
  starting transfers between devices  22.7 us (33%)
  Pallas kernels  5.96 us (9%)
  local copies, waits for them, and re-layouts  1.42 us (2%)
  other arithmetic  1.05 us (2%)
    ppermute x15, waiting for transfers between devices, send(): return lax.ppermute(x, axis, [(i, partner(i)) for i in range(size)])  38.1 us
    ppermute x15, starting transfers between devices, send(): return lax.ppermute(x, axis, [(i, partner(i)) for i in range(size)])  22.7 us
    pallas_call x1, Pallas kernels, contract(): pl.pallas_call(functools.partial(contract_kernel, len(groups), len(groups...  4.16 us
    pallas_call x1, Pallas kernels, pack(): pl.pallas_call(pack_kernel, out_shape=[out] * 4, in_specs=[pl.BlockSpec(m...  1.48 us
  transfers between devices with their start and end apart: 15, of which 10 were waited for; matrix products, arithmetic and copies ran while one was open for 2% of the time, Pallas kernels for 3%

profile of v12, /device:TPU:0, one launch (start us, length us, event | category | flops | bytes accessed | tf_op | source)
XLA Modules:
  0.0 69.6 jit_solution(8576963919104863584)
XLA Ops:
  0.0 0.0 copy-start
  0.0 4.0 %collective-permute-start = (f32[1,256,128]{2,1,0:T(8,128)}, f32[1,256,128]{2,1,0:T(8,128)S(1)}, u32[]{:S(2)}, u32[]{:S(2)}) collective-permute-start(f32[1,256,128]{2,1,0:T(8,128)} %bitcast.41), channel_id=1, source_target_pairs={{0,8},{1,9},{2,10},{3,11},{4,12},{5,13},{6,14},{7,15},{8,0},{9,1},... | collective-permute-start | bytes 393224 | tf_op jit(solution)/shard_map/ppermute | solution.py:203
  4.0 0.7 fusion.1.words_ref
  4.7 0.0 copy-start.1
  4.7 1.0 %copy-done.1 = f32[16,64,128]{2,1,0:T(8,128)S(1)} copy-done((f32[16,64,128]{2,1,0:T(8,128)S(1)}, f32[16,64,128]{2,1,0:T(8,128)}, u32[]{:S(2)}) %copy-start.1) | copy-done | bytes 524312
  5.8 0.0 copy-start.2
  5.8 1.5 %shard_map.64 = (f32[4,136,128]{2,1,0:T(8,128)S(1)}, f32[4,136,128]{2,1,0:T(8,128)S(1)}, f32[4,136,128]{2,1,0:T(8,128)S(1)}, f32[4,136,128]{2,1,0:T(8,128)S(1)}) custom-call(s32[16]{0:T(128)S(1)} %fusion.1.words_ref, f32[16,64,128]{2,1,0:T(8,128)S(1)} %copy-done.1), custom_call_target="tpu_custom_call" | custom-call | bytes 1572864 | tf_op jit(solution)/shard_map/pallas_call | solution.py:58
  7.3 1.6 %collective-permute-start.2 = (f32[4,136,128]{2,1,0:T(8,128)S(1)}, f32[4,136,128]{2,1,0:T(8,128)S(1)}, u32[]{:S(2)}, u32[]{:S(2)}) collective-permute-start(f32[4,136,128]{2,1,0:T(8,128)S(1)} %get-tuple-element.17), channel_id=1, source_target_pairs={{0,2},{1,3},{2,0},{3,1},{4,6},{5,7},{6,4},{7,5},{8,10},{9,11},{10,... | collective-permute-start | bytes 835592 | tf_op jit(solution)/shard_map/ppermute | solution.py:203
  8.8 1.5 %collective-permute-start.4 = (f32[4,136,128]{2,1,0:T(8,128)S(1)}, f32[4,136,128]{2,1,0:T(8,128)S(1)}, u32[]{:S(2)}, u32[]{:S(2)}) collective-permute-start(f32[4,136,128]{2,1,0:T(8,128)S(1)} %get-tuple-element.19), channel_id=1, source_target_pairs={{0,1},{1,0},{2,3},{3,2},{4,5},{5,4},{6,7},{7,6},{8,9},{9,8},{10,11... | collective-permute-start | bytes 835592 | tf_op jit(solution)/shard_map/ppermute | solution.py:203
  10.4 0.0 copy-done
  10.4 0.1 shard_map.66.refs_4_
  10.5 0.1 collective-permute-done
  10.6 0.0 copy-done.2
  10.6 1.6 %collective-permute-start.1 = (f32[2,256,128]{2,1,0:T(8,128)S(1)}, f32[2,256,128]{2,1,0:T(8,128)S(1)}, u32[]{:S(2)}, u32[]{:S(2)}) collective-permute-start(f32[2,256,128]{2,1,0:T(8,128)S(1)} %pad_maximum_fusion.10.refs_0_), channel_id=1, source_target_pairs={{0,4},{1,5},{2,6},{3,7},{4,0},{5,1},{6,2},{7,3},{8,12},{9,13},{10,... | collective-permute-start | bytes 786440 | tf_op jit(solution)/shard_map/ppermute | solution.py:203
  12.2 3.3 %collective-permute-done.2 = f32[4,136,128]{2,1,0:T(8,128)S(1)} collective-permute-done((f32[4,136,128]{2,1,0:T(8,128)S(1)}, f32[4,136,128]{2,1,0:T(8,128)S(1)}, u32[]{:S(2)}, u32[]{:S(2)}) %collective-permute-start.2) | collective-permute-done | bytes 278560 | tf_op jit(solution)/shard_map/ppermute | solution.py:203
  15.5 1.2 %collective-permute-done.4 = f32[4,136,128]{2,1,0:T(8,128)S(1)} collective-permute-done((f32[4,136,128]{2,1,0:T(8,128)S(1)}, f32[4,136,128]{2,1,0:T(8,128)S(1)}, u32[]{:S(2)}, u32[]{:S(2)}) %collective-permute-start.4) | collective-permute-done | bytes 278560 | tf_op jit(solution)/shard_map/ppermute | solution.py:203
  16.7 1.4 %collective-permute-done.1.refs_1_ = f32[2,256,128]{2,1,0:T(8,128)S(1)} collective-permute-done((f32[2,256,128]{2,1,0:T(8,128)S(1)}, f32[2,256,128]{2,1,0:T(8,128)S(1)}, u32[]{:S(2)}, u32[]{:S(2)}) %collective-permute-start.1) | collective-permute-done | bytes 262176 | tf_op jit(solution)/shard_map/ppermute | solution.py:203
  18.2 0.1 pad_maximum_fusion.4
  18.3 1.4 %collective-permute-start.5 = (f32[1312,128]{1,0:T(8,128)S(1)}, f32[1312,128]{1,0:T(8,128)S(1)}, u32[]{:S(2)}, u32[]{:S(2)}) collective-permute-start(f32[1312,128]{1,0:T(8,128)S(1)} %pad_maximum_fusion.1), channel_id=1, source_target_pairs={{0,2},{1,3},{2,0},{3,1},{4,6},{5,7},{6,4},{7,5},{8,10},{9,11},{10,... | collective-permute-start | bytes 2015240 | tf_op jit(solution)/shard_map/ppermute | solution.py:203
  19.7 1.6 %collective-permute-start.3 = (f32[1312,128]{1,0:T(8,128)S(1)}, f32[1312,128]{1,0:T(8,128)S(1)}, u32[]{:S(2)}, u32[]{:S(2)}) collective-permute-start(f32[1312,128]{1,0:T(8,128)S(1)} %pad_maximum_fusion), channel_id=1, source_target_pairs={{0,1},{1,0},{2,3},{3,2},{4,5},{5,4},{6,7},{7,6},{8,9},{9,8},{10,11... | collective-permute-start | bytes 2015240 | tf_op jit(solution)/shard_map/ppermute | solution.py:203
  21.3 4.5 %collective-permute-start.9 = (f32[2,136,128]{2,1,0:T(8,128)S(1)}, f32[2,136,128]{2,1,0:T(8,128)S(1)}, u32[]{:S(2)}, u32[]{:S(2)}) collective-permute-start(f32[2,136,128]{2,1,0:T(8,128)S(1)} %pad_maximum_fusion.16), channel_id=1, source_target_pairs={{0,12},{1,13},{2,14},{3,15},{4,8},{5,9},{6,10},{7,11},{8,4},{9,5},... | collective-permute-start | bytes 417800 | tf_op jit(solution)/shard_map/ppermute | solution.py:203
  25.8 0.1 collective-permute-start.8
  25.9 7.8 %collective-permute-done.5 = f32[1312,128]{1,0:T(8,128)S(1)} collective-permute-done((f32[1312,128]{1,0:T(8,128)S(1)}, f32[1312,128]{1,0:T(8,128)S(1)}, u32[]{:S(2)}, u32[]{:S(2)}) %collective-permute-start.5) | collective-permute-done | bytes 671776 | tf_op jit(solution)/shard_map/ppermute | solution.py:203
  33.7 1.2 %collective-permute-done.3 = f32[1312,128]{1,0:T(8,128)S(1)} collective-permute-done((f32[1312,128]{1,0:T(8,128)S(1)}, f32[1312,128]{1,0:T(8,128)S(1)}, u32[]{:S(2)}, u32[]{:S(2)}) %collective-permute-start.3) | collective-permute-done | bytes 671776 | tf_op jit(solution)/shard_map/ppermute | solution.py:203
  35.0 0.0 collective-permute-done.9
  35.0 1.3 %collective-permute-done.8 = f32[2,136,128]{2,1,0:T(8,128)S(1)} collective-permute-done((f32[2,136,128]{2,1,0:T(8,128)S(1)}, f32[2,136,128]{2,1,0:T(8,128)S(1)}, u32[]{:S(2)}, u32[]{:S(2)}) %collective-permute-start.8) | collective-permute-done | bytes 139296 | tf_op jit(solution)/shard_map/ppermute | solution.py:203
  36.4 3.1 %collective-permute-start.12 = (f32[2,136,128]{2,1,0:T(8,128)S(1)}, f32[2,136,128]{2,1,0:T(8,128)S(1)}, u32[]{:S(2)}, u32[]{:S(2)}) collective-permute-start(f32[2,136,128]{2,1,0:T(8,128)S(1)} %get-tuple-element.24), channel_id=1, source_target_pairs={{0,8},{1,9},{2,10},{3,11},{4,12},{5,13},{6,14},{7,15},{8,0},{9,1},... | collective-permute-start | bytes 417800 | tf_op jit(solution)/shard_map/ppermute | solution.py:203
  39.4 0.9 %collective-permute-start.13 = (f32[2,136,128]{2,1,0:T(8,128)S(1)}, f32[2,136,128]{2,1,0:T(8,128)S(1)}, u32[]{:S(2)}, u32[]{:S(2)}) collective-permute-start(f32[2,136,128]{2,1,0:T(8,128)S(1)} %get-tuple-element.25), channel_id=1, source_target_pairs={{0,12},{1,13},{2,14},{3,15},{4,8},{5,9},{6,10},{7,11},{8,4},{9,5},... | collective-permute-start | bytes 417800 | tf_op jit(solution)/shard_map/ppermute | solution.py:203
  40.4 0.6 collective-permute-start.11
  41.0 0.1 collective-permute-start.10
  41.1 11.3 %collective-permute-done.11 = f32[4,136,128]{2,1,0:T(8,128)S(1)} collective-permute-done((f32[4,136,128]{2,1,0:T(8,128)S(1)}, f32[4,136,128]{2,1,0:T(8,128)S(1)}, u32[]{:S(2)}, u32[]{:S(2)}) %collective-permute-start.11) | collective-permute-done | bytes 278560 | tf_op jit(solution)/shard_map/ppermute | solution.py:203
  52.4 0.0 collective-permute-done.12
  52.4 0.0 collective-permute-done.13
  52.5 0.1 collective-permute-start.14
  52.6 1.2 %collective-permute-start.6 = (f32[3,256,128]{2,1,0:T(8,128)S(1)}, f32[3,256,128]{2,1,0:T(8,128)S(1)}, u32[]{:S(2)}, u32[]{:S(2)}) collective-permute-start(f32[3,256,128]{2,1,0:T(8,128)S(1)} %pad_maximum_fusion.5), channel_id=1, source_target_pairs={{0,1},{1,0},{2,3},{3,2},{4,5},{5,4},{6,7},{7,6},{8,9},{9,8},{10,11... | collective-permute-start | bytes 1179656 | tf_op jit(solution)/shard_map/ppermute | solution.py:203
  53.8 0.6 collective-permute-start.7
  54.5 9.7 %collective-permute-done.6 = f32[3,256,128]{2,1,0:T(8,128)S(1)} collective-permute-done((f32[3,256,128]{2,1,0:T(8,128)S(1)}, f32[3,256,128]{2,1,0:T(8,128)S(1)}, u32[]{:S(2)}, u32[]{:S(2)}) %collective-permute-start.6) | collective-permute-done | bytes 393248 | tf_op jit(solution)/shard_map/ppermute | solution.py:203
  64.2 0.9 %collective-permute-done.7 = f32[3,256,128]{2,1,0:T(8,128)S(1)} collective-permute-done((f32[3,256,128]{2,1,0:T(8,128)S(1)}, f32[3,256,128]{2,1,0:T(8,128)S(1)}, u32[]{:S(2)}, u32[]{:S(2)}) %collective-permute-start.7) | collective-permute-done | bytes 393248 | tf_op jit(solution)/shard_map/ppermute | solution.py:203
  65.2 0.3 shard_map.65.split_ref
  65.4 0.0 collective-permute-done.10.refs_1_
  65.4 0.0 collective-permute-done.14.refs_3_
  65.4 4.2 %shard_map.67 = f32[256,1024]{1,0:T(8,128)} custom-call(bf16[16,256,256]{2,1,0:T(8,128)(2,1)S(1)} %shard_map.65.split_ref, f32[8,136,128]{2,1,0:T(8,128)S(1)} %constant_dynamic-update-slice_fusion.refs_0_, f32[8,136,128]{2,1,0:T(8,128)S(1)} %collective-permute-done.10.refs_1_, f32[8,136,128]{2,1,0:T(8,128)S(1)} %constant_dynamic-update-slice_fusion.3.refs_2_, ...), custom_call_target="tpu_custom_call" | custom-call | tf_op jit(solution)/shard_map/pallas_call | solution.py:173
  (37 shorter events, 0.7 us)
Async XLA Ops:
  0.0 10.4 %copy-start = (f32[256,1024]{1,0:T(8,128)S(1)}, f32[256,1024]{1,0:T(8,128)}, u32[]{:S(2)}) copy-start(f32[256,1024]{1,0:T(8,128)} %x_ref.1) | copy-start | bytes 3145732
  0.0 10.5 %collective-permute-start = (f32[1,256,128]{2,1,0:T(8,128)}, f32[1,256,128]{2,1,0:T(8,128)S(1)}, u32[]{:S(2)}, u32[]{:S(2)}) collective-permute-start(f32[1,256,128]{2,1,0:T(8,128)} %bitcast.41), channel_id=1, source_target_pairs={{0,8},{1,9},{2,10},{3,11},{4,12},{5,13},{6,14},{7,15},{8,0},{9,1},... | collective-permute-start | bytes 393224 | tf_op jit(solution)/shard_map/ppermute | solution.py:203
  4.7 1.0 %copy-start.1 = (f32[16,64,128]{2,1,0:T(8,128)S(1)}, f32[16,64,128]{2,1,0:T(8,128)}, u32[]{:S(2)}) copy-start(f32[16,64,128]{2,1,0:T(8,128)} %tiles_ref.1) | copy-start | bytes 1572868
  5.8 4.8 %copy-start.2 = (f32[256,128]{1,0:T(8,128)S(1)}, f32[256,128]{1,0:T(8,128)}, u32[]{:S(2)}) copy-start(f32[256,128]{1,0:T(8,128)} %param.7) | copy-start | bytes 393220
  7.3 8.2 %collective-permute-start.2 = (f32[4,136,128]{2,1,0:T(8,128)S(1)}, f32[4,136,128]{2,1,0:T(8,128)S(1)}, u32[]{:S(2)}, u32[]{:S(2)}) collective-permute-start(f32[4,136,128]{2,1,0:T(8,128)S(1)} %get-tuple-element.17), channel_id=1, source_target_pairs={{0,2},{1,3},{2,0},{3,1},{4,6},{5,7},{6,4},{7,5},{8,10},{9,11},{10,... | collective-permute-start | bytes 835592 | tf_op jit(solution)/shard_map/ppermute | solution.py:203
  8.8 7.8 %collective-permute-start.4 = (f32[4,136,128]{2,1,0:T(8,128)S(1)}, f32[4,136,128]{2,1,0:T(8,128)S(1)}, u32[]{:S(2)}, u32[]{:S(2)}) collective-permute-start(f32[4,136,128]{2,1,0:T(8,128)S(1)} %get-tuple-element.19), channel_id=1, source_target_pairs={{0,1},{1,0},{2,3},{3,2},{4,5},{5,4},{6,7},{7,6},{8,9},{9,8},{10,11... | collective-permute-start | bytes 835592 | tf_op jit(solution)/shard_map/ppermute | solution.py:203
  10.6 7.6 %collective-permute-start.1 = (f32[2,256,128]{2,1,0:T(8,128)S(1)}, f32[2,256,128]{2,1,0:T(8,128)S(1)}, u32[]{:S(2)}, u32[]{:S(2)}) collective-permute-start(f32[2,256,128]{2,1,0:T(8,128)S(1)} %pad_maximum_fusion.10.refs_0_), channel_id=1, source_target_pairs={{0,4},{1,5},{2,6},{3,7},{4,0},{5,1},{6,2},{7,3},{8,12},{9,13},{10,... | collective-permute-start | bytes 786440 | tf_op jit(solution)/shard_map/ppermute | solution.py:203
  18.3 15.4 %collective-permute-start.5 = (f32[1312,128]{1,0:T(8,128)S(1)}, f32[1312,128]{1,0:T(8,128)S(1)}, u32[]{:S(2)}, u32[]{:S(2)}) collective-permute-start(f32[1312,128]{1,0:T(8,128)S(1)} %pad_maximum_fusion.1), channel_id=1, source_target_pairs={{0,2},{1,3},{2,0},{3,1},{4,6},{5,7},{6,4},{7,5},{8,10},{9,11},{10,... | collective-permute-start | bytes 2015240 | tf_op jit(solution)/shard_map/ppermute | solution.py:203
  19.7 15.2 %collective-permute-start.3 = (f32[1312,128]{1,0:T(8,128)S(1)}, f32[1312,128]{1,0:T(8,128)S(1)}, u32[]{:S(2)}, u32[]{:S(2)}) collective-permute-start(f32[1312,128]{1,0:T(8,128)S(1)} %pad_maximum_fusion), channel_id=1, source_target_pairs={{0,1},{1,0},{2,3},{3,2},{4,5},{5,4},{6,7},{7,6},{8,9},{9,8},{10,11... | collective-permute-start | bytes 2015240 | tf_op jit(solution)/shard_map/ppermute | solution.py:203
  21.3 13.7 %collective-permute-start.9 = (f32[2,136,128]{2,1,0:T(8,128)S(1)}, f32[2,136,128]{2,1,0:T(8,128)S(1)}, u32[]{:S(2)}, u32[]{:S(2)}) collective-permute-start(f32[2,136,128]{2,1,0:T(8,128)S(1)} %pad_maximum_fusion.16), channel_id=1, source_target_pairs={{0,12},{1,13},{2,14},{3,15},{4,8},{5,9},{6,10},{7,11},{8,4},{9,5},... | collective-permute-start | bytes 417800 | tf_op jit(solution)/shard_map/ppermute | solution.py:203
  25.8 10.5 %collective-permute-start.8 = (f32[2,136,128]{2,1,0:T(8,128)S(1)}, f32[2,136,128]{2,1,0:T(8,128)S(1)}, u32[]{:S(2)}, u32[]{:S(2)}) collective-permute-start(f32[2,136,128]{2,1,0:T(8,128)S(1)} %pad_maximum_fusion.15), channel_id=1, source_target_pairs={{0,8},{1,9},{2,10},{3,11},{4,12},{5,13},{6,14},{7,15},{8,0},{9,1},... | collective-permute-start | bytes 417800 | tf_op jit(solution)/shard_map/ppermute | solution.py:203
  36.4 16.0 %collective-permute-start.12 = (f32[2,136,128]{2,1,0:T(8,128)S(1)}, f32[2,136,128]{2,1,0:T(8,128)S(1)}, u32[]{:S(2)}, u32[]{:S(2)}) collective-permute-start(f32[2,136,128]{2,1,0:T(8,128)S(1)} %get-tuple-element.24), channel_id=1, source_target_pairs={{0,8},{1,9},{2,10},{3,11},{4,12},{5,13},{6,14},{7,15},{8,0},{9,1},... | collective-permute-start | bytes 417800 | tf_op jit(solution)/shard_map/ppermute | solution.py:203
  39.4 13.0 %collective-permute-start.13 = (f32[2,136,128]{2,1,0:T(8,128)S(1)}, f32[2,136,128]{2,1,0:T(8,128)S(1)}, u32[]{:S(2)}, u32[]{:S(2)}) collective-permute-start(f32[2,136,128]{2,1,0:T(8,128)S(1)} %get-tuple-element.25), channel_id=1, source_target_pairs={{0,12},{1,13},{2,14},{3,15},{4,8},{5,9},{6,10},{7,11},{8,4},{9,5},... | collective-permute-start | bytes 417800 | tf_op jit(solution)/shard_map/ppermute | solution.py:203
  40.4 12.0 %collective-permute-start.11 = (f32[4,136,128]{2,1,0:T(8,128)S(1)}, f32[4,136,128]{2,1,0:T(8,128)S(1)}, u32[]{:S(2)}, u32[]{:S(2)}) collective-permute-start(f32[4,136,128]{2,1,0:T(8,128)S(1)} %pad_maximum_fusion.9), channel_id=1, source_target_pairs={{0,4},{1,5},{2,6},{3,7},{4,0},{5,1},{6,2},{7,3},{8,12},{9,13},{10,... | collective-permute-start | bytes 835592 | tf_op jit(solution)/shard_map/ppermute | solution.py:203
  41.0 24.4 %collective-permute-start.10 = (f32[8,136,128]{2,1,0:T(8,128)S(1)}, f32[8,136,128]{2,1,0:T(8,128)S(1)}, u32[]{:S(2)}, u32[]{:S(2)}) collective-permute-start(f32[8,136,128]{2,1,0:T(8,128)S(1)} %constant_dynamic-update-slice_fusion.refs_0_), channel_id=1, source_target_pairs={{0,16},{16,0},{1,17},{17,1},{2,18},{18,2},{3,19},{19,3},{4,20},{20... | collective-permute-start | bytes 1671176 | tf_op jit(solution)/shard_map/ppermute | solution.py:203
  52.5 13.0 %collective-permute-start.14 = (f32[8,136,128]{2,1,0:T(8,128)S(1)}, f32[8,136,128]{2,1,0:T(8,128)S(1)}, u32[]{:S(2)}, u32[]{:S(2)}) collective-permute-start(f32[8,136,128]{2,1,0:T(8,128)S(1)} %constant_dynamic-update-slice_fusion.3.refs_2_), channel_id=1, source_target_pairs={{0,16},{16,0},{1,17},{17,1},{2,18},{18,2},{3,19},{19,3},{4,20},{20... | collective-permute-start | bytes 1671176 | tf_op jit(solution)/shard_map/ppermute | solution.py:203
  52.6 11.6 %collective-permute-start.6 = (f32[3,256,128]{2,1,0:T(8,128)S(1)}, f32[3,256,128]{2,1,0:T(8,128)S(1)}, u32[]{:S(2)}, u32[]{:S(2)}) collective-permute-start(f32[3,256,128]{2,1,0:T(8,128)S(1)} %pad_maximum_fusion.5), channel_id=1, source_target_pairs={{0,1},{1,0},{2,3},{3,2},{4,5},{5,4},{6,7},{7,6},{8,9},{9,8},{10,11... | collective-permute-start | bytes 1179656 | tf_op jit(solution)/shard_map/ppermute | solution.py:203
  53.8 11.3 %collective-permute-start.7 = (f32[3,256,128]{2,1,0:T(8,128)S(1)}, f32[3,256,128]{2,1,0:T(8,128)S(1)}, u32[]{:S(2)}, u32[]{:S(2)}) collective-permute-start(f32[3,256,128]{2,1,0:T(8,128)S(1)} %pad_maximum_fusion.6), channel_id=1, source_target_pairs={{0,2},{1,3},{2,0},{3,1},{4,6},{5,7},{6,4},{7,5},{8,10},{9,11},{10,... | collective-permute-start | bytes 1179656 | tf_op jit(solution)/shard_map/ppermute | solution.py:203

commit v13 on v12

--- a/solution.py
+++ b/solution.py
@@ -251,6 +251,7 @@
     size = len(at)
     last_x = hop(jnp.concatenate([late_b, over_y[:cut], over_y[size:]]), 1)
     last_y = hop(jnp.concatenate([late_a, over_x[cut:]]), 2)
+    come_last, last_x, last_y = lax.optimization_barrier((come_last, last_x, last_y))
     at_a, at_b = tuple(p ^ 4 for p in at[:cut]), tuple(p ^ 4 for p in at[cut:])
     places = (
         (held, 0, at),
@@ -265,7 +266,7 @@
     pieces = [piece for piece, _, _ in places]
     positions = [tuple(p ^ step for p in part) for _, step, part in places]
     groups = []
-    for planes in (near[:1] + come_first, near[1:] + come_last):
+    for planes in (near[:1] + come_first, near[1:], come_last):
         mine = jnp.concatenate(planes, axis=0)
         groups.append(
             [mine] + [send(mine, "row", lambda i: (i + q) % rows_axis) for q in range(1, rows_axis)]

time: 69.8 us -> 62.5 us (0.90)
  waiting for transfers between devices: 38.1 us -> 29 us
  local copies, waits for them, and re-layouts: 1.42 us -> 2.61 us
    ppermute x15 -> x16, waiting for transfers between devices: 38.1 us -> 29 us  [send(): return lax.ppermute(x, axis, [(i, partner(i)) for i in range(size)])]
    unnamed x10 -> x11, local copies, waits for them, and re-layouts: 1.1 us -> 2.32 us
    ppermute x15 -> x16, starting transfers between devices: 22.7 us -> 23.3 us  [send(): return lax.ppermute(x, axis, [(i, partner(i)) for i in range(size)])]
  transfers between devices with their start and end apart: 15 -> 16, of which waited for: 10 -> 9; matrix products, arithmetic and copies ran while one was open for 2% -> 2% of each run, Pallas kernels for 3% -> 3%
where the time goes in v13:
time: 62.5 us; the launch traced here: 62.3 us
  waiting for transfers between devices  29 us (46%)
  starting transfers between devices  23.3 us (37%)
  Pallas kernels  5.96 us (10%)
  local copies, waits for them, and re-layouts  2.61 us (4%)
  other arithmetic  1.05 us (2%)
    ppermute x16, waiting for transfers between devices, send(): return lax.ppermute(x, axis, [(i, partner(i)) for i in range(size)])  29 us
    ppermute x16, starting transfers between devices, send(): return lax.ppermute(x, axis, [(i, partner(i)) for i in range(size)])  23.3 us
    pallas_call x1, Pallas kernels, contract(): pl.pallas_call(functools.partial(contract_kernel, len(groups), len(groups...  4.16 us
    unnamed x11, local copies, waits for them, and re-layouts  2.32 us
    pallas_call x1, Pallas kernels, pack(): pl.pallas_call(pack_kernel, out_shape=[out] * 4, in_specs=[pl.BlockSpec(m...  1.48 us
  transfers between devices with their start and end apart: 16, of which 9 were waited for; matrix products, arithmetic and copies ran while one was open for 2% of the time, Pallas kernels for 3%

profile of v13, /device:TPU:0, one launch (start us, length us, event | category | flops | bytes accessed | tf_op | source)
XLA Modules:
  0.0 62.3 jit_solution(7477330725597672072)
XLA Ops:
  0.0 4.0 %collective-permute-start = (f32[1,256,128]{2,1,0:T(8,128)}, f32[1,256,128]{2,1,0:T(8,128)S(1)}, u32[]{:S(2)}, u32[]{:S(2)}) collective-permute-start(f32[1,256,128]{2,1,0:T(8,128)} %bitcast.41), channel_id=1, source_target_pairs={{0,8},{1,9},{2,10},{3,11},{4,12},{5,13},{6,14},{7,15},{8,0},{9,1},... | collective-permute-start | bytes 393224 | tf_op jit(solution)/shard_map/ppermute | solution.py:203
  4.0 0.7 %fusion.1.words_ref = s32[16]{0:T(128)S(1)} fusion(s32[16]{0:T(128)} %param.11, s32[16]{0:T(128)} %param.10, s32[16,1]{0,1:T(1,128)} %param.9), kind=kLoop, calls=%fused_computation.36 | loop fusion | flops 64 | bytes 256 | tf_op jit(solution)/shard_map/add | solution.py:56
  4.7 0.0 copy-start.1
  4.7 1.0 %copy-done.1 = f32[16,64,128]{2,1,0:T(8,128)S(1)} copy-done((f32[16,64,128]{2,1,0:T(8,128)S(1)}, f32[16,64,128]{2,1,0:T(8,128)}, u32[]{:S(2)}) %copy-start.1) | copy-done | bytes 524312
  5.8 0.0 copy-start.2
  5.8 1.5 %shard_map.64 = (f32[4,136,128]{2,1,0:T(8,128)S(1)}, f32[4,136,128]{2,1,0:T(8,128)S(1)}, f32[4,136,128]{2,1,0:T(8,128)S(1)}, f32[4,136,128]{2,1,0:T(8,128)S(1)}) custom-call(s32[16]{0:T(128)S(1)} %fusion.1.words_ref, f32[16,64,128]{2,1,0:T(8,128)S(1)} %copy-done.1), custom_call_target="tpu_custom_call" | custom-call | bytes 1572864 | tf_op jit(solution)/shard_map/pallas_call | solution.py:58
  7.3 1.6 %collective-permute-start.2 = (f32[4,136,128]{2,1,0:T(8,128)S(1)}, f32[4,136,128]{2,1,0:T(8,128)S(1)}, u32[]{:S(2)}, u32[]{:S(2)}) collective-permute-start(f32[4,136,128]{2,1,0:T(8,128)S(1)} %get-tuple-element.21), channel_id=1, source_target_pairs={{0,2},{1,3},{2,0},{3,1},{4,6},{5,7},{6,4},{7,5},{8,10},{9,11},{10,... | collective-permute-start | bytes 835592 | tf_op jit(solution)/shard_map/ppermute | solution.py:203
  8.8 1.5 %collective-permute-start.4 = (f32[4,136,128]{2,1,0:T(8,128)S(1)}, f32[4,136,128]{2,1,0:T(8,128)S(1)}, u32[]{:S(2)}, u32[]{:S(2)}) collective-permute-start(f32[4,136,128]{2,1,0:T(8,128)S(1)} %get-tuple-element.23), channel_id=1, source_target_pairs={{0,1},{1,0},{2,3},{3,2},{4,5},{5,4},{6,7},{7,6},{8,9},{9,8},{10,11... | collective-permute-start | bytes 835592 | tf_op jit(solution)/shard_map/ppermute | solution.py:203
  10.4 0.0 copy-start
  10.4 1.2 %copy-done = f32[256,1024]{1,0:T(8,128)S(1)} copy-done((f32[256,1024]{1,0:T(8,128)S(1)}, f32[256,1024]{1,0:T(8,128)}, u32[]{:S(2)}) %copy-start) | copy-done | bytes 1048600
  11.6 0.1 shard_map.65.refs_6_
  11.7 0.0 collective-permute-done
  11.7 0.0 copy-done.2
  11.8 1.6 %collective-permute-start.1 = (f32[2,256,128]{2,1,0:T(8,128)S(1)}, f32[2,256,128]{2,1,0:T(8,128)S(1)}, u32[]{:S(2)}, u32[]{:S(2)}) collective-permute-start(f32[2,256,128]{2,1,0:T(8,128)S(1)} %pad_maximum_fusion.10.refs_0_), channel_id=1, source_target_pairs={{0,4},{1,5},{2,6},{3,7},{4,0},{5,1},{6,2},{7,3},{8,12},{9,13},{10,... | collective-permute-start | bytes 786440 | tf_op jit(solution)/shard_map/ppermute | solution.py:203
  13.4 2.0 %collective-permute-done.2 = f32[4,136,128]{2,1,0:T(8,128)S(1)} collective-permute-done((f32[4,136,128]{2,1,0:T(8,128)S(1)}, f32[4,136,128]{2,1,0:T(8,128)S(1)}, u32[]{:S(2)}, u32[]{:S(2)}) %collective-permute-start.2) | collective-permute-done | bytes 278560 | tf_op jit(solution)/shard_map/ppermute | solution.py:203
  15.5 1.4 %collective-permute-start.7 = (f32[2,136,128]{2,1,0:T(8,128)S(1)}, f32[2,136,128]{2,1,0:T(8,128)S(1)}, u32[]{:S(2)}, u32[]{:S(2)}) collective-permute-start(f32[2,136,128]{2,1,0:T(8,128)S(1)} %pad_maximum_fusion.16), channel_id=1, source_target_pairs={{0,12},{1,13},{2,14},{3,15},{4,8},{5,9},{6,10},{7,11},{8,4},{9,5},... | collective-permute-start | bytes 417800 | tf_op jit(solution)/shard_map/ppermute | solution.py:203
  16.9 0.0 collective-permute-done.4
  16.9 2.7 %collective-permute-done.1.refs_1_ = f32[2,256,128]{2,1,0:T(8,128)S(1)} collective-permute-done((f32[2,256,128]{2,1,0:T(8,128)S(1)}, f32[2,256,128]{2,1,0:T(8,128)S(1)}, u32[]{:S(2)}, u32[]{:S(2)}) %collective-permute-start.1) | collective-permute-done | bytes 262176 | tf_op jit(solution)/shard_map/ppermute | solution.py:203
  19.6 0.1 pad_maximum_fusion.4
  19.7 0.7 %collective-permute-start.5 = (f32[1312,128]{1,0:T(8,128)S(1)}, f32[1312,128]{1,0:T(8,128)S(1)}, u32[]{:S(2)}, u32[]{:S(2)}) collective-permute-start(f32[1312,128]{1,0:T(8,128)S(1)} %pad_maximum_fusion.1), channel_id=1, source_target_pairs={{0,2},{1,3},{2,0},{3,1},{4,6},{5,7},{6,4},{7,5},{8,10},{9,11},{10,... | collective-permute-start | bytes 2015240 | tf_op jit(solution)/shard_map/ppermute | solution.py:203
  20.5 4.8 %collective-permute-start.6 = (f32[2,136,128]{2,1,0:T(8,128)S(1)}, f32[2,136,128]{2,1,0:T(8,128)S(1)}, u32[]{:S(2)}, u32[]{:S(2)}) collective-permute-start(f32[2,136,128]{2,1,0:T(8,128)S(1)} %pad_maximum_fusion.15), channel_id=1, source_target_pairs={{0,8},{1,9},{2,10},{3,11},{4,12},{5,13},{6,14},{7,15},{8,0},{9,1},... | collective-permute-start | bytes 417800 | tf_op jit(solution)/shard_map/ppermute | solution.py:203
  25.4 1.6 %collective-permute-start.3 = (f32[1312,128]{1,0:T(8,128)S(1)}, f32[1312,128]{1,0:T(8,128)S(1)}, u32[]{:S(2)}, u32[]{:S(2)}) collective-permute-start(f32[1312,128]{1,0:T(8,128)S(1)} %pad_maximum_fusion), channel_id=1, source_target_pairs={{0,1},{1,0},{2,3},{3,2},{4,5},{5,4},{6,7},{7,6},{8,9},{9,8},{10,11... | collective-permute-start | bytes 2015240 | tf_op jit(solution)/shard_map/ppermute | solution.py:203
  26.9 7.3 %collective-permute-done.5 = f32[1312,128]{1,0:T(8,128)S(1)} collective-permute-done((f32[1312,128]{1,0:T(8,128)S(1)}, f32[1312,128]{1,0:T(8,128)S(1)}, u32[]{:S(2)}, u32[]{:S(2)}) %collective-permute-start.5) | collective-permute-done | bytes 671776 | tf_op jit(solution)/shard_map/ppermute | solution.py:203
  34.3 0.6 %collective-permute-start.10 = (f32[3,256,128]{2,1,0:T(8,128)S(1)}, f32[3,256,128]{2,1,0:T(8,128)S(1)}, u32[]{:S(2)}, u32[]{:S(2)}) collective-permute-start(f32[3,256,128]{2,1,0:T(8,128)S(1)} %pad_maximum_fusion.5), channel_id=1, source_target_pairs={{0,1},{1,0},{2,3},{3,2},{4,5},{5,4},{6,7},{7,6},{8,9},{9,8},{10,11... | collective-permute-start | bytes 1179656 | tf_op jit(solution)/shard_map/ppermute | solution.py:203
  35.0 8.3 %collective-permute-done.3 = f32[1312,128]{1,0:T(8,128)S(1)} collective-permute-done((f32[1312,128]{1,0:T(8,128)S(1)}, f32[1312,128]{1,0:T(8,128)S(1)}, u32[]{:S(2)}, u32[]{:S(2)}) %collective-permute-start.3) | collective-permute-done | bytes 671776 | tf_op jit(solution)/shard_map/ppermute | solution.py:203
  43.5 0.0 collective-permute-done.7
  43.5 0.0 collective-permute-done.6
  43.5 0.1 collective-permute-start.8
  43.6 5.0 %collective-permute-start.9 = (f32[2,136,128]{2,1,0:T(8,128)S(1)}, f32[2,136,128]{2,1,0:T(8,128)S(1)}, u32[]{:S(2)}, u32[]{:S(2)}) collective-permute-start(f32[2,136,128]{2,1,0:T(8,128)S(1)} %get-tuple-element.25), channel_id=1, source_target_pairs={{0,12},{1,13},{2,14},{3,15},{4,8},{5,9},{6,10},{7,11},{8,4},{9,5},... | collective-permute-start | bytes 417800 | tf_op jit(solution)/shard_map/ppermute | solution.py:203
  48.6 0.1 collective-permute-start.13
  48.6 0.1 collective-permute-start.11
  48.8 0.7 %collective-permute-done.8 = f32[2,136,128]{2,1,0:T(8,128)S(1)} collective-permute-done((f32[2,136,128]{2,1,0:T(8,128)S(1)}, f32[2,136,128]{2,1,0:T(8,128)S(1)}, u32[]{:S(2)}, u32[]{:S(2)}) %collective-permute-start.8) | collective-permute-done | bytes 139296 | tf_op jit(solution)/shard_map/ppermute | solution.py:203
  49.5 0.0 collective-permute-start.12
  49.5 6.6 %collective-permute-done.13.refs_2_ = f32[4,136,128]{2,1,0:T(8,128)S(1)} collective-permute-done((f32[4,136,128]{2,1,0:T(8,128)S(1)}, f32[4,136,128]{2,1,0:T(8,128)S(1)}, u32[]{:S(2)}, u32[]{:S(2)}) %collective-permute-start.13) | collective-permute-done | bytes 278560 | tf_op jit(solution)/shard_map/ppermute | solution.py:203
  56.1 0.0 collective-permute-start.14
  56.1 0.0 collective-permute-done.9
  56.1 0.0 collective-permute-done.10
  56.1 0.3 collective-permute-done.11
  56.5 0.3 collective-permute-start.15
  56.9 0.3 shard_map.66.split_ref
  57.2 0.5 collective-permute-done.14.refs_3_
  57.7 0.0 collective-permute-done.12.refs_1_
  57.7 0.4 collective-permute-done.15.refs_5_
  58.1 4.2 %shard_map.67 = f32[256,1024]{1,0:T(8,128)} custom-call(bf16[16,256,256]{2,1,0:T(8,128)(2,1)S(1)} %shard_map.66.split_ref, f32[8,136,128]{2,1,0:T(8,128)S(1)} %constant_dynamic-update-slice_fusion.refs_0_, f32[8,136,128]{2,1,0:T(8,128)S(1)} %collective-permute-done.12.refs_1_, f32[4,136,128]{2,1,0:T(8,128)S(1)} %collective-permute-done.13.refs_2_, ...), custom_call_target="tpu_custom_call" | custom-call | tf_op jit(solution)/shard_map/pallas_call | solution.py:173
  (36 shorter events, 0.6 us)
Async XLA Ops:
  0.0 11.7 %collective-permute-start = (f32[1,256,128]{2,1,0:T(8,128)}, f32[1,256,128]{2,1,0:T(8,128)S(1)}, u32[]{:S(2)}, u32[]{:S(2)}) collective-permute-start(f32[1,256,128]{2,1,0:T(8,128)} %bitcast.41), channel_id=1, source_target_pairs={{0,8},{1,9},{2,10},{3,11},{4,12},{5,13},{6,14},{7,15},{8,0},{9,1},... | collective-permute-start | bytes 393224 | tf_op jit(solution)/shard_map/ppermute | solution.py:203
  4.7 1.0 %copy-start.1 = (f32[16,64,128]{2,1,0:T(8,128)S(1)}, f32[16,64,128]{2,1,0:T(8,128)}, u32[]{:S(2)}) copy-start(f32[16,64,128]{2,1,0:T(8,128)} %tiles_ref.1) | copy-start | bytes 1572868
  5.8 5.9 %copy-start.2 = (f32[256,128]{1,0:T(8,128)S(1)}, f32[256,128]{1,0:T(8,128)}, u32[]{:S(2)}) copy-start(f32[256,128]{1,0:T(8,128)} %param.7) | copy-start | bytes 393220
  7.3 8.2 %collective-permute-start.2 = (f32[4,136,128]{2,1,0:T(8,128)S(1)}, f32[4,136,128]{2,1,0:T(8,128)S(1)}, u32[]{:S(2)}, u32[]{:S(2)}) collective-permute-start(f32[4,136,128]{2,1,0:T(8,128)S(1)} %get-tuple-element.21), channel_id=1, source_target_pairs={{0,2},{1,3},{2,0},{3,1},{4,6},{5,7},{6,4},{7,5},{8,10},{9,11},{10,... | collective-permute-start | bytes 835592 | tf_op jit(solution)/shard_map/ppermute | solution.py:203
  8.8 8.0 %collective-permute-start.4 = (f32[4,136,128]{2,1,0:T(8,128)S(1)}, f32[4,136,128]{2,1,0:T(8,128)S(1)}, u32[]{:S(2)}, u32[]{:S(2)}) collective-permute-start(f32[4,136,128]{2,1,0:T(8,128)S(1)} %get-tuple-element.23), channel_id=1, source_target_pairs={{0,1},{1,0},{2,3},{3,2},{4,5},{5,4},{6,7},{7,6},{8,9},{9,8},{10,11... | collective-permute-start | bytes 835592 | tf_op jit(solution)/shard_map/ppermute | solution.py:203
  10.4 1.2 %copy-start = (f32[256,1024]{1,0:T(8,128)S(1)}, f32[256,1024]{1,0:T(8,128)}, u32[]{:S(2)}) copy-start(f32[256,1024]{1,0:T(8,128)} %x_ref.1) | copy-start | bytes 3145732
  11.8 7.9 %collective-permute-start.1 = (f32[2,256,128]{2,1,0:T(8,128)S(1)}, f32[2,256,128]{2,1,0:T(8,128)S(1)}, u32[]{:S(2)}, u32[]{:S(2)}) collective-permute-start(f32[2,256,128]{2,1,0:T(8,128)S(1)} %pad_maximum_fusion.10.refs_0_), channel_id=1, source_target_pairs={{0,4},{1,5},{2,6},{3,7},{4,0},{5,1},{6,2},{7,3},{8,12},{9,13},{10,... | collective-permute-start | bytes 786440 | tf_op jit(solution)/shard_map/ppermute | solution.py:203
  15.5 28.0 %collective-permute-start.7 = (f32[2,136,128]{2,1,0:T(8,128)S(1)}, f32[2,136,128]{2,1,0:T(8,128)S(1)}, u32[]{:S(2)}, u32[]{:S(2)}) collective-permute-start(f32[2,136,128]{2,1,0:T(8,128)S(1)} %pad_maximum_fusion.16), channel_id=1, source_target_pairs={{0,12},{1,13},{2,14},{3,15},{4,8},{5,9},{6,10},{7,11},{8,4},{9,5},... | collective-permute-start | bytes 417800 | tf_op jit(solution)/shard_map/ppermute | solution.py:203
  19.7 14.5 %collective-permute-start.5 = (f32[1312,128]{1,0:T(8,128)S(1)}, f32[1312,128]{1,0:T(8,128)S(1)}, u32[]{:S(2)}, u32[]{:S(2)}) collective-permute-start(f32[1312,128]{1,0:T(8,128)S(1)} %pad_maximum_fusion.1), channel_id=1, source_target_pairs={{0,2},{1,3},{2,0},{3,1},{4,6},{5,7},{6,4},{7,5},{8,10},{9,11},{10,... | collective-permute-start | bytes 2015240 | tf_op jit(solution)/shard_map/ppermute | solution.py:203
  20.5 23.0 %collective-permute-start.6 = (f32[2,136,128]{2,1,0:T(8,128)S(1)}, f32[2,136,128]{2,1,0:T(8,128)S(1)}, u32[]{:S(2)}, u32[]{:S(2)}) collective-permute-start(f32[2,136,128]{2,1,0:T(8,128)S(1)} %pad_maximum_fusion.15), channel_id=1, source_target_pairs={{0,8},{1,9},{2,10},{3,11},{4,12},{5,13},{6,14},{7,15},{8,0},{9,1},... | collective-permute-start | bytes 417800 | tf_op jit(solution)/shard_map/ppermute | solution.py:203
  25.4 18.0 %collective-permute-start.3 = (f32[1312,128]{1,0:T(8,128)S(1)}, f32[1312,128]{1,0:T(8,128)S(1)}, u32[]{:S(2)}, u32[]{:S(2)}) collective-permute-start(f32[1312,128]{1,0:T(8,128)S(1)} %pad_maximum_fusion), channel_id=1, source_target_pairs={{0,1},{1,0},{2,3},{3,2},{4,5},{5,4},{6,7},{7,6},{8,9},{9,8},{10,11... | collective-permute-start | bytes 2015240 | tf_op jit(solution)/shard_map/ppermute | solution.py:203
  34.3 21.8 %collective-permute-start.10 = (f32[3,256,128]{2,1,0:T(8,128)S(1)}, f32[3,256,128]{2,1,0:T(8,128)S(1)}, u32[]{:S(2)}, u32[]{:S(2)}) collective-permute-start(f32[3,256,128]{2,1,0:T(8,128)S(1)} %pad_maximum_fusion.5), channel_id=1, source_target_pairs={{0,1},{1,0},{2,3},{3,2},{4,5},{5,4},{6,7},{7,6},{8,9},{9,8},{10,11... | collective-permute-start | bytes 1179656 | tf_op jit(solution)/shard_map/ppermute | solution.py:203
  43.5 6.0 %collective-permute-start.8 = (f32[2,136,128]{2,1,0:T(8,128)S(1)}, f32[2,136,128]{2,1,0:T(8,128)S(1)}, u32[]{:S(2)}, u32[]{:S(2)}) collective-permute-start(f32[2,136,128]{2,1,0:T(8,128)S(1)} %get-tuple-element.24), channel_id=1, source_target_pairs={{0,8},{1,9},{2,10},{3,11},{4,12},{5,13},{6,14},{7,15},{8,0},{9,1},... | collective-permute-start | bytes 417800 | tf_op jit(solution)/shard_map/ppermute | solution.py:203
  43.6 12.6 %collective-permute-start.9 = (f32[2,136,128]{2,1,0:T(8,128)S(1)}, f32[2,136,128]{2,1,0:T(8,128)S(1)}, u32[]{:S(2)}, u32[]{:S(2)}) collective-permute-start(f32[2,136,128]{2,1,0:T(8,128)S(1)} %get-tuple-element.25), channel_id=1, source_target_pairs={{0,12},{1,13},{2,14},{3,15},{4,8},{5,9},{6,10},{7,11},{8,4},{9,5},... | collective-permute-start | bytes 417800 | tf_op jit(solution)/shard_map/ppermute | solution.py:203
  48.6 7.6 %collective-permute-start.13 = (f32[4,136,128]{2,1,0:T(8,128)S(1)}, f32[4,136,128]{2,1,0:T(8,128)S(1)}, u32[]{:S(2)}, u32[]{:S(2)}) collective-permute-start(f32[4,136,128]{2,1,0:T(8,128)S(1)} %pad_maximum_fusion.9), channel_id=1, source_target_pairs={{0,4},{1,5},{2,6},{3,7},{4,0},{5,1},{6,2},{7,3},{8,12},{9,13},{10,... | collective-permute-start | bytes 835592 | tf_op jit(solution)/shard_map/ppermute | solution.py:203
  48.6 7.8 %collective-permute-start.11 = (f32[3,256,128]{2,1,0:T(8,128)S(1)}, f32[3,256,128]{2,1,0:T(8,128)S(1)}, u32[]{:S(2)}, u32[]{:S(2)}) collective-permute-start(f32[3,256,128]{2,1,0:T(8,128)S(1)} %pad_maximum_fusion.6), channel_id=1, source_target_pairs={{0,2},{1,3},{2,0},{3,1},{4,6},{5,7},{6,4},{7,5},{8,10},{9,11},{10,... | collective-permute-start | bytes 1179656 | tf_op jit(solution)/shard_map/ppermute | solution.py:203
  49.5 8.2 %collective-permute-start.12 = (f32[8,136,128]{2,1,0:T(8,128)S(1)}, f32[8,136,128]{2,1,0:T(8,128)S(1)}, u32[]{:S(2)}, u32[]{:S(2)}) collective-permute-start(f32[8,136,128]{2,1,0:T(8,128)S(1)} %constant_dynamic-update-slice_fusion.refs_0_), channel_id=1, source_target_pairs={{0,16},{16,0},{1,17},{17,1},{2,18},{18,2},{3,19},{19,3},{4,20},{20... | collective-permute-start | bytes 1671176 | tf_op jit(solution)/shard_map/ppermute | solution.py:203
  56.1 1.6 %collective-permute-start.14 = (f32[4,136,128]{2,1,0:T(8,128)S(1)}, f32[4,136,128]{2,1,0:T(8,128)S(1)}, u32[]{:S(2)}, u32[]{:S(2)}) collective-permute-start(f32[4,136,128]{2,1,0:T(8,128)S(1)} %collective-permute-done.13.refs_2_), channel_id=1, source_target_pairs={{0,16},{16,0},{1,17},{17,1},{2,18},{18,2},{3,19},{19,3},{4,20},{20... | collective-permute-start | bytes 835592 | tf_op jit(solution)/shard_map/ppermute | solution.py:203
  56.5 1.6 %collective-permute-start.15 = (f32[4,136,128]{2,1,0:T(8,128)S(1)}, f32[4,136,128]{2,1,0:T(8,128)S(1)}, u32[]{:S(2)}, u32[]{:S(2)}) collective-permute-start(f32[4,136,128]{2,1,0:T(8,128)S(1)} %constant_dynamic-update-slice_fusion.3.refs_4_), channel_id=1, source_target_pairs={{0,16},{16,0},{1,17},{17,1},{2,18},{18,2},{3,19},{19,3},{4,20},{20... | collective-permute-start | bytes 835592 | tf_op jit(solution)/shard_map/ppermute | solution.py:203

commit v14 on v12

--- a/solution.py
+++ b/solution.py
@@ -265,7 +265,7 @@
     pieces = [piece for piece, _, _ in places]
     positions = [tuple(p ^ step for p in part) for _, step, part in places]
     groups = []
-    for planes in (near[:1] + come_first, near[1:] + come_last):
+    for planes in (near[:1], come_first, near[1:], come_last[: half // 2], come_last[half // 2 :]):
         mine = jnp.concatenate(planes, axis=0)
         groups.append(
             [mine] + [send(mine, "row", lambda i: (i + q) % rows_axis) for q in range(1, rows_axis)]

time: 69.8 us -> 61.7 us (0.88)
  waiting for transfers between devices: 38.1 us -> 25.7 us
  starting transfers between devices: 22.7 us -> 25.7 us
  local copies, waits for them, and re-layouts: 1.42 us -> 2.58 us
    ppermute x15 -> x18, waiting for transfers between devices: 38.1 us -> 25.7 us  [send(): return lax.ppermute(x, axis, [(i, partner(i)) for i in range(size)])]
    ppermute x15 -> x18, starting transfers between devices: 22.7 us -> 25.7 us  [send(): return lax.ppermute(x, axis, [(i, partner(i)) for i in range(size)])]
    unnamed x10 -> x7, local copies, waits for them, and re-layouts: 1.1 us -> 2.27 us
  transfers between devices with their start and end apart: 15 -> 18, of which waited for: 10 -> 8; matrix products, arithmetic and copies ran while one was open for 2% -> 2% of each run, Pallas kernels for 3% -> 3%
where the time goes in v14:
time: 61.7 us; the launch traced here: 61.5 us
  starting transfers between devices  25.7 us (42%)
  waiting for transfers between devices  25.7 us (42%)
  Pallas kernels  6.13 us (10%)
  local copies, waits for them, and re-layouts  2.58 us (4%)
  other arithmetic  1.08 us (2%)
    ppermute x18, starting transfers between devices, send(): return lax.ppermute(x, axis, [(i, partner(i)) for i in range(size)])  25.7 us
    ppermute x18, waiting for transfers between devices, send(): return lax.ppermute(x, axis, [(i, partner(i)) for i in range(size)])  25.7 us
    pallas_call x1, Pallas kernels, contract(): pl.pallas_call(functools.partial(contract_kernel, len(groups), len(groups...  4.33 us
    unnamed x7, local copies, waits for them, and re-layouts  2.27 us
    pallas_call x1, Pallas kernels, pack(): pl.pallas_call(pack_kernel, out_shape=[out] * 4, in_specs=[pl.BlockSpec(m...  1.48 us
  transfers between devices with their start and end apart: 18, of which 8 were waited for; matrix products, arithmetic and copies ran while one was open for 2% of the time, Pallas kernels for 3%

profile of v14, /device:TPU:0, one launch (start us, length us, event | category | flops | bytes accessed | tf_op | source)
XLA Modules:
  0.0 61.5 jit_solution(18110690045961084575)
XLA Ops:
  0.0 4.0 %collective-permute-start = (f32[1,256,128]{2,1,0:T(8,128)}, f32[1,256,128]{2,1,0:T(8,128)S(1)}, u32[]{:S(2)}, u32[]{:S(2)}) collective-permute-start(f32[1,256,128]{2,1,0:T(8,128)} %bitcast.41), channel_id=1, source_target_pairs={{0,8},{1,9},{2,10},{3,11},{4,12},{5,13},{6,14},{7,15},{8,0},{9,1},... | collective-permute-start | bytes 393224 | tf_op jit(solution)/shard_map/ppermute | solution.py:203
  4.0 0.7 %fusion.1.words_ref = s32[16]{0:T(128)S(1)} fusion(s32[16]{0:T(128)} %param.11, s32[16]{0:T(128)} %param.10, s32[16,1]{0,1:T(1,128)} %param.9), kind=kLoop, calls=%fused_computation.32 | loop fusion | flops 64 | bytes 256 | tf_op jit(solution)/shard_map/add | solution.py:56
  4.7 0.0 copy-start.1
  4.7 1.0 %copy-done.1 = f32[16,64,128]{2,1,0:T(8,128)S(1)} copy-done((f32[16,64,128]{2,1,0:T(8,128)S(1)}, f32[16,64,128]{2,1,0:T(8,128)}, u32[]{:S(2)}) %copy-start.1) | copy-done | bytes 524312
  5.8 0.0 copy-start.2
  5.8 1.5 %shard_map.64 = (f32[4,136,128]{2,1,0:T(8,128)S(1)}, f32[4,136,128]{2,1,0:T(8,128)S(1)}, f32[4,136,128]{2,1,0:T(8,128)S(1)}, f32[4,136,128]{2,1,0:T(8,128)S(1)}) custom-call(s32[16]{0:T(128)S(1)} %fusion.1.words_ref, f32[16,64,128]{2,1,0:T(8,128)S(1)} %copy-done.1), custom_call_target="tpu_custom_call" | custom-call | bytes 1572864 | tf_op jit(solution)/shard_map/pallas_call | solution.py:58
  7.3 1.6 %collective-permute-start.2 = (f32[4,136,128]{2,1,0:T(8,128)S(1)}, f32[4,136,128]{2,1,0:T(8,128)S(1)}, u32[]{:S(2)}, u32[]{:S(2)}) collective-permute-start(f32[4,136,128]{2,1,0:T(8,128)S(1)} %get-tuple-element.17), channel_id=1, source_target_pairs={{0,2},{1,3},{2,0},{3,1},{4,6},{5,7},{6,4},{7,5},{8,10},{9,11},{10,... | collective-permute-start | bytes 835592 | tf_op jit(solution)/shard_map/ppermute | solution.py:203
  8.8 1.5 %collective-permute-start.4 = (f32[4,136,128]{2,1,0:T(8,128)S(1)}, f32[4,136,128]{2,1,0:T(8,128)S(1)}, u32[]{:S(2)}, u32[]{:S(2)}) collective-permute-start(f32[4,136,128]{2,1,0:T(8,128)S(1)} %get-tuple-element.19), channel_id=1, source_target_pairs={{0,1},{1,0},{2,3},{3,2},{4,5},{5,4},{6,7},{7,6},{8,9},{9,8},{10,11... | collective-permute-start | bytes 835592 | tf_op jit(solution)/shard_map/ppermute | solution.py:203
  10.4 0.0 copy-start
  10.4 1.2 %copy-done = f32[256,1024]{1,0:T(8,128)S(1)} copy-done((f32[256,1024]{1,0:T(8,128)S(1)}, f32[256,1024]{1,0:T(8,128)}, u32[]{:S(2)}) %copy-start) | copy-done | bytes 1048600
  11.6 0.1 shard_map.66.refs_10_
  11.7 0.0 collective-permute-done
  11.7 0.0 copy-done.2
  11.8 1.6 %collective-permute-start.1 = (f32[2,256,128]{2,1,0:T(8,128)S(1)}, f32[2,256,128]{2,1,0:T(8,128)S(1)}, u32[]{:S(2)}, u32[]{:S(2)}) collective-permute-start(f32[2,256,128]{2,1,0:T(8,128)S(1)} %pad_maximum_fusion.11.refs_0_), channel_id=1, source_target_pairs={{0,4},{1,5},{2,6},{3,7},{4,0},{5,1},{6,2},{7,3},{8,12},{9,13},{10,... | collective-permute-start | bytes 786440 | tf_op jit(solution)/shard_map/ppermute | solution.py:203
  13.4 3.3 %collective-permute-done.4 = f32[4,136,128]{2,1,0:T(8,128)S(1)} collective-permute-done((f32[4,136,128]{2,1,0:T(8,128)S(1)}, f32[4,136,128]{2,1,0:T(8,128)S(1)}, u32[]{:S(2)}, u32[]{:S(2)}) %collective-permute-start.4) | collective-permute-done | bytes 278560 | tf_op jit(solution)/shard_map/ppermute | solution.py:203
  16.7 0.4 collective-permute-start.8
  17.1 0.0 collective-permute-done.2
  17.2 3.3 %collective-permute-done.1.refs_1_ = f32[2,256,128]{2,1,0:T(8,128)S(1)} collective-permute-done((f32[2,256,128]{2,1,0:T(8,128)S(1)}, f32[2,256,128]{2,1,0:T(8,128)S(1)}, u32[]{:S(2)}, u32[]{:S(2)}) %collective-permute-start.1) | collective-permute-done | bytes 262176 | tf_op jit(solution)/shard_map/ppermute | solution.py:203
  20.5 0.1 pad_maximum_fusion.4
  20.7 0.6 collective-permute-start.5
  21.3 1.5 %collective-permute-start.3 = (f32[1312,128]{1,0:T(8,128)S(1)}, f32[1312,128]{1,0:T(8,128)S(1)}, u32[]{:S(2)}, u32[]{:S(2)}) collective-permute-start(f32[1312,128]{1,0:T(8,128)S(1)} %pad_maximum_fusion), channel_id=1, source_target_pairs={{0,1},{1,0},{2,3},{3,2},{4,5},{5,4},{6,7},{7,6},{8,9},{9,8},{10,11... | collective-permute-start | bytes 2015240 | tf_op jit(solution)/shard_map/ppermute | solution.py:203
  22.8 5.0 %collective-permute-start.9 = (f32[2,136,128]{2,1,0:T(8,128)S(1)}, f32[2,136,128]{2,1,0:T(8,128)S(1)}, u32[]{:S(2)}, u32[]{:S(2)}) collective-permute-start(f32[2,136,128]{2,1,0:T(8,128)S(1)} %pad_maximum_fusion.17), channel_id=1, source_target_pairs={{0,12},{1,13},{2,14},{3,15},{4,8},{5,9},{6,10},{7,11},{8,4},{9,5},... | collective-permute-start | bytes 417800 | tf_op jit(solution)/shard_map/ppermute | solution.py:203
  27.9 6.9 %collective-permute-done.5 = f32[1312,128]{1,0:T(8,128)S(1)} collective-permute-done((f32[1312,128]{1,0:T(8,128)S(1)}, f32[1312,128]{1,0:T(8,128)S(1)}, u32[]{:S(2)}, u32[]{:S(2)}) %collective-permute-start.5) | collective-permute-done | bytes 671776 | tf_op jit(solution)/shard_map/ppermute | solution.py:203
  34.8 0.4 collective-permute-start.6
  35.3 1.4 %collective-permute-done.3 = f32[1312,128]{1,0:T(8,128)S(1)} collective-permute-done((f32[1312,128]{1,0:T(8,128)S(1)}, f32[1312,128]{1,0:T(8,128)S(1)}, u32[]{:S(2)}, u32[]{:S(2)}) %collective-permute-start.3) | collective-permute-done | bytes 671776 | tf_op jit(solution)/shard_map/ppermute | solution.py:203
  36.8 2.1 %collective-permute-start.7 = (f32[3,256,128]{2,1,0:T(8,128)S(1)}, f32[3,256,128]{2,1,0:T(8,128)S(1)}, u32[]{:S(2)}, u32[]{:S(2)}) collective-permute-start(f32[3,256,128]{2,1,0:T(8,128)S(1)} %pad_maximum_fusion.6), channel_id=1, source_target_pairs={{0,2},{1,3},{2,0},{3,1},{4,6},{5,7},{6,4},{7,5},{8,10},{9,11},{10,... | collective-permute-start | bytes 1179656 | tf_op jit(solution)/shard_map/ppermute | solution.py:203
  38.9 0.0 collective-permute-done.8
  38.9 0.0 collective-permute-done.9
  39.0 0.8 %collective-permute-start.12 = (f32[4,136,128]{2,1,0:T(8,128)S(1)}, f32[4,136,128]{2,1,0:T(8,128)S(1)}, u32[]{:S(2)}, u32[]{:S(2)}) collective-permute-start(f32[4,136,128]{2,1,0:T(8,128)S(1)} %pad_maximum_fusion.10), channel_id=1, source_target_pairs={{0,4},{1,5},{2,6},{3,7},{4,0},{5,1},{6,2},{7,3},{8,12},{9,13},{10,... | collective-permute-start | bytes 835592 | tf_op jit(solution)/shard_map/ppermute | solution.py:203
  39.8 5.1 %collective-permute-start.14 = (f32[2,136,128]{2,1,0:T(8,128)S(1)}, f32[2,136,128]{2,1,0:T(8,128)S(1)}, u32[]{:S(2)}, u32[]{:S(2)}) collective-permute-start(f32[2,136,128]{2,1,0:T(8,128)S(1)} %get-tuple-element.24), channel_id=1, source_target_pairs={{0,8},{1,9},{2,10},{3,11},{4,12},{5,13},{6,14},{7,15},{8,0},{9,1},... | collective-permute-start | bytes 417800 | tf_op jit(solution)/shard_map/ppermute | solution.py:203
  44.9 0.0 collective-permute-start.16
  45.0 4.7 %collective-permute-done.14.refs_6_ = f32[2,136,128]{2,1,0:T(8,128)S(1)} collective-permute-done((f32[2,136,128]{2,1,0:T(8,128)S(1)}, f32[2,136,128]{2,1,0:T(8,128)S(1)}, u32[]{:S(2)}, u32[]{:S(2)}) %collective-permute-start.14) | collective-permute-done | bytes 139296 | tf_op jit(solution)/shard_map/ppermute | solution.py:203
  49.7 0.0 collective-permute-start.10
  49.7 5.1 %collective-permute-done.16.refs_8_ = f32[2,136,128]{2,1,0:T(8,128)S(1)} collective-permute-done((f32[2,136,128]{2,1,0:T(8,128)S(1)}, f32[2,136,128]{2,1,0:T(8,128)S(1)}, u32[]{:S(2)}, u32[]{:S(2)}) %collective-permute-start.16) | collective-permute-done | bytes 139296 | tf_op jit(solution)/shard_map/ppermute | solution.py:203
  54.8 0.0 collective-permute-start.11
  54.8 0.0 collective-permute-done.12.refs_4_
  54.8 0.5 collective-permute-start.13
  55.3 0.0 collective-permute-done.6
  55.3 0.1 collective-permute-start.15
  55.4 0.0 collective-permute-done.7
  55.4 0.4 collective-permute-start.17
  56.0 0.3 shard_map.65.split_ref
  56.3 0.7 %collective-permute-done.15.refs_7_ = f32[2,136,128]{2,1,0:T(8,128)S(1)} collective-permute-done((f32[2,136,128]{2,1,0:T(8,128)S(1)}, f32[2,136,128]{2,1,0:T(8,128)S(1)}, u32[]{:S(2)}, u32[]{:S(2)}) %collective-permute-start.15) | collective-permute-done | bytes 139296 | tf_op jit(solution)/shard_map/ppermute | solution.py:203
  57.0 0.2 collective-permute-done.17.refs_9_
  57.2 0.0 collective-permute-done.10.refs_1_
  57.2 0.0 collective-permute-done.11.refs_3_
  57.2 0.0 collective-permute-done.13.refs_5_
  57.2 4.3 %shard_map.67 = f32[256,1024]{1,0:T(8,128)} custom-call(bf16[16,256,256]{2,1,0:T(8,128)(2,1)S(1)} %shard_map.65.split_ref, f32[4,136,128]{2,1,0:T(8,128)S(1)} %pad_maximum_fusion.9.refs_0_, f32[4,136,128]{2,1,0:T(8,128)S(1)} %collective-permute-done.10.refs_1_, f32[4,136,128]{2,1,0:T(8,128)S(1)} %constant_dynamic-update-slice_fusion.refs_2_, ...), custom_call_target="tpu_custom_call" | custom-call | tf_op jit(solution)/shard_map/pallas_call | solution.py:173
  (34 shorter events, 0.6 us)
Async XLA Ops:
  0.0 11.7 %collective-permute-start = (f32[1,256,128]{2,1,0:T(8,128)}, f32[1,256,128]{2,1,0:T(8,128)S(1)}, u32[]{:S(2)}, u32[]{:S(2)}) collective-permute-start(f32[1,256,128]{2,1,0:T(8,128)} %bitcast.41), channel_id=1, source_target_pairs={{0,8},{1,9},{2,10},{3,11},{4,12},{5,13},{6,14},{7,15},{8,0},{9,1},... | collective-permute-start | bytes 393224 | tf_op jit(solution)/shard_map/ppermute | solution.py:203
  4.7 1.0 %copy-start.1 = (f32[16,64,128]{2,1,0:T(8,128)S(1)}, f32[16,64,128]{2,1,0:T(8,128)}, u32[]{:S(2)}) copy-start(f32[16,64,128]{2,1,0:T(8,128)} %tiles_ref.1) | copy-start | bytes 1572868
  5.8 5.9 %copy-start.2 = (f32[256,128]{1,0:T(8,128)S(1)}, f32[256,128]{1,0:T(8,128)}, u32[]{:S(2)}) copy-start(f32[256,128]{1,0:T(8,128)} %param.7) | copy-start | bytes 393220
  7.3 9.9 %collective-permute-start.2 = (f32[4,136,128]{2,1,0:T(8,128)S(1)}, f32[4,136,128]{2,1,0:T(8,128)S(1)}, u32[]{:S(2)}, u32[]{:S(2)}) collective-permute-start(f32[4,136,128]{2,1,0:T(8,128)S(1)} %get-tuple-element.17), channel_id=1, source_target_pairs={{0,2},{1,3},{2,0},{3,1},{4,6},{5,7},{6,4},{7,5},{8,10},{9,11},{10,... | collective-permute-start | bytes 835592 | tf_op jit(solution)/shard_map/ppermute | solution.py:203
  8.8 7.8 %collective-permute-start.4 = (f32[4,136,128]{2,1,0:T(8,128)S(1)}, f32[4,136,128]{2,1,0:T(8,128)S(1)}, u32[]{:S(2)}, u32[]{:S(2)}) collective-permute-start(f32[4,136,128]{2,1,0:T(8,128)S(1)} %get-tuple-element.19), channel_id=1, source_target_pairs={{0,1},{1,0},{2,3},{3,2},{4,5},{5,4},{6,7},{7,6},{8,9},{9,8},{10,11... | collective-permute-start | bytes 835592 | tf_op jit(solution)/shard_map/ppermute | solution.py:203
  10.4 1.2 %copy-start = (f32[256,1024]{1,0:T(8,128)S(1)}, f32[256,1024]{1,0:T(8,128)}, u32[]{:S(2)}) copy-start(f32[256,1024]{1,0:T(8,128)} %x_ref.1) | copy-start | bytes 3145732
  11.8 8.8 %collective-permute-start.1 = (f32[2,256,128]{2,1,0:T(8,128)S(1)}, f32[2,256,128]{2,1,0:T(8,128)S(1)}, u32[]{:S(2)}, u32[]{:S(2)}) collective-permute-start(f32[2,256,128]{2,1,0:T(8,128)S(1)} %pad_maximum_fusion.11.refs_0_), channel_id=1, source_target_pairs={{0,4},{1,5},{2,6},{3,7},{4,0},{5,1},{6,2},{7,3},{8,12},{9,13},{10,... | collective-permute-start | bytes 786440 | tf_op jit(solution)/shard_map/ppermute | solution.py:203
  16.7 22.2 %collective-permute-start.8 = (f32[2,136,128]{2,1,0:T(8,128)S(1)}, f32[2,136,128]{2,1,0:T(8,128)S(1)}, u32[]{:S(2)}, u32[]{:S(2)}) collective-permute-start(f32[2,136,128]{2,1,0:T(8,128)S(1)} %pad_maximum_fusion.16), channel_id=1, source_target_pairs={{0,8},{1,9},{2,10},{3,11},{4,12},{5,13},{6,14},{7,15},{8,0},{9,1},... | collective-permute-start | bytes 417800 | tf_op jit(solution)/shard_map/ppermute | solution.py:203
  20.7 14.1 %collective-permute-start.5 = (f32[1312,128]{1,0:T(8,128)S(1)}, f32[1312,128]{1,0:T(8,128)S(1)}, u32[]{:S(2)}, u32[]{:S(2)}) collective-permute-start(f32[1312,128]{1,0:T(8,128)S(1)} %pad_maximum_fusion.1), channel_id=1, source_target_pairs={{0,2},{1,3},{2,0},{3,1},{4,6},{5,7},{6,4},{7,5},{8,10},{9,11},{10,... | collective-permute-start | bytes 2015240 | tf_op jit(solution)/shard_map/ppermute | solution.py:203
  21.3 15.4 %collective-permute-start.3 = (f32[1312,128]{1,0:T(8,128)S(1)}, f32[1312,128]{1,0:T(8,128)S(1)}, u32[]{:S(2)}, u32[]{:S(2)}) collective-permute-start(f32[1312,128]{1,0:T(8,128)S(1)} %pad_maximum_fusion), channel_id=1, source_target_pairs={{0,1},{1,0},{2,3},{3,2},{4,5},{5,4},{6,7},{7,6},{8,9},{9,8},{10,11... | collective-permute-start | bytes 2015240 | tf_op jit(solution)/shard_map/ppermute | solution.py:203
  22.8 16.1 %collective-permute-start.9 = (f32[2,136,128]{2,1,0:T(8,128)S(1)}, f32[2,136,128]{2,1,0:T(8,128)S(1)}, u32[]{:S(2)}, u32[]{:S(2)}) collective-permute-start(f32[2,136,128]{2,1,0:T(8,128)S(1)} %pad_maximum_fusion.17), channel_id=1, source_target_pairs={{0,12},{1,13},{2,14},{3,15},{4,8},{5,9},{6,10},{7,11},{8,4},{9,5},... | collective-permute-start | bytes 417800 | tf_op jit(solution)/shard_map/ppermute | solution.py:203
  34.8 20.5 %collective-permute-start.6 = (f32[3,256,128]{2,1,0:T(8,128)S(1)}, f32[3,256,128]{2,1,0:T(8,128)S(1)}, u32[]{:S(2)}, u32[]{:S(2)}) collective-permute-start(f32[3,256,128]{2,1,0:T(8,128)S(1)} %pad_maximum_fusion.5), channel_id=1, source_target_pairs={{0,1},{1,0},{2,3},{3,2},{4,5},{5,4},{6,7},{7,6},{8,9},{9,8},{10,11... | collective-permute-start | bytes 1179656 | tf_op jit(solution)/shard_map/ppermute | solution.py:203
  36.8 18.7 %collective-permute-start.7 = (f32[3,256,128]{2,1,0:T(8,128)S(1)}, f32[3,256,128]{2,1,0:T(8,128)S(1)}, u32[]{:S(2)}, u32[]{:S(2)}) collective-permute-start(f32[3,256,128]{2,1,0:T(8,128)S(1)} %pad_maximum_fusion.6), channel_id=1, source_target_pairs={{0,2},{1,3},{2,0},{3,1},{4,6},{5,7},{6,4},{7,5},{8,10},{9,11},{10,... | collective-permute-start | bytes 1179656 | tf_op jit(solution)/shard_map/ppermute | solution.py:203
  39.0 15.9 %collective-permute-start.12 = (f32[4,136,128]{2,1,0:T(8,128)S(1)}, f32[4,136,128]{2,1,0:T(8,128)S(1)}, u32[]{:S(2)}, u32[]{:S(2)}) collective-permute-start(f32[4,136,128]{2,1,0:T(8,128)S(1)} %pad_maximum_fusion.10), channel_id=1, source_target_pairs={{0,4},{1,5},{2,6},{3,7},{4,0},{5,1},{6,2},{7,3},{8,12},{9,13},{10,... | collective-permute-start | bytes 835592 | tf_op jit(solution)/shard_map/ppermute | solution.py:203
  39.8 9.9 %collective-permute-start.14 = (f32[2,136,128]{2,1,0:T(8,128)S(1)}, f32[2,136,128]{2,1,0:T(8,128)S(1)}, u32[]{:S(2)}, u32[]{:S(2)}) collective-permute-start(f32[2,136,128]{2,1,0:T(8,128)S(1)} %get-tuple-element.24), channel_id=1, source_target_pairs={{0,8},{1,9},{2,10},{3,11},{4,12},{5,13},{6,14},{7,15},{8,0},{9,1},... | collective-permute-start | bytes 417800 | tf_op jit(solution)/shard_map/ppermute | solution.py:203
  44.9 9.9 %collective-permute-start.16 = (f32[2,136,128]{2,1,0:T(8,128)S(1)}, f32[2,136,128]{2,1,0:T(8,128)S(1)}, u32[]{:S(2)}, u32[]{:S(2)}) collective-permute-start(f32[2,136,128]{2,1,0:T(8,128)S(1)} %get-tuple-element.25), channel_id=1, source_target_pairs={{0,12},{1,13},{2,14},{3,15},{4,8},{5,9},{6,10},{7,11},{8,4},{9,5},... | collective-permute-start | bytes 417800 | tf_op jit(solution)/shard_map/ppermute | solution.py:203
  49.7 7.5 %collective-permute-start.10 = (f32[4,136,128]{2,1,0:T(8,128)S(1)}, f32[4,136,128]{2,1,0:T(8,128)S(1)}, u32[]{:S(2)}, u32[]{:S(2)}) collective-permute-start(f32[4,136,128]{2,1,0:T(8,128)S(1)} %pad_maximum_fusion.9.refs_0_), channel_id=1, source_target_pairs={{0,16},{16,0},{1,17},{17,1},{2,18},{18,2},{3,19},{19,3},{4,20},{20... | collective-permute-start | bytes 835592 | tf_op jit(solution)/shard_map/ppermute | solution.py:203
  54.8 2.4 %collective-permute-start.11 = (f32[4,136,128]{2,1,0:T(8,128)S(1)}, f32[4,136,128]{2,1,0:T(8,128)S(1)}, u32[]{:S(2)}, u32[]{:S(2)}) collective-permute-start(f32[4,136,128]{2,1,0:T(8,128)S(1)} %constant_dynamic-update-slice_fusion.refs_2_), channel_id=1, source_target_pairs={{0,16},{16,0},{1,17},{17,1},{2,18},{18,2},{3,19},{19,3},{4,20},{20... | collective-permute-start | bytes 835592 | tf_op jit(solution)/shard_map/ppermute | solution.py:203
  54.8 2.4 %collective-permute-start.13 = (f32[4,136,128]{2,1,0:T(8,128)S(1)}, f32[4,136,128]{2,1,0:T(8,128)S(1)}, u32[]{:S(2)}, u32[]{:S(2)}) collective-permute-start(f32[4,136,128]{2,1,0:T(8,128)S(1)} %collective-permute-done.12.refs_4_), channel_id=1, source_target_pairs={{0,16},{16,0},{1,17},{17,1},{2,18},{18,2},{3,19},{19,3},{4,20},{20... | collective-permute-start | bytes 835592 | tf_op jit(solution)/shard_map/ppermute | solution.py:203
  55.3 1.6 %collective-permute-start.15 = (f32[2,136,128]{2,1,0:T(8,128)S(1)}, f32[2,136,128]{2,1,0:T(8,128)S(1)}, u32[]{:S(2)}, u32[]{:S(2)}) collective-permute-start(f32[2,136,128]{2,1,0:T(8,128)S(1)} %collective-permute-done.14.refs_6_), channel_id=1, source_target_pairs={{0,16},{16,0},{1,17},{17,1},{2,18},{18,2},{3,19},{19,3},{4,20},{20... | collective-permute-start | bytes 417800 | tf_op jit(solution)/shard_map/ppermute | solution.py:203
  55.4 1.8 %collective-permute-start.17 = (f32[2,136,128]{2,1,0:T(8,128)S(1)}, f32[2,136,128]{2,1,0:T(8,128)S(1)}, u32[]{:S(2)}, u32[]{:S(2)}) collective-permute-start(f32[2,136,128]{2,1,0:T(8,128)S(1)} %collective-permute-done.16.refs_8_), channel_id=1, source_target_pairs={{0,16},{16,0},{1,17},{17,1},{2,18},{18,2},{3,19},{19,3},{4,20},{20... | collective-permute-start | bytes 417800 | tf_op jit(solution)/shard_map/ppermute | solution.py:203

commit v15 on v11

--- a/solution.py
+++ b/solution.py
@@ -251,8 +251,10 @@
     pieces += [hop(late_y[:cut], 1), hop(late_x[cut:], 2)]
     positions = [tuple(p ^ step for p in at) for step in (0, 4, 1, 2, 5, 6)]
     positions += [tuple(p ^ step for p in part) for step in (3, 7) for part in (at[:cut], at[cut:])]
+    ends = (come_last, near[1:], pieces[-2], pieces[-1])
+    come_last, near[1:], pieces[-2], pieces[-1] = lax.optimization_barrier(ends)
     groups = []
-    for planes in (near[:1] + come_first, near[1:] + come_last):
+    for planes in (near[:1] + come_first, near[1:], come_last):
         mine = jnp.concatenate(planes, axis=0)
         groups.append(
             [mine] + [send(mine, "row", lambda i: (i + q) % rows_axis) for q in range(1, rows_axis)]

time: 57.6 us -> 56.1 us (0.974)
  waiting for transfers between devices: 25.1 us -> 23.2 us
    ppermute x17 -> x18, waiting for transfers between devices: 25.1 us -> 23.2 us  [send(): return lax.ppermute(x, axis, [(i, partner(i)) for i in range(size)])]
    ppermute x17 -> x18, starting transfers between devices: 23.7 us -> 24.1 us  [send(): return lax.ppermute(x, axis, [(i, partner(i)) for i in range(size)])]
  transfers between devices with their start and end apart: 17 -> 18, of which waited for: 8 -> 11; matrix products, arithmetic and copies ran while one was open for 2% -> 2% of each run, Pallas kernels for 3% -> 3%
where the time goes in v15:
time: 56.1 us; the launch traced here: 56 us
  starting transfers between devices  24.1 us (43%)
  waiting for transfers between devices  23.2 us (41%)
  Pallas kernels  5.96 us (11%)
  local copies, waits for them, and re-layouts  1.36 us (2%)
  other arithmetic  0.99 us (2%)
    ppermute x18, starting transfers between devices, send(): return lax.ppermute(x, axis, [(i, partner(i)) for i in range(size)])  24.1 us
    ppermute x18, waiting for transfers between devices, send(): return lax.ppermute(x, axis, [(i, partner(i)) for i in range(size)])  23.2 us
    pallas_call x1, Pallas kernels, contract(): pl.pallas_call(functools.partial(contract_kernel, len(groups), len(groups...  4.15 us
    pallas_call x1, Pallas kernels, pack(): pl.pallas_call(pack_kernel, out_shape=[out] * 4, in_specs=[pl.BlockSpec(m...  1.48 us
  transfers between devices with their start and end apart: 18, of which 11 were waited for; matrix products, arithmetic and copies ran while one was open for 2% of the time, Pallas kernels for 3%

profile of v15, /device:TPU:0, one launch (start us, length us, event | category | flops | bytes accessed | tf_op | source)
XLA Modules:
  0.0 56.0 jit_solution(4237586183304495164)
XLA Ops:
  0.0 0.0 copy-start
  0.0 4.0 %collective-permute-start = (f32[1,256,128]{2,1,0:T(8,128)}, f32[1,256,128]{2,1,0:T(8,128)S(1)}, u32[]{:S(2)}, u32[]{:S(2)}) collective-permute-start(f32[1,256,128]{2,1,0:T(8,128)} %bitcast.37), channel_id=1, source_target_pairs={{0,8},{1,9},{2,10},{3,11},{4,12},{5,13},{6,14},{7,15},{8,0},{9,1},... | collective-permute-start | bytes 393224 | tf_op jit(solution)/shard_map/ppermute | solution.py:203
  4.0 0.7 %fusion.1.words_ref = s32[16]{0:T(128)S(1)} fusion(s32[16]{0:T(128)} %param.11, s32[16]{0:T(128)} %param.10, s32[16,1]{0,1:T(1,128)} %param.9), kind=kLoop, calls=%fused_computation.33 | loop fusion | flops 64 | bytes 256 | tf_op jit(solution)/shard_map/add | solution.py:56
  4.7 0.0 copy-start.1
  4.7 1.0 %copy-done.1 = f32[16,64,128]{2,1,0:T(8,128)S(1)} copy-done((f32[16,64,128]{2,1,0:T(8,128)S(1)}, f32[16,64,128]{2,1,0:T(8,128)}, u32[]{:S(2)}) %copy-start.1) | copy-done | bytes 524312
  5.8 0.0 copy-start.2
  5.8 1.5 %shard_map.64 = (f32[4,136,128]{2,1,0:T(8,128)S(1)}, f32[4,136,128]{2,1,0:T(8,128)S(1)}, f32[4,136,128]{2,1,0:T(8,128)S(1)}, f32[4,136,128]{2,1,0:T(8,128)S(1)}) custom-call(s32[16]{0:T(128)S(1)} %fusion.1.words_ref, f32[16,64,128]{2,1,0:T(8,128)S(1)} %copy-done.1), custom_call_target="tpu_custom_call" | custom-call | bytes 1572864 | tf_op jit(solution)/shard_map/pallas_call | solution.py:58
  7.3 1.6 %collective-permute-start.2 = (f32[4,136,128]{2,1,0:T(8,128)S(1)}, f32[4,136,128]{2,1,0:T(8,128)S(1)}, u32[]{:S(2)}, u32[]{:S(2)}) collective-permute-start(f32[4,136,128]{2,1,0:T(8,128)S(1)} %get-tuple-element.22), channel_id=1, source_target_pairs={{0,2},{1,3},{2,0},{3,1},{4,6},{5,7},{6,4},{7,5},{8,10},{9,11},{10,... | collective-permute-start | bytes 835592 | tf_op jit(solution)/shard_map/ppermute | solution.py:203
  8.8 1.5 %collective-permute-start.4 = (f32[4,136,128]{2,1,0:T(8,128)S(1)}, f32[4,136,128]{2,1,0:T(8,128)S(1)}, u32[]{:S(2)}, u32[]{:S(2)}) collective-permute-start(f32[4,136,128]{2,1,0:T(8,128)S(1)} %get-tuple-element.24), channel_id=1, source_target_pairs={{0,1},{1,0},{2,3},{3,2},{4,5},{5,4},{6,7},{7,6},{8,9},{9,8},{10,11... | collective-permute-start | bytes 835592 | tf_op jit(solution)/shard_map/ppermute | solution.py:203
  10.4 0.0 copy-done
  10.4 0.1 shard_map.65.refs_6_
  10.5 0.1 collective-permute-done
  10.6 0.0 copy-done.2
  10.6 1.6 %collective-permute-start.1 = (f32[2,256,128]{2,1,0:T(8,128)S(1)}, f32[2,256,128]{2,1,0:T(8,128)S(1)}, u32[]{:S(2)}, u32[]{:S(2)}) collective-permute-start(f32[2,256,128]{2,1,0:T(8,128)S(1)} %pad_maximum_fusion.7.refs_0_), channel_id=1, source_target_pairs={{0,4},{1,5},{2,6},{3,7},{4,0},{5,1},{6,2},{7,3},{8,12},{9,13},{10,... | collective-permute-start | bytes 786440 | tf_op jit(solution)/shard_map/ppermute | solution.py:203
  12.2 3.3 %collective-permute-done.2 = f32[4,136,128]{2,1,0:T(8,128)S(1)} collective-permute-done((f32[4,136,128]{2,1,0:T(8,128)S(1)}, f32[4,136,128]{2,1,0:T(8,128)S(1)}, u32[]{:S(2)}, u32[]{:S(2)}) %collective-permute-start.2) | collective-permute-done | bytes 278560 | tf_op jit(solution)/shard_map/ppermute | solution.py:203
  15.5 1.2 %collective-permute-done.4 = f32[4,136,128]{2,1,0:T(8,128)S(1)} collective-permute-done((f32[4,136,128]{2,1,0:T(8,128)S(1)}, f32[4,136,128]{2,1,0:T(8,128)S(1)}, u32[]{:S(2)}, u32[]{:S(2)}) %collective-permute-start.4) | collective-permute-done | bytes 278560 | tf_op jit(solution)/shard_map/ppermute | solution.py:203
  16.7 0.1 pad_maximum_fusion
  16.8 0.6 %collective-permute-start.5 = (f32[1056,128]{1,0:T(8,128)S(1)}, f32[1056,128]{1,0:T(8,128)S(1)}, u32[]{:S(2)}, u32[]{:S(2)}) collective-permute-start(f32[1056,128]{1,0:T(8,128)S(1)} %get-tuple-element.59), channel_id=1, source_target_pairs={{0,2},{1,3},{2,0},{3,1},{4,6},{5,7},{6,4},{7,5},{8,10},{9,11},{10,... | collective-permute-start | bytes 1622024 | tf_op jit(solution)/shard_map/ppermute | solution.py:203
  17.4 1.5 %collective-permute-start.9 = (f32[2,136,128]{2,1,0:T(8,128)S(1)}, f32[2,136,128]{2,1,0:T(8,128)S(1)}, u32[]{:S(2)}, u32[]{:S(2)}) collective-permute-start(f32[2,136,128]{2,1,0:T(8,128)S(1)} %pad_maximum_fusion.13), channel_id=1, source_target_pairs={{0,12},{1,13},{2,14},{3,15},{4,8},{5,9},{6,10},{7,11},{8,4},{9,5},... | collective-permute-start | bytes 417800 | tf_op jit(solution)/shard_map/ppermute | solution.py:203
  18.9 1.5 %collective-permute-start.3 = (f32[1056,128]{1,0:T(8,128)S(1)}, f32[1056,128]{1,0:T(8,128)S(1)}, u32[]{:S(2)}, u32[]{:S(2)}) collective-permute-start(f32[1056,128]{1,0:T(8,128)S(1)} %get-tuple-element.60), channel_id=1, source_target_pairs={{0,1},{1,0},{2,3},{3,2},{4,5},{5,4},{6,7},{7,6},{8,9},{9,8},{10,11... | collective-permute-start | bytes 1622024 | tf_op jit(solution)/shard_map/ppermute | solution.py:203
  20.4 1.7 %collective-permute-start.8 = (f32[2,136,128]{2,1,0:T(8,128)S(1)}, f32[2,136,128]{2,1,0:T(8,128)S(1)}, u32[]{:S(2)}, u32[]{:S(2)}) collective-permute-start(f32[2,136,128]{2,1,0:T(8,128)S(1)} %pad_maximum_fusion.12), channel_id=1, source_target_pairs={{0,8},{1,9},{2,10},{3,11},{4,12},{5,13},{6,14},{7,15},{8,0},{9,1},... | collective-permute-start | bytes 417800 | tf_op jit(solution)/shard_map/ppermute | solution.py:203
  22.1 7.3 %collective-permute-done.5 = f32[1056,128]{1,0:T(8,128)S(1)} collective-permute-done((f32[1056,128]{1,0:T(8,128)S(1)}, f32[1056,128]{1,0:T(8,128)S(1)}, u32[]{:S(2)}, u32[]{:S(2)}) %collective-permute-start.5) | collective-permute-done | bytes 540704 | tf_op jit(solution)/shard_map/ppermute | solution.py:203
  29.4 1.7 %collective-permute-done.3 = f32[1056,128]{1,0:T(8,128)S(1)} collective-permute-done((f32[1056,128]{1,0:T(8,128)S(1)}, f32[1056,128]{1,0:T(8,128)S(1)}, u32[]{:S(2)}, u32[]{:S(2)}) %collective-permute-start.3) | collective-permute-done | bytes 540704 | tf_op jit(solution)/shard_map/ppermute | solution.py:203
  31.1 0.0 collective-permute-done.1.refs_1_
  31.1 0.1 pad_maximum_fusion.2
  31.2 1.5 %collective-permute-start.7 = (f32[3,256,128]{2,1,0:T(8,128)S(1)}, f32[3,256,128]{2,1,0:T(8,128)S(1)}, u32[]{:S(2)}, u32[]{:S(2)}) collective-permute-start(f32[3,256,128]{2,1,0:T(8,128)S(1)} %get-tuple-element.57), channel_id=1, source_target_pairs={{0,2},{1,3},{2,0},{3,1},{4,6},{5,7},{6,4},{7,5},{8,10},{9,11},{10,... | collective-permute-start | bytes 1179656 | tf_op jit(solution)/shard_map/ppermute | solution.py:203
  32.7 0.0 collective-permute-done.9
  32.7 0.0 collective-permute-done.8
  32.8 1.6 %collective-permute-start.10 = (f32[2,136,128]{2,1,0:T(8,128)S(1)}, f32[2,136,128]{2,1,0:T(8,128)S(1)}, u32[]{:S(2)}, u32[]{:S(2)}) collective-permute-start(f32[2,136,128]{2,1,0:T(8,128)S(1)} %get-tuple-element.25), channel_id=1, source_target_pairs={{0,8},{1,9},{2,10},{3,11},{4,12},{5,13},{6,14},{7,15},{8,0},{9,1},... | collective-permute-start | bytes 417800 | tf_op jit(solution)/shard_map/ppermute | solution.py:203
  34.4 1.3 %collective-permute-start.11 = (f32[2,136,128]{2,1,0:T(8,128)S(1)}, f32[2,136,128]{2,1,0:T(8,128)S(1)}, u32[]{:S(2)}, u32[]{:S(2)}) collective-permute-start(f32[2,136,128]{2,1,0:T(8,128)S(1)} %get-tuple-element.26), channel_id=1, source_target_pairs={{0,12},{1,13},{2,14},{3,15},{4,8},{5,9},{6,10},{7,11},{8,4},{9,5},... | collective-permute-start | bytes 417800 | tf_op jit(solution)/shard_map/ppermute | solution.py:203
  35.6 0.8 %collective-permute-start.12 = (f32[4,136,128]{2,1,0:T(8,128)S(1)}, f32[4,136,128]{2,1,0:T(8,128)S(1)}, u32[]{:S(2)}, u32[]{:S(2)}) collective-permute-start(f32[4,136,128]{2,1,0:T(8,128)S(1)} %pad_maximum_fusion.6), channel_id=1, source_target_pairs={{0,4},{1,5},{2,6},{3,7},{4,0},{5,1},{6,2},{7,3},{8,12},{9,13},{10,... | collective-permute-start | bytes 835592 | tf_op jit(solution)/shard_map/ppermute | solution.py:203
  36.4 1.5 %collective-permute-start.6 = (f32[3,256,128]{2,1,0:T(8,128)S(1)}, f32[3,256,128]{2,1,0:T(8,128)S(1)}, u32[]{:S(2)}, u32[]{:S(2)}) collective-permute-start(f32[3,256,128]{2,1,0:T(8,128)S(1)} %get-tuple-element.58), channel_id=1, source_target_pairs={{0,1},{1,0},{2,3},{3,2},{4,5},{5,4},{6,7},{7,6},{8,9},{9,8},{10,11... | collective-permute-start | bytes 1179656 | tf_op jit(solution)/shard_map/ppermute | solution.py:203
  37.9 1.4 %collective-permute-done.7 = f32[3,256,128]{2,1,0:T(8,128)S(1)} collective-permute-done((f32[3,256,128]{2,1,0:T(8,128)S(1)}, f32[3,256,128]{2,1,0:T(8,128)S(1)}, u32[]{:S(2)}, u32[]{:S(2)}) %collective-permute-start.7) | collective-permute-done | bytes 393248 | tf_op jit(solution)/shard_map/ppermute | solution.py:203
  39.4 1.6 %collective-permute-start.13 = (f32[1,256,128]{2,1,0:T(8,128)S(1)}, f32[1,256,128]{2,1,0:T(8,128)S(1)}, u32[]{:S(2)}, u32[]{:S(2)}) collective-permute-start(f32[1,256,128]{2,1,0:T(8,128)S(1)} %get-tuple-element.47), channel_id=1, source_target_pairs={{0,1},{1,0},{2,3},{3,2},{4,5},{5,4},{6,7},{7,6},{8,9},{9,8},{10,11... | collective-permute-start | bytes 393224 | tf_op jit(solution)/shard_map/ppermute | solution.py:203
  40.9 3.8 %collective-permute-done.6 = f32[3,256,128]{2,1,0:T(8,128)S(1)} collective-permute-done((f32[3,256,128]{2,1,0:T(8,128)S(1)}, f32[3,256,128]{2,1,0:T(8,128)S(1)}, u32[]{:S(2)}, u32[]{:S(2)}) %collective-permute-start.6) | collective-permute-done | bytes 393248 | tf_op jit(solution)/shard_map/ppermute | solution.py:203
  44.7 1.4 %collective-permute-start.14 = (f32[1,256,128]{2,1,0:T(8,128)S(1)}, f32[1,256,128]{2,1,0:T(8,128)S(1)}, u32[]{:S(2)}, u32[]{:S(2)}) collective-permute-start(f32[1,256,128]{2,1,0:T(8,128)S(1)} %get-tuple-element.45), channel_id=1, source_target_pairs={{0,2},{1,3},{2,0},{3,1},{4,6},{5,7},{6,4},{7,5},{8,10},{9,11},{10,... | collective-permute-start | bytes 393224 | tf_op jit(solution)/shard_map/ppermute | solution.py:203
  46.2 0.0 collective-permute-done.10
  46.2 0.1 collective-permute-start.15
  46.3 0.0 collective-permute-done.11
  46.3 0.1 collective-permute-done.12.refs_2_
  46.4 0.0 collective-permute-done.13.refs_8_
  46.4 3.3 %collective-permute-done.14.refs_9_ = f32[1,256,128]{2,1,0:T(8,128)S(1)} collective-permute-done((f32[1,256,128]{2,1,0:T(8,128)S(1)}, f32[1,256,128]{2,1,0:T(8,128)S(1)}, u32[]{:S(2)}, u32[]{:S(2)}) %collective-permute-start.14) | collective-permute-done | bytes 131104 | tf_op jit(solution)/shard_map/ppermute | solution.py:203
  49.8 0.1 collective-permute-start.17
  49.9 0.5 collective-permute-start.16
  50.5 0.3 shard_map.66.split_ref
  50.7 0.0 collective-permute-done.15.refs_1_
  50.8 0.7 %collective-permute-done.17.refs_5_ = f32[4,136,128]{2,1,0:T(8,128)S(1)} collective-permute-done((f32[4,136,128]{2,1,0:T(8,128)S(1)}, f32[4,136,128]{2,1,0:T(8,128)S(1)}, u32[]{:S(2)}, u32[]{:S(2)}) %collective-permute-start.17) | collective-permute-done | bytes 278560 | tf_op jit(solution)/shard_map/ppermute | solution.py:203
  51.4 0.4 collective-permute-done.16.refs_3_
  51.8 4.2 %shard_map.67 = f32[256,1024]{1,0:T(8,128)} custom-call(bf16[16,256,256]{2,1,0:T(8,128)(2,1)S(1)} %shard_map.66.split_ref, f32[8,136,128]{2,1,0:T(8,128)S(1)} %constant_dynamic-update-slice_fusion.refs_0_, f32[8,136,128]{2,1,0:T(8,128)S(1)} %collective-permute-done.15.refs_1_, f32[4,136,128]{2,1,0:T(8,128)S(1)} %collective-permute-done.12.refs_2_, ...), custom_call_target="tpu_custom_call" | custom-call | tf_op jit(solution)/shard_map/pallas_call | solution.py:173
  (31 shorter events, 0.5 us)
Async XLA Ops:
  0.0 10.4 %copy-start = (f32[256,1024]{1,0:T(8,128)S(1)}, f32[256,1024]{1,0:T(8,128)}, u32[]{:S(2)}) copy-start(f32[256,1024]{1,0:T(8,128)} %x_ref.1) | copy-start | bytes 3145732
  0.0 10.5 %collective-permute-start = (f32[1,256,128]{2,1,0:T(8,128)}, f32[1,256,128]{2,1,0:T(8,128)S(1)}, u32[]{:S(2)}, u32[]{:S(2)}) collective-permute-start(f32[1,256,128]{2,1,0:T(8,128)} %bitcast.37), channel_id=1, source_target_pairs={{0,8},{1,9},{2,10},{3,11},{4,12},{5,13},{6,14},{7,15},{8,0},{9,1},... | collective-permute-start | bytes 393224 | tf_op jit(solution)/shard_map/ppermute | solution.py:203
  4.7 1.0 %copy-start.1 = (f32[16,64,128]{2,1,0:T(8,128)S(1)}, f32[16,64,128]{2,1,0:T(8,128)}, u32[]{:S(2)}) copy-start(f32[16,64,128]{2,1,0:T(8,128)} %tiles_ref.1) | copy-start | bytes 1572868
  5.8 4.8 %copy-start.2 = (f32[256,128]{1,0:T(8,128)S(1)}, f32[256,128]{1,0:T(8,128)}, u32[]{:S(2)}) copy-start(f32[256,128]{1,0:T(8,128)} %param.7) | copy-start | bytes 393220
  7.3 8.2 %collective-permute-start.2 = (f32[4,136,128]{2,1,0:T(8,128)S(1)}, f32[4,136,128]{2,1,0:T(8,128)S(1)}, u32[]{:S(2)}, u32[]{:S(2)}) collective-permute-start(f32[4,136,128]{2,1,0:T(8,128)S(1)} %get-tuple-element.22), channel_id=1, source_target_pairs={{0,2},{1,3},{2,0},{3,1},{4,6},{5,7},{6,4},{7,5},{8,10},{9,11},{10,... | collective-permute-start | bytes 835592 | tf_op jit(solution)/shard_map/ppermute | solution.py:203
  8.8 7.8 %collective-permute-start.4 = (f32[4,136,128]{2,1,0:T(8,128)S(1)}, f32[4,136,128]{2,1,0:T(8,128)S(1)}, u32[]{:S(2)}, u32[]{:S(2)}) collective-permute-start(f32[4,136,128]{2,1,0:T(8,128)S(1)} %get-tuple-element.24), channel_id=1, source_target_pairs={{0,1},{1,0},{2,3},{3,2},{4,5},{5,4},{6,7},{7,6},{8,9},{9,8},{10,11... | collective-permute-start | bytes 835592 | tf_op jit(solution)/shard_map/ppermute | solution.py:203
  10.6 20.5 %collective-permute-start.1 = (f32[2,256,128]{2,1,0:T(8,128)S(1)}, f32[2,256,128]{2,1,0:T(8,128)S(1)}, u32[]{:S(2)}, u32[]{:S(2)}) collective-permute-start(f32[2,256,128]{2,1,0:T(8,128)S(1)} %pad_maximum_fusion.7.refs_0_), channel_id=1, source_target_pairs={{0,4},{1,5},{2,6},{3,7},{4,0},{5,1},{6,2},{7,3},{8,12},{9,13},{10,... | collective-permute-start | bytes 786440 | tf_op jit(solution)/shard_map/ppermute | solution.py:203
  16.8 12.6 %collective-permute-start.5 = (f32[1056,128]{1,0:T(8,128)S(1)}, f32[1056,128]{1,0:T(8,128)S(1)}, u32[]{:S(2)}, u32[]{:S(2)}) collective-permute-start(f32[1056,128]{1,0:T(8,128)S(1)} %get-tuple-element.59), channel_id=1, source_target_pairs={{0,2},{1,3},{2,0},{3,1},{4,6},{5,7},{6,4},{7,5},{8,10},{9,11},{10,... | collective-permute-start | bytes 1622024 | tf_op jit(solution)/shard_map/ppermute | solution.py:203
  17.4 15.3 %collective-permute-start.9 = (f32[2,136,128]{2,1,0:T(8,128)S(1)}, f32[2,136,128]{2,1,0:T(8,128)S(1)}, u32[]{:S(2)}, u32[]{:S(2)}) collective-permute-start(f32[2,136,128]{2,1,0:T(8,128)S(1)} %pad_maximum_fusion.13), channel_id=1, source_target_pairs={{0,12},{1,13},{2,14},{3,15},{4,8},{5,9},{6,10},{7,11},{8,4},{9,5},... | collective-permute-start | bytes 417800 | tf_op jit(solution)/shard_map/ppermute | solution.py:203
  18.9 12.2 %collective-permute-start.3 = (f32[1056,128]{1,0:T(8,128)S(1)}, f32[1056,128]{1,0:T(8,128)S(1)}, u32[]{:S(2)}, u32[]{:S(2)}) collective-permute-start(f32[1056,128]{1,0:T(8,128)S(1)} %get-tuple-element.60), channel_id=1, source_target_pairs={{0,1},{1,0},{2,3},{3,2},{4,5},{5,4},{6,7},{7,6},{8,9},{9,8},{10,11... | collective-permute-start | bytes 1622024 | tf_op jit(solution)/shard_map/ppermute | solution.py:203
  20.4 12.3 %collective-permute-start.8 = (f32[2,136,128]{2,1,0:T(8,128)S(1)}, f32[2,136,128]{2,1,0:T(8,128)S(1)}, u32[]{:S(2)}, u32[]{:S(2)}) collective-permute-start(f32[2,136,128]{2,1,0:T(8,128)S(1)} %pad_maximum_fusion.12), channel_id=1, source_target_pairs={{0,8},{1,9},{2,10},{3,11},{4,12},{5,13},{6,14},{7,15},{8,0},{9,1},... | collective-permute-start | bytes 417800 | tf_op jit(solution)/shard_map/ppermute | solution.py:203
  31.2 8.2 %collective-permute-start.7 = (f32[3,256,128]{2,1,0:T(8,128)S(1)}, f32[3,256,128]{2,1,0:T(8,128)S(1)}, u32[]{:S(2)}, u32[]{:S(2)}) collective-permute-start(f32[3,256,128]{2,1,0:T(8,128)S(1)} %get-tuple-element.57), channel_id=1, source_target_pairs={{0,2},{1,3},{2,0},{3,1},{4,6},{5,7},{6,4},{7,5},{8,10},{9,11},{10,... | collective-permute-start | bytes 1179656 | tf_op jit(solution)/shard_map/ppermute | solution.py:203
  32.8 13.4 %collective-permute-start.10 = (f32[2,136,128]{2,1,0:T(8,128)S(1)}, f32[2,136,128]{2,1,0:T(8,128)S(1)}, u32[]{:S(2)}, u32[]{:S(2)}) collective-permute-start(f32[2,136,128]{2,1,0:T(8,128)S(1)} %get-tuple-element.25), channel_id=1, source_target_pairs={{0,8},{1,9},{2,10},{3,11},{4,12},{5,13},{6,14},{7,15},{8,0},{9,1},... | collective-permute-start | bytes 417800 | tf_op jit(solution)/shard_map/ppermute | solution.py:203
  34.4 11.9 %collective-permute-start.11 = (f32[2,136,128]{2,1,0:T(8,128)S(1)}, f32[2,136,128]{2,1,0:T(8,128)S(1)}, u32[]{:S(2)}, u32[]{:S(2)}) collective-permute-start(f32[2,136,128]{2,1,0:T(8,128)S(1)} %get-tuple-element.26), channel_id=1, source_target_pairs={{0,12},{1,13},{2,14},{3,15},{4,8},{5,9},{6,10},{7,11},{8,4},{9,5},... | collective-permute-start | bytes 417800 | tf_op jit(solution)/shard_map/ppermute | solution.py:203
  35.6 10.8 %collective-permute-start.12 = (f32[4,136,128]{2,1,0:T(8,128)S(1)}, f32[4,136,128]{2,1,0:T(8,128)S(1)}, u32[]{:S(2)}, u32[]{:S(2)}) collective-permute-start(f32[4,136,128]{2,1,0:T(8,128)S(1)} %pad_maximum_fusion.6), channel_id=1, source_target_pairs={{0,4},{1,5},{2,6},{3,7},{4,0},{5,1},{6,2},{7,3},{8,12},{9,13},{10,... | collective-permute-start | bytes 835592 | tf_op jit(solution)/shard_map/ppermute | solution.py:203
  36.4 8.3 %collective-permute-start.6 = (f32[3,256,128]{2,1,0:T(8,128)S(1)}, f32[3,256,128]{2,1,0:T(8,128)S(1)}, u32[]{:S(2)}, u32[]{:S(2)}) collective-permute-start(f32[3,256,128]{2,1,0:T(8,128)S(1)} %get-tuple-element.58), channel_id=1, source_target_pairs={{0,1},{1,0},{2,3},{3,2},{4,5},{5,4},{6,7},{7,6},{8,9},{9,8},{10,11... | collective-permute-start | bytes 1179656 | tf_op jit(solution)/shard_map/ppermute | solution.py:203
  39.4 7.1 %collective-permute-start.13 = (f32[1,256,128]{2,1,0:T(8,128)S(1)}, f32[1,256,128]{2,1,0:T(8,128)S(1)}, u32[]{:S(2)}, u32[]{:S(2)}) collective-permute-start(f32[1,256,128]{2,1,0:T(8,128)S(1)} %get-tuple-element.47), channel_id=1, source_target_pairs={{0,1},{1,0},{2,3},{3,2},{4,5},{5,4},{6,7},{7,6},{8,9},{9,8},{10,11... | collective-permute-start | bytes 393224 | tf_op jit(solution)/shard_map/ppermute | solution.py:203
  44.7 5.0 %collective-permute-start.14 = (f32[1,256,128]{2,1,0:T(8,128)S(1)}, f32[1,256,128]{2,1,0:T(8,128)S(1)}, u32[]{:S(2)}, u32[]{:S(2)}) collective-permute-start(f32[1,256,128]{2,1,0:T(8,128)S(1)} %get-tuple-element.45), channel_id=1, source_target_pairs={{0,2},{1,3},{2,0},{3,1},{4,6},{5,7},{6,4},{7,5},{8,10},{9,11},{10,... | collective-permute-start | bytes 393224 | tf_op jit(solution)/shard_map/ppermute | solution.py:203
  46.2 4.5 %collective-permute-start.15 = (f32[8,136,128]{2,1,0:T(8,128)S(1)}, f32[8,136,128]{2,1,0:T(8,128)S(1)}, u32[]{:S(2)}, u32[]{:S(2)}) collective-permute-start(f32[8,136,128]{2,1,0:T(8,128)S(1)} %constant_dynamic-update-slice_fusion.refs_0_), channel_id=1, source_target_pairs={{0,16},{16,0},{1,17},{17,1},{2,18},{18,2},{3,19},{19,3},{4,20},{20... | collective-permute-start | bytes 1671176 | tf_op jit(solution)/shard_map/ppermute | solution.py:203
  49.8 1.6 %collective-permute-start.17 = (f32[4,136,128]{2,1,0:T(8,128)S(1)}, f32[4,136,128]{2,1,0:T(8,128)S(1)}, u32[]{:S(2)}, u32[]{:S(2)}) collective-permute-start(f32[4,136,128]{2,1,0:T(8,128)S(1)} %constant_dynamic-update-slice_fusion.3.refs_4_), channel_id=1, source_target_pairs={{0,16},{16,0},{1,17},{17,1},{2,18},{18,2},{3,19},{19,3},{4,20},{20... | collective-permute-start | bytes 835592 | tf_op jit(solution)/shard_map/ppermute | solution.py:203
  49.9 1.9 %collective-permute-start.16 = (f32[4,136,128]{2,1,0:T(8,128)S(1)}, f32[4,136,128]{2,1,0:T(8,128)S(1)}, u32[]{:S(2)}, u32[]{:S(2)}) collective-permute-start(f32[4,136,128]{2,1,0:T(8,128)S(1)} %collective-permute-done.12.refs_2_), channel_id=1, source_target_pairs={{0,16},{16,0},{1,17},{17,1},{2,18},{18,2},{3,19},{19,3},{4,20},{20... | collective-permute-start | bytes 835592 | tf_op jit(solution)/shard_map/ppermute | solution.py:203

commit v16 on v15

--- a/solution.py
+++ b/solution.py
@@ -254,7 +254,7 @@
     ends = (come_last, near[1:], pieces[-2], pieces[-1])
     come_last, near[1:], pieces[-2], pieces[-1] = lax.optimization_barrier(ends)
     groups = []
-    for planes in (near[:1] + come_first, near[1:], come_last):
+    for planes in (near[:1], come_first, near[1:], come_last):
         mine = jnp.concatenate(planes, axis=0)
         groups.append(
             [mine] + [send(mine, "row", lambda i: (i + q) % rows_axis) for q in range(1, rows_axis)]

time: 56.1 us -> 53 us (0.945)
  waiting for transfers between devices: 23.2 us -> 19.8 us
    ppermute x18 -> x19, waiting for transfers between devices: 23.2 us -> 19.8 us  [send(): return lax.ppermute(x, axis, [(i, partner(i)) for i in range(size)])]
    ppermute x18 -> x19, starting transfers between devices: 24.1 us -> 24.4 us  [send(): return lax.ppermute(x, axis, [(i, partner(i)) for i in range(size)])]
  transfers between devices with their start and end apart: 18 -> 19, of which waited for: 11 -> 11; matrix products, arithmetic and copies ran while one was open for 2% -> 2% of each run, Pallas kernels for 3% -> 3%
where the time goes in v16:
time: 53 us; the launch traced here: 52.9 us
  starting transfers between devices  24.4 us (46%)
  waiting for transfers between devices  19.8 us (37%)
  Pallas kernels  5.95 us (11%)
  local copies, waits for them, and re-layouts  1.35 us (3%)
  other arithmetic  1.02 us (2%)
    ppermute x19, starting transfers between devices, send(): return lax.ppermute(x, axis, [(i, partner(i)) for i in range(size)])  24.4 us
    ppermute x19, waiting for transfers between devices, send(): return lax.ppermute(x, axis, [(i, partner(i)) for i in range(size)])  19.8 us
    pallas_call x1, Pallas kernels, contract(): pl.pallas_call(functools.partial(contract_kernel, len(groups), len(groups...  4.14 us
    pallas_call x1, Pallas kernels, pack(): pl.pallas_call(pack_kernel, out_shape=[out] * 4, in_specs=[pl.BlockSpec(m...  1.48 us
    unnamed x8, local copies, waits for them, and re-layouts  1.07 us
  transfers between devices with their start and end apart: 19, of which 11 were waited for; matrix products, arithmetic and copies ran while one was open for 2% of the time, Pallas kernels for 3%

profile of v16, /device:TPU:0, one launch (start us, length us, event | category | flops | bytes accessed | tf_op | source)
XLA Modules:
  0.0 52.9 jit_solution(9118427257174125049)
XLA Ops:
  0.0 0.0 copy-start
  0.0 4.0 %collective-permute-start = (f32[1,256,128]{2,1,0:T(8,128)}, f32[1,256,128]{2,1,0:T(8,128)S(1)}, u32[]{:S(2)}, u32[]{:S(2)}) collective-permute-start(f32[1,256,128]{2,1,0:T(8,128)} %bitcast.37), channel_id=1, source_target_pairs={{0,8},{1,9},{2,10},{3,11},{4,12},{5,13},{6,14},{7,15},{8,0},{9,1},... | collective-permute-start | bytes 393224 | tf_op jit(solution)/shard_map/ppermute | solution.py:203
  4.0 0.7 %fusion.1.words_ref = s32[16]{0:T(128)S(1)} fusion(s32[16]{0:T(128)} %param.11, s32[16]{0:T(128)} %param.10, s32[16,1]{0,1:T(1,128)} %param.9), kind=kLoop, calls=%fused_computation.31 | loop fusion | flops 64 | bytes 256 | tf_op jit(solution)/shard_map/add | solution.py:56
  4.7 0.0 copy-start.1
  4.7 1.0 %copy-done.1 = f32[16,64,128]{2,1,0:T(8,128)S(1)} copy-done((f32[16,64,128]{2,1,0:T(8,128)S(1)}, f32[16,64,128]{2,1,0:T(8,128)}, u32[]{:S(2)}) %copy-start.1) | copy-done | bytes 524312
  5.8 0.0 copy-start.2
  5.8 1.5 %shard_map.64 = (f32[4,136,128]{2,1,0:T(8,128)S(1)}, f32[4,136,128]{2,1,0:T(8,128)S(1)}, f32[4,136,128]{2,1,0:T(8,128)S(1)}, f32[4,136,128]{2,1,0:T(8,128)S(1)}) custom-call(s32[16]{0:T(128)S(1)} %fusion.1.words_ref, f32[16,64,128]{2,1,0:T(8,128)S(1)} %copy-done.1), custom_call_target="tpu_custom_call" | custom-call | bytes 1572864 | tf_op jit(solution)/shard_map/pallas_call | solution.py:58
  7.3 1.6 %collective-permute-start.4 = (f32[4,136,128]{2,1,0:T(8,128)S(1)}, f32[4,136,128]{2,1,0:T(8,128)S(1)}, u32[]{:S(2)}, u32[]{:S(2)}) collective-permute-start(f32[4,136,128]{2,1,0:T(8,128)S(1)} %get-tuple-element.24), channel_id=1, source_target_pairs={{0,1},{1,0},{2,3},{3,2},{4,5},{5,4},{6,7},{7,6},{8,9},{9,8},{10,11... | collective-permute-start | bytes 835592 | tf_op jit(solution)/shard_map/ppermute | solution.py:203
  8.8 1.5 %collective-permute-start.2 = (f32[4,136,128]{2,1,0:T(8,128)S(1)}, f32[4,136,128]{2,1,0:T(8,128)S(1)}, u32[]{:S(2)}, u32[]{:S(2)}) collective-permute-start(f32[4,136,128]{2,1,0:T(8,128)S(1)} %get-tuple-element.22), channel_id=1, source_target_pairs={{0,2},{1,3},{2,0},{3,1},{4,6},{5,7},{6,4},{7,5},{8,10},{9,11},{10,... | collective-permute-start | bytes 835592 | tf_op jit(solution)/shard_map/ppermute | solution.py:203
  10.4 0.0 copy-done
  10.4 0.1 shard_map.65.refs_8_
  10.5 0.1 collective-permute-done
  10.6 0.0 copy-done.2
  10.6 1.6 %collective-permute-start.1 = (f32[2,256,128]{2,1,0:T(8,128)S(1)}, f32[2,256,128]{2,1,0:T(8,128)S(1)}, u32[]{:S(2)}, u32[]{:S(2)}) collective-permute-start(f32[2,256,128]{2,1,0:T(8,128)S(1)} %pad_maximum_fusion.8.refs_0_), channel_id=1, source_target_pairs={{0,4},{1,5},{2,6},{3,7},{4,0},{5,1},{6,2},{7,3},{8,12},{9,13},{10,... | collective-permute-start | bytes 786440 | tf_op jit(solution)/shard_map/ppermute | solution.py:203
  12.2 3.3 %collective-permute-done.4 = f32[4,136,128]{2,1,0:T(8,128)S(1)} collective-permute-done((f32[4,136,128]{2,1,0:T(8,128)S(1)}, f32[4,136,128]{2,1,0:T(8,128)S(1)}, u32[]{:S(2)}, u32[]{:S(2)}) %collective-permute-start.4) | collective-permute-done | bytes 278560 | tf_op jit(solution)/shard_map/ppermute | solution.py:203
  15.5 1.2 %collective-permute-done.2 = f32[4,136,128]{2,1,0:T(8,128)S(1)} collective-permute-done((f32[4,136,128]{2,1,0:T(8,128)S(1)}, f32[4,136,128]{2,1,0:T(8,128)S(1)}, u32[]{:S(2)}, u32[]{:S(2)}) %collective-permute-start.2) | collective-permute-done | bytes 278560 | tf_op jit(solution)/shard_map/ppermute | solution.py:203
  16.7 0.1 pad_maximum_fusion
  16.8 0.6 %collective-permute-start.3 = (f32[1056,128]{1,0:T(8,128)S(1)}, f32[1056,128]{1,0:T(8,128)S(1)}, u32[]{:S(2)}, u32[]{:S(2)}) collective-permute-start(f32[1056,128]{1,0:T(8,128)S(1)} %get-tuple-element.60), channel_id=1, source_target_pairs={{0,1},{1,0},{2,3},{3,2},{4,5},{5,4},{6,7},{7,6},{8,9},{9,8},{10,11... | collective-permute-start | bytes 1622024 | tf_op jit(solution)/shard_map/ppermute | solution.py:203
  17.4 1.5 %collective-permute-start.5 = (f32[1056,128]{1,0:T(8,128)S(1)}, f32[1056,128]{1,0:T(8,128)S(1)}, u32[]{:S(2)}, u32[]{:S(2)}) collective-permute-start(f32[1056,128]{1,0:T(8,128)S(1)} %get-tuple-element.59), channel_id=1, source_target_pairs={{0,2},{1,3},{2,0},{3,1},{4,6},{5,7},{6,4},{7,5},{8,10},{9,11},{10,... | collective-permute-start | bytes 1622024 | tf_op jit(solution)/shard_map/ppermute | solution.py:203
  18.9 0.5 collective-permute-start.8
  19.4 3.6 %collective-permute-start.9 = (f32[2,136,128]{2,1,0:T(8,128)S(1)}, f32[2,136,128]{2,1,0:T(8,128)S(1)}, u32[]{:S(2)}, u32[]{:S(2)}) collective-permute-start(f32[2,136,128]{2,1,0:T(8,128)S(1)} %pad_maximum_fusion.14), channel_id=1, source_target_pairs={{0,12},{1,13},{2,14},{3,15},{4,8},{5,9},{6,10},{7,11},{8,4},{9,5},... | collective-permute-start | bytes 417800 | tf_op jit(solution)/shard_map/ppermute | solution.py:203
  23.0 6.3 %collective-permute-done.3 = f32[1056,128]{1,0:T(8,128)S(1)} collective-permute-done((f32[1056,128]{1,0:T(8,128)S(1)}, f32[1056,128]{1,0:T(8,128)S(1)}, u32[]{:S(2)}, u32[]{:S(2)}) %collective-permute-start.3) | collective-permute-done | bytes 540704 | tf_op jit(solution)/shard_map/ppermute | solution.py:203
  29.4 0.3 collective-permute-done.5
  29.7 0.0 collective-permute-done.1.refs_1_
  29.8 0.1 pad_maximum_fusion.2
  29.8 1.5 %collective-permute-start.6 = (f32[3,256,128]{2,1,0:T(8,128)S(1)}, f32[3,256,128]{2,1,0:T(8,128)S(1)}, u32[]{:S(2)}, u32[]{:S(2)}) collective-permute-start(f32[3,256,128]{2,1,0:T(8,128)S(1)} %get-tuple-element.58), channel_id=1, source_target_pairs={{0,1},{1,0},{2,3},{3,2},{4,5},{5,4},{6,7},{7,6},{8,9},{9,8},{10,11... | collective-permute-start | bytes 1179656 | tf_op jit(solution)/shard_map/ppermute | solution.py:203
  31.3 1.5 %collective-permute-start.7 = (f32[3,256,128]{2,1,0:T(8,128)S(1)}, f32[3,256,128]{2,1,0:T(8,128)S(1)}, u32[]{:S(2)}, u32[]{:S(2)}) collective-permute-start(f32[3,256,128]{2,1,0:T(8,128)S(1)} %get-tuple-element.57), channel_id=1, source_target_pairs={{0,2},{1,3},{2,0},{3,1},{4,6},{5,7},{6,4},{7,5},{8,10},{9,11},{10,... | collective-permute-start | bytes 1179656 | tf_op jit(solution)/shard_map/ppermute | solution.py:203
  32.9 0.0 collective-permute-done.8
  32.9 0.0 collective-permute-done.9
  32.9 0.6 %collective-permute-start.10 = (f32[2,136,128]{2,1,0:T(8,128)S(1)}, f32[2,136,128]{2,1,0:T(8,128)S(1)}, u32[]{:S(2)}, u32[]{:S(2)}) collective-permute-start(f32[2,136,128]{2,1,0:T(8,128)S(1)} %get-tuple-element.25), channel_id=1, source_target_pairs={{0,8},{1,9},{2,10},{3,11},{4,12},{5,13},{6,14},{7,15},{8,0},{9,1},... | collective-permute-start | bytes 417800 | tf_op jit(solution)/shard_map/ppermute | solution.py:203
  33.5 3.4 %collective-permute-start.11 = (f32[2,136,128]{2,1,0:T(8,128)S(1)}, f32[2,136,128]{2,1,0:T(8,128)S(1)}, u32[]{:S(2)}, u32[]{:S(2)}) collective-permute-start(f32[2,136,128]{2,1,0:T(8,128)S(1)} %get-tuple-element.26), channel_id=1, source_target_pairs={{0,12},{1,13},{2,14},{3,15},{4,8},{5,9},{6,10},{7,11},{8,4},{9,5},... | collective-permute-start | bytes 417800 | tf_op jit(solution)/shard_map/ppermute | solution.py:203
  37.0 0.1 collective-permute-start.12
  37.0 2.8 %collective-permute-done.7 = f32[3,256,128]{2,1,0:T(8,128)S(1)} collective-permute-done((f32[3,256,128]{2,1,0:T(8,128)S(1)}, f32[3,256,128]{2,1,0:T(8,128)S(1)}, u32[]{:S(2)}, u32[]{:S(2)}) %collective-permute-start.7) | collective-permute-done | bytes 393248 | tf_op jit(solution)/shard_map/ppermute | solution.py:203
  39.8 0.3 collective-permute-start.13
  40.2 0.0 collective-permute-done.6
  40.2 1.6 %collective-permute-start.14 = (f32[1,256,128]{2,1,0:T(8,128)S(1)}, f32[1,256,128]{2,1,0:T(8,128)S(1)}, u32[]{:S(2)}, u32[]{:S(2)}) collective-permute-start(f32[1,256,128]{2,1,0:T(8,128)S(1)} %get-tuple-element.45), channel_id=1, source_target_pairs={{0,2},{1,3},{2,0},{3,1},{4,6},{5,7},{6,4},{7,5},{8,10},{9,11},{10,... | collective-permute-start | bytes 393224 | tf_op jit(solution)/shard_map/ppermute | solution.py:203
  41.8 0.7 %collective-permute-done.10 = f32[2,136,128]{2,1,0:T(8,128)S(1)} collective-permute-done((f32[2,136,128]{2,1,0:T(8,128)S(1)}, f32[2,136,128]{2,1,0:T(8,128)S(1)}, u32[]{:S(2)}, u32[]{:S(2)}) %collective-permute-start.10) | collective-permute-done | bytes 139296 | tf_op jit(solution)/shard_map/ppermute | solution.py:203
  42.6 0.0 collective-permute-start.15
  42.6 1.3 %collective-permute-done.11 = f32[2,136,128]{2,1,0:T(8,128)S(1)} collective-permute-done((f32[2,136,128]{2,1,0:T(8,128)S(1)}, f32[2,136,128]{2,1,0:T(8,128)S(1)}, u32[]{:S(2)}, u32[]{:S(2)}) %collective-permute-start.11) | collective-permute-done | bytes 139296 | tf_op jit(solution)/shard_map/ppermute | solution.py:203
  43.9 0.0 collective-permute-start.16
  43.9 2.8 %collective-permute-done.12.refs_4_ = f32[4,136,128]{2,1,0:T(8,128)S(1)} collective-permute-done((f32[4,136,128]{2,1,0:T(8,128)S(1)}, f32[4,136,128]{2,1,0:T(8,128)S(1)}, u32[]{:S(2)}, u32[]{:S(2)}) %collective-permute-start.12) | collective-permute-done | bytes 278560 | tf_op jit(solution)/shard_map/ppermute | solution.py:203
  46.7 0.0 collective-permute-done.13.refs_8_
  46.8 0.0 collective-permute-done.14.refs_9_
  46.8 0.0 collective-permute-start.17
  46.8 0.6 %collective-permute-start.18 = (f32[4,136,128]{2,1,0:T(8,128)S(1)}, f32[4,136,128]{2,1,0:T(8,128)S(1)}, u32[]{:S(2)}, u32[]{:S(2)}) collective-permute-start(f32[4,136,128]{2,1,0:T(8,128)S(1)} %constant_dynamic-update-slice_fusion.2.refs_6_), channel_id=1, source_target_pairs={{0,16},{16,0},{1,17},{17,1},{2,18},{18,2},{3,19},{19,3},{4,20},{20... | collective-permute-start | bytes 835592 | tf_op jit(solution)/shard_map/ppermute | solution.py:203
  47.5 0.3 shard_map.66.split_ref
  47.7 0.0 collective-permute-done.15.refs_1_
  47.7 0.0 collective-permute-done.16.refs_3_
  47.8 0.6 %collective-permute-done.17.refs_5_ = f32[4,136,128]{2,1,0:T(8,128)S(1)} collective-permute-done((f32[4,136,128]{2,1,0:T(8,128)S(1)}, f32[4,136,128]{2,1,0:T(8,128)S(1)}, u32[]{:S(2)}, u32[]{:S(2)}) %collective-permute-start.17) | collective-permute-done | bytes 278560 | tf_op jit(solution)/shard_map/ppermute | solution.py:203
  48.3 0.4 collective-permute-done.18.refs_7_
  48.7 4.1 %shard_map.67 = f32[256,1024]{1,0:T(8,128)} custom-call(bf16[16,256,256]{2,1,0:T(8,128)(2,1)S(1)} %shard_map.66.split_ref, f32[4,136,128]{2,1,0:T(8,128)S(1)} %pad_maximum_fusion.7.refs_0_, f32[4,136,128]{2,1,0:T(8,128)S(1)} %collective-permute-done.15.refs_1_, f32[4,136,128]{2,1,0:T(8,128)S(1)} %constant_dynamic-update-slice_fusion.refs_2_, ...), custom_call_target="tpu_custom_call" | custom-call | tf_op jit(solution)/shard_map/pallas_call | solution.py:173
  (31 shorter events, 0.5 us)
Async XLA Ops:
  0.0 10.4 %copy-start = (f32[256,1024]{1,0:T(8,128)S(1)}, f32[256,1024]{1,0:T(8,128)}, u32[]{:S(2)}) copy-start(f32[256,1024]{1,0:T(8,128)} %x_ref.1) | copy-start | bytes 3145732
  0.0 10.5 %collective-permute-start = (f32[1,256,128]{2,1,0:T(8,128)}, f32[1,256,128]{2,1,0:T(8,128)S(1)}, u32[]{:S(2)}, u32[]{:S(2)}) collective-permute-start(f32[1,256,128]{2,1,0:T(8,128)} %bitcast.37), channel_id=1, source_target_pairs={{0,8},{1,9},{2,10},{3,11},{4,12},{5,13},{6,14},{7,15},{8,0},{9,1},... | collective-permute-start | bytes 393224 | tf_op jit(solution)/shard_map/ppermute | solution.py:203
  4.7 1.0 %copy-start.1 = (f32[16,64,128]{2,1,0:T(8,128)S(1)}, f32[16,64,128]{2,1,0:T(8,128)}, u32[]{:S(2)}) copy-start(f32[16,64,128]{2,1,0:T(8,128)} %tiles_ref.1) | copy-start | bytes 1572868
  5.8 4.8 %copy-start.2 = (f32[256,128]{1,0:T(8,128)S(1)}, f32[256,128]{1,0:T(8,128)}, u32[]{:S(2)}) copy-start(f32[256,128]{1,0:T(8,128)} %param.7) | copy-start | bytes 393220
  7.3 8.2 %collective-permute-start.4 = (f32[4,136,128]{2,1,0:T(8,128)S(1)}, f32[4,136,128]{2,1,0:T(8,128)S(1)}, u32[]{:S(2)}, u32[]{:S(2)}) collective-permute-start(f32[4,136,128]{2,1,0:T(8,128)S(1)} %get-tuple-element.24), channel_id=1, source_target_pairs={{0,1},{1,0},{2,3},{3,2},{4,5},{5,4},{6,7},{7,6},{8,9},{9,8},{10,11... | collective-permute-start | bytes 835592 | tf_op jit(solution)/shard_map/ppermute | solution.py:203
  8.8 7.8 %collective-permute-start.2 = (f32[4,136,128]{2,1,0:T(8,128)S(1)}, f32[4,136,128]{2,1,0:T(8,128)S(1)}, u32[]{:S(2)}, u32[]{:S(2)}) collective-permute-start(f32[4,136,128]{2,1,0:T(8,128)S(1)} %get-tuple-element.22), channel_id=1, source_target_pairs={{0,2},{1,3},{2,0},{3,1},{4,6},{5,7},{6,4},{7,5},{8,10},{9,11},{10,... | collective-permute-start | bytes 835592 | tf_op jit(solution)/shard_map/ppermute | solution.py:203
  10.6 19.2 %collective-permute-start.1 = (f32[2,256,128]{2,1,0:T(8,128)S(1)}, f32[2,256,128]{2,1,0:T(8,128)S(1)}, u32[]{:S(2)}, u32[]{:S(2)}) collective-permute-start(f32[2,256,128]{2,1,0:T(8,128)S(1)} %pad_maximum_fusion.8.refs_0_), channel_id=1, source_target_pairs={{0,4},{1,5},{2,6},{3,7},{4,0},{5,1},{6,2},{7,3},{8,12},{9,13},{10,... | collective-permute-start | bytes 786440 | tf_op jit(solution)/shard_map/ppermute | solution.py:203
  16.8 12.6 %collective-permute-start.3 = (f32[1056,128]{1,0:T(8,128)S(1)}, f32[1056,128]{1,0:T(8,128)S(1)}, u32[]{:S(2)}, u32[]{:S(2)}) collective-permute-start(f32[1056,128]{1,0:T(8,128)S(1)} %get-tuple-element.60), channel_id=1, source_target_pairs={{0,1},{1,0},{2,3},{3,2},{4,5},{5,4},{6,7},{7,6},{8,9},{9,8},{10,11... | collective-permute-start | bytes 1622024 | tf_op jit(solution)/shard_map/ppermute | solution.py:203
  17.4 12.3 %collective-permute-start.5 = (f32[1056,128]{1,0:T(8,128)S(1)}, f32[1056,128]{1,0:T(8,128)S(1)}, u32[]{:S(2)}, u32[]{:S(2)}) collective-permute-start(f32[1056,128]{1,0:T(8,128)S(1)} %get-tuple-element.59), channel_id=1, source_target_pairs={{0,2},{1,3},{2,0},{3,1},{4,6},{5,7},{6,4},{7,5},{8,10},{9,11},{10,... | collective-permute-start | bytes 1622024 | tf_op jit(solution)/shard_map/ppermute | solution.py:203
  18.9 14.0 %collective-permute-start.8 = (f32[2,136,128]{2,1,0:T(8,128)S(1)}, f32[2,136,128]{2,1,0:T(8,128)S(1)}, u32[]{:S(2)}, u32[]{:S(2)}) collective-permute-start(f32[2,136,128]{2,1,0:T(8,128)S(1)} %pad_maximum_fusion.13), channel_id=1, source_target_pairs={{0,8},{1,9},{2,10},{3,11},{4,12},{5,13},{6,14},{7,15},{8,0},{9,1},... | collective-permute-start | bytes 417800 | tf_op jit(solution)/shard_map/ppermute | solution.py:203
  19.4 13.5 %collective-permute-start.9 = (f32[2,136,128]{2,1,0:T(8,128)S(1)}, f32[2,136,128]{2,1,0:T(8,128)S(1)}, u32[]{:S(2)}, u32[]{:S(2)}) collective-permute-start(f32[2,136,128]{2,1,0:T(8,128)S(1)} %pad_maximum_fusion.14), channel_id=1, source_target_pairs={{0,12},{1,13},{2,14},{3,15},{4,8},{5,9},{6,10},{7,11},{8,4},{9,5},... | collective-permute-start | bytes 417800 | tf_op jit(solution)/shard_map/ppermute | solution.py:203
  29.8 10.4 %collective-permute-start.6 = (f32[3,256,128]{2,1,0:T(8,128)S(1)}, f32[3,256,128]{2,1,0:T(8,128)S(1)}, u32[]{:S(2)}, u32[]{:S(2)}) collective-permute-start(f32[3,256,128]{2,1,0:T(8,128)S(1)} %get-tuple-element.58), channel_id=1, source_target_pairs={{0,1},{1,0},{2,3},{3,2},{4,5},{5,4},{6,7},{7,6},{8,9},{9,8},{10,11... | collective-permute-start | bytes 1179656 | tf_op jit(solution)/shard_map/ppermute | solution.py:203
  31.3 8.6 %collective-permute-start.7 = (f32[3,256,128]{2,1,0:T(8,128)S(1)}, f32[3,256,128]{2,1,0:T(8,128)S(1)}, u32[]{:S(2)}, u32[]{:S(2)}) collective-permute-start(f32[3,256,128]{2,1,0:T(8,128)S(1)} %get-tuple-element.57), channel_id=1, source_target_pairs={{0,2},{1,3},{2,0},{3,1},{4,6},{5,7},{6,4},{7,5},{8,10},{9,11},{10,... | collective-permute-start | bytes 1179656 | tf_op jit(solution)/shard_map/ppermute | solution.py:203
  32.9 9.7 %collective-permute-start.10 = (f32[2,136,128]{2,1,0:T(8,128)S(1)}, f32[2,136,128]{2,1,0:T(8,128)S(1)}, u32[]{:S(2)}, u32[]{:S(2)}) collective-permute-start(f32[2,136,128]{2,1,0:T(8,128)S(1)} %get-tuple-element.25), channel_id=1, source_target_pairs={{0,8},{1,9},{2,10},{3,11},{4,12},{5,13},{6,14},{7,15},{8,0},{9,1},... | collective-permute-start | bytes 417800 | tf_op jit(solution)/shard_map/ppermute | solution.py:203
  33.5 10.4 %collective-permute-start.11 = (f32[2,136,128]{2,1,0:T(8,128)S(1)}, f32[2,136,128]{2,1,0:T(8,128)S(1)}, u32[]{:S(2)}, u32[]{:S(2)}) collective-permute-start(f32[2,136,128]{2,1,0:T(8,128)S(1)} %get-tuple-element.26), channel_id=1, source_target_pairs={{0,12},{1,13},{2,14},{3,15},{4,8},{5,9},{6,10},{7,11},{8,4},{9,5},... | collective-permute-start | bytes 417800 | tf_op jit(solution)/shard_map/ppermute | solution.py:203
  37.0 9.8 %collective-permute-start.12 = (f32[4,136,128]{2,1,0:T(8,128)S(1)}, f32[4,136,128]{2,1,0:T(8,128)S(1)}, u32[]{:S(2)}, u32[]{:S(2)}) collective-permute-start(f32[4,136,128]{2,1,0:T(8,128)S(1)} %pad_maximum_fusion.6), channel_id=1, source_target_pairs={{0,4},{1,5},{2,6},{3,7},{4,0},{5,1},{6,2},{7,3},{8,12},{9,13},{10,... | collective-permute-start | bytes 835592 | tf_op jit(solution)/shard_map/ppermute | solution.py:203
  39.8 6.9 %collective-permute-start.13 = (f32[1,256,128]{2,1,0:T(8,128)S(1)}, f32[1,256,128]{2,1,0:T(8,128)S(1)}, u32[]{:S(2)}, u32[]{:S(2)}) collective-permute-start(f32[1,256,128]{2,1,0:T(8,128)S(1)} %get-tuple-element.47), channel_id=1, source_target_pairs={{0,1},{1,0},{2,3},{3,2},{4,5},{5,4},{6,7},{7,6},{8,9},{9,8},{10,11... | collective-permute-start | bytes 393224 | tf_op jit(solution)/shard_map/ppermute | solution.py:203
  40.2 6.6 %collective-permute-start.14 = (f32[1,256,128]{2,1,0:T(8,128)S(1)}, f32[1,256,128]{2,1,0:T(8,128)S(1)}, u32[]{:S(2)}, u32[]{:S(2)}) collective-permute-start(f32[1,256,128]{2,1,0:T(8,128)S(1)} %get-tuple-element.45), channel_id=1, source_target_pairs={{0,2},{1,3},{2,0},{3,1},{4,6},{5,7},{6,4},{7,5},{8,10},{9,11},{10,... | collective-permute-start | bytes 393224 | tf_op jit(solution)/shard_map/ppermute | solution.py:203
  42.6 5.2 %collective-permute-start.15 = (f32[4,136,128]{2,1,0:T(8,128)S(1)}, f32[4,136,128]{2,1,0:T(8,128)S(1)}, u32[]{:S(2)}, u32[]{:S(2)}) collective-permute-start(f32[4,136,128]{2,1,0:T(8,128)S(1)} %pad_maximum_fusion.7.refs_0_), channel_id=1, source_target_pairs={{0,16},{16,0},{1,17},{17,1},{2,18},{18,2},{3,19},{19,3},{4,20},{20... | collective-permute-start | bytes 835592 | tf_op jit(solution)/shard_map/ppermute | solution.py:203
  43.9 3.8 %collective-permute-start.16 = (f32[4,136,128]{2,1,0:T(8,128)S(1)}, f32[4,136,128]{2,1,0:T(8,128)S(1)}, u32[]{:S(2)}, u32[]{:S(2)}) collective-permute-start(f32[4,136,128]{2,1,0:T(8,128)S(1)} %constant_dynamic-update-slice_fusion.refs_2_), channel_id=1, source_target_pairs={{0,16},{16,0},{1,17},{17,1},{2,18},{18,2},{3,19},{19,3},{4,20},{20... | collective-permute-start | bytes 835592 | tf_op jit(solution)/shard_map/ppermute | solution.py:203
  46.8 1.6 %collective-permute-start.17 = (f32[4,136,128]{2,1,0:T(8,128)S(1)}, f32[4,136,128]{2,1,0:T(8,128)S(1)}, u32[]{:S(2)}, u32[]{:S(2)}) collective-permute-start(f32[4,136,128]{2,1,0:T(8,128)S(1)} %collective-permute-done.12.refs_4_), channel_id=1, source_target_pairs={{0,16},{16,0},{1,17},{17,1},{2,18},{18,2},{3,19},{19,3},{4,20},{20... | collective-permute-start | bytes 835592 | tf_op jit(solution)/shard_map/ppermute | solution.py:203
  46.8 1.9 %collective-permute-start.18 = (f32[4,136,128]{2,1,0:T(8,128)S(1)}, f32[4,136,128]{2,1,0:T(8,128)S(1)}, u32[]{:S(2)}, u32[]{:S(2)}) collective-permute-start(f32[4,136,128]{2,1,0:T(8,128)S(1)} %constant_dynamic-update-slice_fusion.2.refs_6_), channel_id=1, source_target_pairs={{0,16},{16,0},{1,17},{17,1},{2,18},{18,2},{3,19},{19,3},{4,20},{20... | collective-permute-start | bytes 835592 | tf_op jit(solution)/shard_map/ppermute | solution.py:203

commit v17 on v16

--- a/solution.py
+++ b/solution.py
@@ -267,7 +267,9 @@
         stacked = stacked[place[wanted]]
         stacked = stacked.transpose(1, 0, 2).reshape(amplitudes.shape[0], KT, width).transpose(1, 0, 2)
         pieces, positions = [stacked], [(None,) * KT]
-    return contract(split(pieces, positions), groups, residual)
+    split_amplitudes = split(pieces, positions)
+    early = contract(split_amplitudes, groups[:2], residual)
+    return contract(split_amplitudes, groups[2:], early)
 
 
 def solution(mesh):

time: 53 us -> 52.6 us (level)
  waiting for transfers between devices: 19.8 us -> 18.9 us
  Pallas kernels: 5.95 us -> 6.48 us
    ppermute x19, waiting for transfers between devices: 19.8 us -> 18.9 us  [send(): return lax.ppermute(x, axis, [(i, partner(i)) for i in range(size)])]
    pallas_call x1 -> x2, Pallas kernels: 4.14 us -> 4.67 us  [contract(): pl.pallas_call(functools.partial(contract_kernel, len(groups), len(groups...]
  transfers between devices with their start and end apart: 19 -> 19, of which waited for: 11 -> 9; matrix products, arithmetic and copies ran while one was open for 2% -> 3% of each run, Pallas kernels for 3% -> 7%
where the time goes in v17:
time: 52.6 us; the launch traced here: 52.5 us
  starting transfers between devices  24.4 us (46%)
  waiting for transfers between devices  18.9 us (36%)
  Pallas kernels  6.48 us (12%)
  local copies, waits for them, and re-layouts  1.35 us (3%)
  other arithmetic  1.02 us (2%)
    ppermute x19, starting transfers between devices, send(): return lax.ppermute(x, axis, [(i, partner(i)) for i in range(size)])  24.4 us
    ppermute x19, waiting for transfers between devices, send(): return lax.ppermute(x, axis, [(i, partner(i)) for i in range(size)])  18.9 us
    pallas_call x2, Pallas kernels, contract(): pl.pallas_call(functools.partial(contract_kernel, len(groups), len(groups...  4.67 us
    pallas_call x1, Pallas kernels, pack(): pl.pallas_call(pack_kernel, out_shape=[out] * 4, in_specs=[pl.BlockSpec(m...  1.48 us
    unnamed x8, local copies, waits for them, and re-layouts  1.07 us
  transfers between devices with their start and end apart: 19, of which 9 were waited for; matrix products, arithmetic and copies ran while one was open for 3% of the time, Pallas kernels for 7%

profile of v17, /device:TPU:0, one launch (start us, length us, event | category | flops | bytes accessed | tf_op | source)
XLA Modules:
  0.0 52.5 jit_solution(5538697608559243699)
XLA Ops:
  0.0 0.0 copy-start
  0.0 4.0 %collective-permute-start = (f32[1,256,128]{2,1,0:T(8,128)}, f32[1,256,128]{2,1,0:T(8,128)S(1)}, u32[]{:S(2)}, u32[]{:S(2)}) collective-permute-start(f32[1,256,128]{2,1,0:T(8,128)} %bitcast.37), channel_id=1, source_target_pairs={{0,8},{1,9},{2,10},{3,11},{4,12},{5,13},{6,14},{7,15},{8,0},{9,1},... | collective-permute-start | bytes 393224 | tf_op jit(solution)/shard_map/ppermute | solution.py:203
  4.0 0.7 %fusion.1.words_ref = s32[16]{0:T(128)S(1)} fusion(s32[16]{0:T(128)} %param.11, s32[16]{0:T(128)} %param.10, s32[16,1]{0,1:T(1,128)} %param.9), kind=kLoop, calls=%fused_computation.31 | loop fusion | flops 64 | bytes 256 | tf_op jit(solution)/shard_map/add | solution.py:56
  4.7 0.0 copy-start.1
  4.7 1.0 %copy-done.1 = f32[16,64,128]{2,1,0:T(8,128)S(1)} copy-done((f32[16,64,128]{2,1,0:T(8,128)S(1)}, f32[16,64,128]{2,1,0:T(8,128)}, u32[]{:S(2)}) %copy-start.1) | copy-done | bytes 524312
  5.8 0.0 copy-start.2
  5.8 1.5 %shard_map.64 = (f32[4,136,128]{2,1,0:T(8,128)S(1)}, f32[4,136,128]{2,1,0:T(8,128)S(1)}, f32[4,136,128]{2,1,0:T(8,128)S(1)}, f32[4,136,128]{2,1,0:T(8,128)S(1)}) custom-call(s32[16]{0:T(128)S(1)} %fusion.1.words_ref, f32[16,64,128]{2,1,0:T(8,128)S(1)} %copy-done.1), custom_call_target="tpu_custom_call" | custom-call | bytes 1572864 | tf_op jit(solution)/shard_map/pallas_call | solution.py:58
  7.3 1.6 %collective-permute-start.4 = (f32[4,136,128]{2,1,0:T(8,128)S(1)}, f32[4,136,128]{2,1,0:T(8,128)S(1)}, u32[]{:S(2)}, u32[]{:S(2)}) collective-permute-start(f32[4,136,128]{2,1,0:T(8,128)S(1)} %get-tuple-element.24), channel_id=1, source_target_pairs={{0,1},{1,0},{2,3},{3,2},{4,5},{5,4},{6,7},{7,6},{8,9},{9,8},{10,11... | collective-permute-start | bytes 835592 | tf_op jit(solution)/shard_map/ppermute | solution.py:203
  8.8 1.5 %collective-permute-start.2 = (f32[4,136,128]{2,1,0:T(8,128)S(1)}, f32[4,136,128]{2,1,0:T(8,128)S(1)}, u32[]{:S(2)}, u32[]{:S(2)}) collective-permute-start(f32[4,136,128]{2,1,0:T(8,128)S(1)} %get-tuple-element.22), channel_id=1, source_target_pairs={{0,2},{1,3},{2,0},{3,1},{4,6},{5,7},{6,4},{7,5},{8,10},{9,11},{10,... | collective-permute-start | bytes 835592 | tf_op jit(solution)/shard_map/ppermute | solution.py:203
  10.4 0.0 copy-done
  10.4 0.1 shard_map.65.refs_4_
  10.5 0.1 collective-permute-done
  10.6 0.0 copy-done.2
  10.6 1.6 %collective-permute-start.1 = (f32[2,256,128]{2,1,0:T(8,128)S(1)}, f32[2,256,128]{2,1,0:T(8,128)S(1)}, u32[]{:S(2)}, u32[]{:S(2)}) collective-permute-start(f32[2,256,128]{2,1,0:T(8,128)S(1)} %pad_maximum_fusion.8.refs_0_), channel_id=1, source_target_pairs={{0,4},{1,5},{2,6},{3,7},{4,0},{5,1},{6,2},{7,3},{8,12},{9,13},{10,... | collective-permute-start | bytes 786440 | tf_op jit(solution)/shard_map/ppermute | solution.py:203
  12.2 3.3 %collective-permute-done.4 = f32[4,136,128]{2,1,0:T(8,128)S(1)} collective-permute-done((f32[4,136,128]{2,1,0:T(8,128)S(1)}, f32[4,136,128]{2,1,0:T(8,128)S(1)}, u32[]{:S(2)}, u32[]{:S(2)}) %collective-permute-start.4) | collective-permute-done | bytes 278560 | tf_op jit(solution)/shard_map/ppermute | solution.py:203
  15.5 1.2 %collective-permute-done.2 = f32[4,136,128]{2,1,0:T(8,128)S(1)} collective-permute-done((f32[4,136,128]{2,1,0:T(8,128)S(1)}, f32[4,136,128]{2,1,0:T(8,128)S(1)}, u32[]{:S(2)}, u32[]{:S(2)}) %collective-permute-start.2) | collective-permute-done | bytes 278560 | tf_op jit(solution)/shard_map/ppermute | solution.py:203
  16.7 0.1 pad_maximum_fusion
  16.8 0.6 %collective-permute-start.3 = (f32[1056,128]{1,0:T(8,128)S(1)}, f32[1056,128]{1,0:T(8,128)S(1)}, u32[]{:S(2)}, u32[]{:S(2)}) collective-permute-start(f32[1056,128]{1,0:T(8,128)S(1)} %get-tuple-element.60), channel_id=1, source_target_pairs={{0,1},{1,0},{2,3},{3,2},{4,5},{5,4},{6,7},{7,6},{8,9},{9,8},{10,11... | collective-permute-start | bytes 1622024 | tf_op jit(solution)/shard_map/ppermute | solution.py:203
  17.4 1.5 %collective-permute-start.5 = (f32[1056,128]{1,0:T(8,128)S(1)}, f32[1056,128]{1,0:T(8,128)S(1)}, u32[]{:S(2)}, u32[]{:S(2)}) collective-permute-start(f32[1056,128]{1,0:T(8,128)S(1)} %get-tuple-element.59), channel_id=1, source_target_pairs={{0,2},{1,3},{2,0},{3,1},{4,6},{5,7},{6,4},{7,5},{8,10},{9,11},{10,... | collective-permute-start | bytes 1622024 | tf_op jit(solution)/shard_map/ppermute | solution.py:203
  18.9 0.5 collective-permute-start.8
  19.4 3.6 %collective-permute-start.9 = (f32[2,136,128]{2,1,0:T(8,128)S(1)}, f32[2,136,128]{2,1,0:T(8,128)S(1)}, u32[]{:S(2)}, u32[]{:S(2)}) collective-permute-start(f32[2,136,128]{2,1,0:T(8,128)S(1)} %pad_maximum_fusion.14), channel_id=1, source_target_pairs={{0,12},{1,13},{2,14},{3,15},{4,8},{5,9},{6,10},{7,11},{8,4},{9,5},... | collective-permute-start | bytes 417800 | tf_op jit(solution)/shard_map/ppermute | solution.py:203
  23.0 6.3 %collective-permute-done.3 = f32[1056,128]{1,0:T(8,128)S(1)} collective-permute-done((f32[1056,128]{1,0:T(8,128)S(1)}, f32[1056,128]{1,0:T(8,128)S(1)}, u32[]{:S(2)}, u32[]{:S(2)}) %collective-permute-start.3) | collective-permute-done | bytes 540704 | tf_op jit(solution)/shard_map/ppermute | solution.py:203
  29.4 0.3 collective-permute-done.5
  29.7 0.0 collective-permute-done.1.refs_1_
  29.8 0.1 pad_maximum_fusion.2
  29.8 1.5 %collective-permute-start.6 = (f32[3,256,128]{2,1,0:T(8,128)S(1)}, f32[3,256,128]{2,1,0:T(8,128)S(1)}, u32[]{:S(2)}, u32[]{:S(2)}) collective-permute-start(f32[3,256,128]{2,1,0:T(8,128)S(1)} %get-tuple-element.58), channel_id=1, source_target_pairs={{0,1},{1,0},{2,3},{3,2},{4,5},{5,4},{6,7},{7,6},{8,9},{9,8},{10,11... | collective-permute-start | bytes 1179656 | tf_op jit(solution)/shard_map/ppermute | solution.py:203
  31.3 1.5 %collective-permute-start.7 = (f32[3,256,128]{2,1,0:T(8,128)S(1)}, f32[3,256,128]{2,1,0:T(8,128)S(1)}, u32[]{:S(2)}, u32[]{:S(2)}) collective-permute-start(f32[3,256,128]{2,1,0:T(8,128)S(1)} %get-tuple-element.57), channel_id=1, source_target_pairs={{0,2},{1,3},{2,0},{3,1},{4,6},{5,7},{6,4},{7,5},{8,10},{9,11},{10,... | collective-permute-start | bytes 1179656 | tf_op jit(solution)/shard_map/ppermute | solution.py:203
  32.9 0.0 collective-permute-done.8
  32.9 0.0 collective-permute-done.9
  32.9 0.6 %collective-permute-start.10 = (f32[2,136,128]{2,1,0:T(8,128)S(1)}, f32[2,136,128]{2,1,0:T(8,128)S(1)}, u32[]{:S(2)}, u32[]{:S(2)}) collective-permute-start(f32[2,136,128]{2,1,0:T(8,128)S(1)} %get-tuple-element.25), channel_id=1, source_target_pairs={{0,8},{1,9},{2,10},{3,11},{4,12},{5,13},{6,14},{7,15},{8,0},{9,1},... | collective-permute-start | bytes 417800 | tf_op jit(solution)/shard_map/ppermute | solution.py:203
  33.5 3.4 %collective-permute-start.11 = (f32[2,136,128]{2,1,0:T(8,128)S(1)}, f32[2,136,128]{2,1,0:T(8,128)S(1)}, u32[]{:S(2)}, u32[]{:S(2)}) collective-permute-start(f32[2,136,128]{2,1,0:T(8,128)S(1)} %get-tuple-element.26), channel_id=1, source_target_pairs={{0,12},{1,13},{2,14},{3,15},{4,8},{5,9},{6,10},{7,11},{8,4},{9,5},... | collective-permute-start | bytes 417800 | tf_op jit(solution)/shard_map/ppermute | solution.py:203
  36.9 0.1 collective-permute-start.12
  37.0 2.8 %collective-permute-done.7 = f32[3,256,128]{2,1,0:T(8,128)S(1)} collective-permute-done((f32[3,256,128]{2,1,0:T(8,128)S(1)}, f32[3,256,128]{2,1,0:T(8,128)S(1)}, u32[]{:S(2)}, u32[]{:S(2)}) %collective-permute-start.7) | collective-permute-done | bytes 393248 | tf_op jit(solution)/shard_map/ppermute | solution.py:203
  39.8 0.3 collective-permute-start.13
  40.2 0.0 collective-permute-done.6
  40.2 1.6 %collective-permute-start.14 = (f32[1,256,128]{2,1,0:T(8,128)S(1)}, f32[1,256,128]{2,1,0:T(8,128)S(1)}, u32[]{:S(2)}, u32[]{:S(2)}) collective-permute-start(f32[1,256,128]{2,1,0:T(8,128)S(1)} %get-tuple-element.45), channel_id=1, source_target_pairs={{0,2},{1,3},{2,0},{3,1},{4,6},{5,7},{6,4},{7,5},{8,10},{9,11},{10,... | collective-permute-start | bytes 393224 | tf_op jit(solution)/shard_map/ppermute | solution.py:203
  41.8 0.7 %collective-permute-done.10 = f32[2,136,128]{2,1,0:T(8,128)S(1)} collective-permute-done((f32[2,136,128]{2,1,0:T(8,128)S(1)}, f32[2,136,128]{2,1,0:T(8,128)S(1)}, u32[]{:S(2)}, u32[]{:S(2)}) %collective-permute-start.10) | collective-permute-done | bytes 139296 | tf_op jit(solution)/shard_map/ppermute | solution.py:203
  42.6 0.0 collective-permute-start.17
  42.6 1.3 %collective-permute-done.11 = f32[2,136,128]{2,1,0:T(8,128)S(1)} collective-permute-done((f32[2,136,128]{2,1,0:T(8,128)S(1)}, f32[2,136,128]{2,1,0:T(8,128)S(1)}, u32[]{:S(2)}, u32[]{:S(2)}) %collective-permute-start.11) | collective-permute-done | bytes 139296 | tf_op jit(solution)/shard_map/ppermute | solution.py:203
  43.9 0.0 collective-permute-start.18
  43.9 2.8 %collective-permute-done.12.refs_0_ = f32[4,136,128]{2,1,0:T(8,128)S(1)} collective-permute-done((f32[4,136,128]{2,1,0:T(8,128)S(1)}, f32[4,136,128]{2,1,0:T(8,128)S(1)}, u32[]{:S(2)}, u32[]{:S(2)}) %collective-permute-start.12) | collective-permute-done | bytes 278560 | tf_op jit(solution)/shard_map/ppermute | solution.py:203
  46.7 0.0 collective-permute-done.13.refs_8_
  46.7 0.0 collective-permute-done.14.refs_9_
  46.8 0.0 collective-permute-start.15
  46.8 0.6 %collective-permute-start.16 = (f32[4,136,128]{2,1,0:T(8,128)S(1)}, f32[4,136,128]{2,1,0:T(8,128)S(1)}, u32[]{:S(2)}, u32[]{:S(2)}) collective-permute-start(f32[4,136,128]{2,1,0:T(8,128)S(1)} %constant_dynamic-update-slice_fusion.refs_2_), channel_id=1, source_target_pairs={{0,16},{16,0},{1,17},{17,1},{2,18},{18,2},{3,19},{19,3},{4,20},{20... | collective-permute-start | bytes 835592 | tf_op jit(solution)/shard_map/ppermute | solution.py:203
  47.5 0.3 shard_map.66.split_ref
  47.7 0.0 collective-permute-done.17.refs_1_
  47.7 0.0 collective-permute-done.18.refs_3_
  47.8 1.9 %shard_map.67.refs_4_ = f32[256,1024]{1,0:T(8,128)S(1)} custom-call(bf16[16,256,256]{2,1,0:T(8,128)(2,1)S(1)} %shard_map.66.split_ref, f32[4,136,128]{2,1,0:T(8,128)S(1)} %pad_maximum_fusion.7.refs_0_, f32[4,136,128]{2,1,0:T(8,128)S(1)} %collective-permute-done.17.refs_1_, f32[4,136,128]{2,1,0:T(8,128)S(1)} %constant_dynamic-update-slice_fusion.2.refs_2_, ...), custom_call_target="tpu_custom_call" | custom-call | tf_op jit(solution)/shard_map/pallas_call | solution.py:173
  49.6 0.0 collective-permute-done.15.refs_1_
  49.6 0.0 collective-permute-done.16.refs_3_
  49.6 2.8 %shard_map.68 = f32[256,1024]{1,0:T(8,128)} custom-call(bf16[16,256,256]{2,1,0:T(8,128)(2,1)S(1)} %shard_map.66.split_ref, f32[4,136,128]{2,1,0:T(8,128)S(1)} %collective-permute-done.12.refs_0_, f32[4,136,128]{2,1,0:T(8,128)S(1)} %collective-permute-done.15.refs_1_, f32[4,136,128]{2,1,0:T(8,128)S(1)} %constant_dynamic-update-slice_fusion.refs_2_, ...), custom_call_target="tpu_custom_call" | custom-call | tf_op jit(solution)/shard_map/pallas_call | solution.py:173
  (31 shorter events, 0.5 us)
Async XLA Ops:
  0.0 10.4 %copy-start = (f32[256,1024]{1,0:T(8,128)S(1)}, f32[256,1024]{1,0:T(8,128)}, u32[]{:S(2)}) copy-start(f32[256,1024]{1,0:T(8,128)} %x_ref.1) | copy-start | bytes 3145732
  0.0 10.5 %collective-permute-start = (f32[1,256,128]{2,1,0:T(8,128)}, f32[1,256,128]{2,1,0:T(8,128)S(1)}, u32[]{:S(2)}, u32[]{:S(2)}) collective-permute-start(f32[1,256,128]{2,1,0:T(8,128)} %bitcast.37), channel_id=1, source_target_pairs={{0,8},{1,9},{2,10},{3,11},{4,12},{5,13},{6,14},{7,15},{8,0},{9,1},... | collective-permute-start | bytes 393224 | tf_op jit(solution)/shard_map/ppermute | solution.py:203
  4.7 1.0 %copy-start.1 = (f32[16,64,128]{2,1,0:T(8,128)S(1)}, f32[16,64,128]{2,1,0:T(8,128)}, u32[]{:S(2)}) copy-start(f32[16,64,128]{2,1,0:T(8,128)} %tiles_ref.1) | copy-start | bytes 1572868
  5.8 4.8 %copy-start.2 = (f32[256,128]{1,0:T(8,128)S(1)}, f32[256,128]{1,0:T(8,128)}, u32[]{:S(2)}) copy-start(f32[256,128]{1,0:T(8,128)} %param.7) | copy-start | bytes 393220
  7.3 8.2 %collective-permute-start.4 = (f32[4,136,128]{2,1,0:T(8,128)S(1)}, f32[4,136,128]{2,1,0:T(8,128)S(1)}, u32[]{:S(2)}, u32[]{:S(2)}) collective-permute-start(f32[4,136,128]{2,1,0:T(8,128)S(1)} %get-tuple-element.24), channel_id=1, source_target_pairs={{0,1},{1,0},{2,3},{3,2},{4,5},{5,4},{6,7},{7,6},{8,9},{9,8},{10,11... | collective-permute-start | bytes 835592 | tf_op jit(solution)/shard_map/ppermute | solution.py:203
  8.8 7.8 %collective-permute-start.2 = (f32[4,136,128]{2,1,0:T(8,128)S(1)}, f32[4,136,128]{2,1,0:T(8,128)S(1)}, u32[]{:S(2)}, u32[]{:S(2)}) collective-permute-start(f32[4,136,128]{2,1,0:T(8,128)S(1)} %get-tuple-element.22), channel_id=1, source_target_pairs={{0,2},{1,3},{2,0},{3,1},{4,6},{5,7},{6,4},{7,5},{8,10},{9,11},{10,... | collective-permute-start | bytes 835592 | tf_op jit(solution)/shard_map/ppermute | solution.py:203
  10.6 19.2 %collective-permute-start.1 = (f32[2,256,128]{2,1,0:T(8,128)S(1)}, f32[2,256,128]{2,1,0:T(8,128)S(1)}, u32[]{:S(2)}, u32[]{:S(2)}) collective-permute-start(f32[2,256,128]{2,1,0:T(8,128)S(1)} %pad_maximum_fusion.8.refs_0_), channel_id=1, source_target_pairs={{0,4},{1,5},{2,6},{3,7},{4,0},{5,1},{6,2},{7,3},{8,12},{9,13},{10,... | collective-permute-start | bytes 786440 | tf_op jit(solution)/shard_map/ppermute | solution.py:203
  16.8 12.6 %collective-permute-start.3 = (f32[1056,128]{1,0:T(8,128)S(1)}, f32[1056,128]{1,0:T(8,128)S(1)}, u32[]{:S(2)}, u32[]{:S(2)}) collective-permute-start(f32[1056,128]{1,0:T(8,128)S(1)} %get-tuple-element.60), channel_id=1, source_target_pairs={{0,1},{1,0},{2,3},{3,2},{4,5},{5,4},{6,7},{7,6},{8,9},{9,8},{10,11... | collective-permute-start | bytes 1622024 | tf_op jit(solution)/shard_map/ppermute | solution.py:203
  17.4 12.3 %collective-permute-start.5 = (f32[1056,128]{1,0:T(8,128)S(1)}, f32[1056,128]{1,0:T(8,128)S(1)}, u32[]{:S(2)}, u32[]{:S(2)}) collective-permute-start(f32[1056,128]{1,0:T(8,128)S(1)} %get-tuple-element.59), channel_id=1, source_target_pairs={{0,2},{1,3},{2,0},{3,1},{4,6},{5,7},{6,4},{7,5},{8,10},{9,11},{10,... | collective-permute-start | bytes 1622024 | tf_op jit(solution)/shard_map/ppermute | solution.py:203
  18.9 14.0 %collective-permute-start.8 = (f32[2,136,128]{2,1,0:T(8,128)S(1)}, f32[2,136,128]{2,1,0:T(8,128)S(1)}, u32[]{:S(2)}, u32[]{:S(2)}) collective-permute-start(f32[2,136,128]{2,1,0:T(8,128)S(1)} %pad_maximum_fusion.13), channel_id=1, source_target_pairs={{0,8},{1,9},{2,10},{3,11},{4,12},{5,13},{6,14},{7,15},{8,0},{9,1},... | collective-permute-start | bytes 417800 | tf_op jit(solution)/shard_map/ppermute | solution.py:203
  19.4 13.5 %collective-permute-start.9 = (f32[2,136,128]{2,1,0:T(8,128)S(1)}, f32[2,136,128]{2,1,0:T(8,128)S(1)}, u32[]{:S(2)}, u32[]{:S(2)}) collective-permute-start(f32[2,136,128]{2,1,0:T(8,128)S(1)} %pad_maximum_fusion.14), channel_id=1, source_target_pairs={{0,12},{1,13},{2,14},{3,15},{4,8},{5,9},{6,10},{7,11},{8,4},{9,5},... | collective-permute-start | bytes 417800 | tf_op jit(solution)/shard_map/ppermute | solution.py:203
  29.8 10.4 %collective-permute-start.6 = (f32[3,256,128]{2,1,0:T(8,128)S(1)}, f32[3,256,128]{2,1,0:T(8,128)S(1)}, u32[]{:S(2)}, u32[]{:S(2)}) collective-permute-start(f32[3,256,128]{2,1,0:T(8,128)S(1)} %get-tuple-element.58), channel_id=1, source_target_pairs={{0,1},{1,0},{2,3},{3,2},{4,5},{5,4},{6,7},{7,6},{8,9},{9,8},{10,11... | collective-permute-start | bytes 1179656 | tf_op jit(solution)/shard_map/ppermute | solution.py:203
  31.3 8.6 %collective-permute-start.7 = (f32[3,256,128]{2,1,0:T(8,128)S(1)}, f32[3,256,128]{2,1,0:T(8,128)S(1)}, u32[]{:S(2)}, u32[]{:S(2)}) collective-permute-start(f32[3,256,128]{2,1,0:T(8,128)S(1)} %get-tuple-element.57), channel_id=1, source_target_pairs={{0,2},{1,3},{2,0},{3,1},{4,6},{5,7},{6,4},{7,5},{8,10},{9,11},{10,... | collective-permute-start | bytes 1179656 | tf_op jit(solution)/shard_map/ppermute | solution.py:203
  32.9 9.7 %collective-permute-start.10 = (f32[2,136,128]{2,1,0:T(8,128)S(1)}, f32[2,136,128]{2,1,0:T(8,128)S(1)}, u32[]{:S(2)}, u32[]{:S(2)}) collective-permute-start(f32[2,136,128]{2,1,0:T(8,128)S(1)} %get-tuple-element.25), channel_id=1, source_target_pairs={{0,8},{1,9},{2,10},{3,11},{4,12},{5,13},{6,14},{7,15},{8,0},{9,1},... | collective-permute-start | bytes 417800 | tf_op jit(solution)/shard_map/ppermute | solution.py:203
  33.5 10.4 %collective-permute-start.11 = (f32[2,136,128]{2,1,0:T(8,128)S(1)}, f32[2,136,128]{2,1,0:T(8,128)S(1)}, u32[]{:S(2)}, u32[]{:S(2)}) collective-permute-start(f32[2,136,128]{2,1,0:T(8,128)S(1)} %get-tuple-element.26), channel_id=1, source_target_pairs={{0,12},{1,13},{2,14},{3,15},{4,8},{5,9},{6,10},{7,11},{8,4},{9,5},... | collective-permute-start | bytes 417800 | tf_op jit(solution)/shard_map/ppermute | solution.py:203
  36.9 9.8 %collective-permute-start.12 = (f32[4,136,128]{2,1,0:T(8,128)S(1)}, f32[4,136,128]{2,1,0:T(8,128)S(1)}, u32[]{:S(2)}, u32[]{:S(2)}) collective-permute-start(f32[4,136,128]{2,1,0:T(8,128)S(1)} %pad_maximum_fusion.6), channel_id=1, source_target_pairs={{0,4},{1,5},{2,6},{3,7},{4,0},{5,1},{6,2},{7,3},{8,12},{9,13},{10,... | collective-permute-start | bytes 835592 | tf_op jit(solution)/shard_map/ppermute | solution.py:203
  39.8 6.9 %collective-permute-start.13 = (f32[1,256,128]{2,1,0:T(8,128)S(1)}, f32[1,256,128]{2,1,0:T(8,128)S(1)}, u32[]{:S(2)}, u32[]{:S(2)}) collective-permute-start(f32[1,256,128]{2,1,0:T(8,128)S(1)} %get-tuple-element.47), channel_id=1, source_target_pairs={{0,1},{1,0},{2,3},{3,2},{4,5},{5,4},{6,7},{7,6},{8,9},{9,8},{10,11... | collective-permute-start | bytes 393224 | tf_op jit(solution)/shard_map/ppermute | solution.py:203
  40.2 6.5 %collective-permute-start.14 = (f32[1,256,128]{2,1,0:T(8,128)S(1)}, f32[1,256,128]{2,1,0:T(8,128)S(1)}, u32[]{:S(2)}, u32[]{:S(2)}) collective-permute-start(f32[1,256,128]{2,1,0:T(8,128)S(1)} %get-tuple-element.45), channel_id=1, source_target_pairs={{0,2},{1,3},{2,0},{3,1},{4,6},{5,7},{6,4},{7,5},{8,10},{9,11},{10,... | collective-permute-start | bytes 393224 | tf_op jit(solution)/shard_map/ppermute | solution.py:203
  42.6 5.2 %collective-permute-start.17 = (f32[4,136,128]{2,1,0:T(8,128)S(1)}, f32[4,136,128]{2,1,0:T(8,128)S(1)}, u32[]{:S(2)}, u32[]{:S(2)}) collective-permute-start(f32[4,136,128]{2,1,0:T(8,128)S(1)} %pad_maximum_fusion.7.refs_0_), channel_id=1, source_target_pairs={{0,16},{16,0},{1,17},{17,1},{2,18},{18,2},{3,19},{19,3},{4,20},{20... | collective-permute-start | bytes 835592 | tf_op jit(solution)/shard_map/ppermute | solution.py:203
  43.9 3.8 %collective-permute-start.18 = (f32[4,136,128]{2,1,0:T(8,128)S(1)}, f32[4,136,128]{2,1,0:T(8,128)S(1)}, u32[]{:S(2)}, u32[]{:S(2)}) collective-permute-start(f32[4,136,128]{2,1,0:T(8,128)S(1)} %constant_dynamic-update-slice_fusion.2.refs_2_), channel_id=1, source_target_pairs={{0,16},{16,0},{1,17},{17,1},{2,18},{18,2},{3,19},{19,3},{4,20},{20... | collective-permute-start | bytes 835592 | tf_op jit(solution)/shard_map/ppermute | solution.py:203
  46.8 2.9 %collective-permute-start.15 = (f32[4,136,128]{2,1,0:T(8,128)S(1)}, f32[4,136,128]{2,1,0:T(8,128)S(1)}, u32[]{:S(2)}, u32[]{:S(2)}) collective-permute-start(f32[4,136,128]{2,1,0:T(8,128)S(1)} %collective-permute-done.12.refs_0_), channel_id=1, source_target_pairs={{0,16},{16,0},{1,17},{17,1},{2,18},{18,2},{3,19},{19,3},{4,20},{20... | collective-permute-start | bytes 835592 | tf_op jit(solution)/shard_map/ppermute | solution.py:203
  46.8 2.8 %collective-permute-start.16 = (f32[4,136,128]{2,1,0:T(8,128)S(1)}, f32[4,136,128]{2,1,0:T(8,128)S(1)}, u32[]{:S(2)}, u32[]{:S(2)}) collective-permute-start(f32[4,136,128]{2,1,0:T(8,128)S(1)} %constant_dynamic-update-slice_fusion.refs_2_), channel_id=1, source_target_pairs={{0,16},{16,0},{1,17},{17,1},{2,18},{18,2},{3,19},{19,3},{4,20},{20... | collective-permute-start | bytes 835592 | tf_op jit(solution)/shard_map/ppermute | solution.py:203

commit v18 on v17

--- a/solution.py
+++ b/solution.py
@@ -251,14 +251,15 @@
     pieces += [hop(late_y[:cut], 1), hop(late_x[cut:], 2)]
     positions = [tuple(p ^ step for p in at) for step in (0, 4, 1, 2, 5, 6)]
     positions += [tuple(p ^ step for p in part) for step in (3, 7) for part in (at[:cut], at[cut:])]
-    ends = (come_last, near[1:], pieces[-2], pieces[-1])
-    come_last, near[1:], pieces[-2], pieces[-1] = lax.optimization_barrier(ends)
-    groups = []
-    for planes in (near[:1], come_first, near[1:], come_last):
+    ends = (come_last, pieces[-2], pieces[-1])
+    come_last, pieces[-2], pieces[-1] = lax.optimization_barrier(ends)
+
+    def swap(planes):
         mine = jnp.concatenate(planes, axis=0)
-        groups.append(
-            [mine] + [send(mine, "row", lambda i: (i + q) % rows_axis) for q in range(1, rows_axis)]
-        )
+        others = [send(mine, "row", lambda i: (i + q) % rows_axis) for q in range(1, rows_axis)]
+        return [mine] + others
+
+    groups = [swap(planes) for planes in (near[:1], come_first, come_last)]
     if amplitudes.shape[1] != width:
         stacked = jnp.concatenate(pieces, axis=0)
         listed = [p for held in positions for p in held]
@@ -269,7 +270,8 @@
         pieces, positions = [stacked], [(None,) * KT]
     split_amplitudes = split(pieces, positions)
     early = contract(split_amplitudes, groups[:2], residual)
-    return contract(split_amplitudes, groups[2:], early)
+    last_near, early = lax.optimization_barrier((near[1:], early))
+    return contract(split_amplitudes, [groups[2], swap(last_near)], early)
 
 
 def solution(mesh):

time: 52.6 us -> 55.5 us (1.055)
  waiting for transfers between devices: 18.9 us -> 20.8 us
  starting transfers between devices: 24.4 us -> 25.4 us
    ppermute x19, waiting for transfers between devices: 18.9 us -> 20.8 us  [send(): return lax.ppermute(x, axis, [(i, partner(i)) for i in range(size)])]
    ppermute x19, starting transfers between devices: 24.4 us -> 25.4 us  [send(): return lax.ppermute(x, axis, [(i, partner(i)) for i in range(size)])]
  transfers between devices with their start and end apart: 19 -> 19, of which waited for: 9 -> 9; matrix products, arithmetic and copies ran while one was open for 3% -> 2% of each run, Pallas kernels for 7% -> 7%
where the time goes in v18:
time: 55.5 us; the launch traced here: 55.3 us
  starting transfers between devices  25.4 us (46%)
  waiting for transfers between devices  20.8 us (37%)
  Pallas kernels  6.48 us (12%)
  local copies, waits for them, and re-layouts  1.35 us (2%)
  other arithmetic  1.02 us (2%)
    ppermute x19, starting transfers between devices, send(): return lax.ppermute(x, axis, [(i, partner(i)) for i in range(size)])  25.4 us
    ppermute x19, waiting for transfers between devices, send(): return lax.ppermute(x, axis, [(i, partner(i)) for i in range(size)])  20.8 us
    pallas_call x2, Pallas kernels, contract(): pl.pallas_call(functools.partial(contract_kernel, len(groups), len(groups...  4.67 us
    pallas_call x1, Pallas kernels, pack(): pl.pallas_call(pack_kernel, out_shape=[out] * 4, in_specs=[pl.BlockSpec(m...  1.48 us
  transfers between devices with their start and end apart: 19, of which 9 were waited for; matrix products, arithmetic and copies ran while one was open for 2% of the time, Pallas kernels for 7%

profile of v18, /device:TPU:0, one launch (start us, length us, event | category | flops | bytes accessed | tf_op | source)
XLA Modules:
  0.0 55.3 jit_solution(13090974472239405312)
XLA Ops:
  0.0 0.0 copy-start
  0.0 4.0 %collective-permute-start = (f32[1,256,128]{2,1,0:T(8,128)}, f32[1,256,128]{2,1,0:T(8,128)S(1)}, u32[]{:S(2)}, u32[]{:S(2)}) collective-permute-start(f32[1,256,128]{2,1,0:T(8,128)} %bitcast.37), channel_id=1, source_target_pairs={{0,8},{1,9},{2,10},{3,11},{4,12},{5,13},{6,14},{7,15},{8,0},{9,1},... | collective-permute-start | bytes 393224 | tf_op jit(solution)/shard_map/ppermute | solution.py:203
  4.0 0.7 %fusion.1.words_ref = s32[16]{0:T(128)S(1)} fusion(s32[16]{0:T(128)} %param.11, s32[16]{0:T(128)} %param.10, s32[16,1]{0,1:T(1,128)} %param.9), kind=kLoop, calls=%fused_computation.31 | loop fusion | flops 64 | bytes 256 | tf_op jit(solution)/shard_map/add | solution.py:56
  4.7 0.0 copy-start.1
  4.7 1.0 %copy-done.1 = f32[16,64,128]{2,1,0:T(8,128)S(1)} copy-done((f32[16,64,128]{2,1,0:T(8,128)S(1)}, f32[16,64,128]{2,1,0:T(8,128)}, u32[]{:S(2)}) %copy-start.1) | copy-done | bytes 524312
  5.8 0.0 copy-start.2
  5.8 1.5 %shard_map.64 = (f32[4,136,128]{2,1,0:T(8,128)S(1)}, f32[4,136,128]{2,1,0:T(8,128)S(1)}, f32[4,136,128]{2,1,0:T(8,128)S(1)}, f32[4,136,128]{2,1,0:T(8,128)S(1)}) custom-call(s32[16]{0:T(128)S(1)} %fusion.1.words_ref, f32[16,64,128]{2,1,0:T(8,128)S(1)} %copy-done.1), custom_call_target="tpu_custom_call" | custom-call | bytes 1572864 | tf_op jit(solution)/shard_map/pallas_call | solution.py:58
  7.3 1.6 %collective-permute-start.4 = (f32[4,136,128]{2,1,0:T(8,128)S(1)}, f32[4,136,128]{2,1,0:T(8,128)S(1)}, u32[]{:S(2)}, u32[]{:S(2)}) collective-permute-start(f32[4,136,128]{2,1,0:T(8,128)S(1)} %get-tuple-element.25), channel_id=1, source_target_pairs={{0,1},{1,0},{2,3},{3,2},{4,5},{5,4},{6,7},{7,6},{8,9},{9,8},{10,11... | collective-permute-start | bytes 835592 | tf_op jit(solution)/shard_map/ppermute | solution.py:203
  8.8 1.5 %collective-permute-start.2 = (f32[4,136,128]{2,1,0:T(8,128)S(1)}, f32[4,136,128]{2,1,0:T(8,128)S(1)}, u32[]{:S(2)}, u32[]{:S(2)}) collective-permute-start(f32[4,136,128]{2,1,0:T(8,128)S(1)} %get-tuple-element.23), channel_id=1, source_target_pairs={{0,2},{1,3},{2,0},{3,1},{4,6},{5,7},{6,4},{7,5},{8,10},{9,11},{10,... | collective-permute-start | bytes 835592 | tf_op jit(solution)/shard_map/ppermute | solution.py:203
  10.4 0.0 copy-done
  10.4 0.1 shard_map.65.refs_4_
  10.5 0.1 collective-permute-done
  10.6 0.0 copy-done.2
  10.6 1.6 %collective-permute-start.1 = (f32[2,256,128]{2,1,0:T(8,128)S(1)}, f32[2,256,128]{2,1,0:T(8,128)S(1)}, u32[]{:S(2)}, u32[]{:S(2)}) collective-permute-start(f32[2,256,128]{2,1,0:T(8,128)S(1)} %pad_maximum_fusion.8.refs_0_), channel_id=1, source_target_pairs={{0,4},{1,5},{2,6},{3,7},{4,0},{5,1},{6,2},{7,3},{8,12},{9,13},{10,... | collective-permute-start | bytes 786440 | tf_op jit(solution)/shard_map/ppermute | solution.py:203
  12.2 3.3 %collective-permute-done.4 = f32[4,136,128]{2,1,0:T(8,128)S(1)} collective-permute-done((f32[4,136,128]{2,1,0:T(8,128)S(1)}, f32[4,136,128]{2,1,0:T(8,128)S(1)}, u32[]{:S(2)}, u32[]{:S(2)}) %collective-permute-start.4) | collective-permute-done | bytes 278560 | tf_op jit(solution)/shard_map/ppermute | solution.py:203
  15.5 1.2 %collective-permute-done.2 = f32[4,136,128]{2,1,0:T(8,128)S(1)} collective-permute-done((f32[4,136,128]{2,1,0:T(8,128)S(1)}, f32[4,136,128]{2,1,0:T(8,128)S(1)}, u32[]{:S(2)}, u32[]{:S(2)}) %collective-permute-start.2) | collective-permute-done | bytes 278560 | tf_op jit(solution)/shard_map/ppermute | solution.py:203
  16.7 0.1 pad_maximum_fusion
  16.8 0.6 %collective-permute-start.3 = (f32[1056,128]{1,0:T(8,128)S(1)}, f32[1056,128]{1,0:T(8,128)S(1)}, u32[]{:S(2)}, u32[]{:S(2)}) collective-permute-start(f32[1056,128]{1,0:T(8,128)S(1)} %get-tuple-element.62), channel_id=1, source_target_pairs={{0,1},{1,0},{2,3},{3,2},{4,5},{5,4},{6,7},{7,6},{8,9},{9,8},{10,11... | collective-permute-start | bytes 1622024 | tf_op jit(solution)/shard_map/ppermute | solution.py:203
  17.4 1.5 %collective-permute-start.5 = (f32[1056,128]{1,0:T(8,128)S(1)}, f32[1056,128]{1,0:T(8,128)S(1)}, u32[]{:S(2)}, u32[]{:S(2)}) collective-permute-start(f32[1056,128]{1,0:T(8,128)S(1)} %get-tuple-element.61), channel_id=1, source_target_pairs={{0,2},{1,3},{2,0},{3,1},{4,6},{5,7},{6,4},{7,5},{8,10},{9,11},{10,... | collective-permute-start | bytes 1622024 | tf_op jit(solution)/shard_map/ppermute | solution.py:203
  18.9 0.5 collective-permute-start.8
  19.4 3.6 %collective-permute-start.9 = (f32[2,136,128]{2,1,0:T(8,128)S(1)}, f32[2,136,128]{2,1,0:T(8,128)S(1)}, u32[]{:S(2)}, u32[]{:S(2)}) collective-permute-start(f32[2,136,128]{2,1,0:T(8,128)S(1)} %pad_maximum_fusion.14), channel_id=1, source_target_pairs={{0,12},{1,13},{2,14},{3,15},{4,8},{5,9},{6,10},{7,11},{8,4},{9,5},... | collective-permute-start | bytes 417800 | tf_op jit(solution)/shard_map/ppermute | solution.py:203
  23.0 6.3 %collective-permute-done.3 = f32[1056,128]{1,0:T(8,128)S(1)} collective-permute-done((f32[1056,128]{1,0:T(8,128)S(1)}, f32[1056,128]{1,0:T(8,128)S(1)}, u32[]{:S(2)}, u32[]{:S(2)}) %collective-permute-start.3) | collective-permute-done | bytes 540704 | tf_op jit(solution)/shard_map/ppermute | solution.py:203
  29.4 0.3 collective-permute-done.5
  29.7 0.0 collective-permute-done.1.refs_1_
  29.8 0.1 pad_maximum_fusion.2
  29.8 1.5 %collective-permute-start.6 = (f32[3,256,128]{2,1,0:T(8,128)S(1)}, f32[3,256,128]{2,1,0:T(8,128)S(1)}, u32[]{:S(2)}, u32[]{:S(2)}) collective-permute-start(f32[3,256,128]{2,1,0:T(8,128)S(1)} %get-tuple-element.60), channel_id=1, source_target_pairs={{0,1},{1,0},{2,3},{3,2},{4,5},{5,4},{6,7},{7,6},{8,9},{9,8},{10,11... | collective-permute-start | bytes 1179656 | tf_op jit(solution)/shard_map/ppermute | solution.py:203
  31.3 1.5 %collective-permute-start.7 = (f32[3,256,128]{2,1,0:T(8,128)S(1)}, f32[3,256,128]{2,1,0:T(8,128)S(1)}, u32[]{:S(2)}, u32[]{:S(2)}) collective-permute-start(f32[3,256,128]{2,1,0:T(8,128)S(1)} %get-tuple-element.59), channel_id=1, source_target_pairs={{0,2},{1,3},{2,0},{3,1},{4,6},{5,7},{6,4},{7,5},{8,10},{9,11},{10,... | collective-permute-start | bytes 1179656 | tf_op jit(solution)/shard_map/ppermute | solution.py:203
  32.9 0.0 collective-permute-done.8
  32.9 0.0 collective-permute-done.9
  32.9 0.6 %collective-permute-start.10 = (f32[2,136,128]{2,1,0:T(8,128)S(1)}, f32[2,136,128]{2,1,0:T(8,128)S(1)}, u32[]{:S(2)}, u32[]{:S(2)}) collective-permute-start(f32[2,136,128]{2,1,0:T(8,128)S(1)} %get-tuple-element.26), channel_id=1, source_target_pairs={{0,8},{1,9},{2,10},{3,11},{4,12},{5,13},{6,14},{7,15},{8,0},{9,1},... | collective-permute-start | bytes 417800 | tf_op jit(solution)/shard_map/ppermute | solution.py:203
  33.5 3.4 %collective-permute-start.11 = (f32[2,136,128]{2,1,0:T(8,128)S(1)}, f32[2,136,128]{2,1,0:T(8,128)S(1)}, u32[]{:S(2)}, u32[]{:S(2)}) collective-permute-start(f32[2,136,128]{2,1,0:T(8,128)S(1)} %get-tuple-element.27), channel_id=1, source_target_pairs={{0,12},{1,13},{2,14},{3,15},{4,8},{5,9},{6,10},{7,11},{8,4},{9,5},... | collective-permute-start | bytes 417800 | tf_op jit(solution)/shard_map/ppermute | solution.py:203
  36.9 0.1 collective-permute-start.16
  37.1 2.1 %collective-permute-done.7 = f32[3,256,128]{2,1,0:T(8,128)S(1)} collective-permute-done((f32[3,256,128]{2,1,0:T(8,128)S(1)}, f32[3,256,128]{2,1,0:T(8,128)S(1)}, u32[]{:S(2)}, u32[]{:S(2)}) %collective-permute-start.7) | collective-permute-done | bytes 393248 | tf_op jit(solution)/shard_map/ppermute | solution.py:203
  39.2 0.0 collective-permute-start.17
  39.2 0.0 collective-permute-done.6
  39.2 0.8 %collective-permute-start.12 = (f32[1,256,128]{2,1,0:T(8,128)S(1)}, f32[1,256,128]{2,1,0:T(8,128)S(1)}, u32[]{:S(2)}, u32[]{:S(2)}) collective-permute-start(f32[1,256,128]{2,1,0:T(8,128)S(1)} %get-tuple-element.49), channel_id=1, source_target_pairs={{0,1},{1,0},{2,3},{3,2},{4,5},{5,4},{6,7},{7,6},{8,9},{9,8},{10,11... | collective-permute-start | bytes 393224 | tf_op jit(solution)/shard_map/ppermute | solution.py:203
  40.0 3.5 %collective-permute-done.10 = f32[2,136,128]{2,1,0:T(8,128)S(1)} collective-permute-done((f32[2,136,128]{2,1,0:T(8,128)S(1)}, f32[2,136,128]{2,1,0:T(8,128)S(1)}, u32[]{:S(2)}, u32[]{:S(2)}) %collective-permute-start.10) | collective-permute-done | bytes 139296 | tf_op jit(solution)/shard_map/ppermute | solution.py:203
  43.5 0.5 collective-permute-start.13
  44.0 0.0 collective-permute-done.11
  44.1 1.5 %collective-permute-start.15 = (f32[4,136,128]{2,1,0:T(8,128)S(1)}, f32[4,136,128]{2,1,0:T(8,128)S(1)}, u32[]{:S(2)}, u32[]{:S(2)}) collective-permute-start(f32[4,136,128]{2,1,0:T(8,128)S(1)} %pad_maximum_fusion.6), channel_id=1, source_target_pairs={{0,4},{1,5},{2,6},{3,7},{4,0},{5,1},{6,2},{7,3},{8,12},{9,13},{10,... | collective-permute-start | bytes 835592 | tf_op jit(solution)/shard_map/ppermute | solution.py:203
  45.7 0.0 collective-permute-done.12.refs_8_
  45.7 2.8 %collective-permute-done.13.refs_9_ = f32[1,256,128]{2,1,0:T(8,128)S(1)} collective-permute-done((f32[1,256,128]{2,1,0:T(8,128)S(1)}, f32[1,256,128]{2,1,0:T(8,128)S(1)}, u32[]{:S(2)}, u32[]{:S(2)}) %collective-permute-start.13) | collective-permute-done | bytes 131104 | tf_op jit(solution)/shard_map/ppermute | solution.py:203
  48.5 0.1 collective-permute-start.14
  48.6 0.3 shard_map.66.split_ref
  48.9 0.0 collective-permute-done.16.refs_1_
  48.9 0.0 collective-permute-done.17.refs_3_
  48.9 1.9 %shard_map.67.refs_4_ = f32[256,1024]{1,0:T(8,128)S(1)} custom-call(bf16[16,256,256]{2,1,0:T(8,128)(2,1)S(1)} %shard_map.66.split_ref, f32[4,136,128]{2,1,0:T(8,128)S(1)} %pad_maximum_fusion.7.refs_0_, f32[4,136,128]{2,1,0:T(8,128)S(1)} %collective-permute-done.16.refs_1_, f32[4,136,128]{2,1,0:T(8,128)S(1)} %constant_dynamic-update-slice_fusion.2.refs_2_, ...), custom_call_target="tpu_custom_call" | custom-call | tf_op jit(solution)/shard_map/pallas_call | solution.py:173
  50.7 0.0 collective-permute-done.15.refs_2_
  50.8 0.6 %collective-permute-start.18 = (f32[4,136,128]{2,1,0:T(8,128)S(1)}, f32[4,136,128]{2,1,0:T(8,128)S(1)}, u32[]{:S(2)}, u32[]{:S(2)}) collective-permute-start(f32[4,136,128]{2,1,0:T(8,128)S(1)} %collective-permute-done.15.refs_2_), channel_id=1, source_target_pairs={{0,16},{16,0},{1,17},{17,1},{2,18},{18,2},{3,19},{19,3},{4,20},{20... | collective-permute-start | bytes 835592 | tf_op jit(solution)/shard_map/ppermute | solution.py:203
  51.3 0.0 collective-permute-done.14.refs_1_
  51.3 1.2 %collective-permute-done.18.refs_3_ = f32[4,136,128]{2,1,0:T(8,128)S(1)} collective-permute-done((f32[4,136,128]{2,1,0:T(8,128)S(1)}, f32[4,136,128]{2,1,0:T(8,128)S(1)}, u32[]{:S(2)}, u32[]{:S(2)}) %collective-permute-start.18) | collective-permute-done | bytes 278560 | tf_op jit(solution)/shard_map/ppermute | solution.py:203
  52.5 2.8 %shard_map.68 = f32[256,1024]{1,0:T(8,128)} custom-call(bf16[16,256,256]{2,1,0:T(8,128)(2,1)S(1)} %shard_map.66.split_ref, f32[4,136,128]{2,1,0:T(8,128)S(1)} %constant_dynamic-update-slice_fusion.refs_0_, f32[4,136,128]{2,1,0:T(8,128)S(1)} %collective-permute-done.14.refs_1_, f32[4,136,128]{2,1,0:T(8,128)S(1)} %collective-permute-done.15.refs_2_, ...), custom_call_target="tpu_custom_call" | custom-call | tf_op jit(solution)/shard_map/pallas_call | solution.py:173
  (31 shorter events, 0.5 us)
Async XLA Ops:
  0.0 10.4 %copy-start = (f32[256,1024]{1,0:T(8,128)S(1)}, f32[256,1024]{1,0:T(8,128)}, u32[]{:S(2)}) copy-start(f32[256,1024]{1,0:T(8,128)} %x_ref.1) | copy-start | bytes 3145732
  0.0 10.5 %collective-permute-start = (f32[1,256,128]{2,1,0:T(8,128)}, f32[1,256,128]{2,1,0:T(8,128)S(1)}, u32[]{:S(2)}, u32[]{:S(2)}) collective-permute-start(f32[1,256,128]{2,1,0:T(8,128)} %bitcast.37), channel_id=1, source_target_pairs={{0,8},{1,9},{2,10},{3,11},{4,12},{5,13},{6,14},{7,15},{8,0},{9,1},... | collective-permute-start | bytes 393224 | tf_op jit(solution)/shard_map/ppermute | solution.py:203
  4.7 1.0 %copy-start.1 = (f32[16,64,128]{2,1,0:T(8,128)S(1)}, f32[16,64,128]{2,1,0:T(8,128)}, u32[]{:S(2)}) copy-start(f32[16,64,128]{2,1,0:T(8,128)} %tiles_ref.1) | copy-start | bytes 1572868
  5.8 4.8 %copy-start.2 = (f32[256,128]{1,0:T(8,128)S(1)}, f32[256,128]{1,0:T(8,128)}, u32[]{:S(2)}) copy-start(f32[256,128]{1,0:T(8,128)} %param.7) | copy-start | bytes 393220
  7.3 8.2 %collective-permute-start.4 = (f32[4,136,128]{2,1,0:T(8,128)S(1)}, f32[4,136,128]{2,1,0:T(8,128)S(1)}, u32[]{:S(2)}, u32[]{:S(2)}) collective-permute-start(f32[4,136,128]{2,1,0:T(8,128)S(1)} %get-tuple-element.25), channel_id=1, source_target_pairs={{0,1},{1,0},{2,3},{3,2},{4,5},{5,4},{6,7},{7,6},{8,9},{9,8},{10,11... | collective-permute-start | bytes 835592 | tf_op jit(solution)/shard_map/ppermute | solution.py:203
  8.8 7.8 %collective-permute-start.2 = (f32[4,136,128]{2,1,0:T(8,128)S(1)}, f32[4,136,128]{2,1,0:T(8,128)S(1)}, u32[]{:S(2)}, u32[]{:S(2)}) collective-permute-start(f32[4,136,128]{2,1,0:T(8,128)S(1)} %get-tuple-element.23), channel_id=1, source_target_pairs={{0,2},{1,3},{2,0},{3,1},{4,6},{5,7},{6,4},{7,5},{8,10},{9,11},{10,... | collective-permute-start | bytes 835592 | tf_op jit(solution)/shard_map/ppermute | solution.py:203
  10.6 19.2 %collective-permute-start.1 = (f32[2,256,128]{2,1,0:T(8,128)S(1)}, f32[2,256,128]{2,1,0:T(8,128)S(1)}, u32[]{:S(2)}, u32[]{:S(2)}) collective-permute-start(f32[2,256,128]{2,1,0:T(8,128)S(1)} %pad_maximum_fusion.8.refs_0_), channel_id=1, source_target_pairs={{0,4},{1,5},{2,6},{3,7},{4,0},{5,1},{6,2},{7,3},{8,12},{9,13},{10,... | collective-permute-start | bytes 786440 | tf_op jit(solution)/shard_map/ppermute | solution.py:203
  16.8 12.6 %collective-permute-start.3 = (f32[1056,128]{1,0:T(8,128)S(1)}, f32[1056,128]{1,0:T(8,128)S(1)}, u32[]{:S(2)}, u32[]{:S(2)}) collective-permute-start(f32[1056,128]{1,0:T(8,128)S(1)} %get-tuple-element.62), channel_id=1, source_target_pairs={{0,1},{1,0},{2,3},{3,2},{4,5},{5,4},{6,7},{7,6},{8,9},{9,8},{10,11... | collective-permute-start | bytes 1622024 | tf_op jit(solution)/shard_map/ppermute | solution.py:203
  17.4 12.3 %collective-permute-start.5 = (f32[1056,128]{1,0:T(8,128)S(1)}, f32[1056,128]{1,0:T(8,128)S(1)}, u32[]{:S(2)}, u32[]{:S(2)}) collective-permute-start(f32[1056,128]{1,0:T(8,128)S(1)} %get-tuple-element.61), channel_id=1, source_target_pairs={{0,2},{1,3},{2,0},{3,1},{4,6},{5,7},{6,4},{7,5},{8,10},{9,11},{10,... | collective-permute-start | bytes 1622024 | tf_op jit(solution)/shard_map/ppermute | solution.py:203
  18.9 14.0 %collective-permute-start.8 = (f32[2,136,128]{2,1,0:T(8,128)S(1)}, f32[2,136,128]{2,1,0:T(8,128)S(1)}, u32[]{:S(2)}, u32[]{:S(2)}) collective-permute-start(f32[2,136,128]{2,1,0:T(8,128)S(1)} %pad_maximum_fusion.13), channel_id=1, source_target_pairs={{0,8},{1,9},{2,10},{3,11},{4,12},{5,13},{6,14},{7,15},{8,0},{9,1},... | collective-permute-start | bytes 417800 | tf_op jit(solution)/shard_map/ppermute | solution.py:203
  19.4 13.5 %collective-permute-start.9 = (f32[2,136,128]{2,1,0:T(8,128)S(1)}, f32[2,136,128]{2,1,0:T(8,128)S(1)}, u32[]{:S(2)}, u32[]{:S(2)}) collective-permute-start(f32[2,136,128]{2,1,0:T(8,128)S(1)} %pad_maximum_fusion.14), channel_id=1, source_target_pairs={{0,12},{1,13},{2,14},{3,15},{4,8},{5,9},{6,10},{7,11},{8,4},{9,5},... | collective-permute-start | bytes 417800 | tf_op jit(solution)/shard_map/ppermute | solution.py:203
  29.8 9.4 %collective-permute-start.6 = (f32[3,256,128]{2,1,0:T(8,128)S(1)}, f32[3,256,128]{2,1,0:T(8,128)S(1)}, u32[]{:S(2)}, u32[]{:S(2)}) collective-permute-start(f32[3,256,128]{2,1,0:T(8,128)S(1)} %get-tuple-element.60), channel_id=1, source_target_pairs={{0,1},{1,0},{2,3},{3,2},{4,5},{5,4},{6,7},{7,6},{8,9},{9,8},{10,11... | collective-permute-start | bytes 1179656 | tf_op jit(solution)/shard_map/ppermute | solution.py:203
  31.3 7.9 %collective-permute-start.7 = (f32[3,256,128]{2,1,0:T(8,128)S(1)}, f32[3,256,128]{2,1,0:T(8,128)S(1)}, u32[]{:S(2)}, u32[]{:S(2)}) collective-permute-start(f32[3,256,128]{2,1,0:T(8,128)S(1)} %get-tuple-element.59), channel_id=1, source_target_pairs={{0,2},{1,3},{2,0},{3,1},{4,6},{5,7},{6,4},{7,5},{8,10},{9,11},{10,... | collective-permute-start | bytes 1179656 | tf_op jit(solution)/shard_map/ppermute | solution.py:203
  32.9 10.6 %collective-permute-start.10 = (f32[2,136,128]{2,1,0:T(8,128)S(1)}, f32[2,136,128]{2,1,0:T(8,128)S(1)}, u32[]{:S(2)}, u32[]{:S(2)}) collective-permute-start(f32[2,136,128]{2,1,0:T(8,128)S(1)} %get-tuple-element.26), channel_id=1, source_target_pairs={{0,8},{1,9},{2,10},{3,11},{4,12},{5,13},{6,14},{7,15},{8,0},{9,1},... | collective-permute-start | bytes 417800 | tf_op jit(solution)/shard_map/ppermute | solution.py:203
  33.5 10.6 %collective-permute-start.11 = (f32[2,136,128]{2,1,0:T(8,128)S(1)}, f32[2,136,128]{2,1,0:T(8,128)S(1)}, u32[]{:S(2)}, u32[]{:S(2)}) collective-permute-start(f32[2,136,128]{2,1,0:T(8,128)S(1)} %get-tuple-element.27), channel_id=1, source_target_pairs={{0,12},{1,13},{2,14},{3,15},{4,8},{5,9},{6,10},{7,11},{8,4},{9,5},... | collective-permute-start | bytes 417800 | tf_op jit(solution)/shard_map/ppermute | solution.py:203
  36.9 11.9 %collective-permute-start.16 = (f32[4,136,128]{2,1,0:T(8,128)S(1)}, f32[4,136,128]{2,1,0:T(8,128)S(1)}, u32[]{:S(2)}, u32[]{:S(2)}) collective-permute-start(f32[4,136,128]{2,1,0:T(8,128)S(1)} %pad_maximum_fusion.7.refs_0_), channel_id=1, source_target_pairs={{0,16},{16,0},{1,17},{17,1},{2,18},{18,2},{3,19},{19,3},{4,20},{20... | collective-permute-start | bytes 835592 | tf_op jit(solution)/shard_map/ppermute | solution.py:203
  39.2 9.7 %collective-permute-start.17 = (f32[4,136,128]{2,1,0:T(8,128)S(1)}, f32[4,136,128]{2,1,0:T(8,128)S(1)}, u32[]{:S(2)}, u32[]{:S(2)}) collective-permute-start(f32[4,136,128]{2,1,0:T(8,128)S(1)} %constant_dynamic-update-slice_fusion.2.refs_2_), channel_id=1, source_target_pairs={{0,16},{16,0},{1,17},{17,1},{2,18},{18,2},{3,19},{19,3},{4,20},{20... | collective-permute-start | bytes 835592 | tf_op jit(solution)/shard_map/ppermute | solution.py:203
  39.2 6.5 %collective-permute-start.12 = (f32[1,256,128]{2,1,0:T(8,128)S(1)}, f32[1,256,128]{2,1,0:T(8,128)S(1)}, u32[]{:S(2)}, u32[]{:S(2)}) collective-permute-start(f32[1,256,128]{2,1,0:T(8,128)S(1)} %get-tuple-element.49), channel_id=1, source_target_pairs={{0,1},{1,0},{2,3},{3,2},{4,5},{5,4},{6,7},{7,6},{8,9},{9,8},{10,11... | collective-permute-start | bytes 393224 | tf_op jit(solution)/shard_map/ppermute | solution.py:203
  43.5 5.0 %collective-permute-start.13 = (f32[1,256,128]{2,1,0:T(8,128)S(1)}, f32[1,256,128]{2,1,0:T(8,128)S(1)}, u32[]{:S(2)}, u32[]{:S(2)}) collective-permute-start(f32[1,256,128]{2,1,0:T(8,128)S(1)} %get-tuple-element.47), channel_id=1, source_target_pairs={{0,2},{1,3},{2,0},{3,1},{4,6},{5,7},{6,4},{7,5},{8,10},{9,11},{10,... | collective-permute-start | bytes 393224 | tf_op jit(solution)/shard_map/ppermute | solution.py:203
  44.1 6.7 %collective-permute-start.15 = (f32[4,136,128]{2,1,0:T(8,128)S(1)}, f32[4,136,128]{2,1,0:T(8,128)S(1)}, u32[]{:S(2)}, u32[]{:S(2)}) collective-permute-start(f32[4,136,128]{2,1,0:T(8,128)S(1)} %pad_maximum_fusion.6), channel_id=1, source_target_pairs={{0,4},{1,5},{2,6},{3,7},{4,0},{5,1},{6,2},{7,3},{8,12},{9,13},{10,... | collective-permute-start | bytes 835592 | tf_op jit(solution)/shard_map/ppermute | solution.py:203
  48.5 2.8 %collective-permute-start.14 = (f32[4,136,128]{2,1,0:T(8,128)S(1)}, f32[4,136,128]{2,1,0:T(8,128)S(1)}, u32[]{:S(2)}, u32[]{:S(2)}) collective-permute-start(f32[4,136,128]{2,1,0:T(8,128)S(1)} %constant_dynamic-update-slice_fusion.refs_0_), channel_id=1, source_target_pairs={{0,16},{16,0},{1,17},{17,1},{2,18},{18,2},{3,19},{19,3},{4,20},{20... | collective-permute-start | bytes 835592 | tf_op jit(solution)/shard_map/ppermute | solution.py:203
  50.8 1.7 %collective-permute-start.18 = (f32[4,136,128]{2,1,0:T(8,128)S(1)}, f32[4,136,128]{2,1,0:T(8,128)S(1)}, u32[]{:S(2)}, u32[]{:S(2)}) collective-permute-start(f32[4,136,128]{2,1,0:T(8,128)S(1)} %collective-permute-done.15.refs_2_), channel_id=1, source_target_pairs={{0,16},{16,0},{1,17},{17,1},{2,18},{18,2},{3,19},{19,3},{4,20},{20... | collective-permute-start | bytes 835592 | tf_op jit(solution)/shard_map/ppermute | solution.py:203

commit v19 on v17

--- a/solution.py
+++ b/solution.py
@@ -240,8 +240,8 @@
     residual = fetch(residual_in)
     last, come_first, residual = lax.optimization_barrier((last, come_first, residual))
     near = [jnp.concatenate([first[z], last[z]]) for z in range(half)]
+    come_last = [hop(last[z], 4 * z) for z in range(half, 2 * half)]
     near = [near[0]] + [hop(plane, 4 * z) for z, plane in enumerate(near) if z]
-    come_last = [hop(last[z], 4 * z) for z in range(half, 2 * half)]
     cut = len(at) // 2
     come = hop(jnp.concatenate([late, over_y[:cut]]), 1)
     late_x, diagonal_x = come[: len(at)], come[len(at) :]
@@ -251,10 +251,10 @@
     pieces += [hop(late_y[:cut], 1), hop(late_x[cut:], 2)]
     positions = [tuple(p ^ step for p in at) for step in (0, 4, 1, 2, 5, 6)]
     positions += [tuple(p ^ step for p in part) for step in (3, 7) for part in (at[:cut], at[cut:])]
-    ends = (come_last, near[1:], pieces[-2], pieces[-1])
-    come_last, near[1:], pieces[-2], pieces[-1] = lax.optimization_barrier(ends)
+    ends = (near[1:], come_last, pieces[-2], pieces[-1])
+    near[1:], come_last, pieces[-2], pieces[-1] = lax.optimization_barrier(ends)
     groups = []
-    for planes in (near[:1], come_first, near[1:], come_last):
+    for planes in (near[:1], come_first, come_last, near[1:]):
         mine = jnp.concatenate(planes, axis=0)
         groups.append(
             [mine] + [send(mine, "row", lambda i: (i + q) % rows_axis) for q in range(1, rows_axis)]

time: 52.6 us -> 52.4 us (level)
  waiting for transfers between devices: 18.9 us -> 17.8 us
  starting transfers between devices: 24.4 us -> 25.3 us
    ppermute x19, waiting for transfers between devices: 18.9 us -> 17.8 us  [send(): return lax.ppermute(x, axis, [(i, partner(i)) for i in range(size)])]
    ppermute x19, starting transfers between devices: 24.4 us -> 25.3 us  [send(): return lax.ppermute(x, axis, [(i, partner(i)) for i in range(size)])]
  transfers between devices with their start and end apart: 19 -> 19, of which waited for: 9 -> 8; matrix products, arithmetic and copies ran while one was open for 3% -> 3% of each run, Pallas kernels for 7% -> 7%
where the time goes in v19:
time: 52.4 us; the launch traced here: 52.2 us
  starting transfers between devices  25.3 us (48%)
  waiting for transfers between devices  17.8 us (34%)
  Pallas kernels  6.48 us (12%)
  local copies, waits for them, and re-layouts  1.35 us (3%)
  other arithmetic  1.02 us (2%)
    ppermute x19, starting transfers between devices, send(): return lax.ppermute(x, axis, [(i, partner(i)) for i in range(size)])  25.3 us
    ppermute x19, waiting for transfers between devices, send(): return lax.ppermute(x, axis, [(i, partner(i)) for i in range(size)])  17.8 us
    pallas_call x2, Pallas kernels, contract(): pl.pallas_call(functools.partial(contract_kernel, len(groups), len(groups...  4.68 us
    pallas_call x1, Pallas kernels, pack(): pl.pallas_call(pack_kernel, out_shape=[out] * 4, in_specs=[pl.BlockSpec(m...  1.48 us
    unnamed x8, local copies, waits for them, and re-layouts  1.07 us
  transfers between devices with their start and end apart: 19, of which 8 were waited for; matrix products, arithmetic and copies ran while one was open for 3% of the time, Pallas kernels for 7%

profile of v19, /device:TPU:0, one launch (start us, length us, event | category | flops | bytes accessed | tf_op | source)
XLA Modules:
  0.0 52.2 jit_solution(8944079213990897740)
XLA Ops:
  0.0 0.0 copy-start
  0.0 4.0 %collective-permute-start = (f32[1,256,128]{2,1,0:T(8,128)}, f32[1,256,128]{2,1,0:T(8,128)S(1)}, u32[]{:S(2)}, u32[]{:S(2)}) collective-permute-start(f32[1,256,128]{2,1,0:T(8,128)} %bitcast.37), channel_id=1, source_target_pairs={{0,8},{1,9},{2,10},{3,11},{4,12},{5,13},{6,14},{7,15},{8,0},{9,1},... | collective-permute-start | bytes 393224 | tf_op jit(solution)/shard_map/ppermute | solution.py:203
  4.0 0.7 %fusion.1.words_ref = s32[16]{0:T(128)S(1)} fusion(s32[16]{0:T(128)} %param.11, s32[16]{0:T(128)} %param.10, s32[16,1]{0,1:T(1,128)} %param.9), kind=kLoop, calls=%fused_computation.31 | loop fusion | flops 64 | bytes 256 | tf_op jit(solution)/shard_map/add | solution.py:56
  4.7 0.0 copy-start.1
  4.7 1.0 %copy-done.1 = f32[16,64,128]{2,1,0:T(8,128)S(1)} copy-done((f32[16,64,128]{2,1,0:T(8,128)S(1)}, f32[16,64,128]{2,1,0:T(8,128)}, u32[]{:S(2)}) %copy-start.1) | copy-done | bytes 524312
  5.8 0.0 copy-start.2
  5.8 1.5 %shard_map.64 = (f32[4,136,128]{2,1,0:T(8,128)S(1)}, f32[4,136,128]{2,1,0:T(8,128)S(1)}, f32[4,136,128]{2,1,0:T(8,128)S(1)}, f32[4,136,128]{2,1,0:T(8,128)S(1)}) custom-call(s32[16]{0:T(128)S(1)} %fusion.1.words_ref, f32[16,64,128]{2,1,0:T(8,128)S(1)} %copy-done.1), custom_call_target="tpu_custom_call" | custom-call | bytes 1572864 | tf_op jit(solution)/shard_map/pallas_call | solution.py:58
  7.3 1.6 %collective-permute-start.4 = (f32[4,136,128]{2,1,0:T(8,128)S(1)}, f32[4,136,128]{2,1,0:T(8,128)S(1)}, u32[]{:S(2)}, u32[]{:S(2)}) collective-permute-start(f32[4,136,128]{2,1,0:T(8,128)S(1)} %get-tuple-element.24), channel_id=1, source_target_pairs={{0,1},{1,0},{2,3},{3,2},{4,5},{5,4},{6,7},{7,6},{8,9},{9,8},{10,11... | collective-permute-start | bytes 835592 | tf_op jit(solution)/shard_map/ppermute | solution.py:203
  8.8 1.5 %collective-permute-start.2 = (f32[4,136,128]{2,1,0:T(8,128)S(1)}, f32[4,136,128]{2,1,0:T(8,128)S(1)}, u32[]{:S(2)}, u32[]{:S(2)}) collective-permute-start(f32[4,136,128]{2,1,0:T(8,128)S(1)} %get-tuple-element.22), channel_id=1, source_target_pairs={{0,2},{1,3},{2,0},{3,1},{4,6},{5,7},{6,4},{7,5},{8,10},{9,11},{10,... | collective-permute-start | bytes 835592 | tf_op jit(solution)/shard_map/ppermute | solution.py:203
  10.4 0.0 copy-done
  10.4 0.1 shard_map.65.refs_4_
  10.5 0.1 collective-permute-done
  10.6 0.0 copy-done.2
  10.6 1.6 %collective-permute-start.1 = (f32[2,256,128]{2,1,0:T(8,128)S(1)}, f32[2,256,128]{2,1,0:T(8,128)S(1)}, u32[]{:S(2)}, u32[]{:S(2)}) collective-permute-start(f32[2,256,128]{2,1,0:T(8,128)S(1)} %pad_maximum_fusion.8.refs_0_), channel_id=1, source_target_pairs={{0,4},{1,5},{2,6},{3,7},{4,0},{5,1},{6,2},{7,3},{8,12},{9,13},{10,... | collective-permute-start | bytes 786440 | tf_op jit(solution)/shard_map/ppermute | solution.py:203
  12.2 3.3 %collective-permute-done.4 = f32[4,136,128]{2,1,0:T(8,128)S(1)} collective-permute-done((f32[4,136,128]{2,1,0:T(8,128)S(1)}, f32[4,136,128]{2,1,0:T(8,128)S(1)}, u32[]{:S(2)}, u32[]{:S(2)}) %collective-permute-start.4) | collective-permute-done | bytes 278560 | tf_op jit(solution)/shard_map/ppermute | solution.py:203
  15.5 1.2 %collective-permute-done.2 = f32[4,136,128]{2,1,0:T(8,128)S(1)} collective-permute-done((f32[4,136,128]{2,1,0:T(8,128)S(1)}, f32[4,136,128]{2,1,0:T(8,128)S(1)}, u32[]{:S(2)}, u32[]{:S(2)}) %collective-permute-start.2) | collective-permute-done | bytes 278560 | tf_op jit(solution)/shard_map/ppermute | solution.py:203
  16.7 0.1 pad_maximum_fusion
  16.8 0.6 %collective-permute-start.3 = (f32[1056,128]{1,0:T(8,128)S(1)}, f32[1056,128]{1,0:T(8,128)S(1)}, u32[]{:S(2)}, u32[]{:S(2)}) collective-permute-start(f32[1056,128]{1,0:T(8,128)S(1)} %get-tuple-element.60), channel_id=1, source_target_pairs={{0,1},{1,0},{2,3},{3,2},{4,5},{5,4},{6,7},{7,6},{8,9},{9,8},{10,11... | collective-permute-start | bytes 1622024 | tf_op jit(solution)/shard_map/ppermute | solution.py:203
  17.4 1.5 %collective-permute-start.5 = (f32[1056,128]{1,0:T(8,128)S(1)}, f32[1056,128]{1,0:T(8,128)S(1)}, u32[]{:S(2)}, u32[]{:S(2)}) collective-permute-start(f32[1056,128]{1,0:T(8,128)S(1)} %get-tuple-element.59), channel_id=1, source_target_pairs={{0,2},{1,3},{2,0},{3,1},{4,6},{5,7},{6,4},{7,5},{8,10},{9,11},{10,... | collective-permute-start | bytes 1622024 | tf_op jit(solution)/shard_map/ppermute | solution.py:203
  18.9 0.5 collective-permute-start.8
  19.4 3.6 %collective-permute-start.9 = (f32[2,136,128]{2,1,0:T(8,128)S(1)}, f32[2,136,128]{2,1,0:T(8,128)S(1)}, u32[]{:S(2)}, u32[]{:S(2)}) collective-permute-start(f32[2,136,128]{2,1,0:T(8,128)S(1)} %pad_maximum_fusion.14), channel_id=1, source_target_pairs={{0,12},{1,13},{2,14},{3,15},{4,8},{5,9},{6,10},{7,11},{8,4},{9,5},... | collective-permute-start | bytes 417800 | tf_op jit(solution)/shard_map/ppermute | solution.py:203
  23.0 6.3 %collective-permute-done.3 = f32[1056,128]{1,0:T(8,128)S(1)} collective-permute-done((f32[1056,128]{1,0:T(8,128)S(1)}, f32[1056,128]{1,0:T(8,128)S(1)}, u32[]{:S(2)}, u32[]{:S(2)}) %collective-permute-start.3) | collective-permute-done | bytes 540704 | tf_op jit(solution)/shard_map/ppermute | solution.py:203
  29.4 0.3 collective-permute-done.5
  29.7 0.0 collective-permute-done.1.refs_1_
  29.8 0.1 pad_maximum_fusion.2
  29.8 1.5 %collective-permute-start.6 = (f32[3,256,128]{2,1,0:T(8,128)S(1)}, f32[3,256,128]{2,1,0:T(8,128)S(1)}, u32[]{:S(2)}, u32[]{:S(2)}) collective-permute-start(f32[3,256,128]{2,1,0:T(8,128)S(1)} %get-tuple-element.58), channel_id=1, source_target_pairs={{0,1},{1,0},{2,3},{3,2},{4,5},{5,4},{6,7},{7,6},{8,9},{9,8},{10,11... | collective-permute-start | bytes 1179656 | tf_op jit(solution)/shard_map/ppermute | solution.py:203
  31.3 1.5 %collective-permute-start.7 = (f32[3,256,128]{2,1,0:T(8,128)S(1)}, f32[3,256,128]{2,1,0:T(8,128)S(1)}, u32[]{:S(2)}, u32[]{:S(2)}) collective-permute-start(f32[3,256,128]{2,1,0:T(8,128)S(1)} %get-tuple-element.57), channel_id=1, source_target_pairs={{0,2},{1,3},{2,0},{3,1},{4,6},{5,7},{6,4},{7,5},{8,10},{9,11},{10,... | collective-permute-start | bytes 1179656 | tf_op jit(solution)/shard_map/ppermute | solution.py:203
  32.9 0.0 collective-permute-done.8
  32.9 0.0 collective-permute-done.9
  33.0 1.6 %collective-permute-start.10 = (f32[4,136,128]{2,1,0:T(8,128)S(1)}, f32[4,136,128]{2,1,0:T(8,128)S(1)}, u32[]{:S(2)}, u32[]{:S(2)}) collective-permute-start(f32[4,136,128]{2,1,0:T(8,128)S(1)} %pad_maximum_fusion.6), channel_id=1, source_target_pairs={{0,4},{1,5},{2,6},{3,7},{4,0},{5,1},{6,2},{7,3},{8,12},{9,13},{10,... | collective-permute-start | bytes 835592 | tf_op jit(solution)/shard_map/ppermute | solution.py:203
  34.6 0.5 collective-permute-start.11
  35.1 2.3 %collective-permute-start.12 = (f32[2,136,128]{2,1,0:T(8,128)S(1)}, f32[2,136,128]{2,1,0:T(8,128)S(1)}, u32[]{:S(2)}, u32[]{:S(2)}) collective-permute-start(f32[2,136,128]{2,1,0:T(8,128)S(1)} %get-tuple-element.27), channel_id=1, source_target_pairs={{0,12},{1,13},{2,14},{3,15},{4,8},{5,9},{6,10},{7,11},{8,4},{9,5},... | collective-permute-start | bytes 417800 | tf_op jit(solution)/shard_map/ppermute | solution.py:203
  37.4 2.4 %collective-permute-done.7 = f32[3,256,128]{2,1,0:T(8,128)S(1)} collective-permute-done((f32[3,256,128]{2,1,0:T(8,128)S(1)}, f32[3,256,128]{2,1,0:T(8,128)S(1)}, u32[]{:S(2)}, u32[]{:S(2)}) %collective-permute-start.7) | collective-permute-done | bytes 393248 | tf_op jit(solution)/shard_map/ppermute | solution.py:203
  39.8 0.3 collective-permute-start.13
  40.2 0.0 collective-permute-done.6
  40.2 1.6 %collective-permute-start.14 = (f32[1,256,128]{2,1,0:T(8,128)S(1)}, f32[1,256,128]{2,1,0:T(8,128)S(1)}, u32[]{:S(2)}, u32[]{:S(2)}) collective-permute-start(f32[1,256,128]{2,1,0:T(8,128)S(1)} %get-tuple-element.45), channel_id=1, source_target_pairs={{0,2},{1,3},{2,0},{3,1},{4,6},{5,7},{6,4},{7,5},{8,10},{9,11},{10,... | collective-permute-start | bytes 393224 | tf_op jit(solution)/shard_map/ppermute | solution.py:203
  41.8 3.7 %collective-permute-done.11 = f32[2,136,128]{2,1,0:T(8,128)S(1)} collective-permute-done((f32[2,136,128]{2,1,0:T(8,128)S(1)}, f32[2,136,128]{2,1,0:T(8,128)S(1)}, u32[]{:S(2)}, u32[]{:S(2)}) %collective-permute-start.11) | collective-permute-done | bytes 139296 | tf_op jit(solution)/shard_map/ppermute | solution.py:203
  45.6 0.0 collective-permute-start.17
  45.6 0.0 collective-permute-done.12
  45.6 0.5 collective-permute-start.18
  46.1 0.0 collective-permute-done.10.refs_2_
  46.1 0.0 collective-permute-done.13.refs_8_
  46.1 0.0 collective-permute-done.14.refs_9_
  46.1 0.1 collective-permute-start.15
  46.2 0.5 collective-permute-start.16
  46.8 0.3 shard_map.66.split_ref
  47.1 0.0 collective-permute-done.17.refs_1_
  47.1 0.4 collective-permute-done.18.refs_3_
  47.5 1.9 %shard_map.67.refs_4_ = f32[256,1024]{1,0:T(8,128)S(1)} custom-call(bf16[16,256,256]{2,1,0:T(8,128)(2,1)S(1)} %shard_map.66.split_ref, f32[4,136,128]{2,1,0:T(8,128)S(1)} %pad_maximum_fusion.7.refs_0_, f32[4,136,128]{2,1,0:T(8,128)S(1)} %collective-permute-done.17.refs_1_, f32[4,136,128]{2,1,0:T(8,128)S(1)} %constant_dynamic-update-slice_fusion.2.refs_2_, ...), custom_call_target="tpu_custom_call" | custom-call | tf_op jit(solution)/shard_map/pallas_call | solution.py:173
  49.4 0.0 collective-permute-done.15.refs_1_
  49.4 0.0 collective-permute-done.16.refs_3_
  49.4 2.8 %shard_map.68 = f32[256,1024]{1,0:T(8,128)} custom-call(bf16[16,256,256]{2,1,0:T(8,128)(2,1)S(1)} %shard_map.66.split_ref, f32[4,136,128]{2,1,0:T(8,128)S(1)} %constant_dynamic-update-slice_fusion.refs_0_, f32[4,136,128]{2,1,0:T(8,128)S(1)} %collective-permute-done.15.refs_1_, f32[4,136,128]{2,1,0:T(8,128)S(1)} %collective-permute-done.10.refs_2_, ...), custom_call_target="tpu_custom_call" | custom-call | tf_op jit(solution)/shard_map/pallas_call | solution.py:173
  (31 shorter events, 0.5 us)
Async XLA Ops:
  0.0 10.4 %copy-start = (f32[256,1024]{1,0:T(8,128)S(1)}, f32[256,1024]{1,0:T(8,128)}, u32[]{:S(2)}) copy-start(f32[256,1024]{1,0:T(8,128)} %x_ref.1) | copy-start | bytes 3145732
  0.0 10.5 %collective-permute-start = (f32[1,256,128]{2,1,0:T(8,128)}, f32[1,256,128]{2,1,0:T(8,128)S(1)}, u32[]{:S(2)}, u32[]{:S(2)}) collective-permute-start(f32[1,256,128]{2,1,0:T(8,128)} %bitcast.37), channel_id=1, source_target_pairs={{0,8},{1,9},{2,10},{3,11},{4,12},{5,13},{6,14},{7,15},{8,0},{9,1},... | collective-permute-start | bytes 393224 | tf_op jit(solution)/shard_map/ppermute | solution.py:203
  4.7 1.0 %copy-start.1 = (f32[16,64,128]{2,1,0:T(8,128)S(1)}, f32[16,64,128]{2,1,0:T(8,128)}, u32[]{:S(2)}) copy-start(f32[16,64,128]{2,1,0:T(8,128)} %tiles_ref.1) | copy-start | bytes 1572868
  5.8 4.8 %copy-start.2 = (f32[256,128]{1,0:T(8,128)S(1)}, f32[256,128]{1,0:T(8,128)}, u32[]{:S(2)}) copy-start(f32[256,128]{1,0:T(8,128)} %param.7) | copy-start | bytes 393220
  7.3 8.2 %collective-permute-start.4 = (f32[4,136,128]{2,1,0:T(8,128)S(1)}, f32[4,136,128]{2,1,0:T(8,128)S(1)}, u32[]{:S(2)}, u32[]{:S(2)}) collective-permute-start(f32[4,136,128]{2,1,0:T(8,128)S(1)} %get-tuple-element.24), channel_id=1, source_target_pairs={{0,1},{1,0},{2,3},{3,2},{4,5},{5,4},{6,7},{7,6},{8,9},{9,8},{10,11... | collective-permute-start | bytes 835592 | tf_op jit(solution)/shard_map/ppermute | solution.py:203
  8.8 7.8 %collective-permute-start.2 = (f32[4,136,128]{2,1,0:T(8,128)S(1)}, f32[4,136,128]{2,1,0:T(8,128)S(1)}, u32[]{:S(2)}, u32[]{:S(2)}) collective-permute-start(f32[4,136,128]{2,1,0:T(8,128)S(1)} %get-tuple-element.22), channel_id=1, source_target_pairs={{0,2},{1,3},{2,0},{3,1},{4,6},{5,7},{6,4},{7,5},{8,10},{9,11},{10,... | collective-permute-start | bytes 835592 | tf_op jit(solution)/shard_map/ppermute | solution.py:203
  10.6 19.2 %collective-permute-start.1 = (f32[2,256,128]{2,1,0:T(8,128)S(1)}, f32[2,256,128]{2,1,0:T(8,128)S(1)}, u32[]{:S(2)}, u32[]{:S(2)}) collective-permute-start(f32[2,256,128]{2,1,0:T(8,128)S(1)} %pad_maximum_fusion.8.refs_0_), channel_id=1, source_target_pairs={{0,4},{1,5},{2,6},{3,7},{4,0},{5,1},{6,2},{7,3},{8,12},{9,13},{10,... | collective-permute-start | bytes 786440 | tf_op jit(solution)/shard_map/ppermute | solution.py:203
  16.8 12.6 %collective-permute-start.3 = (f32[1056,128]{1,0:T(8,128)S(1)}, f32[1056,128]{1,0:T(8,128)S(1)}, u32[]{:S(2)}, u32[]{:S(2)}) collective-permute-start(f32[1056,128]{1,0:T(8,128)S(1)} %get-tuple-element.60), channel_id=1, source_target_pairs={{0,1},{1,0},{2,3},{3,2},{4,5},{5,4},{6,7},{7,6},{8,9},{9,8},{10,11... | collective-permute-start | bytes 1622024 | tf_op jit(solution)/shard_map/ppermute | solution.py:203
  17.4 12.3 %collective-permute-start.5 = (f32[1056,128]{1,0:T(8,128)S(1)}, f32[1056,128]{1,0:T(8,128)S(1)}, u32[]{:S(2)}, u32[]{:S(2)}) collective-permute-start(f32[1056,128]{1,0:T(8,128)S(1)} %get-tuple-element.59), channel_id=1, source_target_pairs={{0,2},{1,3},{2,0},{3,1},{4,6},{5,7},{6,4},{7,5},{8,10},{9,11},{10,... | collective-permute-start | bytes 1622024 | tf_op jit(solution)/shard_map/ppermute | solution.py:203
  18.9 14.0 %collective-permute-start.8 = (f32[2,136,128]{2,1,0:T(8,128)S(1)}, f32[2,136,128]{2,1,0:T(8,128)S(1)}, u32[]{:S(2)}, u32[]{:S(2)}) collective-permute-start(f32[2,136,128]{2,1,0:T(8,128)S(1)} %pad_maximum_fusion.13), channel_id=1, source_target_pairs={{0,8},{1,9},{2,10},{3,11},{4,12},{5,13},{6,14},{7,15},{8,0},{9,1},... | collective-permute-start | bytes 417800 | tf_op jit(solution)/shard_map/ppermute | solution.py:203
  19.4 13.5 %collective-permute-start.9 = (f32[2,136,128]{2,1,0:T(8,128)S(1)}, f32[2,136,128]{2,1,0:T(8,128)S(1)}, u32[]{:S(2)}, u32[]{:S(2)}) collective-permute-start(f32[2,136,128]{2,1,0:T(8,128)S(1)} %pad_maximum_fusion.14), channel_id=1, source_target_pairs={{0,12},{1,13},{2,14},{3,15},{4,8},{5,9},{6,10},{7,11},{8,4},{9,5},... | collective-permute-start | bytes 417800 | tf_op jit(solution)/shard_map/ppermute | solution.py:203
  29.8 10.4 %collective-permute-start.6 = (f32[3,256,128]{2,1,0:T(8,128)S(1)}, f32[3,256,128]{2,1,0:T(8,128)S(1)}, u32[]{:S(2)}, u32[]{:S(2)}) collective-permute-start(f32[3,256,128]{2,1,0:T(8,128)S(1)} %get-tuple-element.58), channel_id=1, source_target_pairs={{0,1},{1,0},{2,3},{3,2},{4,5},{5,4},{6,7},{7,6},{8,9},{9,8},{10,11... | collective-permute-start | bytes 1179656 | tf_op jit(solution)/shard_map/ppermute | solution.py:203
  31.3 8.6 %collective-permute-start.7 = (f32[3,256,128]{2,1,0:T(8,128)S(1)}, f32[3,256,128]{2,1,0:T(8,128)S(1)}, u32[]{:S(2)}, u32[]{:S(2)}) collective-permute-start(f32[3,256,128]{2,1,0:T(8,128)S(1)} %get-tuple-element.57), channel_id=1, source_target_pairs={{0,2},{1,3},{2,0},{3,1},{4,6},{5,7},{6,4},{7,5},{8,10},{9,11},{10,... | collective-permute-start | bytes 1179656 | tf_op jit(solution)/shard_map/ppermute | solution.py:203
  33.0 13.1 %collective-permute-start.10 = (f32[4,136,128]{2,1,0:T(8,128)S(1)}, f32[4,136,128]{2,1,0:T(8,128)S(1)}, u32[]{:S(2)}, u32[]{:S(2)}) collective-permute-start(f32[4,136,128]{2,1,0:T(8,128)S(1)} %pad_maximum_fusion.6), channel_id=1, source_target_pairs={{0,4},{1,5},{2,6},{3,7},{4,0},{5,1},{6,2},{7,3},{8,12},{9,13},{10,... | collective-permute-start | bytes 835592 | tf_op jit(solution)/shard_map/ppermute | solution.py:203
  34.6 11.0 %collective-permute-start.11 = (f32[2,136,128]{2,1,0:T(8,128)S(1)}, f32[2,136,128]{2,1,0:T(8,128)S(1)}, u32[]{:S(2)}, u32[]{:S(2)}) collective-permute-start(f32[2,136,128]{2,1,0:T(8,128)S(1)} %get-tuple-element.26), channel_id=1, source_target_pairs={{0,8},{1,9},{2,10},{3,11},{4,12},{5,13},{6,14},{7,15},{8,0},{9,1},... | collective-permute-start | bytes 417800 | tf_op jit(solution)/shard_map/ppermute | solution.py:203
  35.1 10.5 %collective-permute-start.12 = (f32[2,136,128]{2,1,0:T(8,128)S(1)}, f32[2,136,128]{2,1,0:T(8,128)S(1)}, u32[]{:S(2)}, u32[]{:S(2)}) collective-permute-start(f32[2,136,128]{2,1,0:T(8,128)S(1)} %get-tuple-element.27), channel_id=1, source_target_pairs={{0,12},{1,13},{2,14},{3,15},{4,8},{5,9},{6,10},{7,11},{8,4},{9,5},... | collective-permute-start | bytes 417800 | tf_op jit(solution)/shard_map/ppermute | solution.py:203
  39.8 6.2 %collective-permute-start.13 = (f32[1,256,128]{2,1,0:T(8,128)S(1)}, f32[1,256,128]{2,1,0:T(8,128)S(1)}, u32[]{:S(2)}, u32[]{:S(2)}) collective-permute-start(f32[1,256,128]{2,1,0:T(8,128)S(1)} %get-tuple-element.47), channel_id=1, source_target_pairs={{0,1},{1,0},{2,3},{3,2},{4,5},{5,4},{6,7},{7,6},{8,9},{9,8},{10,11... | collective-permute-start | bytes 393224 | tf_op jit(solution)/shard_map/ppermute | solution.py:203
  40.2 5.9 %collective-permute-start.14 = (f32[1,256,128]{2,1,0:T(8,128)S(1)}, f32[1,256,128]{2,1,0:T(8,128)S(1)}, u32[]{:S(2)}, u32[]{:S(2)}) collective-permute-start(f32[1,256,128]{2,1,0:T(8,128)S(1)} %get-tuple-element.45), channel_id=1, source_target_pairs={{0,2},{1,3},{2,0},{3,1},{4,6},{5,7},{6,4},{7,5},{8,10},{9,11},{10,... | collective-permute-start | bytes 393224 | tf_op jit(solution)/shard_map/ppermute | solution.py:203
  45.6 1.6 %collective-permute-start.17 = (f32[4,136,128]{2,1,0:T(8,128)S(1)}, f32[4,136,128]{2,1,0:T(8,128)S(1)}, u32[]{:S(2)}, u32[]{:S(2)}) collective-permute-start(f32[4,136,128]{2,1,0:T(8,128)S(1)} %pad_maximum_fusion.7.refs_0_), channel_id=1, source_target_pairs={{0,16},{16,0},{1,17},{17,1},{2,18},{18,2},{3,19},{19,3},{4,20},{20... | collective-permute-start | bytes 835592 | tf_op jit(solution)/shard_map/ppermute | solution.py:203
  45.6 2.0 %collective-permute-start.18 = (f32[4,136,128]{2,1,0:T(8,128)S(1)}, f32[4,136,128]{2,1,0:T(8,128)S(1)}, u32[]{:S(2)}, u32[]{:S(2)}) collective-permute-start(f32[4,136,128]{2,1,0:T(8,128)S(1)} %constant_dynamic-update-slice_fusion.2.refs_2_), channel_id=1, source_target_pairs={{0,16},{16,0},{1,17},{17,1},{2,18},{18,2},{3,19},{19,3},{4,20},{20... | collective-permute-start | bytes 835592 | tf_op jit(solution)/shard_map/ppermute | solution.py:203
  46.1 3.3 %collective-permute-start.15 = (f32[4,136,128]{2,1,0:T(8,128)S(1)}, f32[4,136,128]{2,1,0:T(8,128)S(1)}, u32[]{:S(2)}, u32[]{:S(2)}) collective-permute-start(f32[4,136,128]{2,1,0:T(8,128)S(1)} %constant_dynamic-update-slice_fusion.refs_0_), channel_id=1, source_target_pairs={{0,16},{16,0},{1,17},{17,1},{2,18},{18,2},{3,19},{19,3},{4,20},{20... | collective-permute-start | bytes 835592 | tf_op jit(solution)/shard_map/ppermute | solution.py:203
  46.2 3.2 %collective-permute-start.16 = (f32[4,136,128]{2,1,0:T(8,128)S(1)}, f32[4,136,128]{2,1,0:T(8,128)S(1)}, u32[]{:S(2)}, u32[]{:S(2)}) collective-permute-start(f32[4,136,128]{2,1,0:T(8,128)S(1)} %collective-permute-done.10.refs_2_), channel_id=1, source_target_pairs={{0,16},{16,0},{1,17},{17,1},{2,18},{18,2},{3,19},{19,3},{4,20},{20... | collective-permute-start | bytes 835592 | tf_op jit(solution)/shard_map/ppermute | solution.py:203
